TPU v7x, 32 devices: a whole 2x2x4 slice. The times are simulated.
32 devices in a mesh: ctx: 8 (over y, x, core), fsdp: 4 (over z).
Axes of the slice: x: 2, y: 2, z: 4, core: 2. Of those that a mesh axis runs over, the one named last changes fastest.
Arguments:
- enc_input: bfloat16 [8, 1024, 768], P('fsdp', 'ctx'), may hold values from -6 to 6
- dec_input: bfloat16 [8, 1024, 768], P('fsdp', 'ctx'), may hold values from -6 to 6
- segments: int32 [8, 1024], P('fsdp', 'ctx'), may hold values from 0 to 7, never falling along the last dimension, each value on 1 to 512 neighbouring positions
- prefix_rows: int32 [8, 8, 20], P('fsdp'), may hold values from 0 to 255
- buckets: int32 [2048], replicated, may hold values from 0 to 31
- memory: bfloat16 [256, 1536], P('fsdp'), may hold values from -3 to 3
- enc_gain: bfloat16 [768], P('fsdp'), may hold values from 0.5 to 1.5
- enc_qkv: bfloat16 [768, 2304], P('fsdp'), may hold values from -0.09375 to 0.09375
- enc_rel: bfloat16 [32, 12], P('fsdp'), may hold values from -3 to 3
- enc_proj: bfloat16 [768, 768], P('fsdp'), may hold values from -1 to 1
- enc_ffnorm: bfloat16 [768], P('fsdp'), may hold values from 0.5 to 1.5
- enc_ffin: bfloat16 [768, 3072], P('fsdp'), may hold values from -0.21875 to 0.21875
- enc_ffout: bfloat16 [3072, 768], P('fsdp'), may hold values from -0.15625 to 0.15625
- dec_gain: bfloat16 [768], P('fsdp'), may hold values from 0.5 to 1.5
- dec_qkv: bfloat16 [768, 2304], P('fsdp'), may hold values from -0.09375 to 0.09375
- dec_rel: bfloat16 [32, 12], P('fsdp'), may hold values from -3 to 3
- dec_proj: bfloat16 [768, 768], P('fsdp'), may hold values from -1 to 1
- cross_gain: bfloat16 [768], P('fsdp'), may hold values from 0.5 to 1.5
- cross_query: bfloat16 [768, 768], P('fsdp'), may hold values from -0.09375 to 0.09375
- cross_kv: bfloat16 [768, 1536], P('fsdp'), may hold values from -0.0625 to 0.0625
- cross_proj: bfloat16 [768, 768], P('fsdp'), may hold values from -1 to 1
- dec_ffnorm: bfloat16 [768], P('fsdp'), may hold values from 0.5 to 1.5
- dec_ffin: bfloat16 [768, 3072], P('fsdp'), may hold values from -0.21875 to 0.21875
- dec_ffout: bfloat16 [3072, 768], P('fsdp'), may hold values from -0.15625 to 0.15625
- enc_cotan: bfloat16 [8, 1024, 768], P('fsdp', 'ctx'), may hold values from -6 to 6
- dec_cotan: bfloat16 [8, 1024, 768], P('fsdp', 'ctx'), may hold values from -6 to 6
Outputs:
- enc_output: bfloat16 [8, 1024, 768], P('fsdp', 'ctx')
- dec_output: bfloat16 [8, 1024, 768], P('fsdp', 'ctx')
- enc_ingrad: float32 [8, 1024, 768], P('fsdp', 'ctx')
- dec_ingrad: float32 [8, 1024, 768], P('fsdp', 'ctx')
- memory_grad: float32 [256, 1536], P('fsdp')
- genc_gain: float32 [768], P('fsdp')
- genc_qkv: float32 [768, 2304], P('fsdp')
- genc_rel: float32 [32, 12], P('fsdp')
- genc_proj: float32 [768, 768], P('fsdp')
- genc_ffnorm: float32 [768], P('fsdp')
- genc_ffin: float32 [768, 3072], P('fsdp')
- genc_ffout: float32 [3072, 768], P('fsdp')
- gdec_gain: float32 [768], P('fsdp')
- gdec_qkv: float32 [768, 2304], P('fsdp')
- gdec_rel: float32 [32, 12], P('fsdp')
- gdec_proj: float32 [768, 768], P('fsdp')
- gcross_gain: float32 [768], P('fsdp')
- gcross_query: float32 [768, 768], P('fsdp')
- gcross_kv: float32 [768, 1536], P('fsdp')
- gcross_proj: float32 [768, 768], P('fsdp')
- gdec_ffnorm: float32 [768], P('fsdp')
- gdec_ffin: float32 [768, 3072], P('fsdp')
- gdec_ffout: float32 [3072, 768], P('fsdp')
All inputs are finite; a program needn't handle non-finite values.
Results may differ from a plain program's by a relative error of at most 0.035.
Values may be sent and summed in bfloat16 or wider, within the bound.
A program may use at most 448 MiB of HBM per device.

v0:
```python
import jax
import jax.numpy as jnp
from jax import lax
from jax.sharding import PartitionSpec as P

D = 768
HEADS = 12
BUCKETS = 32
PREFIX = 20


epsilon = 1e-06
masked = -1e30
per_step = 4


def rms_norm(values, gains):
    return values * lax.rsqrt(jnp.mean(values * values, axis=-1, keepdims=True) + epsilon) * gains


def smooth_act(values):
    return jax.nn.gelu(values, approximate=True)


def smooth_back(pre_act, grad_rows):
    return jax.vjp(smooth_act, pre_act)[1](grad_rows)[0]


def matmul(former, latter):
    return jnp.dot(former, latter, preferred_element_type=jnp.float32)


def matmul_tn(former, latter):
    return lax.dot_general(
        former, latter, (((0,), (0,)), ((), ())), preferred_element_type=jnp.float32
    )


def matmul_nt(former, latter):
    return lax.dot_general(
        former, latter, (((1,), (1,)), ((), ())), preferred_element_type=jnp.float32
    )


def to_groups(values, groups):
    return values.reshape(values.shape[0], groups, -1).transpose(1, 0, 2)


def from_groups(values):
    return values.transpose(1, 0, 2).reshape(values.shape[1], -1)


def split_rel(rel_table, groups):
    if rel_table is None:
        return None
    return rel_table.reshape(rel_table.shape[0], groups, per_step).transpose(1, 0, 2)


def merge_rel(rel_table):
    return rel_table.transpose(1, 0, 2).reshape(rel_table.shape[1], -1)


def split_memory(mem_rows, offset, groups):
    if mem_rows is None:
        return None
    sliced = mem_rows[:, :, offset : offset + D]
    return sliced.reshape(sliced.shape[0], sliced.shape[1], groups, -1).transpose(2, 0, 1, 3)


def merge_memory(values):
    return values.transpose(1, 2, 0, 3).reshape(values.shape[1], values.shape[2], -1)


def split_heads(values):
    return values.reshape(values.shape[0], per_step, -1)


def split_memory_heads(values):
    return values.reshape(values.shape[0], values.shape[1], per_step, -1)


def bias_rows(onehot, rel_part):
    if rel_part is None:
        return None
    return jnp.einsum("qbk,bh->hqk", onehot, rel_part, preferred_element_type=jnp.float32)


def head_scores(query_heads, key_heads, rel_bias, allowed):
    scores = jnp.einsum("qhd,khd->hqk", query_heads, key_heads, preferred_element_type=jnp.float32)
    if rel_bias is not None:
        scores = scores + rel_bias
    return jnp.where(allowed[None], scores, masked)


def attention_forward(queries, kv_rows, allowed, onehot, rel_table, mem_rows):
    groups = HEADS // per_step
    members = (
        to_groups(queries, groups),
        to_groups(kv_rows[:, :D], groups),
        to_groups(kv_rows[:, D:], groups),
        split_rel(rel_table, groups),
        split_memory(mem_rows, 0, groups),
        split_memory(mem_rows, D, groups),
    )

    def one_group(member):
        query_part, key_part, value_part, rel_part, memkey_part, memval_part = member
        row_count = query_part.shape[0]
        query_heads = split_heads(query_part)
        scores = head_scores(
            query_heads, split_heads(key_part), bias_rows(onehot, rel_part), allowed
        )
        row_max = jnp.max(scores, axis=-1)
        if memkey_part is not None:
            mem_scores = jnp.einsum(
                "qhd,qphd->hqp",
                query_heads,
                split_memory_heads(memkey_part),
                preferred_element_type=jnp.float32,
            )
            row_max = jnp.maximum(row_max, jnp.max(mem_scores, axis=-1))
        exp_scores = jnp.exp(scores - row_max[..., None])
        row_sum = jnp.sum(exp_scores, axis=-1)
        if memkey_part is not None:
            mem_exp = jnp.exp(mem_scores - row_max[..., None])
            row_sum = row_sum + jnp.sum(mem_exp, axis=-1)
        weights = (exp_scores / row_sum[..., None]).astype(jnp.bfloat16)
        result = jnp.einsum(
            "hqk,khd->qhd", weights, split_heads(value_part), preferred_element_type=jnp.float32
        )
        if memkey_part is not None:
            mem_weights = (mem_exp / row_sum[..., None]).astype(jnp.bfloat16)
            result = result + jnp.einsum(
                "hqp,qphd->qhd",
                mem_weights,
                split_memory_heads(memval_part),
                preferred_element_type=jnp.float32,
            )
        return (result.reshape(row_count, -1), row_max + jnp.log(row_sum))

    results, log_sums = lax.map(one_group, members)
    return (from_groups(results), log_sums)


def attention_backward(grad_rows, queries, kv_rows, log_sums, allowed, onehot, rel_table, mem_rows):
    groups = HEADS // per_step
    members = (
        to_groups(grad_rows, groups),
        to_groups(queries, groups),
        to_groups(kv_rows[:, :D], groups),
        to_groups(kv_rows[:, D:], groups),
        log_sums,
        split_rel(rel_table, groups),
        split_memory(mem_rows, 0, groups),
        split_memory(mem_rows, D, groups),
    )

    def one_group(member):
        (
            grad_part,
            query_part,
            key_part,
            value_part,
            lse_part,
            rel_part,
            memkey_part,
            memval_part,
        ) = member
        row_count = query_part.shape[0]
        grad_heads = split_heads(grad_part)
        query_heads = split_heads(query_part)
        key_heads = split_heads(key_part)
        value_heads = split_heads(value_part)
        prob_rows = jnp.exp(
            head_scores(query_heads, key_heads, bias_rows(onehot, rel_part), allowed)
            - lse_part[..., None]
        )
        prob_grad = jnp.einsum(
            "qhd,khd->hqk", grad_heads, value_heads, preferred_element_type=jnp.float32
        )
        row_dot = jnp.sum(prob_rows * prob_grad, axis=-1)
        if memkey_part is not None:
            mem_keys = split_memory_heads(memkey_part)
            mem_values = split_memory_heads(memval_part)
            mem_probs = jnp.exp(
                jnp.einsum(
                    "qhd,qphd->hqp", query_heads, mem_keys, preferred_element_type=jnp.float32
                )
                - lse_part[..., None]
            )
            mem_grad = jnp.einsum(
                "qhd,qphd->hqp", grad_heads, mem_values, preferred_element_type=jnp.float32
            )
            row_dot = row_dot + jnp.sum(mem_probs * mem_grad, axis=-1)
        score_grad = (prob_rows * (prob_grad - row_dot[..., None])).astype(jnp.bfloat16)
        query_grad = jnp.einsum(
            "hqk,khd->qhd", score_grad, key_heads, preferred_element_type=jnp.float32
        )
        key_grad = None
        value_grad = None
        key_grad = jnp.einsum(
            "hqk,qhd->khd", score_grad, query_heads, preferred_element_type=jnp.float32
        )
        key_grad = key_grad.reshape(key_grad.shape[0], -1)
        value_grad = jnp.einsum(
            "hqk,qhd->khd",
            prob_rows.astype(jnp.bfloat16),
            grad_heads,
            preferred_element_type=jnp.float32,
        )
        value_grad = value_grad.reshape(value_grad.shape[0], -1)
        rel_grad = None
        if rel_part is not None:
            rel_grad = jnp.einsum(
                "hqk,qbk->bh", score_grad, onehot, preferred_element_type=jnp.float32
            )
        memkey_grad = None
        memval_grad = None
        if memkey_part is not None:
            mem_score_grad = (mem_probs * (mem_grad - row_dot[..., None])).astype(jnp.bfloat16)
            query_grad = query_grad + jnp.einsum(
                "hqp,qphd->qhd", mem_score_grad, mem_keys, preferred_element_type=jnp.float32
            )
            memkey_grad = jnp.einsum(
                "hqp,qhd->qphd", mem_score_grad, query_heads, preferred_element_type=jnp.float32
            ).reshape(row_count, PREFIX, -1)
            memval_grad = jnp.einsum(
                "hqp,qhd->qphd",
                mem_probs.astype(jnp.bfloat16),
                grad_heads,
                preferred_element_type=jnp.float32,
            ).reshape(row_count, PREFIX, -1)
        return (
            query_grad.reshape(row_count, -1),
            key_grad,
            value_grad,
            rel_grad,
            memkey_grad,
            memval_grad,
            row_dot,
        )

    query_grad, key_grad, value_grad, rel_grad, memkey_grad, memval_grad, row_dots = lax.map(
        one_group, members
    )
    kv_grad = None
    kv_grad = jnp.concatenate([from_groups(key_grad), from_groups(value_grad)], axis=1)
    rel_total = None
    if rel_grad is not None:
        rel_total = merge_rel(rel_grad)
    mem_total = None
    if memkey_grad is not None:
        mem_total = jnp.concatenate([merge_memory(memkey_grad), merge_memory(memval_grad)], axis=-1)
    return (from_groups(query_grad), kv_grad, rel_total, mem_total, row_dots)


def fetch_keys(kv_rows, seg_rows):
    return (
        lax.all_gather(kv_rows, "ctx", axis=0, tiled=True),
        lax.all_gather(seg_rows, "ctx", axis=0, tiled=True),
    )


def backward_keys(kv_rows):
    return lax.all_gather(kv_rows, "ctx", axis=0, tiled=True)


def attention_back(grad_rows, queries, kv_rows, log_sums, allowed, onehot, rel_table, mem_rows):
    keys_back = backward_keys(kv_rows)
    query_grad, kv_grad, rel_grad, mem_grad, row_dots = attention_backward(
        grad_rows, queries, keys_back, log_sums, allowed, onehot, rel_table, mem_rows
    )
    return (
        query_grad,
        lax.psum_scatter(kv_grad, "ctx", scatter_dimension=0, tiled=True),
        rel_grad,
        mem_grad,
    )


def feed_forward_back(upstream, normed, active, pre_act, w_in, w_out, back_norm):
    out_grad = upstream.astype(jnp.bfloat16)
    grad_out = matmul_tn(active, out_grad)
    pre_grad = smooth_back(pre_act, matmul_nt(out_grad, w_out)).astype(jnp.bfloat16)
    grad_in = matmul_tn(normed, pre_grad)
    back_rows, grad_gain = back_norm(matmul_nt(pre_grad, w_in))
    return (upstream + back_rows, grad_gain, grad_in, grad_out)


def per_device(
    enc_input,
    dec_input,
    segments,
    prefix_rows,
    buckets,
    memory,
    enc_gain,
    enc_qkv,
    enc_rel,
    enc_proj,
    enc_ffnorm,
    enc_ffin,
    enc_ffout,
    dec_gain,
    dec_qkv,
    dec_rel,
    dec_proj,
    cross_gain,
    cross_query,
    cross_kv,
    cross_proj,
    dec_ffnorm,
    dec_ffin,
    dec_ffout,
    enc_cotan,
    dec_cotan,
):
    shards = (
        memory,
        enc_gain,
        enc_qkv,
        enc_rel,
        enc_proj,
        enc_ffnorm,
        enc_ffin,
        enc_ffout,
        dec_gain,
        dec_qkv,
        dec_rel,
        dec_proj,
        cross_gain,
        cross_query,
        cross_kv,
        cross_proj,
        dec_ffnorm,
        dec_ffin,
        dec_ffout,
    )
    length = buckets.shape[0] // 2
    tokens = enc_input.shape[1]
    places = lax.axis_index("ctx") * tokens + jnp.arange(tokens, dtype=jnp.int32)
    key_places = jnp.arange(length, dtype=jnp.int32)
    bucket_ids = jnp.arange(BUCKETS, dtype=jnp.int32)
    rel_index = jnp.take(buckets, key_places[None, :] - places[:, None] + length)
    rel_onehot = (rel_index[:, None, :] == bucket_ids[None, :, None]).astype(jnp.bfloat16)
    before = key_places[None, :] <= places[:, None]
    fsdp_size = lax.axis_size("fsdp")
    totals = [
        jnp.zeros((weight_shard.shape[0] * fsdp_size,) + weight_shard.shape[1:], jnp.float32)
        for weight_shard in shards
    ]
    enc_outputs = []
    dec_outputs = []
    enc_grads = []
    dec_grads = []
    for micro_step in range(enc_input.shape[0]):
        gathered = (
            lax.all_gather(memory, "fsdp", axis=0, tiled=True),
            lax.all_gather(enc_gain, "fsdp", axis=0, tiled=True),
            lax.all_gather(enc_qkv, "fsdp", axis=0, tiled=True),
            lax.all_gather(enc_rel, "fsdp", axis=0, tiled=True),
            lax.all_gather(enc_proj, "fsdp", axis=0, tiled=True),
            lax.all_gather(enc_ffnorm, "fsdp", axis=0, tiled=True),
            lax.all_gather(enc_ffin, "fsdp", axis=0, tiled=True),
            lax.all_gather(enc_ffout, "fsdp", axis=0, tiled=True),
            lax.all_gather(dec_gain, "fsdp", axis=0, tiled=True),
            lax.all_gather(dec_qkv, "fsdp", axis=0, tiled=True),
            lax.all_gather(dec_rel, "fsdp", axis=0, tiled=True),
            lax.all_gather(dec_proj, "fsdp", axis=0, tiled=True),
            lax.all_gather(cross_gain, "fsdp", axis=0, tiled=True),
            lax.all_gather(cross_query, "fsdp", axis=0, tiled=True),
            lax.all_gather(cross_kv, "fsdp", axis=0, tiled=True),
            lax.all_gather(cross_proj, "fsdp", axis=0, tiled=True),
            lax.all_gather(dec_ffnorm, "fsdp", axis=0, tiled=True),
            lax.all_gather(dec_ffin, "fsdp", axis=0, tiled=True),
            lax.all_gather(dec_ffout, "fsdp", axis=0, tiled=True),
        )
        (
            w_memory,
            w_egain,
            w_eqkv,
            w_erel,
            w_eproj,
            w_effnorm,
            w_effin,
            w_effout,
            w_dgain,
            w_dqkv,
            w_drel,
            w_dproj,
            w_cgain,
            w_cquery,
            w_ckv,
            w_cproj,
            w_dffnorm,
            w_dffin,
            w_dffout,
        ) = gathered
        seg_rows = segments[micro_step]
        mem_index = jnp.take(prefix_rows[micro_step], seg_rows, axis=0)
        mem_rows = jnp.take(w_memory, mem_index, axis=0)
        enc_rows = enc_input[micro_step].astype(jnp.float32)
        normed, back_enorm = jax.vjp(rms_norm, enc_rows, w_egain.astype(jnp.float32))
        enc_normed = normed.astype(jnp.bfloat16)
        enc_projected = matmul(enc_normed, w_eqkv).astype(jnp.bfloat16)
        enc_keys, key_segs = fetch_keys(enc_projected[:, D:], seg_rows)
        same_doc = seg_rows[:, None] == key_segs[None, :]
        causal = same_doc & before
        enc_att, enc_lse = attention_forward(
            enc_projected[:, :D], enc_keys, same_doc, rel_onehot, w_erel, mem_rows
        )
        enc_attended = enc_att.astype(jnp.bfloat16)
        enc_mid = enc_rows + matmul(enc_attended, w_eproj)
        normed, back_effnorm = jax.vjp(rms_norm, enc_mid, w_effnorm.astype(jnp.float32))
        enc_ffnormed = normed.astype(jnp.bfloat16)
        enc_pre = matmul(enc_ffnormed, w_effin)
        enc_active = smooth_act(enc_pre).astype(jnp.bfloat16)
        enc_result = enc_mid + matmul(enc_active, w_effout)
        enc_low = enc_result.astype(jnp.bfloat16)
        dec_rows = dec_input[micro_step].astype(jnp.float32)
        normed, back_dnorm = jax.vjp(rms_norm, dec_rows, w_dgain.astype(jnp.float32))
        dec_normed = normed.astype(jnp.bfloat16)
        dec_projected = matmul(dec_normed, w_dqkv).astype(jnp.bfloat16)
        dec_keys = fetch_keys(dec_projected[:, D:], seg_rows)[0]
        dec_att, dec_lse = attention_forward(
            dec_projected[:, :D], dec_keys, causal, rel_onehot, w_drel, None
        )
        dec_attended = dec_att.astype(jnp.bfloat16)
        dec_mid = dec_rows + matmul(dec_attended, w_dproj)
        normed, back_cnorm = jax.vjp(rms_norm, dec_mid, w_cgain.astype(jnp.float32))
        cross_normed = normed.astype(jnp.bfloat16)
        cross_queries = matmul(cross_normed, w_cquery).astype(jnp.bfloat16)
        cross_rows = matmul(enc_low, w_ckv).astype(jnp.bfloat16)
        cross_keys = fetch_keys(cross_rows, seg_rows)[0]
        cross_att, cross_lse = attention_forward(
            cross_queries, cross_keys, same_doc, None, None, None
        )
        cross_attended = cross_att.astype(jnp.bfloat16)
        dec_cross = dec_mid + matmul(cross_attended, w_cproj)
        normed, back_dffnorm = jax.vjp(rms_norm, dec_cross, w_dffnorm.astype(jnp.float32))
        dec_ffnormed = normed.astype(jnp.bfloat16)
        dec_pre = matmul(dec_ffnormed, w_dffin)
        dec_active = smooth_act(dec_pre).astype(jnp.bfloat16)
        dec_result = dec_cross + matmul(dec_active, w_dffout)
        enc_outputs.append(enc_low)
        dec_outputs.append(dec_result.astype(jnp.bfloat16))
        upstream = dec_cotan[micro_step].astype(jnp.float32)
        upstream, g_dffnorm, g_dffin, g_dffout = feed_forward_back(
            upstream, dec_ffnormed, dec_active, dec_pre, w_dffin, w_dffout, back_dffnorm
        )
        out_grad = upstream.astype(jnp.bfloat16)
        g_cproj = matmul_tn(cross_attended, out_grad)
        att_grad = matmul_nt(out_grad, w_cproj).astype(jnp.bfloat16)
        results = attention_back(
            att_grad, cross_queries, cross_rows, cross_lse, same_doc, None, None, None
        )
        kv_low = results[1].astype(jnp.bfloat16)
        g_ckv = matmul_tn(enc_low, kv_low)
        enc_extra = matmul_nt(kv_low, w_ckv)
        query_low = results[0].astype(jnp.bfloat16)
        g_cquery = matmul_tn(cross_normed, query_low)
        back_rows, g_cgain = back_cnorm(matmul_nt(query_low, w_cquery))
        upstream = upstream + back_rows
        out_grad = upstream.astype(jnp.bfloat16)
        g_dproj = matmul_tn(dec_attended, out_grad)
        att_grad = matmul_nt(out_grad, w_dproj).astype(jnp.bfloat16)
        results = attention_back(
            att_grad,
            dec_projected[:, :D],
            dec_projected[:, D:],
            dec_lse,
            causal,
            rel_onehot,
            w_drel,
            None,
        )
        qkv_low = jnp.concatenate([results[0], results[1]], axis=1).astype(jnp.bfloat16)
        g_drel = results[2]
        g_dqkv = matmul_tn(dec_normed, qkv_low)
        back_rows, g_dgain = back_dnorm(matmul_nt(qkv_low, w_dqkv))
        dec_grads.append(upstream + back_rows)
        upstream = enc_cotan[micro_step].astype(jnp.float32) + enc_extra
        upstream, g_effnorm, g_effin, g_effout = feed_forward_back(
            upstream, enc_ffnormed, enc_active, enc_pre, w_effin, w_effout, back_effnorm
        )
        out_grad = upstream.astype(jnp.bfloat16)
        g_eproj = matmul_tn(enc_attended, out_grad)
        att_grad = matmul_nt(out_grad, w_eproj).astype(jnp.bfloat16)
        results = attention_back(
            att_grad,
            enc_projected[:, :D],
            enc_projected[:, D:],
            enc_lse,
            same_doc,
            rel_onehot,
            w_erel,
            mem_rows,
        )
        qkv_low = jnp.concatenate([results[0], results[1]], axis=1).astype(jnp.bfloat16)
        g_erel = results[2]
        g_memory = jax.ops.segment_sum(
            results[3].reshape(-1, 2 * D), mem_index.reshape(-1), num_segments=w_memory.shape[0]
        )
        g_eqkv = matmul_tn(enc_normed, qkv_low)
        back_rows, g_egain = back_enorm(matmul_nt(qkv_low, w_eqkv))
        enc_grads.append(upstream + back_rows)
        pieces = [
            g_memory,
            g_egain,
            g_eqkv,
            g_erel,
            g_eproj,
            g_effnorm,
            g_effin,
            g_effout,
            g_dgain,
            g_dqkv,
            g_drel,
            g_dproj,
            g_cgain,
            g_cquery,
            g_ckv,
            g_cproj,
            g_dffnorm,
            g_dffin,
            g_dffout,
        ]
        totals = [total + piece_grad for total, piece_grad in zip(totals, pieces)]
    local = (
        lax.psum_scatter(totals[0], "fsdp", scatter_dimension=0, tiled=True),
        lax.psum_scatter(totals[1], "fsdp", scatter_dimension=0, tiled=True),
        lax.psum_scatter(totals[2], "fsdp", scatter_dimension=0, tiled=True),
        lax.psum_scatter(totals[3], "fsdp", scatter_dimension=0, tiled=True),
        lax.psum_scatter(totals[4], "fsdp", scatter_dimension=0, tiled=True),
        lax.psum_scatter(totals[5], "fsdp", scatter_dimension=0, tiled=True),
        lax.psum_scatter(totals[6], "fsdp", scatter_dimension=0, tiled=True),
        lax.psum_scatter(totals[7], "fsdp", scatter_dimension=0, tiled=True),
        lax.psum_scatter(totals[8], "fsdp", scatter_dimension=0, tiled=True),
        lax.psum_scatter(totals[9], "fsdp", scatter_dimension=0, tiled=True),
        lax.psum_scatter(totals[10], "fsdp", scatter_dimension=0, tiled=True),
        lax.psum_scatter(totals[11], "fsdp", scatter_dimension=0, tiled=True),
        lax.psum_scatter(totals[12], "fsdp", scatter_dimension=0, tiled=True),
        lax.psum_scatter(totals[13], "fsdp", scatter_dimension=0, tiled=True),
        lax.psum_scatter(totals[14], "fsdp", scatter_dimension=0, tiled=True),
        lax.psum_scatter(totals[15], "fsdp", scatter_dimension=0, tiled=True),
        lax.psum_scatter(totals[16], "fsdp", scatter_dimension=0, tiled=True),
        lax.psum_scatter(totals[17], "fsdp", scatter_dimension=0, tiled=True),
        lax.psum_scatter(totals[18], "fsdp", scatter_dimension=0, tiled=True),
    )
    summed = lax.psum(
        (
            local[0],
            local[1],
            local[2],
            local[3],
            local[4],
            local[5],
            local[6],
            local[7],
            local[8],
            local[9],
            local[10],
            local[11],
            local[12],
            local[13],
            local[14],
            local[15],
            local[16],
            local[17],
            local[18],
        ),
        "ctx",
    )
    return (
        jnp.stack(enc_outputs),
        jnp.stack(dec_outputs),
        jnp.stack(enc_grads),
        jnp.stack(dec_grads),
        summed[0],
        summed[1],
        summed[2],
        summed[3],
        summed[4],
        summed[5],
        summed[6],
        summed[7],
        summed[8],
        summed[9],
        summed[10],
        summed[11],
        summed[12],
        summed[13],
        summed[14],
        summed[15],
        summed[16],
        summed[17],
        summed[18],
    )


def solution(mesh):
    placed = (
        P("fsdp", "ctx", None),
        P("fsdp", "ctx", None),
        P("fsdp", "ctx"),
        P("fsdp", None, None),
        P(),
        P("fsdp", None),
        P("fsdp"),
        P("fsdp", None),
        P("fsdp", None),
        P("fsdp", None),
        P("fsdp"),
        P("fsdp", None),
        P("fsdp", None),
        P("fsdp"),
        P("fsdp", None),
        P("fsdp", None),
        P("fsdp", None),
        P("fsdp"),
        P("fsdp", None),
        P("fsdp", None),
        P("fsdp", None),
        P("fsdp"),
        P("fsdp", None),
        P("fsdp", None),
        P("fsdp", "ctx", None),
        P("fsdp", "ctx", None),
    )
    return jax.shard_map(
        per_device,
        mesh=mesh,
        in_specs=placed,
        out_specs=(
            P("fsdp", "ctx", None),
            P("fsdp", "ctx", None),
            P("fsdp", "ctx", None),
            P("fsdp", "ctx", None),
            P("fsdp", None),
            P("fsdp"),
            P("fsdp", None),
            P("fsdp", None),
            P("fsdp", None),
            P("fsdp"),
            P("fsdp", None),
            P("fsdp", None),
            P("fsdp"),
            P("fsdp", None),
            P("fsdp", None),
            P("fsdp", None),
            P("fsdp"),
            P("fsdp", None),
            P("fsdp", None),
            P("fsdp", None),
            P("fsdp"),
            P("fsdp", None),
            P("fsdp", None),
        ),
        check_vma=False,
    )
```

profile of v0, /device:TPU:0, one launch (start us, length us, event | category | flops | bytes accessed | tf_op | source)
XLA Modules:
  0.0 3686.9 jit_solution(17893730507598198631)
XLA Ops:
  14.9 21.7 all-reduce.15
  37.9 44.7 %all-gather.20.cloned.1.call-done = bf16[768,2304]{1,0:T(8,128)(2,1)} async-done(((bf16[192,2304]{1,0:T(8,128)(2,1)}), bf16[768,2304]{1,0:T(8,128)(2,1)}) %all-gather.20.cloned.1.call-update) | async-done | bytes 3538960 | tf_op jit(solution)/shard_map/all_gather | solution.py:360
  95.1 57.7 %all-gather.32.cloned.1.call-done = bf16[768,2304]{1,0:T(8,128)(2,1)} async-done(((bf16[192,2304]{1,0:T(8,128)(2,1)}), bf16[768,2304]{1,0:T(8,128)(2,1)}) %all-gather.32.cloned.1.call-update) | async-done | bytes 3538960 | tf_op jit(solution)/shard_map/all_gather | solution.py:367
  158.6 17.7 all_gather.111
  177.9 9.6 gather_fusion.4
  187.4 12.5 reshape.1212
  202.3 9.6 gather_fusion.2
  211.9 12.4 reshape.1206
  224.3 8.2 broadcast_select_fusion
  232.5 8.2 broadcast_select_fusion.1
  240.7 8.1 fusion.347
  248.8 12.1 all_gather.110
  284.2 724.9 %gather_fusion = s32[131072]{0:T(1024)S(1)} fusion(s32[2048]{0:T(1024)S(1)} %copy-done, s32[131072]{0:T(1024)S(1)} %broadcast_clamp_fusion), kind=kCustom, calls=%fused_computation.4 | custom fusion | bytes 1572864 | tf_op jit(solution)/shard_map/jit(_take)/gather | solution.py:344
  1041.1 8.7 all-gather.1
  1049.8 8.7 all-gather
  1076.1 35.5 while.185
  1130.8 35.6 while.184
  1181.5 11.9 all_gather.121
  1201.5 20.6 while.188
  1234.7 23.2 while.186
  1268.0 12.6 while.189
  1294.4 16.2 while.187
  1314.1 16.3 all-gather.46.cloned.1.call-done
  1334.9 84.8 %all-gather.48.cloned.1.call-done = bf16[3072,768]{1,0:T(8,128)(2,1)} async-done(((bf16[768,768]{1,0:T(8,128)(2,1)}), bf16[3072,768]{1,0:T(8,128)(2,1)}) %all-gather.48.cloned.1.call-update) | async-done | bytes 4718608 | tf_op jit(solution)/shard_map/all_gather | solution.py:376
  1441.2 28.6 while.190
  1486.0 22.3 while.192
  1527.7 118.0 %while.195 = (s32[]{:T(128)}, bf16[3,128,256]{1,2,0:T(8,128)(2,1)S(1)}, f32[3,1024,256]{1,2,0:T(8,128)}, f32[3,1024,256]{1,2,0:T(8,128)}, f32[3,32,4]{1,2,0:T(4,...) while((s32[]{:T(128)}, ...), condition=%wide.region_71.74_spmd.clone, body=%wide.region_69.73_spmd.clone.sunk | while | flops 424541696 | bytes 74926360 | solution.py:243
  1538.3 14.1 copy.444
  1578.6 13.7 copy.444
  1617.5 13.6 copy.444
  1657.0 117.2 %while.194 = (s32[]{:T(128)}, bf16[3,128,256]{1,2,0:T(8,128)(2,1)S(1)}, f32[3,1024,256]{1,2,0:T(8,128)}, f32[3,1024,256]{1,2,0:T(8,128)}, f32[3,32,4]{1,2,0:T(4,...) while((s32[]{:T(128)}, ...), condition=%wide.region_65.68_spmd.clone, body=%wide.region_63.67_spmd.clone.sunk | while | flops 424541696 | bytes 74926360 | solution.py:243
  1667.9 13.9 copy.442
  1707.2 13.6 copy.442
  1746.0 13.6 copy.442
  1817.6 141.7 %while.193 = (s32[]{:T(128)}, bf16[3,128,256]{1,2,0:T(8,128)(2,1)}, f32[3,1024,256]{1,2,0:T(8,128)}, f32[3,1024,256]{1,2,0:T(8,128)}, f32[3,32,4]{1,2,0:T(4,128)...) while((s32[]{:T(128)}, bf16[3,128,256]{1,2,0:T(8,128)(2,1)}, ...), condition=%wide.region_59.62_spmd.clone, body=%wide.region_56.61_spmd.clone.sunk | while | flops 431744512 | bytes 101916584 | solution.py:243
  1829.4 13.8 copy.440
  1876.8 13.6 copy.440
  1923.8 13.6 copy.440
  1982.7 141.8 %while.191 = (s32[]{:T(128)}, bf16[3,128,256]{1,2,0:T(8,128)(2,1)}, f32[3,1024,256]{1,2,0:T(8,128)}, f32[3,1024,256]{1,2,0:T(8,128)}, f32[3,32,4]{1,2,0:T(4,128)...) while((s32[]{:T(128)}, bf16[3,128,256]{1,2,0:T(8,128)(2,1)}, ...), condition=%wide.region_47.50_spmd.clone, body=%wide.region_44.49_spmd.clone.sunk | while | flops 431744512 | bytes 101916584 | solution.py:243
  1994.8 13.6 copy.438
  2041.9 13.6 copy.438
  2089.0 13.6 copy.438
  2142.7 11.8 copy.296
  2154.5 9.4 copy.387
  2164.0 11.5 copy.295
  2175.4 9.1 copy.386
  2184.5 11.6 copy.298
  2196.2 9.0 copy.389
  2205.2 11.6 copy.297
  2216.8 9.1 copy.388
  2225.9 28.0 scatter_custom_fusion
  2253.8 27.7 scatter_custom_fusion.1
  2344.0 37.5 %reduce-scatter.33.cloned.1.call-done = f32[64,1536]{1,0:T(8,128)} async-done(((f32[256,1536]{1,0:T(8,128)}), f32[64,1536]{1,0:T(8,128)}) %reduce-scatter.33.cloned.1.call-update) | async-done | bytes 393232 | tf_op jit(solution)/shard_map/reduce_scatter | solution.py:530
  2381.6 49.9 %reduce-scatter.37.cloned.1.call-done = f32[192,768]{1,0:T(8,128)} async-done(((f32[768,768]{1,0:T(8,128)}), f32[192,768]{1,0:T(8,128)}) %reduce-scatter.37.cloned.1.call-update) | async-done | bytes 589840 | tf_op jit(solution)/shard_map/reduce_scatter | solution.py:534
  2431.5 163.2 %reduce-scatter.53.cloned.1.call-done = f32[192,3072]{1,0:T(8,128)} async-done(((f32[768,3072]{1,0:T(8,128)}), f32[192,3072]{1,0:T(8,128)}) %reduce-scatter.53.cloned.1.call-update) | async-done | bytes 2359312 | tf_op jit(solution)/shard_map/reduce_scatter | solution.py:547
  2594.6 164.4 %reduce-scatter.55.cloned.1.call-done = f32[768,768]{1,0:T(8,128)} async-done(((f32[3072,768]{1,0:T(8,128)}), f32[768,768]{1,0:T(8,128)}) %reduce-scatter.55.cloned.1.call-update) | async-done | bytes 2359312 | tf_op jit(solution)/shard_map/reduce_scatter | solution.py:548
  2759.0 88.4 %reduce-scatter.49.cloned.1.call-done = f32[192,1536]{1,0:T(8,128)} async-done(((f32[768,1536]{1,0:T(8,128)}), f32[192,1536]{1,0:T(8,128)}) %reduce-scatter.49.cloned.1.call-update) | async-done | bytes 1179664 | tf_op jit(solution)/shard_map/reduce_scatter | solution.py:544
  2847.4 126.4 %reduce-scatter.43.cloned.1.call-done = f32[192,2304]{1,0:T(8,128)} async-done(((f32[768,2304]{1,0:T(8,128)}), f32[192,2304]{1,0:T(8,128)}) %reduce-scatter.43.cloned.1.call-update) | async-done | bytes 1769488 | tf_op jit(solution)/shard_map/reduce_scatter | solution.py:539
  2973.8 164.0 %reduce-scatter.39.cloned.1.call-done = f32[192,3072]{1,0:T(8,128)} async-done(((f32[768,3072]{1,0:T(8,128)}), f32[192,3072]{1,0:T(8,128)}) %reduce-scatter.39.cloned.1.call-update) | async-done | bytes 2359312 | tf_op jit(solution)/shard_map/reduce_scatter | solution.py:536
  3137.8 164.5 %reduce-scatter.41.cloned.1.call-done = f32[768,768]{1,0:T(8,128)} async-done(((f32[3072,768]{1,0:T(8,128)}), f32[768,768]{1,0:T(8,128)}) %reduce-scatter.41.cloned.1.call-update) | async-done | bytes 2359312 | tf_op jit(solution)/shard_map/reduce_scatter | solution.py:537
  3302.3 126.7 %reduce-scatter.35.cloned.1.call-done = f32[192,2304]{1,0:T(8,128)} async-done(((f32[768,2304]{1,0:T(8,128)}), f32[192,2304]{1,0:T(8,128)}) %reduce-scatter.35.cloned.1.call-update) | async-done | bytes 1769488 | tf_op jit(solution)/shard_map/reduce_scatter | solution.py:532
  3453.3 18.6 all-reduce.14
  3472.3 24.5 all-reduce.12
  3499.4 161.4 %all-reduce.18.cloned.1.call-done = (f32[64,1536]{1,0:T(8,128)}, f32[192,2304]{1,0:T(8,128)}, f32[192,768]{1,0:T(8,128)}, f32[192,3072]{1,0:T(8,128)}, f32[768,7...) async-done(((f32[64,1536]{1,0:T(8,128)}, ...) | async-done | bytes 16908304 | tf_op jit(solution)/shard_map/psum | solution.py:550
  (1564 shorter events, 993.6 us)
Async XLA Ops:
  7.2 277.0 %copy-start = (s32[2048]{0:T(1024)S(1)}, s32[2048]{0:T(1024)}, u32[]{:S(2)}) copy-start(s32[2048]{0:T(1024)} %param.58) | copy-start | bytes 24580
  7.2 29.4 copy-start.36
  7.2 75.4 %all-gather.20.cloned.1.call-start = ((), (), s32[]{:S(2)}) async-start(), calls=%async_computation.18 | async-start | bytes 4423680 | tf_op jit(solution)/shard_map/all_gather | solution.py:360
  8.0 144.9 %all-gather.32.cloned.1.call-start = ((), (), s32[]{:S(2)}) async-start(), calls=%async_computation.24 | async-start | bytes 4423680 | tf_op jit(solution)/shard_map/all_gather | solution.py:367
  8.7 1061.3 %all-gather.30.cloned.1.call-start = ((), (), s32[]{:S(2)}) async-start(), calls=%async_computation.23 | async-start | bytes 3538944 | tf_op jit(solution)/shard_map/all_gather | solution.py:259
  36.6 51.3 %copy-start.165 = (f32[768]{0:T(1024)}, f32[768]{0:T(1024)S(1)}, u32[]{:S(2)}) copy-start(f32[768]{0:T(1024)S(1)} %convert_element_type.355) | copy-start | bytes 9220
  37.9 47.7 %copy-start.220 = (f32[128]{0:T(128)}, f32[128]{0:T(128)S(1)}, u32[]{:S(2)}) copy-start(f32[128]{0:T(128)S(1)} %fusion.319) | copy-start | bytes 1540
  87.2 1025.0 %all-gather.22.cloned.1.call-start = ((), (), s32[]{:S(2)}) async-start(), calls=%async_computation.19 | async-start | bytes 3538944 | tf_op jit(solution)/shard_map/all_gather | solution.py:259
  91.2 1026.4 %all-gather.24.cloned.1.call-start = ((), (), s32[]{:S(2)}) async-start(), calls=%async_computation.20 | async-start | bytes 1474560 | tf_op jit(solution)/shard_map/all_gather | solution.py:362
  91.7 1027.6 %all-gather.26.cloned.1.call-start = ((), (), s32[]{:S(2)}) async-start(), calls=%async_computation.21 | async-start | bytes 5898240 | tf_op jit(solution)/shard_map/all_gather | solution.py:364
  92.3 1030.3 %all-gather.28.cloned.1.call-start = ((), (), s32[]{:S(2)}) async-start(), calls=%async_computation.22 | async-start | bytes 5898240 | tf_op jit(solution)/shard_map/all_gather | solution.py:365
  93.1 1033.6 %all-gather.38.cloned.1.call-start = ((), (), s32[]{:S(2)}) async-start(), calls=%async_computation.27 | async-start | bytes 2949120 | tf_op jit(solution)/shard_map/all_gather | solution.py:372
  93.8 1101.8 %all-gather.50.cloned.1.call-start = ((), (), s32[]{:S(2)}) async-start(), calls=%async_computation.33 | async-start | bytes 3538944 | tf_op jit(solution)/shard_map/all_gather | solution.py:259
  93.9 61.7 %copy-start.167 = (f32[768]{0:T(1024)}, f32[768]{0:T(1024)S(1)}, u32[]{:S(2)}) copy-start(f32[768]{0:T(1024)S(1)} %convert_element_type.378) | copy-start | bytes 9220
  95.1 60.4 %copy-start.223 = (f32[128]{0:T(128)}, f32[128]{0:T(128)S(1)}, u32[]{:S(2)}) copy-start(f32[128]{0:T(128)S(1)} %fusion.324) | copy-start | bytes 1540
  95.1 63.4 %copy-start.177 = (bf16[64,1536]{1,0:T(8,128)(2,1)S(1)}, bf16[64,1536]{1,0:T(8,128)(2,1)}, u32[]{:S(2)}) copy-start(bf16[64,1536]{1,0:T(8,128)(2,1)} %param.59) | copy-start | bytes 589828
  156.4 19.9 copy-start.208
  156.4 19.9 copy-start.226
  157.2 1065.0 %all-gather.36.cloned.1.call-start = ((), (), s32[]{:S(2)}) async-start(), calls=%async_computation.26 | async-start | bytes 1474560 | tf_op jit(solution)/shard_map/all_gather | solution.py:369
  157.8 1066.8 %all-gather.42.cloned.1.call-start = ((), (), s32[]{:S(2)}) async-start(), calls=%async_computation.29 | async-start | bytes 1474560 | tf_op jit(solution)/shard_map/all_gather | solution.py:371
  158.5 1068.7 %all-gather.34.cloned.1.call-start = ((), (), s32[]{:S(2)}) async-start(), calls=%async_computation.25 | async-start | bytes 3538944 | tf_op jit(solution)/shard_map/all_gather | solution.py:259
  284.2 725.8 %copy-start.239 = (bf16[768]{0:T(1024)(128)(2,1)S(1)}, bf16[768]{0:T(1024)(128)(2,1)}, u32[]{:S(2)}) copy-start(bf16[768]{0:T(1024)(128)(2,1)} %get-tuple-element.1891) | copy-start | bytes 4612
  1036.4 22.1 copy-start.231
  1036.4 22.6 copy-start.113
  1036.4 22.6 copy-start.170
  1036.4 30.3 copy-start.17
  1070.0 190.6 %all-gather.52.cloned.1.call-start = ((), (), s32[]{:S(2)}) async-start(), calls=%async_computation.34 | async-start | bytes 3538944 | tf_op jit(solution)/shard_map/all_gather | solution.py:259
  1129.7 150.9 %all-gather.40.cloned.1.call-start = ((), (), s32[]{:S(2)}) async-start(), calls=%async_computation.28 | async-start | bytes 3538944 | tf_op jit(solution)/shard_map/all_gather | solution.py:259
  1177.6 111.9 %all-gather.44.cloned.1.call-start = ((), (), s32[]{:S(2)}) async-start(), calls=%async_computation.30 | async-start | bytes 1474560 | tf_op jit(solution)/shard_map/all_gather | solution.py:373
  1178.2 152.1 %all-gather.46.cloned.1.call-start = ((), (), s32[]{:S(2)}) async-start(), calls=%async_computation.31 | async-start | bytes 5898240 | tf_op jit(solution)/shard_map/all_gather | solution.py:375
  1178.8 240.9 %all-gather.48.cloned.1.call-start = ((), (), s32[]{:S(2)}) async-start(), calls=%async_computation.32 | async-start | bytes 5898240 | tf_op jit(solution)/shard_map/all_gather | solution.py:376
  1179.4 601.9 %reduce-scatter.21.cloned.1.call-start = ((), (), s32[]{:S(2)}) async-start(), calls=%async_computation.35 | async-start | bytes 7077888 | tf_op jit(solution)/shard_map/reduce_scatter | solution.py:275
  1201.5 21.3 copy-start.33
  1201.5 23.1 copy-start.174
  1224.5 288.3 %copy-start.25 = (f32[128,768]{1,0:T(8,128)}, f32[128,768]{1,0:T(8,128)S(1)}, u32[]{:S(2)}) copy-start(f32[128,768]{1,0:T(8,128)S(1)} %get-tuple-element.2016) | copy-start | bytes 1179652
  1234.7 23.3 copy-start.22
  1476.6 308.3 %reduce-scatter.25.cloned.1.call-start = ((), (), s32[]{:S(2)}) async-start(), calls=%async_computation.37 | async-start | bytes 7077888 | tf_op jit(solution)/shard_map/reduce_scatter | solution.py:275
  1523.5 784.1 %reduce-scatter.31.cloned.1.call-start = ((), (), s32[]{:S(2)}) async-start(), calls=%async_computation.40 | async-start | bytes 7077888 | tf_op jit(solution)/shard_map/reduce_scatter | solution.py:275
  1528.8 30.0 copy-start.8
  1569.1 28.8 copy-start.8
  1608.0 28.7 copy-start.8
  1652.4 656.5 %reduce-scatter.29.cloned.1.call-start = ((), (), s32[]{:S(2)}) async-start(), calls=%async_computation.39 | async-start | bytes 7077888 | tf_op jit(solution)/shard_map/reduce_scatter | solution.py:275
  1658.1 29.4 copy-start.10
  1697.6 28.8 copy-start.10
  1736.6 28.7 copy-start.10
  1781.0 551.1 %reduce-scatter.27.cloned.1.call-start = ((), (), s32[]{:S(2)}) async-start(), calls=%async_computation.38 | async-start | bytes 7077888 | tf_op jit(solution)/shard_map/reduce_scatter | solution.py:275
  1968.0 365.4 %reduce-scatter.23.cloned.1.call-start = ((), (), s32[]{:S(2)}) async-start(), calls=%async_computation.36 | async-start | bytes 7077888 | tf_op jit(solution)/shard_map/reduce_scatter | solution.py:275
  2131.2 209.4 %reduce-scatter.45.cloned.1.call-start = ((), (), s32[]{:S(2)}) async-start(), calls=%async_computation.47 | async-start | bytes 2949120 | tf_op jit(solution)/shard_map/reduce_scatter | solution.py:541
  2134.6 206.0 %reduce-scatter.47.cloned.1.call-start = ((), (), s32[]{:S(2)}) async-start(), calls=%async_computation.48 | async-start | bytes 2949120 | tf_op jit(solution)/shard_map/reduce_scatter | solution.py:543
  2138.2 205.9 %reduce-scatter.51.cloned.1.call-start = ((), (), s32[]{:S(2)}) async-start(), calls=%async_computation.50 | async-start | bytes 2949120 | tf_op jit(solution)/shard_map/reduce_scatter | solution.py:545
  2141.7 239.9 %reduce-scatter.33.cloned.1.call-start = ((), (), s32[]{:S(2)}) async-start(), calls=%async_computation.41 | async-start | bytes 1966080 | tf_op jit(solution)/shard_map/reduce_scatter | solution.py:530
  2282.9 148.5 %reduce-scatter.37.cloned.1.call-start = ((), (), s32[]{:S(2)}) async-start(), calls=%async_computation.43 | async-start | bytes 2949120 | tf_op jit(solution)/shard_map/reduce_scatter | solution.py:534
  2286.4 308.3 %reduce-scatter.53.cloned.1.call-start = ((), (), s32[]{:S(2)}) async-start(), calls=%async_computation.51 | async-start | bytes 11796480 | tf_op jit(solution)/shard_map/reduce_scatter | solution.py:547
  2294.2 464.8 %reduce-scatter.55.cloned.1.call-start = ((), (), s32[]{:S(2)}) async-start(), calls=%async_computation.52 | async-start | bytes 11796480 | tf_op jit(solution)/shard_map/reduce_scatter | solution.py:548
  2302.6 544.8 %reduce-scatter.49.cloned.1.call-start = ((), (), s32[]{:S(2)}) async-start(), calls=%async_computation.49 | async-start | bytes 5898240 | tf_op jit(solution)/shard_map/reduce_scatter | solution.py:544
  2307.6 666.2 %reduce-scatter.43.cloned.1.call-start = ((), (), s32[]{:S(2)}) async-start(), calls=%async_computation.46 | async-start | bytes 8847360 | tf_op jit(solution)/shard_map/reduce_scatter | solution.py:539
  2315.8 822.0 %reduce-scatter.39.cloned.1.call-start = ((), (), s32[]{:S(2)}) async-start(), calls=%async_computation.44 | async-start | bytes 11796480 | tf_op jit(solution)/shard_map/reduce_scatter | solution.py:536
  2323.7 978.7 %reduce-scatter.41.cloned.1.call-start = ((), (), s32[]{:S(2)}) async-start(), calls=%async_computation.45 | async-start | bytes 11796480 | tf_op jit(solution)/shard_map/reduce_scatter | solution.py:537
  2332.1 1096.9 %reduce-scatter.35.cloned.1.call-start = ((), (), s32[]{:S(2)}) async-start(), calls=%async_computation.42 | async-start | bytes 8847360 | tf_op jit(solution)/shard_map/reduce_scatter | solution.py:532
  2340.3 1320.6 %all-reduce.18.cloned.1.call-start = ((), (), s32[]{:S(2)}) async-start(), calls=%async_computation.53 | async-start | bytes 33816576 | tf_op jit(solution)/shard_map/psum | solution.py:550
  3451.7 46.5 %copy-start.228 = (f32[128]{0:T(128)S(1)}, f32[128]{0:T(128)}, u32[]{:S(2)}) copy-start(f32[128]{0:T(128)} %get-tuple-element.1562) | copy-start | bytes 1540
  3451.7 46.5 %copy-start.230 = (f32[128]{0:T(128)S(1)}, f32[128]{0:T(128)}, u32[]{:S(2)}) copy-start(f32[128]{0:T(128)} %copy-done.229) | copy-start | bytes 1540
  3451.8 46.5 %copy-start.71 = (f32[128,768]{1,0:T(8,128)S(1)}, f32[128,768]{1,0:T(8,128)}, u32[]{:S(2)}) copy-start(f32[128,768]{1,0:T(8,128)} %get-tuple-element.1997) | copy-start | bytes 1179652
  3451.8 46.5 %copy-start.79 = (f32[128,768]{1,0:T(8,128)S(1)}, f32[128,768]{1,0:T(8,128)}, u32[]{:S(2)}) copy-start(f32[128,768]{1,0:T(8,128)} %copy-done.77) | copy-start | bytes 1179652
  (275 other events, 754.5 us)
Sparse Core Ops, SparseCore 0:
  9.6 72.9 all-gather.19
  84.2 68.6 all-gather.31
  155.3 30.9 all-gather.29
  188.6 32.3 all-gather.21
  222.4 30.4 all-gather.23
  254.3 88.5 all-gather.25
  344.4 87.8 all-gather.27
  433.9 48.9 all-gather.37
  485.3 31.1 all-gather.49
  517.9 30.4 all-gather.35
  549.9 29.5 all-gather.41
  1070.1 30.0 all-gather.33
  1129.8 30.3 all-gather.51
  1177.7 30.6 all-gather.39
  1209.8 30.4 all-gather.43
  1241.8 88.5 all-gather.45
  1331.8 87.8 all-gather.47
  1476.7 60.1 reduce-scatter.20
  1540.7 61.7 reduce-scatter.24
  1652.6 60.3 reduce-scatter.30
  1781.1 60.7 reduce-scatter.28
  1968.1 60.6 reduce-scatter.26
  2131.3 61.1 reduce-scatter.22
  2195.2 47.9 reduce-scatter.44
  2246.2 47.5 reduce-scatter.46
  2296.5 47.5 reduce-scatter.50
  2346.7 34.7 reduce-scatter.32
  2384.4 46.9 reduce-scatter.36
  2433.8 160.7 reduce-scatter.52
  2596.8 162.1 reduce-scatter.54
  2761.3 86.0 reduce-scatter.48
  2849.7 124.0 reduce-scatter.42
  2976.0 161.7 reduce-scatter.38
  3140.2 162.1 reduce-scatter.40
  3304.6 124.3 reduce-scatter.34
  3435.2 225.5 all-reduce.17
where the time goes:
time: 3710 us; the launch traced here: 3690 us
  local copies, waits for them, and re-layouts  1460 us (39%)
  waiting for transfers between devices  1460 us (39%)
  matrix products  362 us (10%)
  other arithmetic  255 us (7%)
  blocking collectives  124 us (3%)
    gather x2, local copies, waits for them, and re-layouts, per_device(): jnp.take(buckets, key_places[None, :] - places[:, None] + length)  726 us
    reduce_scatter x1, waiting for transfers between devices, per_device(): lax.psum_scatter(totals[7], 'fsdp', scatter_dimension=0, tiled=True)  165 us
    reduce_scatter x1, waiting for transfers between devices, per_device(): lax.psum_scatter(totals[18], 'fsdp', scatter_dimension=0, tiled=True)  164 us
    convert_element_type x12, local copies, waits for them, and re-layouts, per_device(): (rel_index[:, None, :] == bucket_ids[None, :, None]).astype(jnp.bfloat16)  164 us
    reduce_scatter x1, waiting for transfers between devices, per_device(): lax.psum_scatter(totals[6], 'fsdp', scatter_dimension=0, tiled=True)  164 us
    reduce_scatter x1, waiting for transfers between devices, per_device(): lax.psum_scatter(totals[17], 'fsdp', scatter_dimension=0, tiled=True)  163 us
    psum x1, waiting for transfers between devices, per_device(): lax.psum((local[0], local[1], local[2], local[3], local[4], local[5], loc...  161 us
    reduce_scatter x1, waiting for transfers between devices, per_device(): lax.psum_scatter(totals[2], 'fsdp', scatter_dimension=0, tiled=True)  127 us
  transfers between devices with their start and end apart: 36, of which 15 were waited for; matrix products, arithmetic and copies ran while one was open for 53% of the time, Pallas kernels for 0%

commit v1 on v0

v1 whole, which is shorter than its diff:
```python
import functools

import jax
import jax.numpy as jnp
import numpy as np
from jax import lax
from jax.experimental import pallas as pl
from jax.experimental.pallas import tpu as pltpu
from jax.sharding import Mesh
from jax.sharding import PartitionSpec as P

D = 768
HEADS = 12
DH = 64
BUCKETS = 32
EPS = 1e-06
MASKED = -1e30
TP = 4
HQ = HEADS // TP
QC = HQ * DH
BF = jnp.bfloat16
F32 = jnp.float32
MESH_ID = pl.DeviceIdType.MESH
MB = 1024 * 1024


def mm(a, b):
    return jnp.dot(a, b, preferred_element_type=F32)


def mm_tn(a, b):
    return lax.dot_general(a, b, (((0,), (0,)), ((), ())), preferred_element_type=F32)


def mm_nt(a, b):
    return lax.dot_general(a, b, (((1,), (1,)), ((), ())), preferred_element_type=F32)


def gelu(v):
    return jax.nn.gelu(v, approximate=True)


def gelu_back(pre, grad):
    return jax.vjp(gelu, pre)[1](grad)[0]


def group_ids():
    me = lax.axis_index("tp")
    core = me + 1 - 2 * lax.rem(me, 2)
    across = lax.rem(me + 2, TP)
    far = lax.rem(core + 2, TP)
    return me, core, across, far


def greet(core, across):
    barrier = pltpu.get_barrier_semaphore()
    pl.semaphore_signal(barrier, inc=1, device_id={"tp": core}, device_id_type=MESH_ID)
    pl.semaphore_signal(barrier, inc=1, device_id={"tp": across}, device_id_type=MESH_ID)
    pl.semaphore_wait(barrier, 2)


def send(src, dst, send_sem, recv_sem, peer):
    return pltpu.make_async_remote_copy(
        src_ref=src,
        dst_ref=dst,
        send_sem=send_sem,
        recv_sem=recv_sem,
        device_id={"tp": peer},
        device_id_type=MESH_ID,
    )


def normed(values, gains):
    return values * lax.rsqrt(jnp.mean(values * values, axis=-1, keepdims=True) + EPS) * gains


class Gatherer:
    def __init__(self, buf, sems, chunk, ids):
        self.buf, self.sems, self.chunk, self.ids = buf, sems, chunk, ids
        self.sends = []

    def rows(self, j, owner):
        return self.buf.at[pl.ds(pl.multiple_of((TP * j + owner) * self.chunk, self.chunk), self.chunk)]

    def put(self, j, value):
        me, core, across, far = self.ids
        mine = self.rows(j, me)
        mine[...] = value
        x_copy = send(mine, mine, self.sems.at[0, j], self.sems.at[1, j], across)
        x_copy.start()
        c_copy = send(mine, mine, self.sems.at[2, j], self.sems.at[3, j], core)
        c_copy.start()
        self.sends += [x_copy, c_copy]

    def forward(self, j):
        me, core, across, far = self.ids
        theirs = self.rows(j, across)
        send(theirs, theirs, self.sems.at[0, j], self.sems.at[1, j], across).wait_recv()
        f_copy = send(theirs, theirs, self.sems.at[4, j], self.sems.at[5, j], core)
        f_copy.start()
        self.sends.append(f_copy)

    def finish(self):
        me, core, across, far = self.ids
        for j in range(2):
            a = self.rows(j, core)
            send(a, a, self.sems.at[2, j], self.sems.at[3, j], core).wait_recv()
            b = self.rows(j, far)
            send(b, b, self.sems.at[4, j], self.sems.at[5, j], core).wait_recv()
        for copy in self.sends:
            copy.wait_send()


def gather_kernel(chunk, x_ref, gain_ref, out_ref, sems):
    ids = group_ids()
    greet(ids[1], ids[2])
    g = Gatherer(out_ref, sems, chunk, ids)
    for j in range(2):
        g.put(j, normed(x_ref[j].astype(F32), gain_ref[...]).astype(BF))
    for j in range(2):
        g.forward(j)
    g.finish()


def gather_norm(number, x, gain):
    chunk = x.shape[1]
    return pl.pallas_call(
        functools.partial(gather_kernel, chunk),
        out_shape=jax.ShapeDtypeStruct((2 * TP * chunk, D), BF),
        in_specs=[pl.BlockSpec(memory_space=pltpu.VMEM)] * 2,
        out_specs=pl.BlockSpec(memory_space=pltpu.VMEM),
        scratch_shapes=[pltpu.SemaphoreType.DMA((6, 2))],
        compiler_params=pltpu.CompilerParams(
            collective_id=number, has_side_effects=True, vmem_limit_bytes=24 * MB
        ),
        name="gather_norm",
    )(x, gain)


def stage_kernel(conf, *refs):
    chunk, flips, back, gather = conf
    refs = list(refs)
    pairs = [(refs.pop(0), refs.pop(0), flip) for flip in flips]
    resid_ref = refs.pop(0)
    gain_ref = refs.pop(0) if (back or gather == "norm") else None
    x_ref = refs.pop(0) if back else None
    given_ref = refs.pop(0) if gather == "given" else None
    y_ref = refs.pop(0)
    gath_ref = refs.pop(0) if gather else None
    dgain_ref = refs.pop(0) if back else None
    s_far, r_far, s_x, r_x, s_core, r_core, keep, own, sems = refs[:9]
    gsems = refs[9] if gather else None
    ids = group_ids()
    me, core, across, far = ids

    def partial(owner, store):
        r0 = pl.multiple_of(owner * chunk, chunk)
        r1 = pl.multiple_of((TP + owner) * chunk, chunk)

        @pl.loop(0, D // 256)
        def _(n):
            cols = pl.ds(pl.multiple_of(n * 256, 256), 256)
            total = None
            for a_ref, w_ref, flip in pairs:
                a = jnp.concatenate([a_ref[pl.ds(r0, chunk)], a_ref[pl.ds(r1, chunk)]], axis=0)
                term = mm_nt(a, w_ref[cols, :]) if flip else mm(a, w_ref[:, cols])
                total = term if total is None else total + term
            for j in range(2):
                store(j, cols, total[j * chunk : (j + 1) * chunk])

    def into(ref):
        def store(j, cols, value):
            ref[j, :, cols] = value.astype(ref.dtype)

        return store

    greet(core, across)
    g = Gatherer(gath_ref, gsems, chunk, ids) if gather else None
    if gather == "given":
        for j in range(2):
            g.put(j, given_ref[j])
    partial(far, into(s_far))
    c_far = send(s_far, r_far, sems.at[0], sems.at[1], core)
    c_far.start()
    partial(across, into(keep))
    c_far.wait_recv()
    c_x = []
    for j in range(2):
        s_x[j] = (keep[j] + r_far[j].astype(F32)).astype(BF)
        c_x.append(send(s_x.at[j], r_x.at[j], sems.at[2 + j], sems.at[4 + j], across))
        c_x[j].start()
    partial(core, into(s_core))
    c_core = send(s_core, r_core, sems.at[6], sems.at[7], core)
    c_core.start()
    partial(me, into(own))
    c_core.wait_recv()
    if gather == "given":
        for j in range(2):
            g.forward(j)
    for j in range(2):
        c_x[j].wait_recv()
        total = own[j] + r_core[j].astype(F32) + r_x[j].astype(F32)
        if back:
            x = x_ref[j].astype(F32)
            gains = gain_ref[...]
            r = lax.rsqrt(jnp.mean(x * x, axis=-1, keepdims=True) + EPS)
            scaled = total * gains
            inner = jnp.mean(scaled * x, axis=-1, keepdims=True)
            y = resid_ref[j].astype(F32) + r * scaled - x * (r * r * r * inner)
            dgain = jnp.sum(total * x * r, axis=0, keepdims=True)
            if j == 0:
                dgain_ref[...] = dgain
            else:
                dgain_ref[...] += dgain
        else:
            y = resid_ref[j].astype(F32) + total
        y_ref[j] = y.astype(y_ref.dtype)
        if gather == "norm":
            g.put(j, normed(y, gain_ref[...]).astype(BF))
        elif gather == "low":
            g.put(j, y.astype(BF))
    if gather in ("norm", "low"):
        for j in range(2):
            g.forward(j)
    if gather:
        g.finish()
    c_far.wait_send()
    c_core.wait_send()
    for j in range(2):
        c_x[j].wait_send()


def stage(number, pairs, resid, *, back=None, gather=None, gain=None, given=None, dtype=F32):
    chunk = resid.shape[1]
    operands, flips = [], []
    for a, w, flip in pairs:
        operands += [a, w]
        flips.append(flip)
    operands.append(resid)
    if back:
        operands += [back[1], back[0]]
    elif gather == "norm":
        operands.append(gain)
    if gather == "given":
        operands.append(given)
    outs = [jax.ShapeDtypeStruct((2, chunk, D), dtype)]
    if gather:
        outs.append(jax.ShapeDtypeStruct((2 * TP * chunk, D), BF))
    if back:
        outs.append(jax.ShapeDtypeStruct((1, D), F32))
    half = pltpu.VMEM((2, chunk, D), BF)
    full = pltpu.VMEM((2, chunk, D), F32)
    scratch = [half] * 6 + [full] * 2 + [pltpu.SemaphoreType.DMA((8,))]
    if gather:
        scratch.append(pltpu.SemaphoreType.DMA((6, 2)))
    vmem = pl.BlockSpec(memory_space=pltpu.VMEM)
    return pl.pallas_call(
        functools.partial(stage_kernel, (chunk, tuple(flips), bool(back), gather)),
        out_shape=tuple(outs),
        in_specs=[vmem] * len(operands),
        out_specs=(vmem,) * len(outs),
        scratch_shapes=scratch,
        compiler_params=pltpu.CompilerParams(
            collective_id=number, has_side_effects=True, vmem_limit_bytes=40 * MB
        ),
        name="stage",
    )(*operands)


def attn_fwd_kernel(conf, pos_ref, *refs):
    chunk, q_off, kv_off, keys, extra, bias, causal = conf
    refs = list(refs)
    q_ref, kv_ref, segq_ref, segk_ref = refs[:4]
    refs = refs[4:]
    bvec_ref = refs.pop(0) if bias else None
    mkv_ref = refs.pop(0) if extra else None
    att_ref, p_ref, qs, ks, vs, os = refs[:6]
    toep = refs[6] if bias else None
    h, b = pl.program_id(0), pl.program_id(1)
    length = keys

    @pl.when((h == 0) & (b == 0))
    def _():
        for i in range(HQ):
            qs[i] = q_ref[:, q_off + DH * i : q_off + DH * (i + 1)]
            ks[i, :keys] = kv_ref[:, kv_off + DH * i : kv_off + DH * (i + 1)]
            vs[i, :keys] = kv_ref[:, kv_off + QC + DH * i : kv_off + QC + DH * (i + 1)]
            if extra:
                ks[i, keys:] = mkv_ref[:, DH * i : DH * (i + 1)]
                vs[i, keys:] = mkv_ref[:, QC + DH * i : QC + DH * (i + 1)]

    if bias:

        @pl.when(b == 0)
        def _():
            row = jnp.broadcast_to(bvec_ref[h], (chunk, 2 * length))
            toep[...] = pltpu.roll(row, 0, 1, stride=1, stride_axis=0)

    rows = pl.ds(pl.multiple_of(b * 2 * chunk, 2 * chunk), 2 * chunk)
    s = mm_nt(qs[h, rows], ks[h])
    allowed = segq_ref[rows] == segk_ref[...]
    if bias:
        parts = []
        for u in range(2):
            off = pl.multiple_of(length - pos_ref[2 * b + u], 128)
            parts.append(toep[:, pl.ds(off, keys)])
        biased = s[:, :keys] + jnp.concatenate(parts, axis=0)
        s = jnp.concatenate([biased, s[:, keys:]], axis=1) if extra else biased
    if causal:
        place = lax.broadcasted_iota(jnp.int32, (chunk, 1), 0)
        places = jnp.concatenate([place + pos_ref[2 * b + u] for u in range(2)], axis=0)
        allowed = allowed & (lax.broadcasted_iota(jnp.int32, (1, keys), 1) <= places)
    s = jnp.where(allowed, s, MASKED)
    top = jnp.max(s, axis=-1, keepdims=True)
    e = jnp.exp(s - top)
    p = (e * (1.0 / jnp.sum(e, axis=-1, keepdims=True))).astype(BF)
    p_ref[0] = p
    os[h, rows] = mm(p, vs[h]).astype(BF)

    @pl.when((h == HQ - 1) & (b == pl.num_programs(1) - 1))
    def _():
        for i in range(HQ):
            att_ref[:, DH * i : DH * (i + 1)] = os[i]


def whole(shape):
    return pl.BlockSpec(shape, lambda h, b, pos: (0,) * len(shape))


def attn_fwd(pos, q, kv, segq, segk, bvec, mkv, causal, q_off, kv_off):
    rows, keys = q.shape[0], kv.shape[0]
    chunk = rows // 8
    extra = 0 if mkv is None else mkv.shape[0]
    total = keys + extra
    conf = (chunk, q_off, kv_off, keys, extra, bvec is not None, causal)
    operands = [q, kv, segq, segk]
    operands += [v for v in (bvec, mkv) if v is not None]
    scratch = [
        pltpu.VMEM((HQ, rows, DH), BF),
        pltpu.VMEM((HQ, total, DH), BF),
        pltpu.VMEM((HQ, total, DH), BF),
        pltpu.VMEM((HQ, rows, DH), BF),
    ]
    if bvec is not None:
        scratch.append(pltpu.VMEM((chunk, 2 * keys), F32))
    return pl.pallas_call(
        functools.partial(attn_fwd_kernel, conf),
        out_shape=(
            jax.ShapeDtypeStruct((rows, QC), BF),
            jax.ShapeDtypeStruct((HQ, rows, total), BF),
        ),
        grid_spec=pltpu.PrefetchScalarGridSpec(
            num_scalar_prefetch=1,
            grid=(HQ, rows // (2 * chunk)),
            in_specs=[whole(v.shape) for v in operands],
            out_specs=(
                whole((rows, QC)),
                pl.BlockSpec((1, 2 * chunk, total), lambda h, b, pos: (h, b, 0)),
            ),
            scratch_shapes=scratch,
        ),
        compiler_params=pltpu.CompilerParams(
            dimension_semantics=("arbitrary", "arbitrary"), vmem_limit_bytes=48 * MB
        ),
        cost_estimate=pl.CostEstimate(
            flops=4 * HQ * rows * total * DH,
            bytes_accessed=HQ * rows * total * 2,
            transcendentals=HQ * rows * total,
        ),
        name="attn_fwd",
    )(pos, *operands)


def attn_bwd_kernel(conf, pos_ref, *refs):
    chunk, q_off, kv_off, keys, extra, bias = conf
    refs = list(refs)
    p_ref, q_ref, kv_ref, do_ref, att_ref = refs[:5]
    refs = refs[5:]
    mkv_ref = refs.pop(0) if extra else None
    dq_ref, dkv_ref = refs[:2]
    refs = refs[2:]
    dbvec_ref = refs.pop(0) if bias else None
    dmkv_ref = refs.pop(0) if extra else None
    qs, ks, vs, dos, rds, dqs, dks, dvs = refs[:8]
    diag = refs[8] if bias else None
    h, b = pl.program_id(0), pl.program_id(1)
    last = pl.num_programs(1) - 1
    length = keys

    @pl.when((h == 0) & (b == 0))
    def _():
        for i in range(HQ):
            qs[i] = q_ref[:, q_off + DH * i : q_off + DH * (i + 1)]
            ks[i, :keys] = kv_ref[:, kv_off + DH * i : kv_off + DH * (i + 1)]
            vs[i, :keys] = kv_ref[:, kv_off + QC + DH * i : kv_off + QC + DH * (i + 1)]
            if extra:
                ks[i, keys:] = mkv_ref[:, DH * i : DH * (i + 1)]
                vs[i, keys:] = mkv_ref[:, QC + DH * i : QC + DH * (i + 1)]
            grad = do_ref[:, DH * i : DH * (i + 1)]
            dos[i] = grad
            out = att_ref[:, DH * i : DH * (i + 1)]
            rds[i] = jnp.sum(grad.astype(F32) * out.astype(F32), axis=-1, keepdims=True)

    @pl.when(b == 0)
    def _():
        dks[h] = jnp.zeros(dks.shape[1:], F32)
        dvs[h] = jnp.zeros(dvs.shape[1:], F32)
        if bias:
            diag[...] = jnp.zeros_like(diag)

    rows = pl.ds(pl.multiple_of(b * 2 * chunk, 2 * chunk), 2 * chunk)
    q, grad, p = qs[h, rows], dos[h, rows], p_ref[0]
    dp = mm_nt(grad, vs[h])
    ds = (p.astype(F32) * (dp - rds[h, rows])).astype(BF)
    dqs[h, rows] = mm(ds, ks[h]).astype(BF)
    dks[h] += mm_tn(ds, q)
    dvs[h] += mm_tn(p, grad)
    if bias:
        for u in range(2):
            off = pl.multiple_of(length - pos_ref[2 * b + u], 128)
            diag[:, pl.ds(off, keys)] += ds[u * chunk : (u + 1) * chunk, :keys].astype(F32)

        @pl.when(b == last)
        def _():
            x = diag[...]
            size = chunk
            while size > 1:
                size //= 2
                x = x[:size] + pltpu.roll(x[size:], 2 * length - size, 1)
            dbvec_ref[h] = x

    @pl.when((h == HQ - 1) & (b == last))
    def _():
        for i in range(HQ):
            dq_ref[:, DH * i : DH * (i + 1)] = dqs[i]
            dkv_ref[:, DH * i : DH * (i + 1)] = dks[i, :keys].astype(dkv_ref.dtype)
            dkv_ref[:, QC + DH * i : QC + DH * (i + 1)] = dvs[i, :keys].astype(dkv_ref.dtype)
            if extra:
                dmkv_ref[:, DH * i : DH * (i + 1)] = dks[i, keys:].astype(BF)
                dmkv_ref[:, QC + DH * i : QC + DH * (i + 1)] = dvs[i, keys:].astype(BF)


def attn_bwd(pos, p, q, kv, grad, att, mkv, bias, q_off, kv_off, dtype):
    rows, keys = q.shape[0], kv.shape[0]
    chunk = rows // 8
    extra = 0 if mkv is None else mkv.shape[0]
    total = keys + extra
    conf = (chunk, q_off, kv_off, keys, extra, bias)
    operands = [q, kv, grad, att] + ([mkv] if extra else [])
    outs = [jax.ShapeDtypeStruct((rows, QC), BF), jax.ShapeDtypeStruct((keys, 2 * QC), dtype)]
    if bias:
        outs.append(jax.ShapeDtypeStruct((HQ, 1, 2 * keys), F32))
    if extra:
        outs.append(jax.ShapeDtypeStruct((extra, 2 * QC), BF))
    scratch = [
        pltpu.VMEM((HQ, rows, DH), BF),
        pltpu.VMEM((HQ, total, DH), BF),
        pltpu.VMEM((HQ, total, DH), BF),
        pltpu.VMEM((HQ, rows, DH), BF),
        pltpu.VMEM((HQ, rows, 1), F32),
        pltpu.VMEM((HQ, rows, DH), BF),
        pltpu.VMEM((HQ, total, DH), F32),
        pltpu.VMEM((HQ, total, DH), F32),
    ]
    if bias:
        scratch.append(pltpu.VMEM((chunk, 2 * keys), F32))
    return pl.pallas_call(
        functools.partial(attn_bwd_kernel, conf),
        out_shape=tuple(outs),
        grid_spec=pltpu.PrefetchScalarGridSpec(
            num_scalar_prefetch=1,
            grid=(HQ, rows // (2 * chunk)),
            in_specs=[pl.BlockSpec((1, 2 * chunk, total), lambda h, b, pos: (h, b, 0))]
            + [whole(v.shape) for v in operands],
            out_specs=tuple(whole(v.shape) for v in outs),
            scratch_shapes=scratch,
        ),
        compiler_params=pltpu.CompilerParams(
            dimension_semantics=("arbitrary", "arbitrary"), vmem_limit_bytes=48 * MB
        ),
        cost_estimate=pl.CostEstimate(
            flops=8 * HQ * rows * total * DH,
            bytes_accessed=HQ * rows * total * 2,
            transcendentals=0,
        ),
        name="attn_bwd",
    )(pos, p, *operands)


ALL = ("seq", "part", "tp", "fsdp")
CTX = ("seq", "part", "tp")


def per_device(
    parts,
    planes,
    enc_input,
    dec_input,
    segments,
    prefix_rows,
    buckets,
    memory,
    enc_gain,
    enc_qkv,
    enc_rel,
    enc_proj,
    enc_ffnorm,
    enc_ffin,
    enc_ffout,
    dec_gain,
    dec_qkv,
    dec_rel,
    dec_proj,
    cross_gain,
    cross_query,
    cross_kv,
    cross_proj,
    dec_ffnorm,
    dec_ffin,
    dec_ffout,
    enc_cotan,
    dec_cotan,
):
    seq, part, tp, plane = (lax.axis_index(name) for name in ALL)
    chunk = enc_input.shape[1]
    length = buckets.shape[0] // 2
    docs, prefix = prefix_rows.shape[1:]

    def swap(x):
        mine = lax.dynamic_index_in_dim(x, seq, 0, keepdims=False)
        other = lax.dynamic_index_in_dim(x, 1 - seq, 0, keepdims=False)
        came = lax.ppermute(other, "seq", [(0, 1), (1, 0)])
        first = seq == 0
        return jnp.stack([jnp.where(first, mine, came), jnp.where(first, came, mine)])

    def fetch(x):
        return lax.all_gather(x, "fsdp", axis=0, tiled=True)

    def cols(w, start, width=QC):
        return lax.dynamic_slice_in_dim(w, start + width * tp, width, 1)

    gains = (enc_gain, enc_ffnorm, dec_gain, cross_gain, dec_ffnorm)
    small = jnp.concatenate(list(gains) + [enc_rel.reshape(-1), dec_rel.reshape(-1)])
    small = lax.all_gather(small, "fsdp", axis=0)
    per = enc_gain.shape[0]
    gain_rows = [small[:, per * i : per * (i + 1)].reshape(1, D).astype(F32) for i in range(5)]
    g_enc, g_effn, g_dec, g_cross, g_dffn = gain_rows
    per_rel = enc_rel.size
    rels = [
        small[:, 5 * per + per_rel * i : 5 * per + per_rel * (i + 1)].reshape(BUCKETS, HEADS)
        for i in range(2)
    ]
    onehot = (buckets[:, None] == jnp.arange(BUCKETS, dtype=jnp.int32)[None, :]).astype(BF)

    def bias_vector(rel):
        own = lax.dynamic_slice_in_dim(rel, HQ * tp, HQ, 1)
        return lax.dot_general(
            own, onehot, (((0,), (1,)), ((), ())), preferred_element_type=F32
        ).reshape(HQ, 1, 2 * length)

    def qkv_part(w):
        return jnp.concatenate([cols(w, D * i) for i in range(w.shape[1] // D)], axis=1)

    hidden = enc_ffout.shape[0] // TP

    def ffin_part(w):
        return jnp.concatenate(
            [cols(w, hidden * TP * i, hidden) for i in range(planes)], axis=1
        )

    def ffout_part(w):
        return lax.dynamic_slice_in_dim(w, hidden * tp, hidden, 0)

    w_eqkv = fetch(qkv_part(enc_qkv))
    table = fetch(qkv_part(memory))
    xe, xd = swap(enc_input), swap(dec_input)
    segs = lax.all_gather(segments, CTX, axis=1, tiled=True)
    seg = lax.dynamic_index_in_dim(segs, seq, 0, keepdims=False)
    pairs = [(i * TP + j, j * TP + i) for i in range(TP) for j in range(TP)]
    projs = jnp.stack([enc_proj, dec_proj, cross_proj])
    if planes == TP:
        projs = lax.ppermute(projs, ("tp", "fsdp"), pairs)
    else:
        projs = lax.all_gather(projs, "fsdp", axis=1, tiled=True)
        projs = lax.dynamic_slice_in_dim(projs, QC * tp, QC, 1)
    w_eproj, w_dproj, w_cproj = projs[0], projs[1], projs[2]
    w_dqkv = fetch(qkv_part(dec_qkv))
    w_effin, w_effout = fetch(ffin_part(enc_ffin)), fetch(ffout_part(enc_ffout))
    w_cq, w_ckv = fetch(qkv_part(cross_query)), fetch(qkv_part(cross_kv))
    w_dffin, w_dffout = fetch(ffin_part(dec_ffin)), fetch(ffout_part(dec_ffout))
    xec, xdc = swap(enc_cotan), swap(dec_cotan)

    index = jnp.arange(2 * TP, dtype=jnp.int32)
    pos = ((index // TP) * TP * parts + TP * part + index % TP) * chunk
    segq = lax.dynamic_index_in_dim(seg.reshape(2, parts, TP * chunk), part, 1, keepdims=False)
    segq = segq.reshape(-1, 1)
    segk = seg.reshape(1, length)
    ids = lax.dynamic_index_in_dim(prefix_rows, seq, 0, keepdims=False).reshape(-1)
    extra = -(-(docs * prefix) // 256) * 256
    ids = jnp.concatenate([ids, jnp.full((extra - docs * prefix,), -1, jnp.int32)])
    mem_doc = np.full((extra,), -1, np.int32)
    mem_doc[: docs * prefix] = np.arange(docs * prefix) // prefix
    segk_mem = jnp.concatenate([segk, jnp.asarray(mem_doc)[None]], axis=1)
    pick = (ids[:, None] == jnp.arange(table.shape[0], dtype=jnp.int32)[None, :]).astype(BF)
    mkv = mm(pick, table).astype(BF)

    def spread(kv):
        if parts == 1:
            return kv
        got = lax.all_gather(kv, "part", axis=0)
        return got.reshape(parts, 2, TP * chunk, -1).transpose(1, 0, 2, 3).reshape(length, -1)

    def collect(dkv):
        if parts == 1:
            return dkv
        split = dkv.reshape(2, parts, TP * chunk, -1).transpose(1, 0, 2, 3)
        split = split.reshape(parts * 2 * TP * chunk, -1)
        return lax.psum_scatter(split, "part", scatter_dimension=0, tiled=True).astype(BF)

    def self_attn(rows, bvec, mem, segk_now, causal):
        if parts == 1:
            q, kv, kv_off = rows, rows, QC
        else:
            q, kv, kv_off = rows[:, :QC], spread(rows[:, QC:]), 0
        att, p = attn_fwd(pos, q, kv, segq, segk_now, bvec, mem, causal, 0, kv_off)

        def back(grad):
            got = attn_bwd(
                pos, p, q, kv, grad, att, mem, bvec is not None, 0, kv_off, BF if parts == 1 else F32
            )
            return got[0], collect(got[1]), got[2:]

        return att, back

    def cross_attn(q, kv_rows):
        kv = spread(kv_rows)
        att, p = attn_fwd(pos, q, kv, segq, segk, None, None, False, 0, 0)

        def back(grad):
            got = attn_bwd(pos, p, q, kv, grad, att, None, False, 0, 0, BF if parts == 1 else F32)
            return got[0], collect(got[1])

        return att, back

    en = gather_norm(0, xe, g_enc)
    e_rows = mm(en, w_eqkv).astype(BF)
    e_att, e_back = self_attn(e_rows, bias_vector(rels[0]), mkv, segk_mem, False)
    e_mid, e_fn = stage(2, [(e_att, w_eproj, False)], xe, gather="norm", gain=g_effn)
    dn = gather_norm(1, xd, g_dec)
    d_rows = mm(dn, w_dqkv).astype(BF)
    d_att, d_back = self_attn(d_rows, bias_vector(rels[1]), None, segk, True)
    e_pre = mm(e_fn, w_effin)
    e_act = gelu(e_pre).astype(BF)
    e_low, e_gath = stage(3, [(e_act, w_effout, False)], e_mid, gather="low", dtype=BF)
    d_mid, c_n = stage(4, [(d_att, w_dproj, False)], xd, gather="norm", gain=g_cross)
    c_q = mm(c_n, w_cq).astype(BF)
    c_kv = mm(e_gath, w_ckv).astype(BF)
    c_att, c_back = cross_attn(c_q, c_kv)
    d_cross, d_fn = stage(5, [(c_att, w_cproj, False)], d_mid, gather="norm", gain=g_dffn)
    d_pre = mm(d_fn, w_dffin)
    d_act = gelu(d_pre).astype(BF)
    d_low, up_g = stage(
        6, [(d_act, w_dffout, False)], d_cross, gather="given", given=xdc, dtype=BF
    )
    enc_output, dec_output = swap(e_low), swap(d_low)

    def ff_back(number, up, up_rows, fn, act, pre, w_in, w_out, mid, gain):
        d_out = mm_tn(act, up_rows).astype(BF)
        pre_grad = gelu_back(pre, mm_nt(up_rows, w_out)).astype(BF)
        d_in = mm_tn(fn, pre_grad).astype(BF)
        got = stage(number, [(pre_grad, w_in, True)], up, back=(mid, gain), gather="low")
        return got, d_in, d_out

    (up, up_g, dg_dffn), g_dffin, g_dffout = ff_back(
        7, xdc, up_g, d_fn, d_act, d_pre, w_dffin, w_dffout, d_cross, g_dffn
    )
    g_cproj = mm_tn(c_att, up_g).astype(BF)
    c_dq, c_dkv = c_back(mm_nt(up_g, w_cproj).astype(BF))
    g_cq = mm_tn(c_n, c_dq).astype(BF)
    g_ckv = mm_tn(e_gath, c_dkv).astype(BF)
    e_up, e_up_g = stage(8, [(c_dkv, w_ckv, True)], xec, gather="low")
    up, up_g, dg_cross = stage(
        9, [(c_dq, w_cq, True)], up, back=(d_mid, g_cross), gather="low"
    )
    g_dproj = mm_tn(d_att, up_g).astype(BF)
    d_dq, d_dkv, (d_dbv,) = d_back(mm_nt(up_g, w_dproj).astype(BF))
    g_dqkv = jnp.concatenate([mm_tn(dn, d_dq), mm_tn(dn, d_dkv)], axis=1).astype(BF)
    d_in, dg_dec = stage(
        10,
        [(d_dq, w_dqkv[:, :QC], True), (d_dkv, w_dqkv[:, QC:], True)],
        up,
        back=(xd, g_dec),
    )
    (e_up, e_up_g, dg_effn), g_effin, g_effout = ff_back(
        11, e_up, e_up_g, e_fn, e_act, e_pre, w_effin, w_effout, e_mid, g_effn
    )
    g_eproj = mm_tn(e_att, e_up_g).astype(BF)
    e_dq, e_dkv, (e_dbv, d_mkv) = e_back(mm_nt(e_up_g, w_eproj).astype(BF))
    g_eqkv = jnp.concatenate([mm_tn(en, e_dq), mm_tn(en, e_dkv)], axis=1).astype(BF)
    g_table = mm_tn(pick, d_mkv).astype(BF)
    e_in, dg_enc = stage(
        12,
        [(e_dq, w_eqkv[:, :QC], True), (e_dkv, w_eqkv[:, QC:], True)],
        e_up,
        back=(xe, g_enc),
    )
    enc_ingrad = swap(e_in.astype(BF)).astype(F32)
    dec_ingrad = swap(d_in.astype(BF)).astype(F32)

    split = 2 * parts

    def reduce_rows(g):
        return lax.psum_scatter(
            g, ("fsdp", "seq", "part"), scatter_dimension=0, tiled=True
        )

    def gather_rows(g):
        got = lax.all_gather(g, CTX, axis=0)
        return got.reshape((split, TP) + g.shape)

    def by_cols(got, width):
        rows = got.shape[2]
        got = got.reshape(split, TP, rows, -1, width).transpose(0, 2, 3, 1, 4)
        return got.reshape(split * rows, -1).astype(F32)

    def by_rows(got):
        return got.transpose(1, 0, 2, 3).reshape(-1, D).astype(F32)

    red = functools.partial(reduce_rows)
    r_dffin, r_dffout, r_cq, r_ckv = red(g_dffin), red(g_dffout), red(g_cq), red(g_ckv)
    r_dqkv, r_effin, r_effout = red(g_dqkv), red(g_effin), red(g_effout)
    r_eqkv, r_table = red(g_eqkv), red(g_table)
    g_projs = [g_eproj, g_dproj, g_cproj]
    if planes == TP:
        r_projs = red(jnp.concatenate(g_projs, axis=1))
        r_projs = lax.ppermute(r_projs, ("tp", "fsdp"), pairs)
        r_projs = gather_rows(r_projs)
        o_projs = [by_rows(r_projs[..., D * i : D * (i + 1)]) for i in range(3)]
    else:
        o_projs = []
        for g in g_projs:
            full = lax.dynamic_update_slice_in_dim(jnp.zeros((D, D), BF), g, QC * tp, 0)
            full = lax.psum_scatter(full, "fsdp", scatter_dimension=0, tiled=True)
            o_projs.append(lax.psum(full.astype(F32), CTX))
    o_eproj, o_dproj, o_cproj = o_projs
    o_dffin = by_cols(gather_rows(r_dffin), hidden)
    o_dffout = by_rows(gather_rows(r_dffout))
    o_cq = by_cols(gather_rows(r_cq), QC)
    o_ckv = by_cols(gather_rows(r_ckv), QC)
    o_dqkv = by_cols(gather_rows(r_dqkv), QC)
    o_effin = by_cols(gather_rows(r_effin), hidden)
    o_effout = by_rows(gather_rows(r_effout))
    o_eqkv = by_cols(gather_rows(r_eqkv), QC)
    o_table = by_cols(gather_rows(r_table), QC)

    def rel_grad(dbv):
        own = lax.dot_general(
            onehot.astype(F32),
            dbv.reshape(HQ, -1),
            (((0,), (1,)), ((), ())),
            precision=lax.Precision.HIGHEST,
            preferred_element_type=F32,
        )
        return lax.dynamic_update_slice_in_dim(jnp.zeros((BUCKETS, HEADS), F32), own, HQ * tp, 1)

    tiny = [dg_enc, dg_effn, dg_dec, dg_cross, dg_dffn]
    tiny = jnp.concatenate([v.reshape(planes, -1) for v in tiny] + [
        rel_grad(v).reshape(planes, -1) for v in (e_dbv, d_dbv)
    ], axis=1)
    tiny = lax.psum(tiny, ALL)
    tiny = lax.dynamic_index_in_dim(tiny, plane, 0, keepdims=False)
    o_gains = [tiny[per * i : per * (i + 1)] for i in range(5)]
    o_rels = [
        tiny[5 * per + per_rel * i : 5 * per + per_rel * (i + 1)].reshape(-1, HEADS)
        for i in range(2)
    ]
    return (
        enc_output,
        dec_output,
        enc_ingrad,
        dec_ingrad,
        o_table,
        o_gains[0],
        o_eqkv,
        o_rels[0],
        o_eproj,
        o_gains[1],
        o_effin,
        o_effout,
        o_gains[2],
        o_dqkv,
        o_rels[1],
        o_dproj,
        o_gains[3],
        o_cq,
        o_ckv,
        o_cproj,
        o_gains[4],
        o_dffin,
        o_dffout,
    )


def solution(mesh):
    ctx, planes = mesh.shape["ctx"], mesh.shape["fsdp"]
    parts = ctx // (2 * TP)
    inner = Mesh(np.asarray(mesh.devices).reshape(2, parts, TP, planes), ALL)
    rows3 = P("fsdp", CTX, None)
    mat, vec = P("fsdp", None), P("fsdp")
    args = (
        (rows3, rows3, P("fsdp", CTX), P("fsdp", None, None), P(), mat)
        + (vec, mat, mat, mat, vec, mat, mat)
        + (vec, mat, mat, mat)
        + (vec, mat, mat, mat)
        + (vec, mat, mat)
        + (rows3, rows3)
    )
    outs = (
        (rows3, rows3, rows3, rows3, mat)
        + (vec, mat, mat, mat, vec, mat, mat)
        + (vec, mat, mat, mat)
        + (vec, mat, mat, mat)
        + (vec, mat, mat)
    )
    return jax.shard_map(
        functools.partial(per_device, parts, planes),
        mesh=inner,
        in_specs=args,
        out_specs=outs,
        check_vma=False,
    )
```

time: 3710 us -> 1300 us (0.35)
  local copies, waits for them, and re-layouts: 1460 us -> 138 us
  waiting for transfers between devices: 1460 us -> 401 us
  Pallas kernels: 0 us -> 356 us
  matrix products: 362 us -> 64.4 us
  other arithmetic: 255 us -> 18.9 us
  blocking collectives: 124 us -> 273 us
    gather x8 -> x0, local copies, waits for them, and re-layouts: 771 us -> none  [the longest x2 726 us: per_device(): jnp.take(buckets, key_places[None, :] - places[:, None] + length)]
    reduce_scatter x18 -> x10, waiting for transfers between devices: 1090 us -> 355 us  [reduce_rows(): lax.psum_scatter(g, ('fsdp', 'seq', 'part'), scatter_dimension=0, tiled=T...]
    pallas_call x0 -> x19, Pallas kernels: none -> 356 us  [the longest x11 236 us: stage(): pl.pallas_call(functools.partial(stage_kernel, (chunk, tuple(flips), bool...]
    dot_general x228 -> x30, matrix products: 362 us -> 64.4 us  [the longest x14 28.6 us: mm_tn(): lax.dot_general(a, b, (((0,), (0,)), ((), ())), preferred_element_type=F32)]
    all_gather x5 -> x13, blocking collectives: 59.1 us -> 233 us  [the longest x5 119 us: fetch(): return lax.all_gather(x, 'fsdp', axis=0, tiled=True)]
    psum x1 -> x0, waiting for transfers between devices: 161 us -> none  [per_device(): lax.psum((local[0], local[1], local[2], local[3], local[4], local[5], loc...]
    all_gather x17 -> x8, waiting for transfers between devices: 204 us -> 44.2 us  [the longest x4 44.2 us: gather_rows(): got = lax.all_gather(g, CTX, axis=0)]
    convert_element_type x32 -> x33, local copies, waits for them, and re-layouts: 180 us -> 60.3 us  [the longest x20 49 us: by_cols(): return got.reshape(split * rows, -1).astype(F32)]
  transfers between devices with their start and end apart: 36 -> 28, of which waited for: 15 -> 10; matrix products, arithmetic and copies ran while one was open for 53% -> 12% of each run, Pallas kernels for 0% -> 21%
where the time goes in v1:
time: 1300 us; the launch traced here: 1290 us
  waiting for transfers between devices  401 us (31%)
  Pallas kernels  356 us (27%)
  blocking collectives  273 us (21%)
  local copies, waits for them, and re-layouts  138 us (11%)
  matrix products  64.4 us (5%)
  starting transfers between devices  20.3 us (2%)
  other arithmetic  18.9 us (1%)
  between operations  16.4 us (1%)
    reduce_scatter x10, waiting for transfers between devices, reduce_rows(): lax.psum_scatter(g, ('fsdp', 'seq', 'part'), scatter_dimension=0, tiled=T...  355 us
    pallas_call x11, Pallas kernels, stage(): pl.pallas_call(functools.partial(stage_kernel, (chunk, tuple(flips), bool...  236 us
    all_gather x5, blocking collectives, fetch(): return lax.all_gather(x, 'fsdp', axis=0, tiled=True)  119 us
    all_gather x6, blocking collectives, gather_rows(): got = lax.all_gather(g, CTX, axis=0)  60.9 us
    unnamed x252, local copies, waits for them, and re-layouts  50.9 us
    pallas_call x3, Pallas kernels, attn_bwd(): pl.pallas_call(functools.partial(attn_bwd_kernel, conf), out_shape=tuple(...  49.8 us
    convert_element_type x20, local copies, waits for them, and re-layouts, by_cols(): return got.reshape(split * rows, -1).astype(F32)  49 us
    all_gather x4, waiting for transfers between devices, gather_rows(): got = lax.all_gather(g, CTX, axis=0)  44.2 us
  transfers between devices with their start and end apart: 28, of which 10 were waited for; matrix products, arithmetic and copies ran while one was open for 12% of the time, Pallas kernels for 21%

profile of v1, /device:TPU:0, one launch (start us, length us, event | category | flops | bytes accessed | tf_op | source)
XLA Modules:
  0.0 1287.8 jit_solution(4368070261910894483)
XLA Ops:
  11.8 3.0 collective-permute-start
  16.0 8.2 collective-permute-start.1
  30.1 11.3 all_gather.99
  41.8 41.9 %all-gather.11 = bf16[4,1,1152]{2,1,0:T(2,128)(2,1)S(1)} all-gather(bf16[1,1,1152]{2,1,0:T(2,128)(2,1)S(1)} %reshape.330), channel_id=2, replica_groups=mesh['seq'=2,'part'=1,'tp'=4,'fsdp'=4] {'fsdp'}, dimensions={0}, use_global_device_ids=true | all-gather | bytes 11520 | tf_op jit(solution)/shard_map/all_gather | solution.py:544
  85.5 34.0 %all_gather.98 = bf16[768,576]{1,0:T(8,128)(2,1)} all-gather(bf16[192,576]{1,0:T(8,128)(2,1)S(1)} %pad_maximum_fusion.12), channel_id=1, replica_groups=mesh['seq'=2,'part'=1,'tp'=4,'fsdp'=4] {'fsdp'}, dimensions={0}, use_global_device_ids=true | all-gather | bytes 1105920 | tf_op jit(solution)/shard_map/all_gather | solution.py:537
  121.4 14.5 %all_gather.100 = bf16[256,384]{1,0:T(8,128)(2,1)S(1)} all-gather(bf16[64,384]{1,0:T(8,128)(2,1)S(1)} %pad_maximum_fusion.15), channel_id=1, replica_groups=mesh['seq'=2,'part'=1,'tp'=4,'fsdp'=4] {'fsdp'}, dimensions={0}, use_global_device_ids=true | all-gather | bytes 245760 | tf_op jit(solution)/shard_map/all_gather | solution.py:537
  136.3 30.8 %all_gather.103 = bf16[768,576]{1,0:T(8,128)(2,1)} all-gather(bf16[192,576]{1,0:T(8,128)(2,1)S(1)} %pad_maximum_fusion.13), channel_id=1, replica_groups=mesh['seq'=2,'part'=1,'tp'=4,'fsdp'=4] {'fsdp'}, dimensions={0}, use_global_device_ids=true | all-gather | bytes 1105920 | tf_op jit(solution)/shard_map/all_gather | solution.py:537
  168.9 17.9 %all_gather.104.refs_1_ = bf16[768,192]{1,0:T(8,128)(2,1)} all-gather(bf16[192,192]{1,0:T(8,128)(2,1)S(1)} %constant_dynamic-slice_fusion.8), channel_id=1, replica_groups=mesh['seq'=2,'part'=1,'tp'=4,'fsdp'=4] {'fsdp'}, dimensions={0}, use_global_device_ids=true | all-gather | bytes 368640 | tf_op jit(solution)/shard_map/all_gather | solution.py:537
  188.4 21.8 %all_gather.105.refs_1_ = bf16[768,384]{1,0:T(8,128)(2,1)} all-gather(bf16[192,384]{1,0:T(8,128)(2,1)S(1)} %pad_maximum_fusion.14), channel_id=1, replica_groups=mesh['seq'=2,'part'=1,'tp'=4,'fsdp'=4] {'fsdp'}, dimensions={0}, use_global_device_ids=true | all-gather | bytes 737280 | tf_op jit(solution)/shard_map/all_gather | solution.py:537
  210.3 13.4 %gather_norm.2 = bf16[1024,768]{1,0:T(8,128)(2,1)S(1)} custom-call(bf16[2,128,768]{2,1,0:T(8,128)(2,1)S(1)} %pad_maximum_fusion.4.x_ref.refs_2_.refs_6_, f32[1,768]{1,0:T(1,128)S(1)} %reshape.274.gain_ref.refs_5_), custom_call_target="tpu_custom_call" | custom-call | tf_op jit(solution)/shard_map/gather_norm/pallas_call | solution.py:127
  226.1 12.8 gather_norm.3
  239.0 16.5 %attn_fwd.3 = (bf16[1024,192]{1,0:T(8,128)(2,1)S(1)}, bf16[3,1024,1280]{2,1,0:T(8,128)(2,1)}) custom-call(s32[8]{0:T(128)S(1)} %fusion.48.pos_ref, bf16[1024,576]{1,0:T(8,128)(2,1)S(1)} %convolution_convert_fusion.1.refs_0_.refs_1_.refs_2_, bf16[1024,576]{1,0:T(8,128)(2,1)S(1)} %convolution_convert_fusion.1.refs_0_.refs_1_.refs_2_, ...), custom_call_target="tpu_custom_call" | custom-call | flops 1006632960 | bytes 7864320 | tf_op jit(solution)/shard_map/attn_fwd/pallas_call | solution.py:346
  258.1 15.0 %attn_fwd.4 = (bf16[1024,192]{1,0:T(8,128)(2,1)S(1)}, bf16[3,1024,1024]{2,1,0:T(8,128)(2,1)}) custom-call(s32[8]{0:T(128)S(1)} %fusion.48.pos_ref, bf16[1024,576]{1,0:T(8,128)(2,1)S(1)} %convolution_convert_fusion.refs_0_.refs_1_.refs_2_, bf16[1024,576]{1,0:T(8,128)(2,1)S(1)} %convolution_convert_fusion.refs_0_.refs_1_.refs_2_, s32[1024,1]{1,0:T(8,128)S(1)} %copy-done.66, ...), custom_call_target="tpu_custom_call" | custom-call | flops 805306368 | bytes 6291456 | tf_op jit(solution)/shard_map/attn_fwd/pallas_call | solution.py:346
  277.6 23.3 %stage.11 = (f32[2,128,768]{2,1,0:T(8,128)S(1)}, bf16[1024,768]{1,0:T(8,128)(2,1)S(1)}) custom-call(bf16[1024,192]{1,0:T(8,128)(2,1)S(1)} %get-tuple-element.63.refs_0_.refs_4_, bf16[192,768]{1,0:T(8,128)(2,1)S(1)} %get-tuple-element.118.refs_1_, bf16[2,128,768]{2,1,0:T(8,128)(2,1)S(1)} %pad_maximum_fusion.4.x_ref.refs_2_.refs_6_, f32[1,768]{1,0:T(1,128)S(1)} %reshape.275.refs_3_), custom_call_target="tpu_custom_call" | custom-call | tf_op jit(solution)/shard_map/stage/pallas_call | solution.py:257
  302.9 23.3 %stage.13 = (f32[2,128,768]{2,1,0:T(8,128)S(1)}, bf16[1024,768]{1,0:T(8,128)(2,1)S(1)}) custom-call(bf16[1024,192]{1,0:T(8,128)(2,1)S(1)} %get-tuple-element.67.refs_0_.refs_4_, bf16[192,768]{1,0:T(8,128)(2,1)S(1)} %get-tuple-element.117.refs_1_, bf16[2,128,768]{2,1,0:T(8,128)(2,1)S(1)} %pad_maximum_fusion.6.x_ref.refs_2_.refs_6_, f32[1,768]{1,0:T(1,128)S(1)} %reshape.277.refs_3_), custom_call_target="tpu_custom_call" | custom-call | tf_op jit(solution)/shard_map/stage/pallas_call | solution.py:257
  329.7 5.6 multiply_convert_fusion.1
  339.1 23.6 %stage.12 = (bf16[2,128,768]{2,1,0:T(8,128)(2,1)S(1)}, bf16[1024,768]{1,0:T(8,128)(2,1)S(1)}) custom-call(bf16[1024,768]{1,0:T(8,128)(2,1)S(1)} %copy-done.25, bf16[768,768]{1,0:T(8,128)(2,1)S(1)} %copy-done.37, f32[2,128,768]{2,1,0:T(8,128)S(1)} %copy-done.8), custom_call_target="tpu_custom_call" | custom-call | tf_op jit(solution)/shard_map/stage/pallas_call | solution.py:257
  365.8 12.6 attn_fwd.5
  378.4 23.4 %stage.14 = (f32[2,128,768]{2,1,0:T(8,128)S(1)}, bf16[1024,768]{1,0:T(8,128)(2,1)S(1)}) custom-call(bf16[1024,192]{1,0:T(8,128)(2,1)S(1)} %get-tuple-element.70.refs_0_.refs_4_, bf16[192,768]{1,0:T(8,128)(2,1)S(1)} %copy-done.39, f32[2,128,768]{2,1,0:T(8,128)S(1)} %copy-done.5, f32[1,768]{1,0:T(1,128)S(1)} %reshape.278.refs_3_), custom_call_target="tpu_custom_call" | custom-call | tf_op jit(solution)/shard_map/stage/pallas_call | solution.py:257
  404.6 5.6 multiply_convert_fusion
  415.1 20.1 %stage.15 = (bf16[2,128,768]{2,1,0:T(8,128)(2,1)S(1)}, bf16[1024,768]{1,0:T(8,128)(2,1)S(1)}) custom-call(bf16[1024,768]{1,0:T(8,128)(2,1)S(1)} %copy-done.33, bf16[768,768]{1,0:T(8,128)(2,1)S(1)} %copy-done.42, f32[2,128,768]{2,1,0:T(8,128)S(1)} %copy-done.11, bf16[2,128,768]{2,1,0:T(8,128)(2,1)S(1)} %copy-done.2), custom_call_target="tpu_custom_call" | custom-call | tf_op jit(solution)/shard_map/stage/pallas_call | solution.py:257
  437.1 5.0 fusion.13.refs_0_
  442.2 23.4 %stage.16 = (f32[2,128,768]{2,1,0:T(8,128)S(1)}, bf16[1024,768]{1,0:T(8,128)(2,1)S(1)}, f32[1,768]{1,0:T(1,128)S(1)}) custom-call(bf16[1024,768]{1,0:T(8,128)(2,1)S(1)} %fusion.13.refs_0_, bf16[768,768]{1,0:T(8,128)(2,1)S(1)} %copy-done.41, bf16[2,128,768]{2,1,0:T(8,128)(2,1)S(1)} %copy-done.3, f32[1,768]{1,0:T(1,128)S(1)} %reshape.278.refs_3_, ...), custom_call_target="tpu_custom_call" | custom-call | tf_op jit(solution)/shard_map/stage/pallas_call | solution.py:257
  476.3 14.5 %attn_bwd.3 = (bf16[1024,192]{1,0:T(8,128)(2,1)S(1)}, bf16[1024,384]{1,0:T(8,128)(2,1)S(1)}) custom-call(s32[8]{0:T(128)S(1)} %fusion.48.pos_ref, bf16[3,1024,1024]{2,1,0:T(8,128)(2,1)} %get-tuple-element.76.refs_0_, bf16[1024,192]{1,0:T(8,128)(2,1)S(1)} %copy-done.64, bf16[1024,384]{1,0:T(8,128)(2,1)S(1)} %copy-done.47, bf16[1024,192]{1,0:T(8,128)(2,1)S(1)} %copy-done.16, ...), custom_call_target="tpu_custom_call" | custom-call | flops 1610612736 | bytes 6291456 | tf_op jit(solution)/shard_map/attn_bwd/pallas_call | solution.py:467
  490.9 23.6 %stage.17 = (f32[2,128,768]{2,1,0:T(8,128)S(1)}, bf16[1024,768]{1,0:T(8,128)(2,1)S(1)}) custom-call(bf16[1024,384]{1,0:T(8,128)(2,1)S(1)} %get-tuple-element.79.refs_0_, bf16[768,384]{1,0:T(8,128)(2,1)S(1)} %copy-done.14, bf16[2,128,768]{2,1,0:T(8,128)(2,1)S(1)} %copy-done.28), custom_call_target="tpu_custom_call" | custom-call | tf_op jit(solution)/shard_map/stage/pallas_call | solution.py:257
  514.5 3.5 fusion.6.refs_0_
  521.7 4.3 convolution_convert_fusion.4
  526.1 4.4 convolution_convert_fusion.3
  530.6 4.3 convolution_convert_fusion.2
  540.0 23.8 %stage.18 = (f32[2,128,768]{2,1,0:T(8,128)S(1)}, bf16[1024,768]{1,0:T(8,128)(2,1)S(1)}, f32[1,768]{1,0:T(1,128)S(1)}) custom-call(bf16[1024,768]{1,0:T(8,128)(2,1)S(1)} %copy-done.27, bf16[768,768]{1,0:T(8,128)(2,1)S(1)} %copy-done.40, f32[2,128,768]{2,1,0:T(8,128)S(1)} %copy-done.60, f32[1,768]{1,0:T(1,128)S(1)} %reshape.275.refs_3_, ...), custom_call_target="tpu_custom_call" | custom-call | tf_op jit(solution)/shard_map/stage/pallas_call | solution.py:257
  573.3 18.2 %attn_bwd.4 = (bf16[1024,192]{1,0:T(8,128)(2,1)S(1)}, bf16[1024,384]{1,0:T(8,128)(2,1)S(1)}, f32[3,1,2048]{2,1,0:T(1,128)S(1)}, bf16[256,384]{1,0:T(8,128)(2,1)S(1)}) custom-call(s32[8]{0:T(128)S(1)} %fusion.48.pos_ref, bf16[3,1024,1280]{2,1,0:T(8,128)(2,1)} %get-tuple-element.75.refs_0_, ...), custom_call_target="tpu_custom_call" | custom-call | flops 2013265920 | bytes 7864320 | tf_op jit(solution)/shard_map/attn_bwd/pallas_call | solution.py:467
  594.3 3.0 convolution_convert_fusion.11
  597.3 3.3 convolution_convert_fusion.7
  610.2 23.4 %stage.20 = (f32[2,128,768]{2,1,0:T(8,128)S(1)}, bf16[1024,768]{1,0:T(8,128)(2,1)S(1)}, f32[1,768]{1,0:T(1,128)S(1)}) custom-call(bf16[1024,192]{1,0:T(8,128)(2,1)S(1)} %copy-done.72, bf16[768,192]{1,0:T(8,128)(2,1)S(1)} %copy-done.36, f32[2,128,768]{2,1,0:T(8,128)S(1)} %copy-done.56, f32[1,768]{1,0:T(1,128)S(1)} %reshape.277.refs_3_, ...), custom_call_target="tpu_custom_call" | custom-call | tf_op jit(solution)/shard_map/stage/pallas_call | solution.py:257
  638.7 2.8 convolution_convert_fusion.12
  642.8 17.1 %attn_bwd.5 = (bf16[1024,192]{1,0:T(8,128)(2,1)S(1)}, bf16[1024,384]{1,0:T(8,128)(2,1)S(1)}, f32[3,1,2048]{2,1,0:T(1,128)S(1)}) custom-call(s32[8]{0:T(128)S(1)} %fusion.48.pos_ref, bf16[3,1024,1024]{2,1,0:T(8,128)(2,1)} %get-tuple-element.87.refs_0_, bf16[1024,576]{1,0:T(8,128)(2,1)S(1)} %convolution_convert_fusion.refs_0_.refs_1_.refs_2_, ...), custom_call_target="tpu_custom_call" | custom-call | flops 1610612736 | bytes 6291456 | tf_op jit(solution)/shard_map/attn_bwd/pallas_call | solution.py:467
  664.4 52.5 %reduce-scatter.27.cloned.1.call-done = bf16[96,768]{1,0:T(8,128)(2,1)} async-done(((bf16[768,768]{1,0:T(8,128)(2,1)}), bf16[96,768]{1,0:T(8,128)(2,1)}) %reduce-scatter.27.cloned.1.call-update) | async-done | bytes 147472 | tf_op jit(solution)/shard_map/reduce_scatter | solution.py:713
  729.4 14.2 %stage.19 = (f32[2,128,768]{2,1,0:T(8,128)S(1)}, f32[1,768]{1,0:T(1,128)S(1)}) custom-call(bf16[1024,192]{1,0:T(8,128)(2,1)S(1)} %copy-done.70, bf16[768,192]{1,0:T(8,128)(2,1)S(1)} %slice.128.refs_1_, bf16[1024,384]{1,0:T(8,128)(2,1)S(1)} %copy-done.52, bf16[768,384]{1,0:T(8,128)(2,1)S(1)} %slice.129.refs_3_, f32[2,128,768]{2,1,0:T(8,128)S(1)} %copy-done.49, ...), custom_call_target="tpu_custom_call" | custom-call | tf_op jit(solution)/shard_map/stage/pallas_call | solution.py:257
  745.0 14.0 %stage.21 = (f32[2,128,768]{2,1,0:T(8,128)S(1)}, f32[1,768]{1,0:T(1,128)S(1)}) custom-call(bf16[1024,192]{1,0:T(8,128)(2,1)S(1)} %copy-done.74, bf16[768,192]{1,0:T(8,128)(2,1)S(1)} %slice.130.refs_1_, bf16[1024,384]{1,0:T(8,128)(2,1)S(1)} %copy-done.58, bf16[768,384]{1,0:T(8,128)(2,1)S(1)} %slice.131.refs_3_, f32[2,128,768]{2,1,0:T(8,128)S(1)} %copy-done.54, ...), custom_call_target="tpu_custom_call" | custom-call | tf_op jit(solution)/shard_map/stage/pallas_call | solution.py:257
  763.9 39.9 %psum.7 = f32[4,1152]{1,0:T(4,128)S(1)} all-reduce(f32[4,1152]{1,0:T(4,128)S(1)} %concatenate.50), channel_id=1, replica_groups=mesh['seq'=2,'part'=1,'tp'=4,'fsdp'=4] {'seq','part','tp','fsdp'}, use_global_device_ids=true, to_apply=%region_1.2 | all-reduce | flops 4608 | bytes 36864 | tf_op jit(solution)/shard_map/psum | solution.py:770
  811.4 36.3 %reduce-scatter.15.cloned.1.call-done = bf16[32,384]{1,0:T(8,128)(2,1)} async-done(((bf16[256,384]{1,0:T(8,128)(2,1)}), bf16[32,384]{1,0:T(8,128)(2,1)}) %reduce-scatter.15.cloned.1.call-update) | async-done | bytes 24592 | tf_op jit(solution)/shard_map/reduce_scatter | solution.py:713
  847.7 9.3 all-gather.1
  859.0 52.2 %reduce-scatter.23.cloned.1.call-done = bf16[96,192]{1,0:T(8,128)(2,1)} async-done(((bf16[768,192]{1,0:T(8,128)(2,1)}), bf16[96,192]{1,0:T(8,128)(2,1)}) %reduce-scatter.23.cloned.1.call-update) | async-done | bytes 36880 | tf_op jit(solution)/shard_map/reduce_scatter | solution.py:713
  911.2 9.7 all-gather.7
  922.8 53.4 %reduce-scatter.25.cloned.1.call-done = bf16[96,384]{1,0:T(8,128)(2,1)} async-done(((bf16[768,384]{1,0:T(8,128)(2,1)}), bf16[96,384]{1,0:T(8,128)(2,1)}) %reduce-scatter.25.cloned.1.call-update) | async-done | bytes 73744 | tf_op jit(solution)/shard_map/reduce_scatter | solution.py:713
  976.3 10.0 all-gather.8
  990.9 51.9 %reduce-scatter.31.cloned.1.call-done = bf16[96,576]{1,0:T(8,128)(2,1)} async-done(((bf16[768,576]{1,0:T(8,128)(2,1)}), bf16[96,576]{1,0:T(8,128)(2,1)}) %reduce-scatter.31.cloned.1.call-update) | async-done | bytes 110608 | tf_op jit(solution)/shard_map/reduce_scatter | solution.py:713
  1042.8 10.8 all-gather.2
  1056.3 2.5 copy.184
  1058.9 3.7 reshape.280
  1062.5 44.5 %reduce-scatter.17.cloned.1.call-done = bf16[24,2304]{1,0:T(8,128)(2,1)} async-done(((bf16[192,2304]{1,0:T(8,128)(2,1)}), bf16[24,2304]{1,0:T(8,128)(2,1)}) %reduce-scatter.17.cloned.1.call-update) | async-done | bytes 110608 | tf_op jit(solution)/shard_map/reduce_scatter | solution.py:713
  1108.6 64.6 %reduce-scatter.33.cloned.1.call-done = bf16[96,576]{1,0:T(8,128)(2,1)} async-done(((bf16[768,576]{1,0:T(8,128)(2,1)}), bf16[96,576]{1,0:T(8,128)(2,1)}) %reduce-scatter.33.cloned.1.call-update) | async-done | bytes 110608 | tf_op jit(solution)/shard_map/reduce_scatter | solution.py:713
  1173.2 10.8 all-gather.6
  1189.2 3.7 reshape.284
  1192.9 10.3 all-gather.3
  1205.9 3.7 reshape.293
  1209.7 3.7 copy.186
  1213.4 4.8 reshape.282
  1218.2 7.2 all-gather.31.cloned.1.call-done
  1228.4 22.9 %all-gather.33.cloned.1.call-done = bf16[768,768]{1,0:T(8,128)(2,1)} async-done(((bf16[96,768]{1,0:T(8,128)(2,1)}), bf16[768,768]{1,0:T(8,128)(2,1)}) %all-gather.33.cloned.1.call-update) | async-done | bytes 1179664 | tf_op jit(solution)/shard_map/all_gather | solution.py:718
  1251.4 3.5 reshape.298
  1254.9 3.7 copy.195
  1258.6 4.8 reshape.289
  1263.4 14.0 %all-gather.35.cloned.1.call-done = bf16[768,768]{1,0:T(8,128)(2,1)} async-done(((bf16[96,768]{1,0:T(8,128)(2,1)}), bf16[768,768]{1,0:T(8,128)(2,1)}) %all-gather.35.cloned.1.call-update) | async-done | bytes 1179664 | tf_op jit(solution)/shard_map/all_gather | solution.py:718
  (450 shorter events, 155.3 us)
Async XLA Ops:
  7.2 322.5 %all-gather.21.cloned.1.call-start = ((), (), s32[]{:S(2)}) async-start(), calls=%async_computation.10 | async-start | bytes 1474560 | tf_op jit(solution)/shard_map/all_gather | solution.py:537
  10.0 325.3 %all-gather.23.cloned.1.call-start = ((), (), s32[]{:S(2)}) async-start(), calls=%async_computation.11 | async-start | bytes 1474560 | tf_op jit(solution)/shard_map/all_gather | solution.py:537
  10.8 393.8 %all-gather.25.cloned.1.call-start = ((), (), s32[]{:S(2)}) async-start(), calls=%async_computation.12 | async-start | bytes 1474560 | tf_op jit(solution)/shard_map/all_gather | solution.py:537
  11.7 15.9 %copy-start.106 = (bf16[2,128,768]{2,1,0:T(8,128)(2,1)S(1)}, bf16[2,128,768]{2,1,0:T(8,128)(2,1)}, u32[]{:S(2)}) copy-start(bf16[2,128,768]{2,1,0:T(8,128)(2,1)} %param.51) | copy-start | bytes 1179652
  11.7 398.5 %all-gather.27.cloned.1.call-start = ((), (), s32[]{:S(2)}) async-start(), calls=%async_computation.13 | async-start | bytes 1474560 | tf_op jit(solution)/shard_map/all_gather | solution.py:537
  11.8 198.4 %collective-permute-start = (bf16[128,768]{1,0:T(8,128)(2,1)S(1)}, bf16[128,768]{1,0:T(8,128)(2,1)S(1)}, u32[]{:S(2)}, u32[]{:S(2)}) collective-permute-start(bf16[128,768]{1,0:T(8,128)(2,1)S(1)} %dynamic-slice_bitcast_fusion.7), channel_id=1, source_target_pairs={{0,16},{16,0},{1,17},{17,1},{2,18},{18,2},{3,19},{19,3},{4,20},{20... | collective-permute-start | bytes 589832 | tf_op jit(solution)/shard_map/ppermute | solution.py:532
  14.9 15.2 %copy-start.114 = (s32[2,128]{1,0:T(2,128)S(1)}, s32[2,128]{1,0:T(2,128)}, u32[]{:S(2)}) copy-start(s32[2,128]{1,0:T(2,128)} %param.29) | copy-start | bytes 3076
  14.9 26.6 %copy-start.111 = (bf16[8,12]{1,0:T(8,128)(2,1)S(1)}, bf16[8,12]{1,0:T(8,128)(2,1)}, u32[]{:S(2)}) copy-start(bf16[8,12]{1,0:T(8,128)(2,1)} %param.35) | copy-start | bytes 580
  14.9 26.7 %copy-start.112 = (bf16[8,12]{1,0:T(8,128)(2,1)S(1)}, bf16[8,12]{1,0:T(8,128)(2,1)}, u32[]{:S(2)}) copy-start(bf16[8,12]{1,0:T(8,128)(2,1)} %param.42) | copy-start | bytes 580
  14.9 26.7 %copy-start.116 = (bf16[192]{0:T(256)(128)(2,1)S(1)}, bf16[192]{0:T(256)(128)(2,1)}, u32[]{:S(2)}) copy-start(bf16[192]{0:T(256)(128)(2,1)} %param.33) | copy-start | bytes 1156
  14.9 26.7 %copy-start.117 = (bf16[192]{0:T(256)(128)(2,1)S(1)}, bf16[192]{0:T(256)(128)(2,1)}, u32[]{:S(2)}) copy-start(bf16[192]{0:T(256)(128)(2,1)} %param.37) | copy-start | bytes 1156
  14.9 26.7 %copy-start.118 = (bf16[192]{0:T(256)(128)(2,1)S(1)}, bf16[192]{0:T(256)(128)(2,1)}, u32[]{:S(2)}) copy-start(bf16[192]{0:T(256)(128)(2,1)} %param.40) | copy-start | bytes 1156
  14.9 26.7 %copy-start.119 = (bf16[192]{0:T(256)(128)(2,1)S(1)}, bf16[192]{0:T(256)(128)(2,1)}, u32[]{:S(2)}) copy-start(bf16[192]{0:T(256)(128)(2,1)} %param.44) | copy-start | bytes 1156
  14.9 26.7 %copy-start.120 = (bf16[192]{0:T(256)(128)(2,1)S(1)}, bf16[192]{0:T(256)(128)(2,1)}, u32[]{:S(2)}) copy-start(bf16[192]{0:T(256)(128)(2,1)} %param.48) | copy-start | bytes 1156
  16.0 259.7 %collective-permute-start.1 = (bf16[3,192,768]{2,1,0:T(8,128)(2,1)}, bf16[3,192,768]{2,1,0:T(8,128)(2,1)}, u32[]{:S(2)}, u32[]{:S(2)}) collective-permute-start(bf16[3,192,768]{2,1,0:T(8,128)(2,1)} %pad_maximum_fusion), channel_id=1, source_target_pairs={{0,0},{1,4},{2,8},{3,12},{4,1},{5,5},{6,9},{7,13},{8,2},{9,6},{10,... | collective-permute-start | bytes 2654216 | tf_op jit(solution)/shard_map/ppermute | solution.py:582
  24.9 200.2 %collective-permute-start.3 = (bf16[128,768]{1,0:T(8,128)(2,1)}, bf16[128,768]{1,0:T(8,128)(2,1)}, u32[]{:S(2)}, u32[]{:S(2)}) collective-permute-start(bf16[128,768]{1,0:T(8,128)(2,1)} %dynamic-slice_bitcast_fusion.5), channel_id=1, source_target_pairs={{0,16},{16,0},{1,17},{17,1},{2,18},{18,2},{3,19},{19,3},{4,20},{20... | collective-permute-start | bytes 589832 | tf_op jit(solution)/shard_map/ppermute | solution.py:532
  25.6 229.9 %collective-permute-start.4 = (bf16[128,768]{1,0:T(8,128)(2,1)}, bf16[128,768]{1,0:T(8,128)(2,1)}, u32[]{:S(2)}, u32[]{:S(2)}) collective-permute-start(bf16[128,768]{1,0:T(8,128)(2,1)} %dynamic-slice_bitcast_fusion.4), channel_id=1, source_target_pairs={{0,16},{16,0},{1,17},{17,1},{2,18},{18,2},{3,19},{19,3},{4,20},{20... | collective-permute-start | bytes 589832 | tf_op jit(solution)/shard_map/ppermute | solution.py:532
  28.3 245.6 %collective-permute-start.6 = (bf16[128,768]{1,0:T(8,128)(2,1)}, bf16[128,768]{1,0:T(8,128)(2,1)}, u32[]{:S(2)}, u32[]{:S(2)}) collective-permute-start(bf16[128,768]{1,0:T(8,128)(2,1)} %dynamic-slice_bitcast_fusion.2), channel_id=1, source_target_pairs={{0,16},{16,0},{1,17},{17,1},{2,18},{18,2},{3,19},{19,3},{4,20},{20... | collective-permute-start | bytes 589832 | tf_op jit(solution)/shard_map/ppermute | solution.py:532
  30.0 633.2 %reduce-scatter.19.cloned.1.call-start = ((), (), s32[]{:S(2)}) async-start(), calls=%async_computation.16 | async-start | bytes 1327104 | tf_op jit(solution)/shard_map/reduce_scatter | solution.py:713
  83.9 36.0 %copy-start.121 = (s32[2048]{0:T(1024)S(1)}, s32[2048]{0:T(1024)}, u32[]{:S(2)}) copy-start(s32[2048]{0:T(1024)} %param.31) | copy-start | bytes 24580
  85.4 50.5 %copy-start.113 = (s32[2,8,20]{2,1,0:T(8,128)S(1)}, s32[2,8,20]{2,1,0:T(8,128)}, u32[]{:S(2)}) copy-start(s32[2,8,20]{2,1,0:T(8,128)} %param.30) | copy-start | bytes 3844
  119.8 119.2 %copy-start.65 = (s32[1024,1]{1,0:T(8,128)}, s32[1024,1]{1,0:T(8,128)S(1)}, u32[]{:S(2)}) copy-start(s32[1024,1]{1,0:T(8,128)S(1)} %copy.171.refs_2_) | copy-start | bytes 12292
  136.2 51.8 %copy-start.115 = (s32[1,256]{1,0:T(1,128)S(1)}, s32[1,256]{1,0:T(1,128)}, u32[]{:S(2)}) copy-start(s32[1,256]{1,0:T(1,128)} %constant.152) | copy-start | bytes 3076
  188.3 50.6 %copy-start.61 = (bf16[256,384]{1,0:T(8,128)(2,1)}, bf16[256,384]{1,0:T(8,128)(2,1)S(1)}, u32[]{:S(2)}) copy-start(bf16[256,384]{1,0:T(8,128)(2,1)S(1)} %convolution_convert_fusion.21.refs_5_) | copy-start | bytes 589828
  238.9 17.7 %copy-start.29 = (bf16[1024,768]{1,0:T(8,128)(2,1)}, bf16[1024,768]{1,0:T(8,128)(2,1)S(1)}, u32[]{:S(2)}) copy-start(bf16[1024,768]{1,0:T(8,128)(2,1)S(1)} %gather_norm.3) | copy-start | bytes 4718596
  238.9 16.5 %copy-start.105 = (bf16[2,128,768]{2,1,0:T(8,128)(2,1)S(1)}, bf16[2,128,768]{2,1,0:T(8,128)(2,1)}, u32[]{:S(2)}) copy-start(bf16[2,128,768]{2,1,0:T(8,128)(2,1)} %param.52) | copy-start | bytes 1179652
  238.9 17.7 %copy-start.100 = (bf16[768,576]{1,0:T(8,128)(2,1)S(1)}, bf16[768,576]{1,0:T(8,128)(2,1)}, u32[]{:S(2)}) copy-start(bf16[768,576]{1,0:T(8,128)(2,1)} %all_gather.103) | copy-start | bytes 2654212
  255.5 22.1 %copy-start.19 = (bf16[1024,192]{1,0:T(8,128)(2,1)}, bf16[1024,192]{1,0:T(8,128)(2,1)S(1)}, u32[]{:S(2)}) copy-start(bf16[1024,192]{1,0:T(8,128)(2,1)S(1)} %get-tuple-element.63.refs_0_.refs_4_) | copy-start | bytes 1179652
  258.1 15.9 %copy-start.107 = (bf16[2,128,768]{2,1,0:T(8,128)(2,1)S(1)}, bf16[2,128,768]{2,1,0:T(8,128)(2,1)}, u32[]{:S(2)}) copy-start(bf16[2,128,768]{2,1,0:T(8,128)(2,1)} %param.51) | copy-start | bytes 1179652
  273.1 29.8 %copy-start.17 = (bf16[1024,192]{1,0:T(8,128)(2,1)}, bf16[1024,192]{1,0:T(8,128)(2,1)S(1)}, u32[]{:S(2)}) copy-start(bf16[1024,192]{1,0:T(8,128)(2,1)S(1)} %get-tuple-element.67.refs_0_.refs_4_) | copy-start | bytes 1179652
  277.6 50.7 %copy-start.35 = (bf16[768,192]{1,0:T(8,128)(2,1)S(1)}, bf16[768,192]{1,0:T(8,128)(2,1)}, u32[]{:S(2)}) copy-start(bf16[768,192]{1,0:T(8,128)(2,1)} %all_gather.104.refs_1_) | copy-start | bytes 884740
  339.1 25.5 %copy-start.13 = (bf16[768,384]{1,0:T(8,128)(2,1)S(1)}, bf16[768,384]{1,0:T(8,128)(2,1)}, u32[]{:S(2)}) copy-start(bf16[768,384]{1,0:T(8,128)(2,1)} %all_gather.105.refs_1_) | copy-start | bytes 1769476
  415.0 22.1 %copy-start.43 = (bf16[768,768]{1,0:T(8,128)(2,1)S(1)}, bf16[768,768]{1,0:T(8,128)(2,1)}, u32[]{:S(2)}) copy-start(bf16[768,768]{1,0:T(8,128)(2,1)} %all-gather.27.cloned.1.call-done.refs_1_) | copy-start | bytes 3538948
  442.1 23.5 %copy-start.34 = (bf16[1024,768]{1,0:T(8,128)(2,1)}, bf16[1024,768]{1,0:T(8,128)(2,1)S(1)}, u32[]{:S(2)}) copy-start(bf16[1024,768]{1,0:T(8,128)(2,1)S(1)} %fusion.13.refs_0_) | copy-start | bytes 4718596
  476.3 14.6 %copy-start.28 = (bf16[2,128,768]{2,1,0:T(8,128)(2,1)S(1)}, bf16[2,128,768]{2,1,0:T(8,128)(2,1)}, u32[]{:S(2)}) copy-start(bf16[2,128,768]{2,1,0:T(8,128)(2,1)} %pad_maximum_fusion.9.refs_2_) | copy-start | bytes 1179652
  476.3 38.2 %copy-start.123 = (f32[1024,768]{1,0:T(8,128)S(1)}, f32[1024,768]{1,0:T(8,128)}, u32[]{:S(2)}) copy-start(f32[1024,768]{1,0:T(8,128)} %get-tuple-element.158) | copy-start | bytes 9437188
  490.8 27.2 %copy-start.44 = (bf16[1024,384]{1,0:T(8,128)(2,1)}, bf16[1024,384]{1,0:T(8,128)(2,1)S(1)}, u32[]{:S(2)}) copy-start(bf16[1024,384]{1,0:T(8,128)(2,1)S(1)} %get-tuple-element.79.refs_0_) | copy-start | bytes 2359300
  490.8 27.2 %copy-start.71 = (bf16[1024,192]{1,0:T(8,128)(2,1)}, bf16[1024,192]{1,0:T(8,128)(2,1)S(1)}, u32[]{:S(2)}) copy-start(bf16[1024,192]{1,0:T(8,128)(2,1)S(1)} %get-tuple-element.88.refs_0_) | copy-start | bytes 1179652
  490.8 23.7 %copy-start.38 = (bf16[768,768]{1,0:T(8,128)(2,1)S(1)}, bf16[768,768]{1,0:T(8,128)(2,1)}, u32[]{:S(2)}) copy-start(bf16[768,768]{1,0:T(8,128)(2,1)} %all-gather.23.cloned.1.call-done.refs_1_) | copy-start | bytes 3538948
  521.7 142.2 %reduce-scatter.21.cloned.1.call-start = ((), (), s32[]{:S(2)}) async-start(), calls=%async_computation.17 | async-start | bytes 1327104 | tf_op jit(solution)/shard_map/reduce_scatter | solution.py:713
  526.1 190.8 %reduce-scatter.27.cloned.1.call-start = ((), (), s32[]{:S(2)}) async-start(), calls=%async_computation.20 | async-start | bytes 1327104 | tf_op jit(solution)/shard_map/reduce_scatter | solution.py:713
  530.6 279.0 %reduce-scatter.29.cloned.1.call-start = ((), (), s32[]{:S(2)}) async-start(), calls=%async_computation.21 | async-start | bytes 1327104 | tf_op jit(solution)/shard_map/reduce_scatter | solution.py:713
  535.0 312.7 %reduce-scatter.15.cloned.1.call-start = ((), (), s32[]{:S(2)}) async-start(), calls=%async_computation.14 | async-start | bytes 221184 | tf_op jit(solution)/shard_map/reduce_scatter | solution.py:713
  594.2 317.0 %reduce-scatter.23.cloned.1.call-start = ((), (), s32[]{:S(2)}) async-start(), calls=%async_computation.18 | async-start | bytes 442368 | tf_op jit(solution)/shard_map/reduce_scatter | solution.py:713
  597.3 379.0 %reduce-scatter.25.cloned.1.call-start = ((), (), s32[]{:S(2)}) async-start(), calls=%async_computation.19 | async-start | bytes 663552 | tf_op jit(solution)/shard_map/reduce_scatter | solution.py:713
  600.6 442.1 %reduce-scatter.31.cloned.1.call-start = ((), (), s32[]{:S(2)}) async-start(), calls=%async_computation.26 | async-start | bytes 1105920 | tf_op jit(solution)/shard_map/reduce_scatter | solution.py:713
  606.9 26.8 %copy-start.24 = (bf16[1024,192]{1,0:T(8,128)(2,1)S(1)}, bf16[1024,192]{1,0:T(8,128)(2,1)}, u32[]{:S(2)}) copy-start(bf16[1024,192]{1,0:T(8,128)(2,1)} %copy-done.22) | copy-start | bytes 1179652
  606.9 500.1 %reduce-scatter.17.cloned.1.call-start = ((), (), s32[]{:S(2)}) async-start(), calls=%async_computation.15 | async-start | bytes 995328 | tf_op jit(solution)/shard_map/reduce_scatter | solution.py:713
  610.2 23.5 %copy-start.84 = (bf16[1024,768]{1,0:T(8,128)(2,1)S(1)}, bf16[1024,768]{1,0:T(8,128)(2,1)}, u32[]{:S(2)}) copy-start(bf16[1024,768]{1,0:T(8,128)(2,1)} %copy-done.83) | copy-start | bytes 4718596
  638.7 534.5 %reduce-scatter.33.cloned.1.call-start = ((), (), s32[]{:S(2)}) async-start(), calls=%async_computation.27 | async-start | bytes 1105920 | tf_op jit(solution)/shard_map/reduce_scatter | solution.py:713
  642.8 17.2 %copy-start.30 = (bf16[1024,768]{1,0:T(8,128)(2,1)S(1)}, bf16[1024,768]{1,0:T(8,128)(2,1)}, u32[]{:S(2)}) copy-start(bf16[1024,768]{1,0:T(8,128)(2,1)} %copy-done.29) | copy-start | bytes 4718596
  663.2 542.7 %all-gather.29.cloned.1.call-start = ((), (), s32[]{:S(2)}) async-start(), calls=%async_computation.22 | async-start | bytes 1327104 | tf_op jit(solution)/shard_map/all_gather | solution.py:718
  663.8 561.6 %all-gather.31.cloned.1.call-start = ((), (), s32[]{:S(2)}) async-start(), calls=%async_computation.23 | async-start | bytes 1327104 | tf_op jit(solution)/shard_map/all_gather | solution.py:718
  664.4 587.0 %all-gather.33.cloned.1.call-start = ((), (), s32[]{:S(2)}) async-start(), calls=%async_computation.24 | async-start | bytes 1327104 | tf_op jit(solution)/shard_map/all_gather | solution.py:718
  716.9 560.5 %all-gather.35.cloned.1.call-start = ((), (), s32[]{:S(2)}) async-start(), calls=%async_computation.25 | async-start | bytes 1327104 | tf_op jit(solution)/shard_map/all_gather | solution.py:718
  723.5 83.3 %collective-permute-start.2 = (bf16[128,768]{1,0:T(8,128)(2,1)}, bf16[128,768]{1,0:T(8,128)(2,1)}, u32[]{:S(2)}, u32[]{:S(2)}) collective-permute-start(bf16[128,768]{1,0:T(8,128)(2,1)} %dynamic-slice_bitcast_fusion.6), channel_id=1, source_target_pairs={{0,16},{16,0},{1,17},{17,1},{2,18},{18,2},{3,19},{19,3},{4,20},{20... | collective-permute-start | bytes 589832 | tf_op jit(solution)/shard_map/ppermute | solution.py:532
  726.3 81.5 %collective-permute-start.5 = (bf16[128,768]{1,0:T(8,128)(2,1)}, bf16[128,768]{1,0:T(8,128)(2,1)}, u32[]{:S(2)}, u32[]{:S(2)}) collective-permute-start(bf16[128,768]{1,0:T(8,128)(2,1)} %dynamic-slice_bitcast_fusion.3), channel_id=1, source_target_pairs={{0,16},{16,0},{1,17},{17,1},{2,18},{18,2},{3,19},{19,3},{4,20},{20... | collective-permute-start | bytes 589832 | tf_op jit(solution)/shard_map/ppermute | solution.py:532
  729.4 15.6 %copy-start.74 = (bf16[1024,192]{1,0:T(8,128)(2,1)S(1)}, bf16[1024,192]{1,0:T(8,128)(2,1)}, u32[]{:S(2)}) copy-start(bf16[1024,192]{1,0:T(8,128)(2,1)} %copy-done.73) | copy-start | bytes 1179652
  743.6 15.4 %copy-start.81 = (f32[1,768]{1,0:T(1,128)}, f32[1,768]{1,0:T(1,128)S(1)}, u32[]{:S(2)}) copy-start(f32[1,768]{1,0:T(1,128)S(1)} %get-tuple-element.96) | copy-start | bytes 9220
  743.7 62.2 %collective-permute-start.7 = (bf16[128,768]{1,0:T(8,128)(2,1)S(1)}, bf16[128,768]{1,0:T(8,128)(2,1)S(1)}, u32[]{:S(2)}, u32[]{:S(2)}) collective-permute-start(bf16[128,768]{1,0:T(8,128)(2,1)S(1)} %dynamic-slice_bitcast_fusion.1), channel_id=1, source_target_pairs={{0,16},{16,0},{1,17},{17,1},{2,18},{18,2},{3,19},{19,3},{4,20},{20... | collective-permute-start | bytes 589832 | tf_op jit(solution)/shard_map/ppermute | solution.py:532
  759.1 47.7 %copy-start.76 = (bf16[2,128,768]{2,1,0:T(8,128)(2,1)S(1)}, bf16[2,128,768]{2,1,0:T(8,128)(2,1)}, u32[]{:S(2)}) copy-start(bf16[2,128,768]{2,1,0:T(8,128)(2,1)} %copy-done.75) | copy-start | bytes 1179652
  759.2 51.3 %collective-permute-start.8 = (bf16[128,768]{1,0:T(8,128)(2,1)S(1)}, bf16[128,768]{1,0:T(8,128)(2,1)S(1)}, u32[]{:S(2)}, u32[]{:S(2)}) collective-permute-start(bf16[128,768]{1,0:T(8,128)(2,1)S(1)} %dynamic-slice_bitcast_fusion), channel_id=1, source_target_pairs={{0,16},{16,0},{1,17},{17,1},{2,18},{18,2},{3,19},{19,3},{4,20},{20... | collective-permute-start | bytes 589832 | tf_op jit(solution)/shard_map/ppermute | solution.py:532
  762.7 45.2 %copy-start.78 = (bf16[2,128,768]{2,1,0:T(8,128)(2,1)S(1)}, bf16[2,128,768]{2,1,0:T(8,128)(2,1)}, u32[]{:S(2)}) copy-start(bf16[2,128,768]{2,1,0:T(8,128)(2,1)} %copy-done.77) | copy-start | bytes 1179652
  1107.1 85.8 %collective-permute-start.9 = (bf16[24,2304]{1,0:T(8,128)(2,1)}, bf16[24,2304]{1,0:T(8,128)(2,1)S(1)}, u32[]{:S(2)}, u32[]{:S(2)}) collective-permute-start(bf16[24,2304]{1,0:T(8,128)(2,1)} %reduce-scatter.17.cloned.1.call-done), channel_id=1, source_target_pairs={{0,0},{1,4},{2,8},{3,12},{4,1},{5,5},{6,9},{7,13},{8,2},{9,6},{10,... | collective-permute-start | bytes 331784 | tf_op jit(solution)/shard_map/ppermute | solution.py:736
  (88 other events, 253.1 us)
Sparse Core Ops, SparseCore 0:
  10.2 60.8 all-gather.20
  73.2 43.7 all-gather.22
  119.1 46.0 all-gather.24
  167.2 40.1 all-gather.26
  521.8 62.4 reduce-scatter.18
  587.5 63.0 reduce-scatter.20
  653.9 62.9 reduce-scatter.26
  720.9 63.3 reduce-scatter.28
  787.5 60.1 reduce-scatter.14
  850.8 60.3 reduce-scatter.22
  915.1 61.1 reduce-scatter.24
  980.4 62.3 reduce-scatter.30
  1046.7 60.2 reduce-scatter.16
  1110.8 62.3 reduce-scatter.32
  1175.1 23.0 all-gather.28
  1200.1 25.2 all-gather.30
  1227.3 24.0 all-gather.32
  1253.3 24.0 all-gather.34

commit v2 on v1

--- a/solution.py
+++ b/solution.py
@@ -1,3 +1,4 @@
+import collections
 import functools
 
 import jax
@@ -22,6 +23,7 @@
 F32 = jnp.float32
 MESH_ID = pl.DeviceIdType.MESH
 MB = 1024 * 1024
+VMEM_LIMIT = 60 * MB
 
 
 def mm(a, b):
@@ -50,13 +52,6 @@
     across = lax.rem(me + 2, TP)
     far = lax.rem(core + 2, TP)
     return me, core, across, far
-
-
-def greet(core, across):
-    barrier = pltpu.get_barrier_semaphore()
-    pl.semaphore_signal(barrier, inc=1, device_id={"tp": core}, device_id_type=MESH_ID)
-    pl.semaphore_signal(barrier, inc=1, device_id={"tp": across}, device_id_type=MESH_ID)
-    pl.semaphore_wait(barrier, 2)
 
 
 def send(src, dst, send_sem, recv_sem, peer):
@@ -75,22 +70,25 @@
 
 
 class Gatherer:
-    def __init__(self, buf, sems, chunk, ids):
-        self.buf, self.sems, self.chunk, self.ids = buf, sems, chunk, ids
-        self.sends = []
+    def __init__(self, buf, stage, sems, chunk, ids):
+        self.buf, self.stage, self.sems, self.chunk, self.ids = buf, stage, sems, chunk, ids
+        self.sends, self.own = [], []
 
     def rows(self, j, owner):
         return self.buf.at[pl.ds(pl.multiple_of((TP * j + owner) * self.chunk, self.chunk), self.chunk)]
 
     def put(self, j, value):
         me, core, across, far = self.ids
-        mine = self.rows(j, me)
+        mine = self.stage.at[j]
         mine[...] = value
-        x_copy = send(mine, mine, self.sems.at[0, j], self.sems.at[1, j], across)
+        x_copy = send(mine, self.rows(j, me), self.sems.at[0, j], self.sems.at[1, j], across)
         x_copy.start()
-        c_copy = send(mine, mine, self.sems.at[2, j], self.sems.at[3, j], core)
+        c_copy = send(mine, self.rows(j, me), self.sems.at[2, j], self.sems.at[3, j], core)
         c_copy.start()
         self.sends += [x_copy, c_copy]
+        own = pltpu.make_async_copy(mine, self.rows(j, me), self.sems.at[6, j])
+        own.start()
+        self.own.append(own)
 
     def forward(self, j):
         me, core, across, far = self.ids
@@ -109,47 +107,365 @@
             send(b, b, self.sems.at[4, j], self.sems.at[5, j], core).wait_recv()
         for copy in self.sends:
             copy.wait_send()
-
-
-def gather_kernel(chunk, x_ref, gain_ref, out_ref, sems):
-    ids = group_ids()
-    greet(ids[1], ids[2])
-    g = Gatherer(out_ref, sems, chunk, ids)
-    for j in range(2):
-        g.put(j, normed(x_ref[j].astype(F32), gain_ref[...]).astype(BF))
-    for j in range(2):
-        g.forward(j)
-    g.finish()
-
-
-def gather_norm(number, x, gain):
+        for copy in self.own:
+            copy.wait()
+
+
+Job = collections.namedtuple("Job", ["axis", "src_axis", "dst_axis", "local", "src", "shape", "finish"])
+
+
+def gather_job(axis, src, size=2, at=0):
+    shape = src.shape[:at] + (size,) + src.shape[at:]
+    return Job(axis, None, at, True, src, shape, None)
+
+
+def total_job(axis, src, size=2):
+    return gather_job(axis, src, size)._replace(finish="sum")
+
+
+def deal_job(axis, src):
+    return Job(axis, 0, 0, True, src, src.shape, "sum")
+
+
+def swap_job(src, at=0, add=False):
+    shape = src.shape[:at] + src.shape[at + 1 :]
+    return Job("seq", at, None, add, src, shape, "add" if add else None)
+
+
+def turn_job(src):
+    return Job("turn", None, None, True, src, src.shape, None)
+
+
+def block_job(src):
+    return Job("ctx", 0, 0, True, src, (2 * TP,) + src.shape[1:], None)
+
+
+def last_job(src, width):
+    return gather_job("core", src, 2, 2)._replace(finish=("layout", width))
+
+
+def result_of(job):
+    if job.finish == "sum":
+        return job.shape[1:], job.src.dtype
+    if isinstance(job.finish, tuple):
+        seqs, halves, cores, rows, cols = job.shape
+        if job.finish[1]:
+            return (seqs * rows, halves * cores * cols), F32
+        return (seqs * halves * cores * rows, cols), F32
+    return job.shape, job.src.dtype
+
+
+def entry(ref, axis, index):
+    return ref if axis is None else ref.at[(slice(None),) * axis + (index,)]
+
+
+class Shipper:
+    def __init__(self, jobs, planes, srcs, outs, scratch, sems):
+        self.jobs, self.planes, self.srcs, self.outs, self.sems = jobs, planes, srcs, outs, sems
+        self.tp, self.seq, self.plane = (lax.axis_index(n) for n in ("tp", "seq", "fsdp"))
+        self.dsts, self.bounce, self.made = [], [], []
+        for job, out in zip(jobs, outs):
+            if job.finish:
+                self.dsts.append(scratch.pop(0))
+                self.bounce.append(scratch.pop(0) if job.finish == "add" else None)
+                self.made.append(scratch.pop(0) if job.finish != "add" else None)
+            else:
+                self.dsts.append(out)
+                self.bounce.append(scratch.pop(0) if job.local else None)
+                self.made.append(None)
+
+    @staticmethod
+    def scratch(jobs):
+        shapes = []
+        for job in jobs:
+            dtype = job.src.dtype
+            if job.finish:
+                shapes.append(pltpu.VMEM(job.shape, dtype))
+                if job.finish == "add":
+                    shapes.append(pltpu.VMEM(job.shape, dtype))
+                else:
+                    shapes.append(pltpu.VMEM(*result_of(job)))
+            elif job.local:
+                drop = job.dst_axis
+                own = job.shape if drop is None else job.shape[:drop] + job.shape[drop + 1 :]
+                shapes.append(pltpu.VMEM(own, dtype))
+        return shapes
+
+    @staticmethod
+    def count(jobs, planes):
+        return sum(2 * Shipper.n_peers(job, planes) + 2 for job in jobs)
+
+    @staticmethod
+    def n_peers(job, planes):
+        return {"fsdp": planes - 1, "ctx": 2 * TP - 1}.get(job.axis, 1)
+
+    def coord(self, axis):
+        half = self.tp // 2
+        return {
+            "fsdp": self.plane,
+            "seq": self.seq,
+            "across": half,
+            "core": self.tp - 2 * half,
+            "ctx": TP * self.seq + self.tp,
+            "turn": None,
+        }[axis]
+
+    def peers(self, axis):
+        if axis == "fsdp":
+            n, z = self.planes, self.plane
+            for k in range(1, n):
+                to = lax.rem(z + k, n)
+                yield to, {"fsdp": to}, lax.rem(z + (n - k), n)
+        elif axis == "ctx":
+            for k in range(1, 2 * TP):
+                to = lax.rem(self.seq + k // TP, 2)
+                to_tp = lax.rem(self.tp + k % TP, TP)
+                from_seq = lax.rem(self.seq + (2 - k // TP), 2)
+                from_tp = lax.rem(self.tp + (TP - k % TP), TP)
+                yield to, {"seq": to, "tp": to_tp}, TP * from_seq + from_tp
+        elif axis == "seq":
+            yield 1 - self.seq, {"seq": 1 - self.seq}, 1 - self.seq
+        elif axis == "turn":
+            yield None, {"fsdp": self.tp, "tp": self.plane}, None
+        else:
+            to = lax.rem(self.tp + 2, TP) if axis == "across" else self.tp + 1 - 2 * lax.rem(self.tp, 2)
+            other = 1 - self.coord(axis)
+            yield other, {"tp": to}, other
+
+    def greet(self, always=("core", "across")):
+        axes = list(always) + sorted({job.axis for job in self.jobs} - set(always))
+        barrier = pltpu.get_barrier_semaphore()
+        total = 0
+        for axis in axes:
+            for _, device, _ in self.peers(axis):
+                if axis == "turn":
+                    continue
+                pl.semaphore_signal(barrier, inc=1, device_id=device, device_id_type=MESH_ID)
+                total += 1
+        if "turn" in axes:
+            moves = self.plane != self.tp
+
+            @pl.when(moves)
+            def _():
+                for _, device, _ in self.peers("turn"):
+                    pl.semaphore_signal(barrier, inc=1, device_id=device, device_id_type=MESH_ID)
+                pl.semaphore_wait(barrier, total + 1)
+
+            @pl.when(jnp.logical_not(moves))
+            def _():
+                pl.semaphore_wait(barrier, total)
+        else:
+            pl.semaphore_wait(barrier, total)
+
+    def each(self, act_remote, act_local):
+        base = 0
+        for n, (job, src, dst) in enumerate(zip(self.jobs, self.srcs, self.dsts)):
+            mine = self.coord(job.axis)
+            peers = list(self.peers(job.axis))
+            for i, (to, device, source) in enumerate(peers):
+                sems = (self.sems.at[base + 2 * i], self.sems.at[base + 2 * i + 1])
+
+                def copy_into(slot, to=to, device=device, sems=sems, src=src, dst=dst, job=job):
+                    return pltpu.make_async_remote_copy(
+                        src_ref=entry(src, job.src_axis, to),
+                        dst_ref=entry(dst, job.dst_axis, slot),
+                        send_sem=sems[0],
+                        recv_sem=sems[1],
+                        device_id=device,
+                        device_id_type=MESH_ID,
+                    )
+
+                def remote(copy_into=copy_into, source=source, mine=mine):
+                    act_remote(copy_into, mine, source)
+
+                if job.axis == "turn":
+                    pl.when(self.plane != self.tp)(remote)
+                else:
+                    remote()
+            if job.local:
+                own = self.seq if job.axis == "ctx" else mine
+
+                def local(n=n, job=job, src=src, dst=dst, own=own, mine=mine, sem=base + 2 * len(peers)):
+                    here, there = entry(src, job.src_axis, own), entry(dst, job.dst_axis, mine)
+                    bounce = self.bounce[n]
+                    if bounce is None:
+                        act_local([(here, there)], self.sems.at[sem])
+                    elif job.finish == "add":
+                        act_local([(here, bounce)], self.sems.at[sem])
+                    else:
+                        act_local([(here, bounce), (bounce, there)], self.sems.at[sem])
+
+                if job.axis == "turn":
+                    pl.when(self.plane == self.tp)(local)
+                else:
+                    local()
+            base += 2 * len(peers) + 2
+        return base
+
+    def start(self):
+        self.each(
+            lambda copy_into, mine, source: copy_into(mine).start(),
+            lambda legs, sem: pltpu.make_async_copy(*legs[0], sem).start(),
+        )
+
+    def finish(self):
+        def turn_round(legs, sem):
+            if len(legs) > 1:
+                pltpu.make_async_copy(*legs[0], sem).wait()
+                pltpu.make_async_copy(*legs[1], sem).start()
+
+        def remote(copy_into, mine, source):
+            copy_into(source).wait_recv()
+            copy_into(mine).wait_send()
+
+        self.each(lambda *_: None, turn_round)
+        self.each(remote, lambda legs, sem: pltpu.make_async_copy(*legs[-1], sem).wait())
+        stores, base = [], 0
+        for job, dst, bounce, made, out in zip(
+            self.jobs, self.dsts, self.bounce, self.made, self.outs
+        ):
+            base += 2 * self.n_peers(job, self.planes) + 2
+            if not job.finish:
+                continue
+            if job.finish == "add":
+                made = bounce
+
+                @pl.loop(0, dst.shape[0])
+                def _(i):
+                    bounce[i] = (bounce[i].astype(F32) + dst[i].astype(F32)).astype(bounce.dtype)
+
+            elif job.finish == "sum":
+                total = dst[0].astype(F32)
+                for i in range(1, dst.shape[0]):
+                    total = total + dst[i].astype(F32)
+                made[...] = total.astype(made.dtype)
+            else:
+                self.lay_out(dst, made, job.finish[1])
+            store = pltpu.make_async_copy(made, out, self.sems.at[base - 1])
+            store.start()
+            stores.append(store)
+        for store in stores:
+            store.wait()
+
+    @staticmethod
+    def lay_out(src, dst, width):
+        seqs, halves, cores, rows, cols = src.shape
+
+        @pl.loop(0, seqs)
+        def _(i):
+            if not width:
+                for q in range(TP):
+                    at = pl.multiple_of((q * seqs + i) * rows, rows)
+                    dst[pl.ds(at, rows)] = src[i, q // 2, q % 2].astype(F32)
+            else:
+                at = pl.multiple_of(i * rows, rows)
+                for n in range(cols // width):
+                    span = slice(n * width, (n + 1) * width)
+                    parts = [src[i, q // 2, q % 2, :, span].astype(F32) for q in range(TP)]
+                    block = slice(n * width * TP, (n + 1) * width * TP)
+                    dst[pl.ds(at, rows), block] = jnp.concatenate(parts, axis=1)
+
+
+HBM_SPEC = pl.BlockSpec(memory_space=pltpu.HBM)
+
+
+class Loaded:
+    def __init__(self, src, dst, sem):
+        self.copy, self.ref, self.waited = pltpu.make_async_copy(src, dst, sem), dst, False
+        self.copy.start()
+
+    def get(self):
+        if not self.waited:
+            self.copy.wait()
+            self.waited = True
+        return self.ref
+
+
+def call_with_jobs(kernel, number, planes, jobs, operands, outs, scratch, name, cost):
+    n_in, n_out, n_job = len(operands), len(outs), len(jobs)
+    n_sems = max(Shipper.count(jobs, planes), 1)
+    plain = [job._replace(src=jax.ShapeDtypeStruct(job.src.shape, job.src.dtype)) for job in jobs]
+    job_scratch = Shipper.scratch(jobs)
+
+    def body(*refs):
+        ins, refs = refs[:n_in], refs[n_in:]
+        srcs, refs = refs[:n_job], refs[n_job:]
+        results, refs = refs[:n_out], refs[n_out:]
+        dsts, refs = refs[:n_job], refs[n_job:]
+        sems, in_sems, refs = refs[0], refs[1], list(refs[2:])
+        loaded = [Loaded(src, refs.pop(0), in_sems.at[i]) for i, src in enumerate(ins)]
+        own = [refs.pop(0) for _ in job_scratch]
+        shipper = Shipper(plain, planes, srcs, dsts, own, sems)
+        kernel(shipper, loaded, list(results), refs)
+
+    results = [result_of(job) for job in jobs]
+    got = pl.pallas_call(
+        body,
+        out_shape=tuple(outs) + tuple(jax.ShapeDtypeStruct(*r) for r in results),
+        in_specs=[HBM_SPEC] * (n_in + n_job),
+        out_specs=(HBM_SPEC,) * (n_out + n_job),
+        scratch_shapes=[
+            pltpu.SemaphoreType.DMA((n_sems,)),
+            pltpu.SemaphoreType.DMA((max(n_in, 1),)),
+        ]
+        + [pltpu.VMEM(v.shape, v.dtype) for v in operands]
+        + job_scratch
+        + scratch,
+        compiler_params=pltpu.CompilerParams(
+            collective_id=number, has_side_effects=True, vmem_limit_bytes=VMEM_LIMIT
+        ),
+        cost_estimate=pl.CostEstimate(flops=cost, bytes_accessed=8 * MB, transcendentals=0),
+        name=name,
+    )(*operands, *[job.src for job in jobs])
+    return got[:n_out], list(got[n_out:])
+
+
+def ship(number, planes, jobs):
+    def kernel(shipper, ins, outs, scratch):
+        shipper.greet(())
+        shipper.start()
+        shipper.finish()
+
+    return call_with_jobs(kernel, number, planes, jobs, [], [], [], "ship", 0)[1]
+
+
+def gather_norm(number, planes, x, gain, jobs):
     chunk = x.shape[1]
-    return pl.pallas_call(
-        functools.partial(gather_kernel, chunk),
-        out_shape=jax.ShapeDtypeStruct((2 * TP * chunk, D), BF),
-        in_specs=[pl.BlockSpec(memory_space=pltpu.VMEM)] * 2,
-        out_specs=pl.BlockSpec(memory_space=pltpu.VMEM),
-        scratch_shapes=[pltpu.SemaphoreType.DMA((6, 2))],
-        compiler_params=pltpu.CompilerParams(
-            collective_id=number, has_side_effects=True, vmem_limit_bytes=24 * MB
-        ),
-        name="gather_norm",
-    )(x, gain)
-
-
-def stage_kernel(conf, *refs):
+
+    def kernel(shipper, ins, outs, scratch):
+        shipper.greet()
+        shipper.start()
+        x_ref, gain_ref = (v.get() for v in ins)
+        g = Gatherer(outs[0], scratch[0], scratch[1], chunk, group_ids())
+        for j in range(2):
+            g.put(j, normed(x_ref[j].astype(F32), gain_ref[...]).astype(BF))
+        for j in range(2):
+            g.forward(j)
+        g.finish()
+        shipper.finish()
+
+    outs = [jax.ShapeDtypeStruct((2 * TP * chunk, D), BF)]
+    scratch = [pltpu.VMEM((2, chunk, D), BF), pltpu.SemaphoreType.DMA((7, 2))]
+    got, moved = call_with_jobs(
+        kernel, number, planes, jobs, [x, gain], outs, scratch, "gather_norm", 10**6
+    )
+    return got[0], moved
+
+
+def stage_kernel(conf, shipper, ins, outs, scratch):
     chunk, flips, back, gather = conf
-    refs = list(refs)
-    pairs = [(refs.pop(0), refs.pop(0), flip) for flip in flips]
-    resid_ref = refs.pop(0)
-    gain_ref = refs.pop(0) if (back or gather == "norm") else None
-    x_ref = refs.pop(0) if back else None
-    given_ref = refs.pop(0) if gather == "given" else None
-    y_ref = refs.pop(0)
-    gath_ref = refs.pop(0) if gather else None
-    dgain_ref = refs.pop(0) if back else None
-    s_far, r_far, s_x, r_x, s_core, r_core, keep, own, sems = refs[:9]
-    gsems = refs[9] if gather else None
+    pairs = [(ins.pop(0), ins.pop(0), flip) for flip in flips]
+    resid_in = ins.pop(0)
+    gain_in = ins.pop(0) if (back or gather == "norm") else None
+    x_in = ins.pop(0) if back else None
+    given_in = ins.pop(0) if gather == "given" else None
+    y_out = outs.pop(0)
+    gath_ref = outs.pop(0) if gather else None
+    dgain_out = outs.pop(0) if back else None
+    s_far, r_far, s_x, r_x, s_core, r_core, keep, own, y_ref, sems = scratch[:10]
+    scratch = scratch[10:]
+    g_stage, g_sems = (scratch.pop(0), scratch.pop(0)) if gather else (None, None)
+    dgain_ref = scratch.pop(0) if back else None
     ids = group_ids()
     me, core, across, far = ids
 
@@ -174,11 +490,13 @@
 
         return store
 
-    greet(core, across)
-    g = Gatherer(gath_ref, gsems, chunk, ids) if gather else None
+    shipper.greet()
+    g = Gatherer(gath_ref, g_stage, g_sems, chunk, ids) if gather else None
     if gather == "given":
+        given_ref = given_in.get()
         for j in range(2):
             g.put(j, given_ref[j])
+    pairs = [(a.get(), w.get(), flip) for a, w, flip in pairs]
     partial(far, into(s_far))
     c_far = send(s_far, r_far, sems.at[0], sems.at[1], core)
     c_far.start()
@@ -189,20 +507,30 @@
         s_x[j] = (keep[j] + r_far[j].astype(F32)).astype(BF)
         c_x.append(send(s_x.at[j], r_x.at[j], sems.at[2 + j], sems.at[4 + j], across))
         c_x[j].start()
+    shipper.start()
     partial(core, into(s_core))
     c_core = send(s_core, r_core, sems.at[6], sems.at[7], core)
     c_core.start()
     partial(me, into(own))
     c_core.wait_recv()
+    resid_ref = resid_in.get()
+    x_ref = x_in.get() if back else None
+    gains = gain_in.get()[...] if gain_in else None
     if gather == "given":
         for j in range(2):
             g.forward(j)
+    stores = []
+
+    def keep_out(src, dst, sem):
+        copy = pltpu.make_async_copy(src, dst, sems.at[sem])
+        copy.start()
+        stores.append(copy)
+
     for j in range(2):
         c_x[j].wait_recv()
         total = own[j] + r_core[j].astype(F32) + r_x[j].astype(F32)
         if back:
             x = x_ref[j].astype(F32)
-            gains = gain_ref[...]
             r = lax.rsqrt(jnp.mean(x * x, axis=-1, keepdims=True) + EPS)
             scaled = total * gains
             inner = jnp.mean(scaled * x, axis=-1, keepdims=True)
@@ -216,9 +544,12 @@
             y = resid_ref[j].astype(F32) + total
         y_ref[j] = y.astype(y_ref.dtype)
         if gather == "norm":
-            g.put(j, normed(y, gain_ref[...]).astype(BF))
+            g.put(j, normed(y, gains).astype(BF))
         elif gather == "low":
             g.put(j, y.astype(BF))
+        keep_out(y_ref.at[j], y_out.at[j], 8 + j)
+    if back:
+        keep_out(dgain_ref, dgain_out, 10)
     if gather in ("norm", "low"):
         for j in range(2):
             g.forward(j)
@@ -228,14 +559,20 @@
     c_core.wait_send()
     for j in range(2):
         c_x[j].wait_send()
-
-
-def stage(number, pairs, resid, *, back=None, gather=None, gain=None, given=None, dtype=F32):
+    shipper.finish()
+    for copy in stores:
+        copy.wait()
+
+
+def stage(
+    number, planes, pairs, resid, *, back=None, gather=None, gain=None, given=None, dtype=F32, jobs=()
+):
     chunk = resid.shape[1]
-    operands, flips = [], []
+    operands, flips, cost = [], [], 0
     for a, w, flip in pairs:
         operands += [a, w]
         flips.append(flip)
+        cost += 2 * a.shape[0] * a.shape[1] * D
     operands.append(resid)
     if back:
         operands += [back[1], back[0]]
@@ -250,21 +587,18 @@
         outs.append(jax.ShapeDtypeStruct((1, D), F32))
     half = pltpu.VMEM((2, chunk, D), BF)
     full = pltpu.VMEM((2, chunk, D), F32)
-    scratch = [half] * 6 + [full] * 2 + [pltpu.SemaphoreType.DMA((8,))]
+    scratch = [half] * 6 + [full] * 2 + [
+        pltpu.VMEM((2, chunk, D), dtype),
+        pltpu.SemaphoreType.DMA((11,)),
+    ]
     if gather:
-        scratch.append(pltpu.SemaphoreType.DMA((6, 2)))
-    vmem = pl.BlockSpec(memory_space=pltpu.VMEM)
-    return pl.pallas_call(
-        functools.partial(stage_kernel, (chunk, tuple(flips), bool(back), gather)),
-        out_shape=tuple(outs),
-        in_specs=[vmem] * len(operands),
-        out_specs=(vmem,) * len(outs),
-        scratch_shapes=scratch,
-        compiler_params=pltpu.CompilerParams(
-            collective_id=number, has_side_effects=True, vmem_limit_bytes=40 * MB
-        ),
-        name="stage",
-    )(*operands)
+        scratch += [half, pltpu.SemaphoreType.DMA((7, 2))]
+    if back:
+        scratch.append(pltpu.VMEM((1, D), F32))
+    kernel = functools.partial(stage_kernel, (chunk, tuple(flips), bool(back), gather))
+    return call_with_jobs(
+        kernel, number, planes, list(jobs), operands, outs, scratch, "stage", cost
+    )
 
 
 def attn_fwd_kernel(conf, pos_ref, *refs):
@@ -360,7 +694,7 @@
             scratch_shapes=scratch,
         ),
         compiler_params=pltpu.CompilerParams(
-            dimension_semantics=("arbitrary", "arbitrary"), vmem_limit_bytes=48 * MB
+            dimension_semantics=("arbitrary", "arbitrary"), vmem_limit_bytes=VMEM_LIMIT
         ),
         cost_estimate=pl.CostEstimate(
             flops=4 * HQ * rows * total * DH,
@@ -377,8 +711,10 @@
     p_ref, q_ref, kv_ref, do_ref, att_ref = refs[:5]
     refs = refs[5:]
     mkv_ref = refs.pop(0) if extra else None
-    dq_ref, dkv_ref = refs[:2]
-    refs = refs[2:]
+    joint = q_ref.shape[1] > QC
+    dq_ref = refs.pop(0)
+    dkv_ref = dq_ref if joint else refs.pop(0)
+    to = QC if joint else 0
     dbvec_ref = refs.pop(0) if bias else None
     dmkv_ref = refs.pop(0) if extra else None
     qs, ks, vs, dos, rds, dqs, dks, dvs = refs[:8]
@@ -433,8 +769,9 @@
     def _():
         for i in range(HQ):
             dq_ref[:, DH * i : DH * (i + 1)] = dqs[i]
-            dkv_ref[:, DH * i : DH * (i + 1)] = dks[i, :keys].astype(dkv_ref.dtype)
-            dkv_ref[:, QC + DH * i : QC + DH * (i + 1)] = dvs[i, :keys].astype(dkv_ref.dtype)
+            at = to + DH * i
+            dkv_ref[:, at : at + DH] = dks[i, :keys].astype(dkv_ref.dtype)
+            dkv_ref[:, at + QC : at + QC + DH] = dvs[i, :keys].astype(dkv_ref.dtype)
             if extra:
                 dmkv_ref[:, DH * i : DH * (i + 1)] = dks[i, keys:].astype(BF)
                 dmkv_ref[:, QC + DH * i : QC + DH * (i + 1)] = dvs[i, keys:].astype(BF)
@@ -447,7 +784,10 @@
     total = keys + extra
     conf = (chunk, q_off, kv_off, keys, extra, bias)
     operands = [q, kv, grad, att] + ([mkv] if extra else [])
-    outs = [jax.ShapeDtypeStruct((rows, QC), BF), jax.ShapeDtypeStruct((keys, 2 * QC), dtype)]
+    if q.shape[1] > QC:
+        outs = [jax.ShapeDtypeStruct((rows, 3 * QC), BF)]
+    else:
+        outs = [jax.ShapeDtypeStruct((rows, QC), BF), jax.ShapeDtypeStruct((keys, 2 * QC), dtype)]
     if bias:
         outs.append(jax.ShapeDtypeStruct((HQ, 1, 2 * keys), F32))
     if extra:
@@ -476,7 +816,7 @@
             scratch_shapes=scratch,
         ),
         compiler_params=pltpu.CompilerParams(
-            dimension_semantics=("arbitrary", "arbitrary"), vmem_limit_bytes=48 * MB
+            dimension_semantics=("arbitrary", "arbitrary"), vmem_limit_bytes=VMEM_LIMIT
         ),
         cost_estimate=pl.CostEstimate(
             flops=8 * HQ * rows * total * DH,
@@ -526,24 +866,70 @@
     length = buckets.shape[0] // 2
     docs, prefix = prefix_rows.shape[1:]
 
-    def swap(x):
+    first = seq == 0
+    split = planes * 2
+
+    def joined(x, came):
         mine = lax.dynamic_index_in_dim(x, seq, 0, keepdims=False)
-        other = lax.dynamic_index_in_dim(x, 1 - seq, 0, keepdims=False)
-        came = lax.ppermute(other, "seq", [(0, 1), (1, 0)])
-        first = seq == 0
+        came = came.astype(x.dtype)
         return jnp.stack([jnp.where(first, mine, came), jnp.where(first, came, mine)])
-
-    def fetch(x):
-        return lax.all_gather(x, "fsdp", axis=0, tiled=True)
 
     def cols(w, start, width=QC):
         return lax.dynamic_slice_in_dim(w, start + width * tp, width, 1)
 
+    def halved(w):
+        rows = w.shape[0] // 2
+        return lax.dynamic_slice_in_dim(w, rows * seq, rows, 0)
+
+    def qkv_part(w):
+        w = halved(w)
+        return jnp.concatenate([cols(w, D * i) for i in range(w.shape[1] // D)], axis=1)
+
+    hidden = enc_ffout.shape[0] // TP
+
+    def ffin_part(w):
+        w = halved(w)
+        return jnp.concatenate(
+            [cols(w, hidden * TP * i, hidden) for i in range(planes)], axis=1
+        )
+
+    def ffout_part(w):
+        rows = hidden // 2
+        return lax.dynamic_slice_in_dim(w, hidden * tp + rows * seq, rows, 0)
+
+    def over_planes(w):
+        return gather_job("fsdp", w, planes)
+
+    def over_seq(w):
+        return gather_job("seq", w, 2, 1)
+
+    def matrix(w):
+        return w.reshape(-1, w.shape[-1])
+
     gains = (enc_gain, enc_ffnorm, dec_gain, cross_gain, dec_ffnorm)
     small = jnp.concatenate(list(gains) + [enc_rel.reshape(-1), dec_rel.reshape(-1)])
-    small = lax.all_gather(small, "fsdp", axis=0)
+    small_size = small.shape[0]
+    small = jnp.pad(small.astype(F32), (0, -small_size % 128)).reshape(-1, 128)
+    segments = segments.reshape(2, 1, chunk)
+    first_jobs = [
+        swap_job(enc_input),
+        gather_job("fsdp", small, planes),
+        over_planes(qkv_part(enc_qkv)),
+        over_planes(qkv_part(memory)),
+        swap_job(dec_input),
+    ]
+    if parts == 1:
+        first_jobs.append(block_job(segments))
+    xe, small, w_eqkv, table, xd, *segs = ship(0, planes, first_jobs)
+    xe, xd = joined(enc_input, xe), joined(dec_input, xd)
+    if parts == 1:
+        seg = segs[0].reshape(-1)
+    else:
+        segs = lax.all_gather(segments.reshape(2, chunk), CTX, axis=1, tiled=True)
+        seg = lax.dynamic_index_in_dim(segs, seq, 0, keepdims=False)
+    small = small.reshape(planes, -1)[:, :small_size]
     per = enc_gain.shape[0]
-    gain_rows = [small[:, per * i : per * (i + 1)].reshape(1, D).astype(F32) for i in range(5)]
+    gain_rows = [small[:, per * i : per * (i + 1)].reshape(1, D) for i in range(5)]
     g_enc, g_effn, g_dec, g_cross, g_dffn = gain_rows
     per_rel = enc_rel.size
     rels = [
@@ -553,42 +939,31 @@
     onehot = (buckets[:, None] == jnp.arange(BUCKETS, dtype=jnp.int32)[None, :]).astype(BF)
 
     def bias_vector(rel):
-        own = lax.dynamic_slice_in_dim(rel, HQ * tp, HQ, 1)
+        own = lax.dynamic_slice_in_dim(rel, HQ * tp, HQ, 1).astype(BF)
         return lax.dot_general(
             own, onehot, (((0,), (1,)), ((), ())), preferred_element_type=F32
         ).reshape(HQ, 1, 2 * length)
 
-    def qkv_part(w):
-        return jnp.concatenate([cols(w, D * i) for i in range(w.shape[1] // D)], axis=1)
-
-    hidden = enc_ffout.shape[0] // TP
-
-    def ffin_part(w):
-        return jnp.concatenate(
-            [cols(w, hidden * TP * i, hidden) for i in range(planes)], axis=1
-        )
-
-    def ffout_part(w):
-        return lax.dynamic_slice_in_dim(w, hidden * tp, hidden, 0)
-
-    w_eqkv = fetch(qkv_part(enc_qkv))
-    table = fetch(qkv_part(memory))
-    xe, xd = swap(enc_input), swap(dec_input)
-    segs = lax.all_gather(segments, CTX, axis=1, tiled=True)
-    seg = lax.dynamic_index_in_dim(segs, seq, 0, keepdims=False)
-    pairs = [(i * TP + j, j * TP + i) for i in range(TP) for j in range(TP)]
-    projs = jnp.stack([enc_proj, dec_proj, cross_proj])
-    if planes == TP:
-        projs = lax.ppermute(projs, ("tp", "fsdp"), pairs)
-    else:
-        projs = lax.all_gather(projs, "fsdp", axis=1, tiled=True)
-        projs = lax.dynamic_slice_in_dim(projs, QC * tp, QC, 1)
-    w_eproj, w_dproj, w_cproj = projs[0], projs[1], projs[2]
-    w_dqkv = fetch(qkv_part(dec_qkv))
-    w_effin, w_effout = fetch(ffin_part(enc_ffin)), fetch(ffout_part(enc_ffout))
-    w_cq, w_ckv = fetch(qkv_part(cross_query)), fetch(qkv_part(cross_kv))
-    w_dffin, w_dffout = fetch(ffin_part(dec_ffin)), fetch(ffout_part(dec_ffout))
-    xec, xdc = swap(enc_cotan), swap(dec_cotan)
+    turned = planes == TP
+
+    def proj_jobs(w):
+        return [turn_job(w)] if turned else []
+
+    def proj_of(got, w):
+        if turned:
+            return got.pop()
+        full = lax.all_gather(w, "fsdp", axis=0, tiled=True)
+        return lax.dynamic_slice_in_dim(full, QC * tp, QC, 0)
+
+    en, (w_eqkv, table, w_dqkv, *got) = gather_norm(
+        1,
+        planes,
+        xe,
+        g_enc,
+        [over_seq(w_eqkv), over_seq(table), over_planes(qkv_part(dec_qkv))] + proj_jobs(enc_proj),
+    )
+    w_eproj = proj_of(got, enc_proj)
+    w_eqkv, table = matrix(w_eqkv), matrix(table)
 
     index = jnp.arange(2 * TP, dtype=jnp.int32)
     pos = ((index // TP) * TP * parts + TP * part + index % TP) * chunk
@@ -628,7 +1003,9 @@
             got = attn_bwd(
                 pos, p, q, kv, grad, att, mem, bvec is not None, 0, kv_off, BF if parts == 1 else F32
             )
-            return got[0], collect(got[1]), got[2:]
+            if parts == 1:
+                return got[0], got[1:]
+            return jnp.concatenate([got[0], collect(got[1])], axis=1), got[2:]
 
         return att, back
 
@@ -642,117 +1019,220 @@
 
         return att, back
 
-    en = gather_norm(0, xe, g_enc)
     e_rows = mm(en, w_eqkv).astype(BF)
     e_att, e_back = self_attn(e_rows, bias_vector(rels[0]), mkv, segk_mem, False)
-    e_mid, e_fn = stage(2, [(e_att, w_eproj, False)], xe, gather="norm", gain=g_effn)
-    dn = gather_norm(1, xd, g_dec)
+    dn, (w_dqkv, w_effin, *got) = gather_norm(
+        2,
+        planes,
+        xd,
+        g_dec,
+        [over_seq(w_dqkv), over_planes(ffin_part(enc_ffin))] + proj_jobs(dec_proj),
+    )
+    w_dproj = proj_of(got, dec_proj)
+    w_dqkv = matrix(w_dqkv)
+    (e_mid, e_fn), (w_effin, w_effout, w_cq, w_ckv) = stage(
+        3,
+        planes,
+        [(e_att, w_eproj, False)],
+        xe,
+        gather="norm",
+        gain=g_effn,
+        jobs=[
+            over_seq(w_effin),
+            over_planes(ffout_part(enc_ffout)),
+            over_planes(qkv_part(cross_query)),
+            over_planes(qkv_part(cross_kv)),
+        ],
+    )
+    w_effin = matrix(w_effin)
+    e_pre = mm(e_fn, w_effin)
+    e_act = gelu(e_pre).astype(BF)
     d_rows = mm(dn, w_dqkv).astype(BF)
     d_att, d_back = self_attn(d_rows, bias_vector(rels[1]), None, segk, True)
-    e_pre = mm(e_fn, w_effin)
-    e_act = gelu(e_pre).astype(BF)
-    e_low, e_gath = stage(3, [(e_act, w_effout, False)], e_mid, gather="low", dtype=BF)
-    d_mid, c_n = stage(4, [(d_att, w_dproj, False)], xd, gather="norm", gain=g_cross)
+    (d_mid, c_n), (w_effout, w_cq, w_ckv, w_dffin, *got) = stage(
+        4,
+        planes,
+        [(d_att, w_dproj, False)],
+        xd,
+        gather="norm",
+        gain=g_cross,
+        jobs=[
+            over_seq(w_effout),
+            over_seq(w_cq),
+            over_seq(w_ckv),
+            over_planes(ffin_part(dec_ffin)),
+        ]
+        + proj_jobs(cross_proj),
+    )
+    w_cproj = proj_of(got, cross_proj)
+    w_effout, w_cq, w_ckv = matrix(w_effout), matrix(w_cq), matrix(w_ckv)
+    (e_low, e_gath), (w_dffin, w_dffout, xdc) = stage(
+        5,
+        planes,
+        [(e_act, w_effout, False)],
+        e_mid,
+        gather="low",
+        dtype=BF,
+        jobs=[over_seq(w_dffin), over_planes(ffout_part(dec_ffout)), swap_job(dec_cotan)],
+    )
+    xdc = joined(dec_cotan, xdc)
+    w_dffin = matrix(w_dffin)
     c_q = mm(c_n, w_cq).astype(BF)
     c_kv = mm(e_gath, w_ckv).astype(BF)
     c_att, c_back = cross_attn(c_q, c_kv)
-    d_cross, d_fn = stage(5, [(c_att, w_cproj, False)], d_mid, gather="norm", gain=g_dffn)
+    (d_cross, d_fn), (w_dffout, xec, came) = stage(
+        6,
+        planes,
+        [(c_att, w_cproj, False)],
+        d_mid,
+        gather="norm",
+        gain=g_dffn,
+        jobs=[over_seq(w_dffout), swap_job(enc_cotan), swap_job(e_low)],
+    )
+    xec = joined(enc_cotan, xec)
+    enc_output = joined(e_low, came)
+    w_dffout = matrix(w_dffout)
     d_pre = mm(d_fn, w_dffin)
     d_act = gelu(d_pre).astype(BF)
-    d_low, up_g = stage(
-        6, [(d_act, w_dffout, False)], d_cross, gather="given", given=xdc, dtype=BF
-    )
-    enc_output, dec_output = swap(e_low), swap(d_low)
-
-    def ff_back(number, up, up_rows, fn, act, pre, w_in, w_out, mid, gain):
+    (d_low, up_g), _ = stage(
+        7, planes, [(d_act, w_dffout, False)], d_cross, gather="given", given=xdc, dtype=BF
+    )
+
+    def pieces(g):
+        if parts > 1:
+            g = lax.psum(g, "part")
+        return g.reshape(planes, 2, g.shape[0] // split, g.shape[1])
+
+    def proj_pieces(g):
+        return pieces(g.reshape(2 * QC, D // 2))
+
+    def step1(gs):
+        return [swap_job(g, 1, True) for g in gs]
+
+    def step2(gs):
+        return [deal_job("fsdp", g) for g in gs]
+
+    def step3(gs):
+        return [gather_job("across", g) for g in gs]
+
+    def step4(gs):
+        return [gather_job("seq", g) for g in gs]
+
+    def step5(gs, widths):
+        return [last_job(g, width) for g, width in zip(gs, widths)]
+
+    ff_widths, qkv_widths, proj_widths = [hidden, 0], [QC, QC], [0]
+
+    def take(got, n):
+        out = got[:n]
+        del got[:n]
+        return out
+
+    def ff_grads(up_rows, fn, act, pre, w_out):
         d_out = mm_tn(act, up_rows).astype(BF)
         pre_grad = gelu_back(pre, mm_nt(up_rows, w_out)).astype(BF)
         d_in = mm_tn(fn, pre_grad).astype(BF)
-        got = stage(number, [(pre_grad, w_in, True)], up, back=(mid, gain), gather="low")
-        return got, d_in, d_out
-
-    (up, up_g, dg_dffn), g_dffin, g_dffout = ff_back(
-        7, xdc, up_g, d_fn, d_act, d_pre, w_dffin, w_dffout, d_cross, g_dffn
-    )
-    g_cproj = mm_tn(c_att, up_g).astype(BF)
+        return pre_grad, [pieces(d_in), pieces(d_out)]
+
+    pre_grad, g_dff = ff_grads(up_g, d_fn, d_act, d_pre, w_dffout)
+    (up, up_g, dg_dffn), got = stage(
+        8,
+        planes,
+        [(pre_grad, w_dffin, True)],
+        xdc,
+        back=(d_cross, g_dffn),
+        gather="low",
+        jobs=step1(g_dff) + [swap_job(d_low)],
+    )
+    dec_output = joined(d_low, got.pop())
+    g_dff = got
     c_dq, c_dkv = c_back(mm_nt(up_g, w_cproj).astype(BF))
-    g_cq = mm_tn(c_n, c_dq).astype(BF)
-    g_ckv = mm_tn(e_gath, c_dkv).astype(BF)
-    e_up, e_up_g = stage(8, [(c_dkv, w_ckv, True)], xec, gather="low")
-    up, up_g, dg_cross = stage(
-        9, [(c_dq, w_cq, True)], up, back=(d_mid, g_cross), gather="low"
-    )
-    g_dproj = mm_tn(d_att, up_g).astype(BF)
-    d_dq, d_dkv, (d_dbv,) = d_back(mm_nt(up_g, w_dproj).astype(BF))
-    g_dqkv = jnp.concatenate([mm_tn(dn, d_dq), mm_tn(dn, d_dkv)], axis=1).astype(BF)
-    d_in, dg_dec = stage(
+    g_c = [pieces(mm_tn(c_n, c_dq).astype(BF)), pieces(mm_tn(e_gath, c_dkv).astype(BF))]
+    if turned:
+        g_c.append(proj_pieces(mm_tn(c_att, up_g).astype(BF)))
+    else:
+        g_cproj = mm_tn(c_att, up_g).astype(BF)
+    (up, up_g, dg_cross), got = stage(
+        9,
+        planes,
+        [(c_dq, w_cq, True)],
+        up,
+        back=(d_mid, g_cross),
+        gather="low",
+        jobs=step1(g_c) + step2(g_dff),
+    )
+    g_c = take(got, len(g_c))
+    g_dff = got
+    (e_up, e_up_g), got = stage(
         10,
-        [(d_dq, w_dqkv[:, :QC], True), (d_dkv, w_dqkv[:, QC:], True)],
+        planes,
+        [(c_dkv, w_ckv, True)],
+        xec,
+        gather="low",
+        jobs=step2(g_c) + step3(g_dff),
+    )
+    g_c = take(got, len(g_c))
+    g_dff = got
+    d_rows_grad, (d_dbv,) = d_back(mm_nt(up_g, w_dproj).astype(BF))
+    g_dqkv = mm_tn(dn, d_rows_grad).astype(BF)
+    g_d = [pieces(g_dqkv)]
+    if turned:
+        g_d.append(proj_pieces(mm_tn(d_att, up_g).astype(BF)))
+        turn = [turn_job(g_c.pop())]
+    else:
+        g_dproj = mm_tn(d_att, up_g).astype(BF)
+        turn = []
+    (d_in, dg_dec), got = stage(
+        11,
+        planes,
+        [(d_rows_grad, w_dqkv, True)],
         up,
         back=(xd, g_dec),
-    )
-    (e_up, e_up_g, dg_effn), g_effin, g_effout = ff_back(
-        11, e_up, e_up_g, e_fn, e_act, e_pre, w_effin, w_effout, e_mid, g_effn
-    )
-    g_eproj = mm_tn(e_att, e_up_g).astype(BF)
-    e_dq, e_dkv, (e_dbv, d_mkv) = e_back(mm_nt(e_up_g, w_eproj).astype(BF))
-    g_eqkv = jnp.concatenate([mm_tn(en, e_dq), mm_tn(en, e_dkv)], axis=1).astype(BF)
-    g_table = mm_tn(pick, d_mkv).astype(BF)
-    e_in, dg_enc = stage(
+        jobs=step1(g_d) + step4(g_dff) + step3(g_c) + turn,
+    )
+    d_in_low = d_in.astype(BF)
+    g_d = take(got, len(g_d))
+    g_dff, g_c = take(got, 2), take(got, 2)
+    g_cp = got
+    pre_grad, g_eff = ff_grads(e_up_g, e_fn, e_act, e_pre, w_effout)
+    (e_up, e_up_g, dg_effn), got = stage(
         12,
-        [(e_dq, w_eqkv[:, :QC], True), (e_dkv, w_eqkv[:, QC:], True)],
+        planes,
+        [(pre_grad, w_effin, True)],
+        e_up,
+        back=(e_mid, g_effn),
+        gather="low",
+        jobs=step1(g_eff)
+        + step5(g_dff, ff_widths)
+        + step4(g_c)
+        + step3(g_cp)
+        + step2(g_d)
+        + [swap_job(d_in_low)],
+    )
+    dec_ingrad = joined(d_in, got.pop())
+    g_eff = take(got, 2)
+    o_dff, g_c, g_cp = take(got, 2), take(got, 2), take(got, len(g_cp))
+    g_d = got
+    e_rows_grad, (e_dbv, d_mkv) = e_back(mm_nt(e_up_g, w_eproj).astype(BF))
+    if turned:
+        g_ep = [proj_pieces(mm_tn(e_att, e_up_g).astype(BF))]
+        turn = [turn_job(g_d.pop())]
+    else:
+        g_eproj = mm_tn(e_att, e_up_g).astype(BF)
+        g_ep, turn = [], []
+    (e_in, dg_enc), got = stage(
+        13,
+        planes,
+        [(e_rows_grad, w_eqkv, True)],
         e_up,
         back=(xe, g_enc),
-    )
-    enc_ingrad = swap(e_in.astype(BF)).astype(F32)
-    dec_ingrad = swap(d_in.astype(BF)).astype(F32)
-
-    split = 2 * parts
-
-    def reduce_rows(g):
-        return lax.psum_scatter(
-            g, ("fsdp", "seq", "part"), scatter_dimension=0, tiled=True
-        )
-
-    def gather_rows(g):
-        got = lax.all_gather(g, CTX, axis=0)
-        return got.reshape((split, TP) + g.shape)
-
-    def by_cols(got, width):
-        rows = got.shape[2]
-        got = got.reshape(split, TP, rows, -1, width).transpose(0, 2, 3, 1, 4)
-        return got.reshape(split * rows, -1).astype(F32)
-
-    def by_rows(got):
-        return got.transpose(1, 0, 2, 3).reshape(-1, D).astype(F32)
-
-    red = functools.partial(reduce_rows)
-    r_dffin, r_dffout, r_cq, r_ckv = red(g_dffin), red(g_dffout), red(g_cq), red(g_ckv)
-    r_dqkv, r_effin, r_effout = red(g_dqkv), red(g_effin), red(g_effout)
-    r_eqkv, r_table = red(g_eqkv), red(g_table)
-    g_projs = [g_eproj, g_dproj, g_cproj]
-    if planes == TP:
-        r_projs = red(jnp.concatenate(g_projs, axis=1))
-        r_projs = lax.ppermute(r_projs, ("tp", "fsdp"), pairs)
-        r_projs = gather_rows(r_projs)
-        o_projs = [by_rows(r_projs[..., D * i : D * (i + 1)]) for i in range(3)]
-    else:
-        o_projs = []
-        for g in g_projs:
-            full = lax.dynamic_update_slice_in_dim(jnp.zeros((D, D), BF), g, QC * tp, 0)
-            full = lax.psum_scatter(full, "fsdp", scatter_dimension=0, tiled=True)
-            o_projs.append(lax.psum(full.astype(F32), CTX))
-    o_eproj, o_dproj, o_cproj = o_projs
-    o_dffin = by_cols(gather_rows(r_dffin), hidden)
-    o_dffout = by_rows(gather_rows(r_dffout))
-    o_cq = by_cols(gather_rows(r_cq), QC)
-    o_ckv = by_cols(gather_rows(r_ckv), QC)
-    o_dqkv = by_cols(gather_rows(r_dqkv), QC)
-    o_effin = by_cols(gather_rows(r_effin), hidden)
-    o_effout = by_rows(gather_rows(r_effout))
-    o_eqkv = by_cols(gather_rows(r_eqkv), QC)
-    o_table = by_cols(gather_rows(r_table), QC)
-
+        jobs=step2(g_eff) + step5(g_c, qkv_widths) + step4(g_cp) + step3(g_d) + turn + step1(g_ep),
+    )
+    g_eff = take(got, 2)
+    o_c, g_cp, g_d, g_dp = take(got, 2), take(got, len(g_cp)), take(got, 1), take(got, len(turn))
+    g_ep = got
+    g_eqkv = mm_tn(en, e_rows_grad).astype(BF)
+    g_e = [pieces(g_eqkv), pieces(mm_tn(pick, d_mkv).astype(BF))]
     def rel_grad(dbv):
         own = lax.dot_general(
             onehot.astype(F32),
@@ -767,8 +1247,67 @@
     tiny = jnp.concatenate([v.reshape(planes, -1) for v in tiny] + [
         rel_grad(v).reshape(planes, -1) for v in (e_dbv, d_dbv)
     ], axis=1)
-    tiny = lax.psum(tiny, ALL)
-    tiny = lax.dynamic_index_in_dim(tiny, plane, 0, keepdims=False)
+    tiny = tiny.reshape(-1, 128)
+    if parts > 1:
+        tiny = lax.psum(tiny, "part")
+    got = ship(
+        14,
+        planes,
+        step1(g_e)
+        + step3(g_eff)
+        + step5(g_cp, proj_widths)
+        + step4(g_d)
+        + step3(g_dp)
+        + step2(g_ep)
+        + [total_job("fsdp", tiny, planes), swap_job(e_in.astype(BF))],
+    )
+    enc_ingrad = joined(e_in, got.pop())
+    tiny = got.pop()
+    g_e = take(got, 2)
+    g_eff, o_cp, g_d = take(got, 2), take(got, len(g_cp)), take(got, 1)
+    g_dp = take(got, len(g_dp))
+    g_ep = got
+    got = ship(
+        15,
+        planes,
+        step2(g_e)
+        + step4(g_eff)
+        + step5(g_d, qkv_widths)
+        + step4(g_dp)
+        + [turn_job(g) for g in g_ep]
+        + [total_job("seq", tiny)],
+    )
+    tiny = got.pop()
+    g_e = take(got, 2)
+    g_eff, o_d, g_dp, g_ep = take(got, 2), take(got, 1), take(got, len(g_dp)), got
+    got = ship(
+        16,
+        planes,
+        step3(g_e + g_ep) + step5(g_eff, ff_widths) + step5(g_dp, proj_widths) + [total_job("across", tiny)],
+    )
+    tiny = got.pop()
+    g_e = take(got, 2 + len(g_ep))
+    o_eff, o_dp = take(got, 2), got
+    got = ship(17, planes, step4(g_e) + [total_job("core", tiny)])
+    tiny = got.pop()
+    got = ship(18, planes, step5(got, qkv_widths + proj_widths))
+    o_e, o_ep = take(got, 2), got
+
+    def proj_rows(got, g):
+        if turned:
+            return got[0].reshape(-1, D)
+        full = lax.dynamic_update_slice_in_dim(jnp.zeros((D, D), BF), g, QC * tp, 0)
+        full = lax.psum_scatter(full, "fsdp", scatter_dimension=0, tiled=True)
+        return lax.psum(full.astype(F32), CTX)
+
+    o_eproj = proj_rows(o_ep, None if turned else g_eproj)
+    o_dproj = proj_rows(o_dp, None if turned else g_dproj)
+    o_cproj = proj_rows(o_cp, None if turned else g_cproj)
+    o_dffin, o_dffout = o_dff
+    o_effin, o_effout = o_eff
+    o_cq, o_ckv = o_c
+    (o_dqkv,), (o_eqkv, o_table) = o_d, o_e
+    tiny = lax.dynamic_index_in_dim(tiny.reshape(planes, -1), plane, 0, keepdims=False)
     o_gains = [tiny[per * i : per * (i + 1)] for i in range(5)]
     o_rels = [
         tiny[5 * per + per_rel * i : 5 * per + per_rel * (i + 1)].reshape(-1, HEADS)

time: 1300 us -> 761 us (0.59)
  waiting for transfers between devices: 401 us -> 0 us
  blocking collectives: 273 us -> 0 us
  Pallas kernels: 356 us -> 615 us
  local copies, waits for them, and re-layouts: 138 us -> 51.9 us
  starting transfers between devices: 20.3 us -> 0 us
  between operations: 16.4 us -> 1.77 us
    reduce_scatter x10 -> x0, waiting for transfers between devices: 355 us -> none  [reduce_rows(): lax.psum_scatter(g, ('fsdp', 'seq', 'part'), scatter_dimension=0, tiled=T...]
    pallas_call x13 -> x19, Pallas kernels: 262 us -> 507 us  [call_with_jobs(): pl.pallas_call(body, out_shape=tuple(outs) + tuple((jax.ShapeDtypeStruct(...]
    all_gather x13 -> x0, blocking collectives: 233 us -> none  [the longest x5 119 us: fetch(): return lax.all_gather(x, 'fsdp', axis=0, tiled=True)]
    convert_element_type x32 -> x5, local copies, waits for them, and re-layouts: 58.3 us -> 5.56 us  [the longest x1 1.32 us: per_device(): g_dqkv = mm_tn(dn, d_rows_grad).astype(BF)]
    all_gather x8 -> x0, waiting for transfers between devices: 44.2 us -> none  [the longest x4 44.2 us: gather_rows(): got = lax.all_gather(g, CTX, axis=0)]
    psum x1 -> x0, blocking collectives: 39.9 us -> none  [per_device(): tiny = lax.psum(tiny, ALL)]
    unnamed x252 -> x146, local copies, waits for them, and re-layouts: 50.9 us -> 16.1 us
    ppermute x10 -> x0, starting transfers between devices: 19.6 us -> none  [the longest x8 9.85 us: swap(): came = lax.ppermute(other, 'seq', [(0, 1), (1, 0)])]
  transfers between devices with their start and end apart: 28 -> 0, of which waited for: 10 -> 0; matrix products, arithmetic and copies ran while one was open for 12% -> 0% of each run, Pallas kernels for 21% -> 0%
where the time goes in v2:
time: 761 us; the launch traced here: 754 us
  Pallas kernels  615 us (81%)
  matrix products  66.1 us (9%)
  local copies, waits for them, and re-layouts  51.9 us (7%)
  other arithmetic  19.6 us (3%)
    pallas_call x19, Pallas kernels, call_with_jobs(): pl.pallas_call(body, out_shape=tuple(outs) + tuple((jax.ShapeDtypeStruct(...  507 us
    pallas_call x3, Pallas kernels, attn_bwd(): pl.pallas_call(functools.partial(attn_bwd_kernel, conf), out_shape=tuple(...  57.3 us
    pallas_call x3, Pallas kernels, attn_fwd(): pl.pallas_call(functools.partial(attn_fwd_kernel, conf), out_shape=(jax.S...  51 us
    dot_general x12, matrix products, mm_tn(): lax.dot_general(a, b, (((0,), (0,)), ((), ())), preferred_element_type=F32)  27.5 us
    dot_general x7, matrix products, mm(): return jnp.dot(a, b, preferred_element_type=F32)  23.4 us
    unnamed x146, local copies, waits for them, and re-layouts  16.1 us

profile of v2, /device:TPU:0, one launch (start us, length us, event | category | flops | bytes accessed | tf_op | source)
XLA Modules:
  0.0 754.4 jit_solution(17056153161316136396)
XLA Ops:
  0.7 1.3 fusion.54
  5.9 3.4 concatenate.30
  9.9 21.0 %ship.6 = (bf16[128,768]{1,0:T(8,128)(2,1)}, f32[4,9,128]{2,1,0:T(8,128)}, bf16[4,96,576]{2,1,0:T(8,128)(2,1)}, bf16[4,32,384]{2,1,0:T(8,128)(2,1)}, bf16[128,768]{1,0:T(8,128)(2,1)}, /*index=5*/s32[8,1,128]{2,1,0:T(1,128)}) custom-call(bf16[2,128,768]{2,1,0:T(8,128)(2,1)} %refs_0_.1, f32[9,128]{1,0:T(8,128)} %bitcast_convert_fusion.refs_1_, ...), custom_call_target="tpu_custom_call" | custom-call | bytes 8388608 | tf_op jit(solution)/shard_map/ship/pallas_call | solution.py:402
  34.2 18.5 %gather_norm.2 = (bf16[1024,768]{1,0:T(8,128)(2,1)}, bf16[4,2,96,576]{3,2,1,0:T(8,128)(2,1)}, bf16[4,2,32,384]{3,2,1,0:T(8,128)(2,1)}, bf16[4,96,576]{2,1,0:T(8,128)(2,1)}, bf16[192,768]{1,0:T(8,128)(2,1)}) custom-call(bf16[2,128,768]{2,1,0:T(8,128)(2,1)} %pad_maximum_fusion.2.refs_0_.refs_2_.refs_4_, f32[1,768]{1,0:T(1,128)} %reshape.215.refs_1_.refs_3_, ...), custom_call_target="tpu_custom_call" | custom-call | flops 1000000 | bytes 8388608 | tf_op jit(solution)/shard_map/gather_norm/pallas_call | solution.py:402
  52.8 4.2 convolution_convert_fusion.1.refs_0_.refs_1_.refs_2_
  61.6 19.3 %attn_fwd.3 = (bf16[1024,192]{1,0:T(8,128)(2,1)}, bf16[3,1024,1280]{2,1,0:T(8,128)(2,1)}) custom-call(s32[8]{0:T(128)} %fusion.50.pos_ref, bf16[1024,576]{1,0:T(8,128)(2,1)} %convolution_convert_fusion.1.refs_0_.refs_1_.refs_2_, bf16[1024,576]{1,0:T(8,128)(2,1)} %convolution_convert_fusion.1.refs_0_.refs_1_.refs_2_, s32[1024,1]{1,0:T(8,128)} %copy.76.refs_2_, ...), custom_call_target="tpu_custom_call" | custom-call | flops 1006632960 | bytes 7864320 | tf_op jit(solution)/shard_map/attn_fwd/pallas_call | solution.py:680
  81.7 1.4 fusion.52
  84.6 23.4 %gather_norm.3 = (bf16[1024,768]{1,0:T(8,128)(2,1)}, bf16[4,2,96,576]{3,2,1,0:T(8,128)(2,1)}, bf16[4,96,768]{2,1,0:T(8,128)(2,1)}, bf16[192,768]{1,0:T(8,128)(2,1)}) custom-call(bf16[2,128,768]{2,1,0:T(8,128)(2,1)} %pad_maximum_fusion.3.refs_0_.refs_2_.refs_4_, f32[1,768]{1,0:T(1,128)} %reshape.223.refs_1_.refs_3_, ...), custom_call_target="tpu_custom_call" | custom-call | flops 1000000 | bytes 8388608 | tf_op jit(solution)/shard_map/gather_norm/pallas_call | solution.py:402
  110.4 1.6 dynamic_slice.129.refs_6_
  112.0 1.7 constant_dynamic-slice_fusion.1
  113.7 41.7 %stage.11 = (f32[2,128,768]{2,1,0:T(8,128)}, bf16[1024,768]{1,0:T(8,128)(2,1)}, bf16[4,2,96,768]{3,2,1,0:T(8,128)(2,1)}, bf16[4,96,768]{2,1,0:T(8,128)(2,1)}, bf...) custom-call(bf16[1024,192]{1,0:T(8,128)(2,1)} %get-tuple-element.169.refs_0_.refs_4_, ...), custom_call_target="tpu_custom_call" | custom-call | flops 301989888 | bytes 8388608 | tf_op jit(solution)/shard_map/stage/pallas_call | solution.py:402
  155.5 5.8 multiply_convert_fusion.1
  161.2 2.5 convolution_convert_fusion.refs_0_.refs_1_.refs_2_
  165.0 17.4 %attn_fwd.4 = (bf16[1024,192]{1,0:T(8,128)(2,1)}, bf16[3,1024,1024]{2,1,0:T(8,128)(2,1)}) custom-call(s32[8]{0:T(128)} %fusion.50.pos_ref, bf16[1024,576]{1,0:T(8,128)(2,1)} %convolution_convert_fusion.refs_0_.refs_1_.refs_2_, bf16[1024,576]{1,0:T(8,128)(2,1)} %convolution_convert_fusion.refs_0_.refs_1_.refs_2_, s32[1024,1]{1,0:T(8,128)} %copy.76.refs_2_, ...), custom_call_target="tpu_custom_call" | custom-call | flops 805306368 | bytes 6291456 | tf_op jit(solution)/shard_map/attn_fwd/pallas_call | solution.py:680
  183.8 32.1 %stage.12 = (f32[2,128,768]{2,1,0:T(8,128)}, bf16[1024,768]{1,0:T(8,128)(2,1)}, bf16[4,2,96,768]{3,2,1,0:T(8,128)(2,1)}, bf16[4,2,96,192]{3,2,1,0:T(8,128)(2,1)}...) custom-call(bf16[1024,192]{1,0:T(8,128)(2,1)} %get-tuple-element.178.refs_0_.refs_4_, ...), custom_call_target="tpu_custom_call" | custom-call | flops 301989888 | bytes 8388608 | tf_op jit(solution)/shard_map/stage/pallas_call | solution.py:402
  215.9 28.2 %stage.13 = (bf16[2,128,768]{2,1,0:T(8,128)(2,1)}, bf16[1024,768]{1,0:T(8,128)(2,1)}, bf16[4,2,96,768]{3,2,1,0:T(8,128)(2,1)}, bf16[4,96,768]{2,1,0:T(8,128)(2,1)}, bf16[128,768]{1,0:T(8,128)(2,1)}) custom-call(bf16[1024,768]{1,0:T(8,128)(2,1)} %get-tuple-element.347.refs_0_, bf16[768,768]{1,0:T(8,128)(2,1)} %bitcast.172, ...), custom_call_target="tpu_custom_call" | custom-call | flops 1207959552 | bytes 8388608 | tf_op jit(solution)/shard_map/stage/pallas_call | solution.py:402
  245.9 3.4 convolution_convert_fusion.8.refs_1_.refs_2_
  249.4 1.4 convolution_convert_fusion.10.refs_0_.refs_1_
  250.7 14.3 %attn_fwd.5 = (bf16[1024,192]{1,0:T(8,128)(2,1)}, bf16[3,1024,1024]{2,1,0:T(8,128)(2,1)}) custom-call(s32[8]{0:T(128)} %fusion.50.pos_ref, bf16[1024,192]{1,0:T(8,128)(2,1)} %convolution_convert_fusion.10.refs_0_.refs_1_, bf16[1024,384]{1,0:T(8,128)(2,1)} %convolution_convert_fusion.8.refs_1_.refs_2_, s32[1024,1]{1,0:T(8,128)} %copy.76.refs_2_, ...), custom_call_target="tpu_custom_call" | custom-call | flops 805306368 | bytes 6291456 | tf_op jit(solution)/shard_map/attn_fwd/pallas_call | solution.py:680
  265.7 27.0 %stage.14 = (f32[2,128,768]{2,1,0:T(8,128)}, bf16[1024,768]{1,0:T(8,128)(2,1)}, bf16[4,2,96,768]{3,2,1,0:T(8,128)(2,1)}, bf16[128,768]{1,0:T(8,128)(2,1)}, bf16[128,768]{1,0:T(8,128)(2,1)}) custom-call(bf16[1024,192]{1,0:T(8,128)(2,1)} %get-tuple-element.191.refs_0_.refs_4_, bf16[192,768]{1,0:T(8,128)(2,1)} %get-tuple-element.192.refs_1_, ...), custom_call_target="tpu_custom_call" | custom-call | flops 301989888 | bytes 8388608 | tf_op jit(solution)/shard_map/stage/pallas_call | solution.py:402
  292.7 5.3 multiply_convert_fusion
  297.9 21.5 %stage.15 = (bf16[2,128,768]{2,1,0:T(8,128)(2,1)}, bf16[1024,768]{1,0:T(8,128)(2,1)}) custom-call(bf16[1024,768]{1,0:T(8,128)(2,1)} %get-tuple-element.349.refs_0_, bf16[768,768]{1,0:T(8,128)(2,1)} %bitcast.202, f32[2,128,768]{2,1,0:T(8,128)} %get-tuple-element.199.refs_2_.refs_4_, bf16[2,128,768]{2,1,0:T(8,128)(2,1)} %pad_maximum_fusion.5.refs_3_.refs_2_), custom_call_target="tpu_custom_call" | custom-call | flops 1207959552 | bytes 8388608 | tf_op jit(solution)/shard_map/stage/pallas_call | solution.py:402
  319.5 4.5 convolution_convert_fusion.4
  324.0 3.7 fusion.13.refs_0_
  327.7 2.5 convolution_convert_fusion.5
  330.2 37.6 %stage.16 = (f32[2,128,768]{2,1,0:T(8,128)}, bf16[1024,768]{1,0:T(8,128)(2,1)}, f32[1,768]{1,0:T(1,128)}, bf16[4,96,768]{2,1,0:T(8,128)(2,1)}, bf16[4,96,768]{2,1,0:T(8,128)(2,1)}, /*index=5*/bf16[128,768]{1,0:T(8,128)(2,1)}) custom-call(bf16[1024,768]{1,0:T(8,128)(2,1)} %copy-done.15, bf16[768,768]{1,0:T(8,128)(2,1)} %bitcast.174, ...), custom_call_target="tpu_custom_call" | custom-call | flops 1207959552 | bytes 8388608 | tf_op jit(solution)/shard_map/stage/pallas_call | solution.py:402
  367.9 2.0 convolution_convert_fusion.16
  370.6 2.1 convolution_convert_fusion.13
  373.7 16.4 %attn_bwd.3 = (bf16[1024,192]{1,0:T(8,128)(2,1)}, bf16[1024,384]{1,0:T(8,128)(2,1)}) custom-call(s32[8]{0:T(128)} %fusion.50.pos_ref, bf16[3,1024,1024]{2,1,0:T(8,128)(2,1)} %get-tuple-element.205.refs_0_, bf16[1024,192]{1,0:T(8,128)(2,1)} %convolution_convert_fusion.10.refs_0_.refs_1_, bf16[1024,384]{1,0:T(8,128)(2,1)} %convolution_convert_fusion.8.refs_1_.refs_2_, ...), custom_call_target="tpu_custom_call" | custom-call | flops 1610612736 | bytes 6291456 | tf_op jit(solution)/shard_map/attn_bwd/pallas_call | solution.py:807
  390.1 3.1 convolution_convert_fusion.9
  394.7 30.2 %stage.17 = (f32[2,128,768]{2,1,0:T(8,128)}, bf16[1024,768]{1,0:T(8,128)(2,1)}, f32[1,768]{1,0:T(1,128)}, bf16[4,96,192]{2,1,0:T(8,128)(2,1)}, bf16[4,96,384]{2,...) custom-call(bf16[1024,192]{1,0:T(8,128)(2,1)} %get-tuple-element.209.refs_0_, ...), custom_call_target="tpu_custom_call" | custom-call | flops 301989888 | bytes 8388608 | tf_op jit(solution)/shard_map/stage/pallas_call | solution.py:402
  424.9 2.0 convolution_convert_fusion.15
  427.7 2.1 convolution_convert_fusion.12
  430.8 19.7 %attn_bwd.4 = (bf16[1024,576]{1,0:T(8,128)(2,1)}, f32[3,1,2048]{2,1,0:T(1,128)}) custom-call(s32[8]{0:T(128)} %fusion.50.pos_ref, bf16[3,1024,1024]{2,1,0:T(8,128)(2,1)} %get-tuple-element.220.refs_0_, bf16[1024,576]{1,0:T(8,128)(2,1)} %convolution_convert_fusion.refs_0_.refs_1_.refs_2_, bf16[1024,576]{1,0:T(8,128)(2,1)} %convolution_convert_fusion.refs_0_.refs_1_.refs_2_, ...), custom_call_target="tpu_custom_call" | custom-call | flops 1610612736 | bytes 6291456 | tf_op jit(solution)/shard_map/attn_bwd/pallas_call | solution.py:807
  450.5 2.4 convolution_convert_fusion.7
  453.0 1.3 copy.84
  455.1 36.1 %stage.18 = (f32[2,128,768]{2,1,0:T(8,128)}, bf16[1024,768]{1,0:T(8,128)(2,1)}, bf16[96,192]{1,0:T(8,128)(2,1)}, bf16[96,384]{1,0:T(8,128)(2,1)}, bf16[48,384]{1...) custom-call(bf16[1024,384]{1,0:T(8,128)(2,1)} %get-tuple-element.207.refs_0_, ...), custom_call_target="tpu_custom_call" | custom-call | flops 603979776 | bytes 8388608 | tf_op jit(solution)/shard_map/stage/pallas_call | solution.py:402
  491.2 34.7 %stage.19 = (f32[2,128,768]{2,1,0:T(8,128)}, f32[1,768]{1,0:T(1,128)}, bf16[4,96,576]{2,1,0:T(8,128)(2,1)}, bf16[4,48,384]{2,1,0:T(8,128)(2,1)}, bf16[2,2,96,768...) custom-call(bf16[1024,576]{1,0:T(8,128)(2,1)} %get-tuple-element.222, ...), custom_call_target="tpu_custom_call" | custom-call | flops 905969664 | bytes 8388608 | tf_op jit(solution)/shard_map/stage/pallas_call | solution.py:402
  525.9 1.9 convert_element_type.125.refs_14_
  527.8 2.5 convolution_convert_fusion.2
  530.3 3.5 fusion.6.refs_0_
  533.8 2.5 convolution_convert_fusion.3
  536.3 45.6 %stage.20 = (f32[2,128,768]{2,1,0:T(8,128)}, bf16[1024,768]{1,0:T(8,128)(2,1)}, f32[1,768]{1,0:T(1,128)}, bf16[4,96,768]{2,1,0:T(8,128)(2,1)}, bf16[4,96,768]{2,...) custom-call(bf16[1024,768]{1,0:T(8,128)(2,1)} %copy-done.13, ...), custom_call_target="tpu_custom_call" | custom-call | flops 1207959552 | bytes 8388608 | tf_op jit(solution)/shard_map/stage/pallas_call | solution.py:402
  582.0 2.0 convolution_convert_fusion.14
  586.5 21.3 %attn_bwd.5 = (bf16[1024,576]{1,0:T(8,128)(2,1)}, f32[3,1,2048]{2,1,0:T(1,128)}, bf16[256,384]{1,0:T(8,128)(2,1)}) custom-call(s32[8]{0:T(128)} %fusion.50.pos_ref, bf16[3,1024,1280]{2,1,0:T(8,128)(2,1)} %get-tuple-element.204.refs_0_, bf16[1024,576]{1,0:T(8,128)(2,1)} %convolution_convert_fusion.1.refs_0_.refs_1_.refs_2_, ...), custom_call_target="tpu_custom_call" | custom-call | flops 2013265920 | bytes 7864320 | tf_op jit(solution)/shard_map/attn_bwd/pallas_call | solution.py:807
  607.8 32.1 %stage.21 = (f32[2,128,768]{2,1,0:T(8,128)}, f32[1,768]{1,0:T(1,128)}, bf16[96,768]{1,0:T(8,128)(2,1)}, bf16[96,768]{1,0:T(8,128)(2,1)}, f32[192,768]{1,0:T(8,12...) custom-call(bf16[1024,576]{1,0:T(8,128)(2,1)} %get-tuple-element.238, ...), custom_call_target="tpu_custom_call" | custom-call | flops 905969664 | bytes 8388608 | tf_op jit(solution)/shard_map/stage/pallas_call | solution.py:402
  639.9 2.0 convert_element_type.130.refs_9_
  646.5 2.6 convolution_convert_fusion.6
  649.0 1.3 copy.86
  651.4 30.1 %ship.7 = (bf16[4,96,576]{2,1,0:T(8,128)(2,1)}, bf16[4,32,384]{2,1,0:T(8,128)(2,1)}, bf16[2,96,768]{2,1,0:T(8,128)(2,1)}, bf16[2,96,768]{2,1,0:T(8,128)(2,1)}, f...) custom-call(bf16[4,2,96,576]{3,2,1,0:T(8,128)(2,1)} %bitcast.166, ...), custom_call_target="tpu_custom_call" | custom-call | bytes 8388608 | tf_op jit(solution)/shard_map/ship/pallas_call | solution.py:402
  681.5 20.3 %ship.8 = (bf16[96,576]{1,0:T(8,128)(2,1)}, bf16[32,384]{1,0:T(8,128)(2,1)}, bf16[2,2,96,768]{3,2,1,0:T(8,128)(2,1)}, bf16[2,2,96,768]{3,2,1,0:T(8,128)(2,1)}, f...) custom-call(bf16[4,96,576]{2,1,0:T(8,128)(2,1)} %get-tuple-element.264.refs_0, ...), custom_call_target="tpu_custom_call" | custom-call | bytes 8388608 | tf_op jit(solution)/shard_map/ship/pallas_call | solution.py:402
  701.7 10.7 %ship.9 = (bf16[2,96,576]{2,1,0:T(8,128)(2,1)}, bf16[2,32,384]{2,1,0:T(8,128)(2,1)}, bf16[2,48,384]{2,1,0:T(8,128)(2,1)}, f32[192,3072]{1,0:T(8,128)}, f32[768,7...) custom-call(bf16[96,576]{1,0:T(8,128)(2,1)} %get-tuple-element.272.refs_0_, ...), custom_call_target="tpu_custom_call" | custom-call | bytes 8388608 | tf_op jit(solution)/shard_map/ship/pallas_call | solution.py:402
  712.4 11.5 %ship.10 = (bf16[2,2,96,576]{3,2,1,0:T(8,128)(2,1)}, bf16[2,2,32,384]{3,2,1,0:T(8,128)(2,1)}, bf16[2,2,48,384]{3,2,1,0:T(8,128)(2,1)}, f32[36,128]{1,0:T(8,128)}) custom-call(bf16[2,96,576]{2,1,0:T(8,128)(2,1)} %get-tuple-element.279.refs_0_, bf16[2,32,384]{2,1,0:T(8,128)(2,1)} %get-tuple-element.280.refs_1_, ...), custom_call_target="tpu_custom_call" | custom-call | bytes 8388608 | tf_op jit(solution)/shard_map/ship/pallas_call | solution.py:402
  724.0 4.4 ship.11
  728.4 2.0 reshape.256
  739.4 1.2 copy.119
  740.6 1.1 copy-done.5
  741.7 1.4 copy.120
  743.1 1.1 copy-done.4
  744.2 1.4 copy.121
  746.5 1.2 copy.122
  750.2 1.4 copy.125
  751.6 1.1 copy-done.2
  752.7 1.4 copy.126
  (221 shorter events, 48.4 us)
Async XLA Ops:
  0.7 56.4 %copy-start = (s32[2,8,20]{2,1,0:T(8,128)S(1)}, s32[2,8,20]{2,1,0:T(8,128)}, u32[]{:S(2)}) copy-start(s32[2,8,20]{2,1,0:T(8,128)} %param.30) | copy-start | bytes 3844
  0.7 30.3 %copy-start.24 = (bf16[2,128,768]{2,1,0:T(8,128)(2,1)S(1)}, bf16[2,128,768]{2,1,0:T(8,128)(2,1)}, u32[]{:S(2)}) copy-start(bf16[2,128,768]{2,1,0:T(8,128)(2,1)} %refs_0_.1) | copy-start | bytes 1179652
  31.0 1.8 copy-start.45
  52.8 4.3 copy-start.40
  52.8 5.3 copy-start.47
  52.8 6.5 copy-start.64
  52.8 7.6 %copy-start.52 = (s32[1,256]{1,0:T(1,128)S(1)}, s32[1,256]{1,0:T(1,128)}, u32[]{:S(2)}) copy-start(s32[1,256]{1,0:T(1,128)} %constant.332) | copy-start | bytes 3076
  61.6 19.3 %copy-start.25 = (bf16[2,128,768]{2,1,0:T(8,128)(2,1)S(1)}, bf16[2,128,768]{2,1,0:T(8,128)(2,1)}, u32[]{:S(2)}) copy-start(bf16[2,128,768]{2,1,0:T(8,128)(2,1)} %refs_4_.2) | copy-start | bytes 1179652
  61.6 19.3 %copy-start.44 = (bf16[128,768]{1,0:T(8,128)(2,1)S(1)}, bf16[128,768]{1,0:T(8,128)(2,1)}, u32[]{:S(2)}) copy-start(bf16[128,768]{1,0:T(8,128)(2,1)} %get-tuple-element.171) | copy-start | bytes 589828
  155.5 5.8 copy-start.20
  155.5 5.8 copy-start.54
  215.9 28.2 %copy-start.21 = (bf16[2,128,768]{2,1,0:T(8,128)(2,1)S(1)}, bf16[2,128,768]{2,1,0:T(8,128)(2,1)}, u32[]{:S(2)}) copy-start(bf16[2,128,768]{2,1,0:T(8,128)(2,1)} %refs_5_.4) | copy-start | bytes 1179652
  244.1 1.8 copy-start.30
  245.9 3.4 copy-start.32
  245.9 3.4 copy-start.55
  265.0 27.7 %copy-start.19 = (bf16[4,2,96,768]{3,2,1,0:T(8,128)(2,1)S(1)}, bf16[4,2,96,768]{3,2,1,0:T(8,128)(2,1)}, u32[]{:S(2)}) copy-start(bf16[4,2,96,768]{3,2,1,0:T(8,128)(2,1)} %get-tuple-element.197) | copy-start | bytes 3538948
  319.5 4.5 copy-start.61
  319.5 4.5 copy-start.65
  319.5 4.5 copy-start.67
  324.0 3.7 copy-start.60
  327.7 2.5 copy-start.15
  330.2 37.6 %copy-start.7 = (bf16[1024,192]{1,0:T(8,128)(2,1)S(1)}, bf16[1024,192]{1,0:T(8,128)(2,1)}, u32[]{:S(2)}) copy-start(bf16[1024,192]{1,0:T(8,128)(2,1)} %get-tuple-element.191.refs_0_.refs_4_) | copy-start | bytes 1179652
  367.8 2.8 copy-start.35
  373.7 16.4 %copy-start.57 = (bf16[1024,768]{1,0:T(8,128)(2,1)S(1)}, bf16[1024,768]{1,0:T(8,128)(2,1)}, u32[]{:S(2)}) copy-start(bf16[1024,768]{1,0:T(8,128)(2,1)} %get-tuple-element.189) | copy-start | bytes 4718596
  390.1 3.1 copy-start.31
  390.1 3.1 copy-start.56
  394.7 30.3 %copy-start.8 = (bf16[1024,192]{1,0:T(8,128)(2,1)S(1)}, bf16[1024,192]{1,0:T(8,128)(2,1)}, u32[]{:S(2)}) copy-start(bf16[1024,192]{1,0:T(8,128)(2,1)} %get-tuple-element.178.refs_0_.refs_4_) | copy-start | bytes 1179652
  424.9 2.8 copy-start.36
  491.2 36.6 %copy-start.14 = (bf16[1024,768]{1,0:T(8,128)(2,1)S(1)}, bf16[1024,768]{1,0:T(8,128)(2,1)}, u32[]{:S(2)}) copy-start(bf16[1024,768]{1,0:T(8,128)(2,1)} %get-tuple-element.347.refs_0_) | copy-start | bytes 4718596
  491.2 36.6 %copy-start.58 = (bf16[1024,768]{1,0:T(8,128)(2,1)S(1)}, bf16[1024,768]{1,0:T(8,128)(2,1)}, u32[]{:S(2)}) copy-start(bf16[1024,768]{1,0:T(8,128)(2,1)} %get-tuple-element.218) | copy-start | bytes 4718596
  527.8 2.5 copy-start.17
  527.8 2.5 copy-start.66
  530.3 3.5 copy-start.53
  533.8 2.5 copy-start.13
  536.3 45.6 %copy-start.6 = (bf16[1024,192]{1,0:T(8,128)(2,1)S(1)}, bf16[1024,192]{1,0:T(8,128)(2,1)}, u32[]{:S(2)}) copy-start(bf16[1024,192]{1,0:T(8,128)(2,1)} %get-tuple-element.169.refs_0_.refs_4_) | copy-start | bytes 1179652
  581.9 2.9 copy-start.34
  581.9 2.9 copy-start.59
  607.8 34.9 %copy-start.63 = (f32[3,1,2048]{2,1,0:T(1,128)S(1)}, f32[3,1,2048]{2,1,0:T(1,128)}, u32[]{:S(2)}) copy-start(f32[3,1,2048]{2,1,0:T(1,128)} %get-tuple-element.260) | copy-start | bytes 73732
  639.8 4.2 copy-start.51
  639.8 4.3 copy-start.50
  639.8 4.4 copy-start.62
  639.9 5.7 copy-start.49
  639.9 5.8 copy-start.48
  639.9 6.6 copy-start.16
  712.4 20.1 %copy-start.29 = (f32[384,384]{1,0:T(8,128)S(1)}, f32[384,384]{1,0:T(8,128)}, u32[]{:S(2)}) copy-start(f32[384,384]{1,0:T(8,128)} %get-tuple-element.293) | copy-start | bytes 1769476
  724.0 6.5 copy-start.46
  724.0 9.6 %copy-start.11 = (f32[2,128,768]{2,1,0:T(8,128)S(1)}, f32[2,128,768]{2,1,0:T(8,128)}, u32[]{:S(2)}) copy-start(f32[2,128,768]{2,1,0:T(8,128)} %get-tuple-element.236) | copy-start | bytes 2359300
  724.0 9.6 %copy-start.37 = (bf16[128,768]{1,0:T(8,128)(2,1)S(1)}, bf16[128,768]{1,0:T(8,128)(2,1)}, u32[]{:S(2)}) copy-start(bf16[128,768]{1,0:T(8,128)(2,1)} %get-tuple-element.263) | copy-start | bytes 589828
  733.5 1.4 copy-start.38
  734.5 1.5 copy-start.28
  735.0 1.9 copy-start.26
  735.0 1.9 copy-start.42
  736.0 1.8 copy-start.23
  736.0 1.8 copy-start.41
  737.0 1.7 copy-start.33
  737.0 2.4 copy-start.10
  739.4 2.3 copy-start.5
  741.7 2.5 copy-start.4
  744.2 2.3 copy-start.9
  746.5 1.4 copy-start.27
  746.5 2.3 copy-start.18
  748.0 2.2 copy-start.3
  750.2 2.5 copy-start.2
  750.2 3.9 copy-start.1
  (4 other events, 5.4 us)

commit v3 on v2

--- a/solution.py
+++ b/solution.py
@@ -24,6 +24,7 @@
 MESH_ID = pl.DeviceIdType.MESH
 MB = 1024 * 1024
 VMEM_LIMIT = 60 * MB
+SHARE = (0.25, 0.34, 0.75)
 
 
 def mm(a, b):
@@ -381,47 +382,73 @@
         return self.ref
 
 
-def call_with_jobs(kernel, number, planes, jobs, operands, outs, scratch, name, cost):
+def call_with_jobs(kernel, number, planes, jobs, operands, outs, scratch, name, cost, filler=None):
+    filler = filler or Idle()
+    jobs = list(jobs)
     n_in, n_out, n_job = len(operands), len(outs), len(jobs)
+    n_load, n_raw, n_fill = len(filler.loads), len(filler.raws), len(filler.outs)
+    loads, raws = list(filler.loads), list(filler.raws)
     n_sems = max(Shipper.count(jobs, planes), 1)
     plain = [job._replace(src=jax.ShapeDtypeStruct(job.src.shape, job.src.dtype)) for job in jobs]
     job_scratch = Shipper.scratch(jobs)
+    n_scratch = len(filler.scratch)
 
     def body(*refs):
-        ins, refs = refs[:n_in], refs[n_in:]
-        srcs, refs = refs[:n_job], refs[n_job:]
-        results, refs = refs[:n_out], refs[n_out:]
-        dsts, refs = refs[:n_job], refs[n_job:]
-        sems, in_sems, refs = refs[0], refs[1], list(refs[2:])
+        refs = list(refs)
+
+        def take(n):
+            out = refs[:n]
+            del refs[:n]
+            return out
+
+        ins, srcs, fills, raw = take(n_in), take(n_job), take(n_load), take(n_raw)
+        results, dsts, fill_outs = take(n_out), take(n_job), take(n_fill)
+        sems, in_sems = take(2)
         loaded = [Loaded(src, refs.pop(0), in_sems.at[i]) for i, src in enumerate(ins)]
-        own = [refs.pop(0) for _ in job_scratch]
-        shipper = Shipper(plain, planes, srcs, dsts, own, sems)
-        kernel(shipper, loaded, list(results), refs)
+        fill_loads = [Loaded(src, refs.pop(0), in_sems.at[n_in + i]) for i, src in enumerate(fills)]
+        shipper = Shipper(plain, planes, srcs, dsts, take(len(job_scratch)), sems)
+        begin = functools.partial(filler.begin, fill_loads, raw, fill_outs, take(n_scratch))
+        kernel(shipper, loaded, list(results), refs, Running(filler, begin))
 
     results = [result_of(job) for job in jobs]
     got = pl.pallas_call(
         body,
-        out_shape=tuple(outs) + tuple(jax.ShapeDtypeStruct(*r) for r in results),
-        in_specs=[HBM_SPEC] * (n_in + n_job),
-        out_specs=(HBM_SPEC,) * (n_out + n_job),
+        out_shape=tuple(outs)
+        + tuple(jax.ShapeDtypeStruct(*r) for r in results)
+        + tuple(filler.outs),
+        in_specs=[HBM_SPEC] * (n_in + n_job + n_load + n_raw),
+        out_specs=(HBM_SPEC,) * (n_out + n_job + n_fill),
         scratch_shapes=[
             pltpu.SemaphoreType.DMA((n_sems,)),
-            pltpu.SemaphoreType.DMA((max(n_in, 1),)),
+            pltpu.SemaphoreType.DMA((max(n_in + n_load, 1),)),
         ]
-        + [pltpu.VMEM(v.shape, v.dtype) for v in operands]
+        + [pltpu.VMEM(v.shape, v.dtype) for v in operands + loads]
         + job_scratch
+        + list(filler.scratch)
         + scratch,
         compiler_params=pltpu.CompilerParams(
             collective_id=number, has_side_effects=True, vmem_limit_bytes=VMEM_LIMIT
         ),
         cost_estimate=pl.CostEstimate(flops=cost, bytes_accessed=8 * MB, transcendentals=0),
         name=name,
-    )(*operands, *[job.src for job in jobs])
-    return got[:n_out], list(got[n_out:])
+    )(*operands, *[job.src for job in jobs], *loads, *raws)
+    return got[:n_out], list(got[n_out : n_out + n_job]), list(got[n_out + n_job :])
+
+
+class Running:
+    def __init__(self, filler, begin):
+        self.begin, self.run, self.end = begin, filler.run, filler.end
+        self.n_steps, self.done = filler.n_steps, 0
+
+    def advance(self, share):
+        high = int(round(share * self.n_steps))
+        if high > self.done:
+            self.run(self.done, high)
+            self.done = high
 
 
 def ship(number, planes, jobs):
-    def kernel(shipper, ins, outs, scratch):
+    def kernel(shipper, ins, outs, scratch, filler):
         shipper.greet(())
         shipper.start()
         shipper.finish()
@@ -429,30 +456,34 @@
     return call_with_jobs(kernel, number, planes, jobs, [], [], [], "ship", 0)[1]
 
 
-def gather_norm(number, planes, x, gain, jobs):
+def gather_norm(number, planes, x, gain, jobs, filler=None):
     chunk = x.shape[1]
 
-    def kernel(shipper, ins, outs, scratch):
+    def kernel(shipper, ins, outs, scratch, filler):
         shipper.greet()
-        shipper.start()
         x_ref, gain_ref = (v.get() for v in ins)
         g = Gatherer(outs[0], scratch[0], scratch[1], chunk, group_ids())
         for j in range(2):
             g.put(j, normed(x_ref[j].astype(F32), gain_ref[...]).astype(BF))
+        shipper.start()
+        filler.begin()
+        filler.advance(0.4)
         for j in range(2):
             g.forward(j)
+        filler.advance(1.0)
         g.finish()
+        filler.end()
         shipper.finish()
 
     outs = [jax.ShapeDtypeStruct((2 * TP * chunk, D), BF)]
     scratch = [pltpu.VMEM((2, chunk, D), BF), pltpu.SemaphoreType.DMA((7, 2))]
-    got, moved = call_with_jobs(
-        kernel, number, planes, jobs, [x, gain], outs, scratch, "gather_norm", 10**6
-    )
-    return got[0], moved
-
-
-def stage_kernel(conf, shipper, ins, outs, scratch):
+    got, moved, made = call_with_jobs(
+        kernel, number, planes, jobs, [x, gain], outs, scratch, "gather_norm", 10**6, filler
+    )
+    return got[0], moved, made
+
+
+def stage_kernel(conf, shipper, ins, outs, scratch, filler):
     chunk, flips, back, gather = conf
     pairs = [(ins.pop(0), ins.pop(0), flip) for flip in flips]
     resid_in = ins.pop(0)
@@ -491,6 +522,7 @@
         return store
 
     shipper.greet()
+    shipper.start()
     g = Gatherer(gath_ref, g_stage, g_sems, chunk, ids) if gather else None
     if gather == "given":
         given_ref = given_in.get()
@@ -507,12 +539,13 @@
         s_x[j] = (keep[j] + r_far[j].astype(F32)).astype(BF)
         c_x.append(send(s_x.at[j], r_x.at[j], sems.at[2 + j], sems.at[4 + j], across))
         c_x[j].start()
-    shipper.start()
     partial(core, into(s_core))
     c_core = send(s_core, r_core, sems.at[6], sems.at[7], core)
     c_core.start()
     partial(me, into(own))
     c_core.wait_recv()
+    filler.begin()
+    filler.advance(SHARE[0])
     resid_ref = resid_in.get()
     x_ref = x_in.get() if back else None
     gains = gain_in.get()[...] if gain_in else None
@@ -528,6 +561,8 @@
 
     for j in range(2):
         c_x[j].wait_recv()
+        if j == 1:
+            filler.advance(SHARE[1])
         total = own[j] + r_core[j].astype(F32) + r_x[j].astype(F32)
         if back:
             x = x_ref[j].astype(F32)
@@ -551,10 +586,13 @@
     if back:
         keep_out(dgain_ref, dgain_out, 10)
     if gather in ("norm", "low"):
+        filler.advance(SHARE[2])
         for j in range(2):
             g.forward(j)
+    filler.advance(1.0)
     if gather:
         g.finish()
+    filler.end()
     c_far.wait_send()
     c_core.wait_send()
     for j in range(2):
@@ -565,7 +603,7 @@
 
 
 def stage(
-    number, planes, pairs, resid, *, back=None, gather=None, gain=None, given=None, dtype=F32, jobs=()
+    number, planes, pairs, resid, *, back=None, gather=None, gain=None, given=None, dtype=F32, jobs=(), filler=None
 ):
     chunk = resid.shape[1]
     operands, flips, cost = [], [], 0
@@ -596,235 +634,278 @@
     if back:
         scratch.append(pltpu.VMEM((1, D), F32))
     kernel = functools.partial(stage_kernel, (chunk, tuple(flips), bool(back), gather))
-    return call_with_jobs(
-        kernel, number, planes, list(jobs), operands, outs, scratch, "stage", cost
-    )
-
-
-def attn_fwd_kernel(conf, pos_ref, *refs):
-    chunk, q_off, kv_off, keys, extra, bias, causal = conf
-    refs = list(refs)
-    q_ref, kv_ref, segq_ref, segk_ref = refs[:4]
-    refs = refs[4:]
-    bvec_ref = refs.pop(0) if bias else None
-    mkv_ref = refs.pop(0) if extra else None
-    att_ref, p_ref, qs, ks, vs, os = refs[:6]
-    toep = refs[6] if bias else None
-    h, b = pl.program_id(0), pl.program_id(1)
-    length = keys
-
-    @pl.when((h == 0) & (b == 0))
-    def _():
+    got, moved, made = call_with_jobs(
+        kernel, number, planes, list(jobs), operands, outs, scratch, "stage", cost, filler
+    )
+    return (got, moved, made) if filler else (got, moved)
+
+
+class Attention:
+    def __init__(self, parts, q, kv, bias, mkv, causal):
+        self.parts, self.causal = parts, causal
+        self.rows, self.keys = q.shape[0], kv.shape[0]
+        self.chunk = self.rows // (2 * TP)
+        self.joint = q is kv
+        self.extra = 0 if mkv is None else mkv.shape[0]
+        self.total = self.keys + self.extra
+        self.bias = bias
+        self.blocks = self.rows // (2 * self.chunk)
+        self.n_steps = HQ * self.blocks
+        self.loads = [q] + ([] if self.joint else [kv]) + ([mkv] if self.extra else [])
+        self.raws = []
+
+    def heads(self, *widths_dtypes):
+        return [pltpu.VMEM((HQ, n, DH), dtype) for n, dtype in widths_dtypes]
+
+    def split_qkv(self, loads, qs, ks, vs):
+        q_ref = loads.pop(0).get()
+        kv_ref = q_ref if self.joint else loads.pop(0).get()
+        at = QC if self.joint else 0
+        keys = self.keys
         for i in range(HQ):
-            qs[i] = q_ref[:, q_off + DH * i : q_off + DH * (i + 1)]
-            ks[i, :keys] = kv_ref[:, kv_off + DH * i : kv_off + DH * (i + 1)]
-            vs[i, :keys] = kv_ref[:, kv_off + QC + DH * i : kv_off + QC + DH * (i + 1)]
-            if extra:
+            qs[i] = q_ref[:, DH * i : DH * (i + 1)]
+            ks[i, :keys] = kv_ref[:, at + DH * i : at + DH * (i + 1)]
+            vs[i, :keys] = kv_ref[:, at + QC + DH * i : at + QC + DH * (i + 1)]
+        if self.extra:
+            mkv_ref = loads.pop(0).get()
+            for i in range(HQ):
                 ks[i, keys:] = mkv_ref[:, DH * i : DH * (i + 1)]
                 vs[i, keys:] = mkv_ref[:, QC + DH * i : QC + DH * (i + 1)]
 
-    if bias:
-
-        @pl.when(b == 0)
-        def _():
-            row = jnp.broadcast_to(bvec_ref[h], (chunk, 2 * length))
-            toep[...] = pltpu.roll(row, 0, 1, stride=1, stride_axis=0)
-
-    rows = pl.ds(pl.multiple_of(b * 2 * chunk, 2 * chunk), 2 * chunk)
-    s = mm_nt(qs[h, rows], ks[h])
-    allowed = segq_ref[rows] == segk_ref[...]
-    if bias:
-        parts = []
-        for u in range(2):
-            off = pl.multiple_of(length - pos_ref[2 * b + u], 128)
-            parts.append(toep[:, pl.ds(off, keys)])
-        biased = s[:, :keys] + jnp.concatenate(parts, axis=0)
-        s = jnp.concatenate([biased, s[:, keys:]], axis=1) if extra else biased
-    if causal:
-        place = lax.broadcasted_iota(jnp.int32, (chunk, 1), 0)
-        places = jnp.concatenate([place + pos_ref[2 * b + u] for u in range(2)], axis=0)
-        allowed = allowed & (lax.broadcasted_iota(jnp.int32, (1, keys), 1) <= places)
-    s = jnp.where(allowed, s, MASKED)
-    top = jnp.max(s, axis=-1, keepdims=True)
-    e = jnp.exp(s - top)
-    p = (e * (1.0 / jnp.sum(e, axis=-1, keepdims=True))).astype(BF)
-    p_ref[0] = p
-    os[h, rows] = mm(p, vs[h]).astype(BF)
-
-    @pl.when((h == HQ - 1) & (b == pl.num_programs(1) - 1))
-    def _():
+    def place(self, row_chunk):
+        upper = row_chunk // TP
+        part = lax.axis_index("part") if self.parts > 1 else 0
+        return (upper * (TP * self.parts) + TP * part + (row_chunk - TP * upper)) * self.chunk
+
+    def step_rows(self, i):
+        h = i // self.blocks
+        b = i - h * self.blocks
+        return h, b, pl.ds(pl.multiple_of(b * (2 * self.chunk), 2 * self.chunk), 2 * self.chunk)
+
+    def diagonal(self, b, u):
+        return pl.ds(pl.multiple_of(self.keys - self.place(2 * b + u), 128), self.keys)
+
+
+class AttentionForward(Attention):
+    def __init__(self, parts, q, kv, segq, segk, bvec, mkv, causal):
+        super().__init__(parts, q, kv, bvec is not None, mkv, causal)
+        self.loads += [segq, segk] + ([bvec] if self.bias else [])
+        self.outs = [
+            jax.ShapeDtypeStruct((self.rows, QC), BF),
+            jax.ShapeDtypeStruct((HQ, self.rows, self.total), BF),
+        ]
+        self.scratch = self.heads((self.rows, BF), (self.total, BF), (self.total, BF), (self.rows, BF))
+        self.scratch += [
+            pltpu.VMEM((2, 2 * self.chunk, self.total), BF),
+            pltpu.VMEM((self.rows, QC), BF),
+            pltpu.SemaphoreType.DMA((3,)),
+        ]
+        if self.bias:
+            self.scratch.append(pltpu.VMEM((self.chunk, 2 * self.keys), F32))
+
+    def begin(self, loads, raws, outs, scratch):
+        self.att_out, self.p_out = outs
+        self.qs, self.ks, self.vs, self.os, self.p_buf, self.att, self.sems = scratch[:7]
+        self.toep = scratch[7] if self.bias else None
+        loads = list(loads)
+        self.split_qkv(loads, self.qs, self.ks, self.vs)
+        self.segq, self.segk = loads.pop(0).get(), loads.pop(0).get()
+        self.bvec = loads.pop(0).get() if self.bias else None
+
+    def keep(self, i):
+        h, b, rows = self.step_rows(i)
+        slot = lax.rem(i, 2)
+        return pltpu.make_async_copy(self.p_buf.at[slot], self.p_out.at[h, rows], self.sems.at[slot])
+
+    def run(self, low, high):
+        keys, chunk = self.keys, self.chunk
+
+        @pl.loop(low, high)
+        def _(i):
+            h, b, rows = self.step_rows(i)
+            slot = lax.rem(i, 2)
+            if self.bias:
+
+                @pl.when(b == 0)
+                def _():
+                    row = jnp.broadcast_to(self.bvec[h], (chunk, 2 * keys))
+                    self.toep[...] = pltpu.roll(row, 0, 1, stride=1, stride_axis=0)
+
+            s = mm_nt(self.qs[h, rows], self.ks[h])
+            allowed = self.segq[rows] == self.segk[...]
+            if self.bias:
+                parts = [self.toep[:, self.diagonal(b, u)] for u in range(2)]
+                biased = s[:, :keys] + jnp.concatenate(parts, axis=0)
+                s = jnp.concatenate([biased, s[:, keys:]], axis=1) if self.extra else biased
+            if self.causal:
+                row = lax.broadcasted_iota(jnp.int32, (chunk, 1), 0)
+                places = jnp.concatenate([row + self.place(2 * b + u) for u in range(2)], axis=0)
+                allowed = allowed & (lax.broadcasted_iota(jnp.int32, (1, keys), 1) <= places)
+            s = jnp.where(allowed, s, MASKED)
+            top = jnp.max(s, axis=-1, keepdims=True)
+            e = jnp.exp(s - top)
+            p = (e * (1.0 / jnp.sum(e, axis=-1, keepdims=True))).astype(BF)
+
+            @pl.when(i >= 2)
+            def _():
+                self.keep(i - 2).wait()
+
+            self.p_buf[slot] = p
+            self.keep(i).start()
+            self.os[h, rows] = mm(p, self.vs[h]).astype(BF)
+
+    def end(self):
         for i in range(HQ):
-            att_ref[:, DH * i : DH * (i + 1)] = os[i]
-
-
-def whole(shape):
-    return pl.BlockSpec(shape, lambda h, b, pos: (0,) * len(shape))
-
-
-def attn_fwd(pos, q, kv, segq, segk, bvec, mkv, causal, q_off, kv_off):
-    rows, keys = q.shape[0], kv.shape[0]
-    chunk = rows // 8
-    extra = 0 if mkv is None else mkv.shape[0]
-    total = keys + extra
-    conf = (chunk, q_off, kv_off, keys, extra, bvec is not None, causal)
-    operands = [q, kv, segq, segk]
-    operands += [v for v in (bvec, mkv) if v is not None]
-    scratch = [
-        pltpu.VMEM((HQ, rows, DH), BF),
-        pltpu.VMEM((HQ, total, DH), BF),
-        pltpu.VMEM((HQ, total, DH), BF),
-        pltpu.VMEM((HQ, rows, DH), BF),
-    ]
-    if bvec is not None:
-        scratch.append(pltpu.VMEM((chunk, 2 * keys), F32))
-    return pl.pallas_call(
-        functools.partial(attn_fwd_kernel, conf),
-        out_shape=(
-            jax.ShapeDtypeStruct((rows, QC), BF),
-            jax.ShapeDtypeStruct((HQ, rows, total), BF),
-        ),
-        grid_spec=pltpu.PrefetchScalarGridSpec(
-            num_scalar_prefetch=1,
-            grid=(HQ, rows // (2 * chunk)),
-            in_specs=[whole(v.shape) for v in operands],
-            out_specs=(
-                whole((rows, QC)),
-                pl.BlockSpec((1, 2 * chunk, total), lambda h, b, pos: (h, b, 0)),
-            ),
-            scratch_shapes=scratch,
-        ),
-        compiler_params=pltpu.CompilerParams(
-            dimension_semantics=("arbitrary", "arbitrary"), vmem_limit_bytes=VMEM_LIMIT
-        ),
-        cost_estimate=pl.CostEstimate(
-            flops=4 * HQ * rows * total * DH,
-            bytes_accessed=HQ * rows * total * 2,
-            transcendentals=HQ * rows * total,
-        ),
-        name="attn_fwd",
-    )(pos, *operands)
-
-
-def attn_bwd_kernel(conf, pos_ref, *refs):
-    chunk, q_off, kv_off, keys, extra, bias = conf
-    refs = list(refs)
-    p_ref, q_ref, kv_ref, do_ref, att_ref = refs[:5]
-    refs = refs[5:]
-    mkv_ref = refs.pop(0) if extra else None
-    joint = q_ref.shape[1] > QC
-    dq_ref = refs.pop(0)
-    dkv_ref = dq_ref if joint else refs.pop(0)
-    to = QC if joint else 0
-    dbvec_ref = refs.pop(0) if bias else None
-    dmkv_ref = refs.pop(0) if extra else None
-    qs, ks, vs, dos, rds, dqs, dks, dvs = refs[:8]
-    diag = refs[8] if bias else None
-    h, b = pl.program_id(0), pl.program_id(1)
-    last = pl.num_programs(1) - 1
-    length = keys
-
-    @pl.when((h == 0) & (b == 0))
-    def _():
+            self.att[:, DH * i : DH * (i + 1)] = self.os[i]
+        out = pltpu.make_async_copy(self.att, self.att_out, self.sems.at[2])
+        out.start()
+        self.keep(self.n_steps - 2).wait()
+        self.keep(self.n_steps - 1).wait()
+        out.wait()
+
+
+class AttentionBackward(Attention):
+    def __init__(self, parts, p, q, kv, grad, att, bias, mkv):
+        super().__init__(parts, q, kv, bias, mkv, False)
+        self.loads += [grad, att]
+        self.raws = [p]
+        rows, total, keys = self.rows, self.total, self.keys
+        if self.joint:
+            self.outs = [jax.ShapeDtypeStruct((rows, 3 * QC), BF)]
+        else:
+            kv_type = BF if parts == 1 else F32
+            self.outs = [
+                jax.ShapeDtypeStruct((rows, QC), BF),
+                jax.ShapeDtypeStruct((keys, 2 * QC), kv_type),
+            ]
+        if bias:
+            self.outs.append(jax.ShapeDtypeStruct((HQ, 1, 2 * keys), F32))
+        if self.extra:
+            self.outs.append(jax.ShapeDtypeStruct((self.extra, 2 * QC), BF))
+        self.scratch = self.heads(
+            (rows, BF), (total, BF), (total, BF), (rows, BF), (rows, BF), (total, F32), (total, F32)
+        )
+        self.scratch += [
+            pltpu.VMEM((HQ, rows, 1), F32),
+            pltpu.VMEM((2, 2 * self.chunk, total), BF),
+            pltpu.SemaphoreType.DMA((2 + len(self.outs),)),
+        ]
+        self.scratch += [pltpu.VMEM(o.shape, o.dtype) for o in self.outs]
+        if bias:
+            self.scratch.append(pltpu.VMEM((self.chunk, 2 * keys), F32))
+
+    def fetch(self, i):
+        h, b, rows = self.step_rows(i)
+        slot = lax.rem(i, 2)
+        return pltpu.make_async_copy(self.p_in.at[h, rows], self.p_buf.at[slot], self.sems.at[slot])
+
+    def begin(self, loads, raws, outs, scratch):
+        self.results, (self.p_in,) = outs, raws
+        scratch, loads = list(scratch), list(loads)
+        self.qs, self.ks, self.vs, self.dos, self.dqs, self.dks, self.dvs = scratch[:7]
+        self.rds, self.p_buf, self.sems = scratch[7:10]
+        self.made = scratch[10 : 10 + len(outs)]
+        self.diag = scratch[-1] if self.bias else None
+        self.fetch(0).start()
+        self.split_qkv(loads, self.qs, self.ks, self.vs)
+        do_ref, att_ref = loads.pop(0).get(), loads.pop(0).get()
         for i in range(HQ):
-            qs[i] = q_ref[:, q_off + DH * i : q_off + DH * (i + 1)]
-            ks[i, :keys] = kv_ref[:, kv_off + DH * i : kv_off + DH * (i + 1)]
-            vs[i, :keys] = kv_ref[:, kv_off + QC + DH * i : kv_off + QC + DH * (i + 1)]
-            if extra:
-                ks[i, keys:] = mkv_ref[:, DH * i : DH * (i + 1)]
-                vs[i, keys:] = mkv_ref[:, QC + DH * i : QC + DH * (i + 1)]
             grad = do_ref[:, DH * i : DH * (i + 1)]
-            dos[i] = grad
+            self.dos[i] = grad
             out = att_ref[:, DH * i : DH * (i + 1)]
-            rds[i] = jnp.sum(grad.astype(F32) * out.astype(F32), axis=-1, keepdims=True)
-
-    @pl.when(b == 0)
-    def _():
-        dks[h] = jnp.zeros(dks.shape[1:], F32)
-        dvs[h] = jnp.zeros(dvs.shape[1:], F32)
-        if bias:
-            diag[...] = jnp.zeros_like(diag)
-
-    rows = pl.ds(pl.multiple_of(b * 2 * chunk, 2 * chunk), 2 * chunk)
-    q, grad, p = qs[h, rows], dos[h, rows], p_ref[0]
-    dp = mm_nt(grad, vs[h])
-    ds = (p.astype(F32) * (dp - rds[h, rows])).astype(BF)
-    dqs[h, rows] = mm(ds, ks[h]).astype(BF)
-    dks[h] += mm_tn(ds, q)
-    dvs[h] += mm_tn(p, grad)
-    if bias:
-        for u in range(2):
-            off = pl.multiple_of(length - pos_ref[2 * b + u], 128)
-            diag[:, pl.ds(off, keys)] += ds[u * chunk : (u + 1) * chunk, :keys].astype(F32)
-
-        @pl.when(b == last)
-        def _():
-            x = diag[...]
-            size = chunk
-            while size > 1:
-                size //= 2
-                x = x[:size] + pltpu.roll(x[size:], 2 * length - size, 1)
-            dbvec_ref[h] = x
-
-    @pl.when((h == HQ - 1) & (b == last))
-    def _():
+            self.rds[i] = jnp.sum(grad.astype(F32) * out.astype(F32), axis=-1, keepdims=True)
+        made = list(self.made)
+        self.dq = made.pop(0)
+        self.dkv = self.dq if self.joint else made.pop(0)
+        self.dbvec = made.pop(0) if self.bias else None
+        self.dmkv = made.pop(0) if self.extra else None
+
+    def run(self, low, high):
+        keys, chunk = self.keys, self.chunk
+
+        @pl.loop(low, high)
+        def _(i):
+            h, b, rows = self.step_rows(i)
+            self.fetch(i).wait()
+
+            @pl.when(i + 1 < self.n_steps)
+            def _():
+                self.fetch(i + 1).start()
+
+            @pl.when(b == 0)
+            def _():
+                self.dks[h] = jnp.zeros(self.dks.shape[1:], F32)
+                self.dvs[h] = jnp.zeros(self.dvs.shape[1:], F32)
+                if self.bias:
+                    self.diag[...] = jnp.zeros_like(self.diag)
+
+            q, grad, p = self.qs[h, rows], self.dos[h, rows], self.p_buf[lax.rem(i, 2)]
+            dp = mm_nt(grad, self.vs[h])
+            ds = (p.astype(F32) * (dp - self.rds[h, rows])).astype(BF)
+            self.dqs[h, rows] = mm(ds, self.ks[h]).astype(BF)
+            self.dks[h] += mm_tn(ds, q)
+            self.dvs[h] += mm_tn(p, grad)
+            if self.bias:
+                for u in range(2):
+                    part = ds[u * chunk : (u + 1) * chunk, :keys]
+                    self.diag[:, self.diagonal(b, u)] += part.astype(F32)
+
+                @pl.when(b == self.blocks - 1)
+                def _():
+                    x = self.diag[...]
+                    size = chunk
+                    while size > 1:
+                        size //= 2
+                        x = x[:size] + pltpu.roll(x[size:], 2 * keys - size, 1)
+                    self.dbvec[h] = x
+
+    def end(self):
+        keys = self.keys
+        to = QC if self.joint else 0
         for i in range(HQ):
-            dq_ref[:, DH * i : DH * (i + 1)] = dqs[i]
+            self.dq[:, DH * i : DH * (i + 1)] = self.dqs[i]
             at = to + DH * i
-            dkv_ref[:, at : at + DH] = dks[i, :keys].astype(dkv_ref.dtype)
-            dkv_ref[:, at + QC : at + QC + DH] = dvs[i, :keys].astype(dkv_ref.dtype)
-            if extra:
-                dmkv_ref[:, DH * i : DH * (i + 1)] = dks[i, keys:].astype(BF)
-                dmkv_ref[:, QC + DH * i : QC + DH * (i + 1)] = dvs[i, keys:].astype(BF)
-
-
-def attn_bwd(pos, p, q, kv, grad, att, mkv, bias, q_off, kv_off, dtype):
-    rows, keys = q.shape[0], kv.shape[0]
-    chunk = rows // 8
-    extra = 0 if mkv is None else mkv.shape[0]
-    total = keys + extra
-    conf = (chunk, q_off, kv_off, keys, extra, bias)
-    operands = [q, kv, grad, att] + ([mkv] if extra else [])
-    if q.shape[1] > QC:
-        outs = [jax.ShapeDtypeStruct((rows, 3 * QC), BF)]
-    else:
-        outs = [jax.ShapeDtypeStruct((rows, QC), BF), jax.ShapeDtypeStruct((keys, 2 * QC), dtype)]
-    if bias:
-        outs.append(jax.ShapeDtypeStruct((HQ, 1, 2 * keys), F32))
-    if extra:
-        outs.append(jax.ShapeDtypeStruct((extra, 2 * QC), BF))
-    scratch = [
-        pltpu.VMEM((HQ, rows, DH), BF),
-        pltpu.VMEM((HQ, total, DH), BF),
-        pltpu.VMEM((HQ, total, DH), BF),
-        pltpu.VMEM((HQ, rows, DH), BF),
-        pltpu.VMEM((HQ, rows, 1), F32),
-        pltpu.VMEM((HQ, rows, DH), BF),
-        pltpu.VMEM((HQ, total, DH), F32),
-        pltpu.VMEM((HQ, total, DH), F32),
-    ]
-    if bias:
-        scratch.append(pltpu.VMEM((chunk, 2 * keys), F32))
-    return pl.pallas_call(
-        functools.partial(attn_bwd_kernel, conf),
-        out_shape=tuple(outs),
-        grid_spec=pltpu.PrefetchScalarGridSpec(
-            num_scalar_prefetch=1,
-            grid=(HQ, rows // (2 * chunk)),
-            in_specs=[pl.BlockSpec((1, 2 * chunk, total), lambda h, b, pos: (h, b, 0))]
-            + [whole(v.shape) for v in operands],
-            out_specs=tuple(whole(v.shape) for v in outs),
-            scratch_shapes=scratch,
-        ),
-        compiler_params=pltpu.CompilerParams(
-            dimension_semantics=("arbitrary", "arbitrary"), vmem_limit_bytes=VMEM_LIMIT
-        ),
-        cost_estimate=pl.CostEstimate(
-            flops=8 * HQ * rows * total * DH,
-            bytes_accessed=HQ * rows * total * 2,
-            transcendentals=0,
-        ),
-        name="attn_bwd",
-    )(pos, p, *operands)
+            self.dkv[:, at : at + DH] = self.dks[i, :keys].astype(self.dkv.dtype)
+            self.dkv[:, at + QC : at + QC + DH] = self.dvs[i, :keys].astype(self.dkv.dtype)
+            if self.extra:
+                self.dmkv[:, DH * i : DH * (i + 1)] = self.dks[i, keys:].astype(BF)
+                self.dmkv[:, QC + DH * i : QC + DH * (i + 1)] = self.dvs[i, keys:].astype(BF)
+        copies = [
+            pltpu.make_async_copy(src, dst, self.sems.at[2 + n])
+            for n, (src, dst) in enumerate(zip(self.made, self.results))
+        ]
+        for copy in copies:
+            copy.start()
+        for copy in copies:
+            copy.wait()
+
+
+class Idle:
+    n_steps, loads, raws, outs, scratch = 0, [], [], [], []
+
+    def begin(self, loads, raws, outs, scratch):
+        pass
+
+    def run(self, low, high):
+        pass
+
+    def end(self):
+        pass
+
+
+def attend(number, planes, filler, jobs):
+    def kernel(shipper, ins, outs, scratch, filler):
+        shipper.greet(())
+        shipper.start()
+        filler.begin()
+        filler.run(0, filler.n_steps)
+        filler.end()
+        shipper.finish()
+
+    _, moved, made = call_with_jobs(
+        kernel, number, planes, jobs, [], [], [], "attend", 4 * 10**9, filler
+    )
+    return made, moved
 
 
 ALL = ("seq", "part", "tp", "fsdp")
@@ -907,35 +988,31 @@
         return w.reshape(-1, w.shape[-1])
 
     gains = (enc_gain, enc_ffnorm, dec_gain, cross_gain, dec_ffnorm)
-    small = jnp.concatenate(list(gains) + [enc_rel.reshape(-1), dec_rel.reshape(-1)])
-    small_size = small.shape[0]
-    small = jnp.pad(small.astype(F32), (0, -small_size % 128)).reshape(-1, 128)
+    gain_stack = jnp.stack(gains).astype(F32)
+    rel_stack = jnp.stack([enc_rel, dec_rel]).astype(F32)
     segments = segments.reshape(2, 1, chunk)
     first_jobs = [
         swap_job(enc_input),
-        gather_job("fsdp", small, planes),
+        gather_job("fsdp", gain_stack, planes),
+        gather_job("fsdp", rel_stack, planes),
         over_planes(qkv_part(enc_qkv)),
         over_planes(qkv_part(memory)),
         swap_job(dec_input),
     ]
     if parts == 1:
         first_jobs.append(block_job(segments))
-    xe, small, w_eqkv, table, xd, *segs = ship(0, planes, first_jobs)
+    xe, gain_stack, rel_stack, w_eqkv, table, xd, *segs = ship(0, planes, first_jobs)
     xe, xd = joined(enc_input, xe), joined(dec_input, xd)
     if parts == 1:
         seg = segs[0].reshape(-1)
     else:
         segs = lax.all_gather(segments.reshape(2, chunk), CTX, axis=1, tiled=True)
         seg = lax.dynamic_index_in_dim(segs, seq, 0, keepdims=False)
-    small = small.reshape(planes, -1)[:, :small_size]
-    per = enc_gain.shape[0]
-    gain_rows = [small[:, per * i : per * (i + 1)].reshape(1, D) for i in range(5)]
-    g_enc, g_effn, g_dec, g_cross, g_dffn = gain_rows
-    per_rel = enc_rel.size
-    rels = [
-        small[:, 5 * per + per_rel * i : 5 * per + per_rel * (i + 1)].reshape(BUCKETS, HEADS)
-        for i in range(2)
+    per, per_rel = enc_gain.shape[0], enc_rel.size
+    g_enc, g_effn, g_dec, g_cross, g_dffn = [
+        gain_stack[:, i].reshape(1, D) for i in range(len(gains))
     ]
+    rels = [rel_stack[:, i].reshape(BUCKETS, HEADS) for i in range(2)]
     onehot = (buckets[:, None] == jnp.arange(BUCKETS, dtype=jnp.int32)[None, :]).astype(BF)
 
     def bias_vector(rel):
@@ -955,7 +1032,7 @@
         full = lax.all_gather(w, "fsdp", axis=0, tiled=True)
         return lax.dynamic_slice_in_dim(full, QC * tp, QC, 0)
 
-    en, (w_eqkv, table, w_dqkv, *got) = gather_norm(
+    en, (w_eqkv, table, w_dqkv, *got), _ = gather_norm(
         1,
         planes,
         xe,
@@ -965,8 +1042,6 @@
     w_eproj = proj_of(got, enc_proj)
     w_eqkv, table = matrix(w_eqkv), matrix(table)
 
-    index = jnp.arange(2 * TP, dtype=jnp.int32)
-    pos = ((index // TP) * TP * parts + TP * part + index % TP) * chunk
     segq = lax.dynamic_index_in_dim(seg.reshape(2, parts, TP * chunk), part, 1, keepdims=False)
     segq = segq.reshape(-1, 1)
     segk = seg.reshape(1, length)
@@ -992,45 +1067,36 @@
         split = split.reshape(parts * 2 * TP * chunk, -1)
         return lax.psum_scatter(split, "part", scatter_dimension=0, tiled=True).astype(BF)
 
-    def self_attn(rows, bvec, mem, segk_now, causal):
+    def self_kv(rows):
+        return (rows, rows) if parts == 1 else (rows[:, :QC], spread(rows[:, QC:]))
+
+    def joint_grad(got):
         if parts == 1:
-            q, kv, kv_off = rows, rows, QC
-        else:
-            q, kv, kv_off = rows[:, :QC], spread(rows[:, QC:]), 0
-        att, p = attn_fwd(pos, q, kv, segq, segk_now, bvec, mem, causal, 0, kv_off)
-
-        def back(grad):
-            got = attn_bwd(
-                pos, p, q, kv, grad, att, mem, bvec is not None, 0, kv_off, BF if parts == 1 else F32
-            )
-            if parts == 1:
-                return got[0], got[1:]
-            return jnp.concatenate([got[0], collect(got[1])], axis=1), got[2:]
-
-        return att, back
-
-    def cross_attn(q, kv_rows):
-        kv = spread(kv_rows)
-        att, p = attn_fwd(pos, q, kv, segq, segk, None, None, False, 0, 0)
-
-        def back(grad):
-            got = attn_bwd(pos, p, q, kv, grad, att, None, False, 0, 0, BF if parts == 1 else F32)
-            return got[0], collect(got[1])
-
-        return att, back
-
-    e_rows = mm(en, w_eqkv).astype(BF)
-    e_att, e_back = self_attn(e_rows, bias_vector(rels[0]), mkv, segk_mem, False)
-    dn, (w_dqkv, w_effin, *got) = gather_norm(
+            return got.pop(0)
+        return jnp.concatenate([got.pop(0), collect(got.pop(0))], axis=1)
+
+    e_qkv = self_kv(mm(en, w_eqkv).astype(BF))
+    e_fill = AttentionForward(
+        parts, *e_qkv, segq, segk_mem, bias_vector(rels[0]), mkv, False
+    )
+    dn, (w_dqkv, w_effin, w_effout, *got), (e_att, e_p) = gather_norm(
         2,
         planes,
         xd,
         g_dec,
-        [over_seq(w_dqkv), over_planes(ffin_part(enc_ffin))] + proj_jobs(dec_proj),
+        [
+            over_seq(w_dqkv),
+            over_planes(ffin_part(enc_ffin)),
+            over_planes(ffout_part(enc_ffout)),
+        ]
+        + proj_jobs(dec_proj),
+        e_fill,
     )
     w_dproj = proj_of(got, dec_proj)
     w_dqkv = matrix(w_dqkv)
-    (e_mid, e_fn), (w_effin, w_effout, w_cq, w_ckv) = stage(
+    d_qkv = self_kv(mm(dn, w_dqkv).astype(BF))
+    d_fill = AttentionForward(parts, *d_qkv, segq, segk, bias_vector(rels[1]), None, True)
+    (e_mid, e_fn), (w_effin, w_effout, w_cq, w_ckv, w_dffin), (d_att, d_p) = stage(
         3,
         planes,
         [(e_att, w_eproj, False)],
@@ -1039,17 +1105,17 @@
         gain=g_effn,
         jobs=[
             over_seq(w_effin),
-            over_planes(ffout_part(enc_ffout)),
+            over_seq(w_effout),
             over_planes(qkv_part(cross_query)),
             over_planes(qkv_part(cross_kv)),
+            over_planes(ffin_part(dec_ffin)),
         ],
-    )
-    w_effin = matrix(w_effin)
+        filler=d_fill,
+    )
+    w_effin, w_effout = matrix(w_effin), matrix(w_effout)
     e_pre = mm(e_fn, w_effin)
     e_act = gelu(e_pre).astype(BF)
-    d_rows = mm(dn, w_dqkv).astype(BF)
-    d_att, d_back = self_attn(d_rows, bias_vector(rels[1]), None, segk, True)
-    (d_mid, c_n), (w_effout, w_cq, w_ckv, w_dffin, *got) = stage(
+    (d_mid, c_n), (w_cq, w_ckv, w_dffin, w_dffout, *got) = stage(
         4,
         planes,
         [(d_att, w_dproj, False)],
@@ -1057,41 +1123,34 @@
         gather="norm",
         gain=g_cross,
         jobs=[
-            over_seq(w_effout),
             over_seq(w_cq),
             over_seq(w_ckv),
-            over_planes(ffin_part(dec_ffin)),
+            over_seq(w_dffin),
+            over_planes(ffout_part(dec_ffout)),
         ]
         + proj_jobs(cross_proj),
     )
     w_cproj = proj_of(got, cross_proj)
-    w_effout, w_cq, w_ckv = matrix(w_effout), matrix(w_cq), matrix(w_ckv)
-    (e_low, e_gath), (w_dffin, w_dffout, xdc) = stage(
+    w_cq, w_ckv, w_dffin = matrix(w_cq), matrix(w_ckv), matrix(w_dffin)
+    (e_low, e_gath), (w_dffout, xdc, xec) = stage(
         5,
         planes,
         [(e_act, w_effout, False)],
         e_mid,
         gather="low",
         dtype=BF,
-        jobs=[over_seq(w_dffin), over_planes(ffout_part(dec_ffout)), swap_job(dec_cotan)],
-    )
-    xdc = joined(dec_cotan, xdc)
-    w_dffin = matrix(w_dffin)
+        jobs=[over_seq(w_dffout), swap_job(dec_cotan), swap_job(enc_cotan)],
+    )
+    xdc, xec = joined(dec_cotan, xdc), joined(enc_cotan, xec)
+    w_dffout = matrix(w_dffout)
     c_q = mm(c_n, w_cq).astype(BF)
-    c_kv = mm(e_gath, w_ckv).astype(BF)
-    c_att, c_back = cross_attn(c_q, c_kv)
-    (d_cross, d_fn), (w_dffout, xec, came) = stage(
-        6,
-        planes,
-        [(c_att, w_cproj, False)],
-        d_mid,
-        gather="norm",
-        gain=g_dffn,
-        jobs=[over_seq(w_dffout), swap_job(enc_cotan), swap_job(e_low)],
-    )
-    xec = joined(enc_cotan, xec)
+    c_kv = spread(mm(e_gath, w_ckv).astype(BF))
+    c_fill = AttentionForward(parts, c_q, c_kv, segq, segk, None, None, False)
+    (c_att, c_p), (came,) = attend(19, planes, c_fill, [swap_job(e_low)])
     enc_output = joined(e_low, came)
-    w_dffout = matrix(w_dffout)
+    (d_cross, d_fn), _ = stage(
+        6, planes, [(c_att, w_cproj, False)], d_mid, gather="norm", gain=g_dffn
+    )
     d_pre = mm(d_fn, w_dffin)
     d_act = gelu(d_pre).astype(BF)
     (d_low, up_g), _ = stage(
@@ -1145,13 +1204,15 @@
         jobs=step1(g_dff) + [swap_job(d_low)],
     )
     dec_output = joined(d_low, got.pop())
-    g_dff = got
-    c_dq, c_dkv = c_back(mm_nt(up_g, w_cproj).astype(BF))
+    c_fill = AttentionBackward(
+        parts, c_p, c_q, c_kv, mm_nt(up_g, w_cproj).astype(BF), c_att, False, None
+    )
+    (c_dq, c_dkv), g_dff = attend(20, planes, c_fill, step2(got))
+    c_dkv = collect(c_dkv)
+    g_cproj = mm_tn(c_att, up_g).astype(BF)
     g_c = [pieces(mm_tn(c_n, c_dq).astype(BF)), pieces(mm_tn(e_gath, c_dkv).astype(BF))]
     if turned:
-        g_c.append(proj_pieces(mm_tn(c_att, up_g).astype(BF)))
-    else:
-        g_cproj = mm_tn(c_att, up_g).astype(BF)
+        g_c.append(proj_pieces(g_cproj))
     (up, up_g, dg_cross), got = stage(
         9,
         planes,
@@ -1159,41 +1220,30 @@
         up,
         back=(d_mid, g_cross),
         gather="low",
-        jobs=step1(g_c) + step2(g_dff),
-    )
-    g_c = take(got, len(g_c))
-    g_dff = got
-    (e_up, e_up_g), got = stage(
+        jobs=step3(g_dff) + step1(g_c),
+    )
+    g_dff, g_c = take(got, 2), got
+    d_fill = AttentionBackward(
+        parts, d_p, *d_qkv, mm_nt(up_g, w_dproj).astype(BF), d_att, True, None
+    )
+    g_dproj = mm_tn(d_att, up_g).astype(BF)
+    (e_up, e_up_g), got, made = stage(
         10,
         planes,
         [(c_dkv, w_ckv, True)],
         xec,
         gather="low",
-        jobs=step2(g_c) + step3(g_dff),
-    )
-    g_c = take(got, len(g_c))
-    g_dff = got
-    d_rows_grad, (d_dbv,) = d_back(mm_nt(up_g, w_dproj).astype(BF))
-    g_dqkv = mm_tn(dn, d_rows_grad).astype(BF)
-    g_d = [pieces(g_dqkv)]
+        jobs=step4(g_dff) + step2(g_c),
+        filler=d_fill,
+    )
+    g_dff, g_c = take(got, 2), got
+    d_rows_grad = joint_grad(made)
+    (d_dbv,) = made
+    g_d = [pieces(mm_tn(dn, d_rows_grad).astype(BF))]
+    turn = []
     if turned:
-        g_d.append(proj_pieces(mm_tn(d_att, up_g).astype(BF)))
+        g_d.append(proj_pieces(g_dproj))
         turn = [turn_job(g_c.pop())]
-    else:
-        g_dproj = mm_tn(d_att, up_g).astype(BF)
-        turn = []
-    (d_in, dg_dec), got = stage(
-        11,
-        planes,
-        [(d_rows_grad, w_dqkv, True)],
-        up,
-        back=(xd, g_dec),
-        jobs=step1(g_d) + step4(g_dff) + step3(g_c) + turn,
-    )
-    d_in_low = d_in.astype(BF)
-    g_d = take(got, len(g_d))
-    g_dff, g_c = take(got, 2), take(got, 2)
-    g_cp = got
     pre_grad, g_eff = ff_grads(e_up_g, e_fn, e_act, e_pre, w_effout)
     (e_up, e_up_g, dg_effn), got = stage(
         12,
@@ -1202,35 +1252,46 @@
         e_up,
         back=(e_mid, g_effn),
         gather="low",
-        jobs=step1(g_eff)
-        + step5(g_dff, ff_widths)
-        + step4(g_c)
-        + step3(g_cp)
-        + step2(g_d)
-        + [swap_job(d_in_low)],
-    )
-    dec_ingrad = joined(d_in, got.pop())
-    g_eff = take(got, 2)
-    o_dff, g_c, g_cp = take(got, 2), take(got, 2), take(got, len(g_cp))
-    g_d = got
-    e_rows_grad, (e_dbv, d_mkv) = e_back(mm_nt(e_up_g, w_eproj).astype(BF))
-    if turned:
-        g_ep = [proj_pieces(mm_tn(e_att, e_up_g).astype(BF))]
-        turn = [turn_job(g_d.pop())]
-    else:
-        g_eproj = mm_tn(e_att, e_up_g).astype(BF)
-        g_ep, turn = [], []
+        jobs=step5(g_dff, ff_widths) + step1(g_d) + step3(g_c) + turn,
+    )
+    o_dff, g_d, g_c, g_cp = take(got, 2), take(got, len(g_d)), take(got, 2), got
+    e_fill = AttentionBackward(
+        parts, e_p, *e_qkv, mm_nt(e_up_g, w_eproj).astype(BF), e_att, True, mkv
+    )
+    g_eproj = mm_tn(e_att, e_up_g).astype(BF)
+    g_ep = [proj_pieces(g_eproj)] if turned else []
+    (d_in, dg_dec), got, made = stage(
+        11,
+        planes,
+        [(d_rows_grad, w_dqkv, True)],
+        up,
+        back=(xd, g_dec),
+        jobs=step1(g_eff) + step1(g_ep) + step2(g_d) + step4(g_c) + step3(g_cp),
+        filler=e_fill,
+    )
+    g_eff, g_ep = take(got, 2), take(got, len(g_ep))
+    g_d, g_c, g_cp = take(got, len(g_d)), take(got, 2), got
+    d_in_low = d_in.astype(BF)
+    e_rows_grad = joint_grad(made)
+    e_dbv, d_mkv = made
+    turn = [turn_job(g_d.pop())] if turned else []
     (e_in, dg_enc), got = stage(
         13,
         planes,
         [(e_rows_grad, w_eqkv, True)],
         e_up,
         back=(xe, g_enc),
-        jobs=step2(g_eff) + step5(g_c, qkv_widths) + step4(g_cp) + step3(g_d) + turn + step1(g_ep),
-    )
-    g_eff = take(got, 2)
-    o_c, g_cp, g_d, g_dp = take(got, 2), take(got, len(g_cp)), take(got, 1), take(got, len(turn))
-    g_ep = got
+        jobs=step2(g_eff)
+        + step2(g_ep)
+        + step3(g_d)
+        + turn
+        + step5(g_c, qkv_widths)
+        + step4(g_cp)
+        + [swap_job(d_in_low)],
+    )
+    dec_ingrad = joined(d_in, got.pop())
+    g_eff, g_ep = take(got, 2), take(got, len(g_ep))
+    g_d, g_dp, o_c, g_cp = take(got, 1), take(got, len(turn)), take(got, 2), got
     g_eqkv = mm_tn(en, e_rows_grad).astype(BF)
     g_e = [pieces(g_eqkv), pieces(mm_tn(pick, d_mkv).astype(BF))]
     def rel_grad(dbv):
@@ -1255,43 +1316,44 @@
         planes,
         step1(g_e)
         + step3(g_eff)
-        + step5(g_cp, proj_widths)
+        + [turn_job(g) for g in g_ep]
         + step4(g_d)
         + step3(g_dp)
-        + step2(g_ep)
+        + step5(g_cp, proj_widths)
         + [total_job("fsdp", tiny, planes), swap_job(e_in.astype(BF))],
     )
     enc_ingrad = joined(e_in, got.pop())
     tiny = got.pop()
-    g_e = take(got, 2)
-    g_eff, o_cp, g_d = take(got, 2), take(got, len(g_cp)), take(got, 1)
-    g_dp = take(got, len(g_dp))
-    g_ep = got
+    g_e, g_eff, g_ep = take(got, 2), take(got, 2), take(got, len(g_ep))
+    g_d, g_dp, o_cp = take(got, 1), take(got, len(g_dp)), got
     got = ship(
         15,
         planes,
         step2(g_e)
         + step4(g_eff)
+        + step3(g_ep)
         + step5(g_d, qkv_widths)
         + step4(g_dp)
-        + [turn_job(g) for g in g_ep]
         + [total_job("seq", tiny)],
     )
     tiny = got.pop()
-    g_e = take(got, 2)
-    g_eff, o_d, g_dp, g_ep = take(got, 2), take(got, 1), take(got, len(g_dp)), got
+    g_e, g_eff, g_ep = take(got, 2), take(got, 2), take(got, len(g_ep))
+    o_d, g_dp = take(got, 1), got
     got = ship(
         16,
         planes,
-        step3(g_e + g_ep) + step5(g_eff, ff_widths) + step5(g_dp, proj_widths) + [total_job("across", tiny)],
+        step3(g_e)
+        + step5(g_eff, ff_widths)
+        + step4(g_ep)
+        + step5(g_dp, proj_widths)
+        + [total_job("across", tiny)],
     )
     tiny = got.pop()
-    g_e = take(got, 2 + len(g_ep))
-    o_eff, o_dp = take(got, 2), got
-    got = ship(17, planes, step4(g_e) + [total_job("core", tiny)])
+    g_e, o_eff, g_ep, o_dp = take(got, 2), take(got, 2), take(got, len(g_ep)), got
+    got = ship(17, planes, step4(g_e) + step5(g_ep, proj_widths) + [total_job("core", tiny)])
     tiny = got.pop()
-    got = ship(18, planes, step5(got, qkv_widths + proj_widths))
-    o_e, o_ep = take(got, 2), got
+    g_e, o_ep = take(got, 2), got
+    o_e = ship(18, planes, step5(g_e, qkv_widths))
 
     def proj_rows(got, g):
         if turned:
@@ -1300,9 +1362,9 @@
         full = lax.psum_scatter(full, "fsdp", scatter_dimension=0, tiled=True)
         return lax.psum(full.astype(F32), CTX)
 
-    o_eproj = proj_rows(o_ep, None if turned else g_eproj)
-    o_dproj = proj_rows(o_dp, None if turned else g_dproj)
-    o_cproj = proj_rows(o_cp, None if turned else g_cproj)
+    o_eproj = proj_rows(o_ep, g_eproj)
+    o_dproj = proj_rows(o_dp, g_dproj)
+    o_cproj = proj_rows(o_cp, g_cproj)
     o_dffin, o_dffout = o_dff
     o_effin, o_effout = o_eff
     o_cq, o_ckv = o_c

time: 761 us -> 684 us (0.90)
  Pallas kernels: 615 us -> 535 us
    pallas_call x6 -> x0, Pallas kernels: 108 us -> none  [the longest x3 57.3 us: attn_bwd(): pl.pallas_call(functools.partial(attn_bwd_kernel, conf), out_shape=tuple(...]
    pallas_call x19 -> x21, Pallas kernels: 507 us -> 535 us  [call_with_jobs(): pl.pallas_call(body, out_shape=tuple(outs) + tuple((jax.ShapeDtypeStruct(...]
    unnamed x146 -> x143, local copies, waits for them, and re-layouts: 16.1 us -> 16.1 us
where the time goes in v3:
time: 684 us; the launch traced here: 677 us
  Pallas kernels  535 us (78%)
  matrix products  70.4 us (10%)
  local copies, waits for them, and re-layouts  50 us (7%)
  other arithmetic  20.4 us (3%)
    pallas_call x21, Pallas kernels, call_with_jobs(): pl.pallas_call(body, out_shape=tuple(outs) + tuple((jax.ShapeDtypeStruct(...  535 us
    dot_general x12, matrix products, mm_tn(): lax.dot_general(a, b, (((0,), (0,)), ((), ())), preferred_element_type=F32)  29.1 us
    dot_general x7, matrix products, mm(): return jnp.dot(a, b, preferred_element_type=F32)  23.2 us
    unnamed x143, local copies, waits for them, and re-layouts  16.1 us
    dot_general x5, matrix products, mm_nt(): lax.dot_general(a, b, (((1,), (1,)), ((), ())), preferred_element_type=F32)  15 us

profile of v3, /device:TPU:0, one launch (start us, length us, event | category | flops | bytes accessed | tf_op | source)
XLA Modules:
  0.0 677.4 jit_solution(10104921422149400673)
XLA Ops:
  0.7 1.3 fusion.51
  8.3 1.3 maximum_convert_fusion.refs_2_
  9.6 22.1 %ship.6 = (bf16[128,768]{1,0:T(8,128)(2,1)}, f32[4,5,192]{2,1,0:T(8,128)}, f32[4,2,8,12]{3,2,1,0:T(8,128)}, bf16[4,96,576]{2,1,0:T(8,128)(2,1)}, bf16[4,32,384]{...) custom-call(bf16[2,128,768]{2,1,0:T(8,128)(2,1)} %refs_0_.1, ...), custom_call_target="tpu_custom_call" | custom-call | bytes 8388608 | tf_op jit(solution)/shard_map/ship/pallas_call | solution.py:414
  35.0 18.8 %gather_norm.2 = (bf16[1024,768]{1,0:T(8,128)(2,1)}, bf16[4,2,96,576]{3,2,1,0:T(8,128)(2,1)}, bf16[4,2,32,384]{3,2,1,0:T(8,128)(2,1)}, bf16[4,96,576]{2,1,0:T(8,128)(2,1)}, bf16[192,768]{1,0:T(8,128)(2,1)}) custom-call(bf16[2,128,768]{2,1,0:T(8,128)(2,1)} %pad_maximum_fusion.3.refs_0_.refs_2_.refs_4_, f32[1,768]{1,0:T(1,128)} %reshape_squeeze.22.refs_1_.refs_3_, ...), custom_call_target="tpu_custom_call" | custom-call | flops 1000000 | bytes 8388608 | tf_op jit(solution)/shard_map/gather_norm/pallas_call | solution.py:414
  53.9 4.2 convolution_convert_fusion.1.refs_6_.refs_13_
  60.0 1.0 copy.76.refs_8_.refs_10_.refs_3_
  61.0 1.4 fusion.49
  65.7 1.7 constant_dynamic-slice_fusion.1
  67.4 40.9 %gather_norm.3 = (bf16[1024,768]{1,0:T(8,128)(2,1)}, bf16[4,2,96,576]{3,2,1,0:T(8,128)(2,1)}, bf16[4,96,768]{2,1,0:T(8,128)(2,1)}, bf16[4,96,768]{2,1,0:T(8,128)...) custom-call(bf16[2,128,768]{2,1,0:T(8,128)(2,1)} %pad_maximum_fusion.2.refs_0_.refs_2_.re, ...), custom_call_target="tpu_custom_call" | custom-call | flops 1000000 | bytes 8388608 | tf_op jit(solution)/shard_map/gather_norm/pallas_call | solution.py:414
  108.3 4.1 convolution_convert_fusion.refs_9_.refs_8_
  115.0 1.0 fusion.53
  116.7 1.6 dynamic_slice.129.refs_6_
  118.3 38.3 %stage.11 = (f32[2,128,768]{2,1,0:T(8,128)}, bf16[1024,768]{1,0:T(8,128)(2,1)}, bf16[4,2,96,768]{3,2,1,0:T(8,128)(2,1)}, bf16[4,2,96,768]{3,2,1,0:T(8,128)(2,1)}...) custom-call(bf16[1024,192]{1,0:T(8,128)(2,1)} %get-tuple-element.173, ...), custom_call_target="tpu_custom_call" | custom-call | flops 301989888 | bytes 8388608 | tf_op jit(solution)/shard_map/stage/pallas_call | solution.py:414
  157.4 28.3 %stage.12 = (f32[2,128,768]{2,1,0:T(8,128)}, bf16[1024,768]{1,0:T(8,128)(2,1)}, bf16[4,2,96,192]{3,2,1,0:T(8,128)(2,1)}, bf16[4,2,96,384]{3,2,1,0:T(8,128)(2,1)}...) custom-call(bf16[1024,192]{1,0:T(8,128)(2,1)} %get-tuple-element.183.refs_0_.refs_10_, ...), custom_call_target="tpu_custom_call" | custom-call | flops 301989888 | bytes 8388608 | tf_op jit(solution)/shard_map/stage/pallas_call | solution.py:414
  185.7 3.9 multiply_convert_fusion.1
  189.5 28.8 %stage.13 = (bf16[2,128,768]{2,1,0:T(8,128)(2,1)}, bf16[1024,768]{1,0:T(8,128)(2,1)}, bf16[4,2,96,768]{3,2,1,0:T(8,128)(2,1)}, bf16[128,768]{1,0:T(8,128)(2,1)}, bf16[128,768]{1,0:T(8,128)(2,1)}) custom-call(bf16[1024,768]{1,0:T(8,128)(2,1)} %get-tuple-element.349.refs_0_, bf16[768,768]{1,0:T(8,128)(2,1)} %bitcast.169, ...), custom_call_target="tpu_custom_call" | custom-call | flops 1207959552 | bytes 8388608 | tf_op jit(solution)/shard_map/stage/pallas_call | solution.py:414
  218.4 1.0 fusion.33
  220.2 3.4 convolution_convert_fusion.8.refs_2_.refs_3_
  223.7 1.4 convolution_convert_fusion.10.refs_1_.refs_2_
  225.0 13.9 %attend.2 = (bf16[128,768]{1,0:T(8,128)(2,1)}, bf16[1024,192]{1,0:T(8,128)(2,1)}, bf16[3,1024,1024]{2,1,0:T(8,128)(2,1)}) custom-call(bf16[2,128,768]{2,1,0:T(8,128)(2,1)} %get-tuple-element.189.refs_0_, bf16[1024,192]{1,0:T(8,128)(2,1)} %convolution_convert_fusion.10.refs_1_.refs_2_, bf16[1024,384]{1,0:T(8,128)(2,1)} %convolution_convert_fusion.8.refs_2_.refs_3_, ...), custom_call_target="tpu_custom_call" | custom-call | flops 4000000000 | bytes 8388608 | tf_op jit(solution)/shard_map/attend/pallas_call | solution.py:414
  239.6 23.9 %stage.14 = (f32[2,128,768]{2,1,0:T(8,128)}, bf16[1024,768]{1,0:T(8,128)(2,1)}) custom-call(bf16[1024,192]{1,0:T(8,128)(2,1)} %get-tuple-element.195.refs_0_.refs_5_, bf16[192,768]{1,0:T(8,128)(2,1)} %get-tuple-element.196.refs_1_, f32[2,128,768]{2,1,0:T(8,128)} %get-tuple-element.197.refs_2_.refs_4_, f32[1,768]{1,0:T(1,128)} %reshape_squeeze.27.refs_3_), custom_call_target="tpu_custom_call" | custom-call | flops 301989888 | bytes 8388608 | tf_op jit(solution)/shard_map/stage/pallas_call | solution.py:414
  263.5 5.3 multiply_convert_fusion
  268.7 22.3 %stage.15 = (bf16[2,128,768]{2,1,0:T(8,128)(2,1)}, bf16[1024,768]{1,0:T(8,128)(2,1)}) custom-call(bf16[1024,768]{1,0:T(8,128)(2,1)} %get-tuple-element.351.refs_0_, bf16[768,768]{1,0:T(8,128)(2,1)} %bitcast.200, f32[2,128,768]{2,1,0:T(8,128)} %get-tuple-element.201.refs_2_.refs_4_, bf16[2,128,768]{2,1,0:T(8,128)(2,1)} %pad_maximum_fusion.5.refs_3_.refs_2_), custom_call_target="tpu_custom_call" | custom-call | flops 1207959552 | bytes 8388608 | tf_op jit(solution)/shard_map/stage/pallas_call | solution.py:414
  291.1 4.5 convolution_convert_fusion.4
  295.6 3.9 fusion.13.refs_0_
  299.5 2.5 convolution_convert_fusion.5
  302.0 33.8 %stage.16 = (f32[2,128,768]{2,1,0:T(8,128)}, bf16[1024,768]{1,0:T(8,128)(2,1)}, f32[1,768]{1,0:T(1,128)}, bf16[4,96,768]{2,1,0:T(8,128)(2,1)}, bf16[4,96,768]{2,1,0:T(8,128)(2,1)}, /*index=5*/bf16[128,768]{1,0:T(8,128)(2,1)}) custom-call(bf16[1024,768]{1,0:T(8,128)(2,1)} %copy-done.14, bf16[768,768]{1,0:T(8,128)(2,1)} %bitcast.171, ...), custom_call_target="tpu_custom_call" | custom-call | flops 1207959552 | bytes 8388608 | tf_op jit(solution)/shard_map/stage/pallas_call | solution.py:414
  335.8 2.0 convolution_convert_fusion.16
  338.6 2.1 convolution_convert_fusion.13
  341.6 26.9 %attend.3 = (bf16[96,768]{1,0:T(8,128)(2,1)}, bf16[96,768]{1,0:T(8,128)(2,1)}, bf16[1024,192]{1,0:T(8,128)(2,1)}, bf16[1024,384]{1,0:T(8,128)(2,1)}) custom-call(bf16[4,96,768]{2,1,0:T(8,128)(2,1)} %get-tuple-element.206.refs_0_, bf16[4,96,768]{2,1,0:T(8,128)(2,1)} %get-tuple-element.207.refs_1_, ...), custom_call_target="tpu_custom_call" | custom-call | flops 4000000000 | bytes 8388608 | tf_op jit(solution)/shard_map/attend/pallas_call | solution.py:414
  368.5 3.0 convolution_convert_fusion.9
  373.0 29.3 %stage.17 = (f32[2,128,768]{2,1,0:T(8,128)}, bf16[1024,768]{1,0:T(8,128)(2,1)}, f32[1,768]{1,0:T(1,128)}, bf16[2,96,768]{2,1,0:T(8,128)(2,1)}, bf16[2,96,768]{2,...) custom-call(bf16[1024,192]{1,0:T(8,128)(2,1)} %get-tuple-element.212.refs_0, ...), custom_call_target="tpu_custom_call" | custom-call | flops 301989888 | bytes 8388608 | tf_op jit(solution)/shard_map/stage/pallas_call | solution.py:414
  402.3 2.0 convolution_convert_fusion.15
  407.7 33.1 %stage.18 = (f32[2,128,768]{2,1,0:T(8,128)}, bf16[1024,768]{1,0:T(8,128)(2,1)}, bf16[2,2,96,768]{3,2,1,0:T(8,128)(2,1)}, bf16[2,2,96,768]{3,2,1,0:T(8,128)(2,1)}...) custom-call(bf16[1024,384]{1,0:T(8,128)(2,1)} %get-tuple-element.210, ...), custom_call_target="tpu_custom_call" | custom-call | flops 603979776 | bytes 8388608 | tf_op jit(solution)/shard_map/stage/pallas_call | solution.py:414
  440.8 2.5 convolution_convert_fusion.7
  443.3 1.3 copy.84
  444.6 6.2 fusion.6.refs_0_
  450.9 29.0 %stage.19 = (f32[2,128,768]{2,1,0:T(8,128)}, bf16[1024,768]{1,0:T(8,128)(2,1)}, f32[1,768]{1,0:T(1,128)}, f32[192,3072]{1,0:T(8,128)}, f32[768,768]{1,0:T(8,128)...) custom-call(bf16[1024,768]{1,0:T(8,128)(2,1)} %fusion.6.refs_0_, ...), custom_call_target="tpu_custom_call" | custom-call | flops 1207959552 | bytes 8388608 | tf_op jit(solution)/shard_map/stage/pallas_call | solution.py:414
  479.9 2.1 convolution_convert_fusion.11
  483.0 2.0 convolution_convert_fusion.14
  485.9 4.0 convolution_convert_fusion.2
  489.9 2.5 convolution_convert_fusion.3
  492.4 39.0 %stage.20 = (f32[2,128,768]{2,1,0:T(8,128)}, f32[1,768]{1,0:T(1,128)}, bf16[4,96,768]{2,1,0:T(8,128)(2,1)}, bf16[4,96,768]{2,1,0:T(8,128)(2,1)}, bf16[4,48,384]{...) custom-call(bf16[1024,576]{1,0:T(8,128)(2,1)} %get-tuple-element.223, ...), custom_call_target="tpu_custom_call" | custom-call | flops 905969664 | bytes 8388608 | tf_op jit(solution)/shard_map/stage/pallas_call | solution.py:414
  531.4 1.9 convert_element_type.126.refs_13_
  533.3 35.3 %stage.21 = (f32[2,128,768]{2,1,0:T(8,128)}, f32[1,768]{1,0:T(1,128)}, bf16[96,768]{1,0:T(8,128)(2,1)}, bf16[96,768]{1,0:T(8,128)(2,1)}, bf16[48,384]{1,0:T(8,12...) custom-call(bf16[1024,576]{1,0:T(8,128)(2,1)} %get-tuple-element.239, ...), custom_call_target="tpu_custom_call" | custom-call | flops 905969664 | bytes 8388608 | tf_op jit(solution)/shard_map/stage/pallas_call | solution.py:414
  568.7 2.0 convert_element_type.129.refs_9_
  575.2 2.6 convolution_convert_fusion.6
  577.8 1.3 copy.86
  579.1 1.0 convolution_convert_fusion.18
  580.2 28.8 %ship.7 = (bf16[4,96,576]{2,1,0:T(8,128)(2,1)}, bf16[4,32,384]{2,1,0:T(8,128)(2,1)}, bf16[2,96,768]{2,1,0:T(8,128)(2,1)}, bf16[2,96,768]{2,1,0:T(8,128)(2,1)}, b...) custom-call(bf16[4,2,96,576]{3,2,1,0:T(8,128)(2,1)} %bitcast.165, ...), custom_call_target="tpu_custom_call" | custom-call | bytes 8388608 | tf_op jit(solution)/shard_map/ship/pallas_call | solution.py:414
  608.9 19.5 %ship.8 = (bf16[96,576]{1,0:T(8,128)(2,1)}, bf16[32,384]{1,0:T(8,128)(2,1)}, bf16[2,2,96,768]{3,2,1,0:T(8,128)(2,1)}, bf16[2,2,96,768]{3,2,1,0:T(8,128)(2,1)}, b...) custom-call(bf16[4,96,576]{2,1,0:T(8,128)(2,1)} %get-tuple-element.267.re, ...), custom_call_target="tpu_custom_call" | custom-call | bytes 8388608 | tf_op jit(solution)/shard_map/ship/pallas_call | solution.py:414
  628.4 8.8 %ship.9 = (bf16[2,96,576]{2,1,0:T(8,128)(2,1)}, bf16[2,32,384]{2,1,0:T(8,128)(2,1)}, f32[192,3072]{1,0:T(8,128)}, f32[768,768]{1,0:T(8,128)}, bf16[2,2,48,384]{3...) custom-call(bf16[96,576]{1,0:T(8,128)(2,1)} %get-tuple-element.275.refs_0_, ...), custom_call_target="tpu_custom_call" | custom-call | bytes 8388608 | tf_op jit(solution)/shard_map/ship/pallas_call | solution.py:414
  637.2 9.9 %ship.10 = (bf16[2,2,96,576]{3,2,1,0:T(8,128)(2,1)}, bf16[2,2,32,384]{3,2,1,0:T(8,128)(2,1)}, f32[384,384]{1,0:T(8,128)}, f32[36,128]{1,0:T(8,128)}) custom-call(bf16[2,96,576]{2,1,0:T(8,128)(2,1)} %get-tuple-element.282.refs_0_, bf16[2,32,384]{2,1,0:T(8,128)(2,1)} %get-tuple-element.283.refs_1_, bf16[2,2,48,384]{3,2,1,0:T(8,128)(2,1)} %get-tuple-element.284.refs_2_, ...), custom_call_target="tpu_custom_call" | custom-call | bytes 8388608 | tf_op jit(solution)/shard_map/ship/pallas_call | solution.py:414
  647.2 4.0 ship.11
  651.2 2.0 reshape.212
  662.2 1.2 copy.116
  663.4 1.1 copy-done.5
  664.5 1.4 copy.117
  665.9 1.1 copy-done.4
  667.0 1.4 copy.118
  669.4 1.2 copy.119
  673.0 1.4 copy.122
  674.4 1.1 copy-done.2
  675.5 1.4 copy.123
  (215 shorter events, 45.2 us)
Async XLA Ops:
  0.7 57.4 %copy-start = (s32[2,8,20]{2,1,0:T(8,128)S(1)}, s32[2,8,20]{2,1,0:T(8,128)}, u32[]{:S(2)}) copy-start(s32[2,8,20]{2,1,0:T(8,128)} %param.30) | copy-start | bytes 3844
  0.7 31.1 %copy-start.22 = (bf16[2,128,768]{2,1,0:T(8,128)(2,1)S(1)}, bf16[2,128,768]{2,1,0:T(8,128)(2,1)}, u32[]{:S(2)}) copy-start(bf16[2,128,768]{2,1,0:T(8,128)(2,1)} %refs_0_.1) | copy-start | bytes 1179652
  31.7 1.8 copy-start.47
  53.8 4.3 copy-start.39
  53.8 5.3 copy-start.23
  53.8 5.3 copy-start.43
  58.0 1.9 copy-start.45
  59.1 4.1 copy-start.48
  59.1 4.1 copy-start.64
  59.2 5.9 copy-start.53
  156.7 28.9 %copy-start.17 = (bf16[4,2,96,768]{3,2,1,0:T(8,128)(2,1)S(1)}, bf16[4,2,96,768]{3,2,1,0:T(8,128)(2,1)}, u32[]{:S(2)}) copy-start(bf16[4,2,96,768]{3,2,1,0:T(8,128)(2,1)} %get-tuple-element.180) | copy-start | bytes 3538948
  156.7 28.9 %copy-start.55 = (bf16[1024,768]{1,0:T(8,128)(2,1)S(1)}, bf16[1024,768]{1,0:T(8,128)(2,1)}, u32[]{:S(2)}) copy-start(bf16[1024,768]{1,0:T(8,128)(2,1)} %get-tuple-element.179) | copy-start | bytes 4718596
  189.5 28.9 %copy-start.20 = (bf16[2,128,768]{2,1,0:T(8,128)(2,1)S(1)}, bf16[2,128,768]{2,1,0:T(8,128)(2,1)}, u32[]{:S(2)}) copy-start(bf16[2,128,768]{2,1,0:T(8,128)(2,1)} %refs_4_.1) | copy-start | bytes 1179652
  218.4 1.8 copy-start.25
  220.2 3.4 copy-start.31
  220.2 3.4 copy-start.57
  238.9 24.5 %copy-start.19 = (bf16[4,2,96,768]{3,2,1,0:T(8,128)(2,1)S(1)}, bf16[4,2,96,768]{3,2,1,0:T(8,128)(2,1)}, u32[]{:S(2)}) copy-start(bf16[4,2,96,768]{3,2,1,0:T(8,128)(2,1)} %get-tuple-element.199) | copy-start | bytes 3538948
  291.0 4.5 copy-start.61
  291.1 4.5 copy-start.65
  291.1 4.5 copy-start.66
  295.6 3.9 copy-start.60
  299.5 2.5 copy-start.14
  302.0 33.8 %copy-start.29 = (bf16[1024,192]{1,0:T(8,128)(2,1)S(1)}, bf16[1024,192]{1,0:T(8,128)(2,1)}, u32[]{:S(2)}) copy-start(bf16[1024,192]{1,0:T(8,128)(2,1)} %get-tuple-element.195.refs_0_.refs_5_) | copy-start | bytes 1179652
  335.8 2.8 copy-start.34
  341.6 26.9 %copy-start.58 = (bf16[1024,768]{1,0:T(8,128)(2,1)S(1)}, bf16[1024,768]{1,0:T(8,128)(2,1)}, u32[]{:S(2)}) copy-start(bf16[1024,768]{1,0:T(8,128)(2,1)} %get-tuple-element.192) | copy-start | bytes 4718596
  368.5 3.0 copy-start.30
  373.0 29.3 %copy-start.6 = (bf16[1024,192]{1,0:T(8,128)(2,1)S(1)}, bf16[1024,192]{1,0:T(8,128)(2,1)}, u32[]{:S(2)}) copy-start(bf16[1024,192]{1,0:T(8,128)(2,1)} %get-tuple-element.183.refs_0_.refs_10_) | copy-start | bytes 1179652
  402.3 2.9 copy-start.33
  402.3 2.9 copy-start.59
  405.2 1.7 copy-start.21
  405.2 1.7 copy-start.42
  407.7 33.1 %copy-start.54 = (bf16[1024,768]{1,0:T(8,128)(2,1)S(1)}, bf16[1024,768]{1,0:T(8,128)(2,1)}, u32[]{:S(2)}) copy-start(bf16[1024,768]{1,0:T(8,128)(2,1)} %get-tuple-element.177) | copy-start | bytes 4718596
  450.9 29.0 %copy-start.35 = (bf16[192,768]{1,0:T(8,128)(2,1)S(1)}, bf16[192,768]{1,0:T(8,128)(2,1)}, u32[]{:S(2)}) copy-start(bf16[192,768]{1,0:T(8,128)(2,1)} %get-tuple-element.174.refs_1_) | copy-start | bytes 884740
  479.9 3.1 copy-start.7
  483.0 2.9 copy-start.12
  485.9 4.1 copy-start.13
  485.9 4.1 copy-start.56
  533.3 38.1 %copy-start.63 = (f32[3,1,2048]{2,1,0:T(1,128)S(1)}, f32[3,1,2048]{2,1,0:T(1,128)}, u32[]{:S(2)}) copy-start(f32[3,1,2048]{2,1,0:T(1,128)} %get-tuple-element.263) | copy-start | bytes 73732
  568.6 4.2 copy-start.52
  568.6 4.3 copy-start.51
  568.6 4.4 copy-start.62
  568.6 5.7 copy-start.50
  568.6 5.8 copy-start.49
  568.6 6.6 copy-start.15
  637.2 18.1 %copy-start.28 = (f32[384,384]{1,0:T(8,128)S(1)}, f32[384,384]{1,0:T(8,128)}, u32[]{:S(2)}) copy-start(f32[384,384]{1,0:T(8,128)} %get-tuple-element.295) | copy-start | bytes 1769476
  647.2 6.1 copy-start.46
  647.2 9.2 %copy-start.10 = (f32[2,128,768]{2,1,0:T(8,128)S(1)}, f32[2,128,768]{2,1,0:T(8,128)}, u32[]{:S(2)}) copy-start(f32[2,128,768]{2,1,0:T(8,128)} %get-tuple-element.249) | copy-start | bytes 2359300
  647.2 9.2 %copy-start.36 = (bf16[128,768]{1,0:T(8,128)(2,1)S(1)}, bf16[128,768]{1,0:T(8,128)(2,1)}, u32[]{:S(2)}) copy-start(bf16[128,768]{1,0:T(8,128)(2,1)} %get-tuple-element.266) | copy-start | bytes 589828
  656.4 1.4 copy-start.37
  657.4 1.5 copy-start.27
  657.9 1.9 copy-start.24
  657.9 1.9 copy-start.41
  658.8 1.8 copy-start.40
  658.8 1.8 copy-start.44
  659.8 1.7 copy-start.32
  659.8 2.4 copy-start.9
  662.2 2.3 copy-start.5
  664.5 2.5 copy-start.4
  667.0 2.3 copy-start.8
  669.4 1.4 copy-start.26
  669.4 2.3 copy-start.16
  670.8 2.2 copy-start.3
  673.0 2.5 copy-start.2
  673.0 3.9 copy-start.1
  (3 other events, 4.0 us)

commit v4 on v3

--- a/solution.py
+++ b/solution.py
@@ -129,7 +129,10 @@
 
 
 def swap_job(src, at=0, add=False):
-    shape = src.shape[:at] + src.shape[at + 1 :]
+    if at == "cols":
+        shape = src.shape[:-1] + (src.shape[-1] // 2,)
+    else:
+        shape = src.shape[:at] + src.shape[at + 1 :]
     return Job("seq", at, None, add, src, shape, "add" if add else None)
 
 
@@ -150,6 +153,8 @@
         return job.shape[1:], job.src.dtype
     if isinstance(job.finish, tuple):
         seqs, halves, cores, rows, cols = job.shape
+        if job.finish[1] < 0:
+            return (halves * cores * rows, seqs * cols), F32
         if job.finish[1]:
             return (seqs * rows, halves * cores * cols), F32
         return (seqs * halves * cores * rows, cols), F32
@@ -157,6 +162,9 @@
 
 
 def entry(ref, axis, index):
+    if axis == "cols":
+        half = ref.shape[-1] // 2
+        return ref.at[:, :, pl.ds(pl.multiple_of(index * half, half), half)]
     return ref if axis is None else ref.at[(slice(None),) * axis + (index,)]
 
 
@@ -233,30 +241,42 @@
             other = 1 - self.coord(axis)
             yield other, {"tp": to}, other
 
-    def greet(self, always=("core", "across")):
+    def signal(self, always=("core", "across")):
         axes = list(always) + sorted({job.axis for job in self.jobs} - set(always))
         barrier = pltpu.get_barrier_semaphore()
-        total = 0
+        self.expected, self.turns = 0, "turn" in axes
         for axis in axes:
             for _, device, _ in self.peers(axis):
                 if axis == "turn":
+
+                    @pl.when(self.plane != self.tp)
+                    def _():
+                        pl.semaphore_signal(
+                            barrier, inc=1, device_id=device, device_id_type=MESH_ID
+                        )
+
                     continue
                 pl.semaphore_signal(barrier, inc=1, device_id=device, device_id_type=MESH_ID)
-                total += 1
-        if "turn" in axes:
+                self.expected += 1
+
+    def met(self):
+        barrier = pltpu.get_barrier_semaphore()
+        if self.turns:
             moves = self.plane != self.tp
 
             @pl.when(moves)
             def _():
-                for _, device, _ in self.peers("turn"):
-                    pl.semaphore_signal(barrier, inc=1, device_id=device, device_id_type=MESH_ID)
-                pl.semaphore_wait(barrier, total + 1)
+                pl.semaphore_wait(barrier, self.expected + 1)
 
             @pl.when(jnp.logical_not(moves))
             def _():
-                pl.semaphore_wait(barrier, total)
+                pl.semaphore_wait(barrier, self.expected)
         else:
-            pl.semaphore_wait(barrier, total)
+            pl.semaphore_wait(barrier, self.expected)
+
+    def greet(self, always=("core", "across")):
+        self.signal(always)
+        self.met()
 
     def each(self, act_remote, act_local):
         base = 0
@@ -351,6 +371,12 @@
     @staticmethod
     def lay_out(src, dst, width):
         seqs, halves, cores, rows, cols = src.shape
+        if width < 0:
+            for i in range(seqs):
+                for q in range(TP):
+                    block = slice(i * cols, (i + 1) * cols)
+                    dst[q * rows : (q + 1) * rows, block] = src[i, q // 2, q % 2].astype(F32)
+            return
 
         @pl.loop(0, seqs)
         def _(i):
@@ -371,9 +397,10 @@
 
 
 class Loaded:
-    def __init__(self, src, dst, sem):
+    def __init__(self, src, dst, sem, start=True):
         self.copy, self.ref, self.waited = pltpu.make_async_copy(src, dst, sem), dst, False
-        self.copy.start()
+        if start:
+            self.copy.start()
 
     def get(self):
         if not self.waited:
@@ -382,7 +409,31 @@
         return self.ref
 
 
-def call_with_jobs(kernel, number, planes, jobs, operands, outs, scratch, name, cost, filler=None):
+class LoadedRows:
+    def __init__(self, src, dst, sems, chunk):
+        self.src, self.ref, self.sems, self.chunk = src, dst, sems, chunk
+
+    def copies(self, owner, slot):
+        for j in range(2):
+            at = pl.multiple_of((TP * j + owner) * self.chunk, self.chunk)
+            rows = pl.ds(at, self.chunk)
+            yield pltpu.make_async_copy(
+                self.src.at[rows], self.ref.at[rows], self.sems.at[2 * slot + j]
+            )
+
+    def start(self, owners):
+        for slot, owner in enumerate(owners):
+            for copy in self.copies(owner, slot):
+                copy.start()
+
+    def wait(self, owner, slot):
+        for copy in self.copies(owner, slot):
+            copy.wait()
+
+
+def call_with_jobs(
+    kernel, number, planes, jobs, operands, outs, scratch, name, cost, filler=None, by_rows=()
+):
     filler = filler or Idle()
     jobs = list(jobs)
     n_in, n_out, n_job = len(operands), len(outs), len(jobs)
@@ -403,12 +454,20 @@
 
         ins, srcs, fills, raw = take(n_in), take(n_job), take(n_load), take(n_raw)
         results, dsts, fill_outs = take(n_out), take(n_job), take(n_fill)
-        sems, in_sems = take(2)
-        loaded = [Loaded(src, refs.pop(0), in_sems.at[i]) for i, src in enumerate(ins)]
-        fill_loads = [Loaded(src, refs.pop(0), in_sems.at[n_in + i]) for i, src in enumerate(fills)]
+        sems, in_sems, row_sems = take(3)
+        loaded = []
+        for i, src in enumerate(ins):
+            if i in by_rows:
+                rows = row_sems.at[by_rows.index(i)]
+                loaded.append(LoadedRows(src, refs.pop(0), rows, src.shape[0] // (2 * TP)))
+            else:
+                loaded.append(Loaded(src, refs.pop(0), in_sems.at[i]))
+        fill_loads = [
+            Loaded(src, refs.pop(0), in_sems.at[n_in + i], False) for i, src in enumerate(fills)
+        ]
         shipper = Shipper(plain, planes, srcs, dsts, take(len(job_scratch)), sems)
         begin = functools.partial(filler.begin, fill_loads, raw, fill_outs, take(n_scratch))
-        kernel(shipper, loaded, list(results), refs, Running(filler, begin))
+        kernel(shipper, loaded, list(results), refs, Running(filler, begin, fill_loads))
 
     results = [result_of(job) for job in jobs]
     got = pl.pallas_call(
@@ -421,6 +480,7 @@
         scratch_shapes=[
             pltpu.SemaphoreType.DMA((n_sems,)),
             pltpu.SemaphoreType.DMA((max(n_in + n_load, 1),)),
+            pltpu.SemaphoreType.DMA((max(len(by_rows), 1), 2 * TP)),
         ]
         + [pltpu.VMEM(v.shape, v.dtype) for v in operands + loads]
         + job_scratch
@@ -436,9 +496,13 @@
 
 
 class Running:
-    def __init__(self, filler, begin):
-        self.begin, self.run, self.end = begin, filler.run, filler.end
+    def __init__(self, filler, begin, loads):
+        self.begin, self.run, self.end, self.loads = begin, filler.run, filler.end, loads
         self.n_steps, self.done = filler.n_steps, 0
+
+    def prefetch(self):
+        for load in self.loads:
+            load.copy.start()
 
     def advance(self, share):
         high = int(round(share * self.n_steps))
@@ -460,19 +524,21 @@
     chunk = x.shape[1]
 
     def kernel(shipper, ins, outs, scratch, filler):
-        shipper.greet()
+        shipper.signal()
         x_ref, gain_ref = (v.get() for v in ins)
+        shipper.met()
+        shipper.start()
         g = Gatherer(outs[0], scratch[0], scratch[1], chunk, group_ids())
         for j in range(2):
             g.put(j, normed(x_ref[j].astype(F32), gain_ref[...]).astype(BF))
-        shipper.start()
+        filler.prefetch()
         filler.begin()
         filler.advance(0.4)
         for j in range(2):
             g.forward(j)
         filler.advance(1.0)
+        filler.end()
         g.finish()
-        filler.end()
         shipper.finish()
 
     outs = [jax.ShapeDtypeStruct((2 * TP * chunk, D), BF)]
@@ -483,9 +549,126 @@
     return got[0], moved, made
 
 
+GELU_C = float(np.sqrt(2.0 / np.pi))
+
+
+def gelu_parts(v):
+    tanh = jnp.tanh(GELU_C * (v + 0.044715 * v * v * v))
+    return tanh, 0.5 * (1.0 + tanh)
+
+
+def gelu_slope(v):
+    tanh, half = gelu_parts(v)
+    return half + 0.5 * v * (1.0 - tanh * tanh) * (GELU_C * (1.0 + 3 * 0.044715 * v * v))
+
+
+class Rows:
+    n_operands, n_outs, n_scratch = 1, 0, 0
+
+    def __init__(self, ins, outs, scratch, chunk):
+        self.rows, self.chunk = ins.pop(0), chunk
+        self.by_rows = [self.rows]
+
+    def prepare(self):
+        self.ref = self.rows.ref
+
+    def make(self, pair, slot):
+        pass
+
+    def finish(self):
+        pass
+
+    def pick(self, ref, pair):
+        return jnp.concatenate([ref[rows] for rows in pair], axis=0)
+
+
+class MadeRows(Rows):
+    def write(self, index, ref, out, slot, pair):
+        for j, rows in enumerate(pair):
+            copy = pltpu.make_async_copy(ref.at[rows], out.at[rows], self.sems.at[index, 2 * slot + j])
+            copy.start()
+            self.copies.append(copy)
+
+    def finish(self):
+        for copy in self.copies:
+            copy.wait()
+
+    def tiles(self, body):
+        @pl.loop(0, self.ref.shape[1] // 256)
+        def _(n):
+            body(pl.ds(pl.multiple_of(n * 256, 256), 256))
+
+
+class FeedForward(MadeRows):
+    n_operands, n_outs, n_scratch = 2, 2, 3
+
+    def __init__(self, ins, outs, scratch, chunk):
+        self.rows, self.w_in, self.chunk, self.copies = ins.pop(0), ins.pop(0), chunk, []
+        self.by_rows = [self.rows]
+        self.pre_out, self.act_out = outs.pop(0), outs.pop(0)
+        self.pre, self.ref, self.sems = scratch.pop(0), scratch.pop(0), scratch.pop(0)
+
+    @staticmethod
+    def extras(n_rows, width):
+        shapes = [((n_rows, width), F32), ((n_rows, width), BF)]
+        scratch = [pltpu.VMEM(*v) for v in shapes] + [pltpu.SemaphoreType.DMA((2, 2 * TP))]
+        return [jax.ShapeDtypeStruct(*v) for v in shapes], scratch
+
+    def prepare(self):
+        self.w_in = self.w_in.get()
+
+    def make(self, pair, slot):
+        x = self.pick(self.rows.ref, pair)
+
+        def tile(cols):
+            v = mm(x, self.w_in[:, cols])
+            act = (v * gelu_parts(v)[1]).astype(BF)
+            for j, rows in enumerate(pair):
+                self.pre[rows, cols] = v[j * self.chunk : (j + 1) * self.chunk]
+                self.ref[rows, cols] = act[j * self.chunk : (j + 1) * self.chunk]
+
+        self.tiles(tile)
+        self.write(0, self.pre, self.pre_out, slot, pair)
+        self.write(1, self.ref, self.act_out, slot, pair)
+
+
+class FeedForwardBack(MadeRows):
+    n_operands, n_outs, n_scratch = 3, 1, 2
+
+    def __init__(self, ins, outs, scratch, chunk):
+        self.rows, self.pre, self.w_out = ins.pop(0), ins.pop(0), ins.pop(0)
+        self.chunk, self.copies = chunk, []
+        self.by_rows = [self.rows, self.pre]
+        self.out, self.ref, self.sems = outs.pop(0), scratch.pop(0), scratch.pop(0)
+
+    @staticmethod
+    def extras(n_rows, width):
+        shape = ((n_rows, width), BF)
+        scratch = [pltpu.VMEM(*shape), pltpu.SemaphoreType.DMA((1, 2 * TP))]
+        return [jax.ShapeDtypeStruct(*shape)], scratch
+
+    def prepare(self):
+        self.w_out = self.w_out.get()
+
+    def make(self, pair, slot):
+        x = self.pick(self.rows.ref, pair)
+
+        def tile(cols):
+            grad = mm_nt(x, self.w_out[cols, :])
+            for j, rows in enumerate(pair):
+                back = gelu_slope(self.pre.ref[rows, cols]) * grad[j * self.chunk : (j + 1) * self.chunk]
+                self.ref[rows, cols] = back.astype(BF)
+
+        self.tiles(tile)
+        self.write(0, self.ref, self.out, slot, pair)
+
+
 def stage_kernel(conf, shipper, ins, outs, scratch, filler):
-    chunk, flips, back, gather = conf
-    pairs = [(ins.pop(0), ins.pop(0), flip) for flip in flips]
+    chunk, maker, flip, back, gather = conf
+    made_outs = [outs.pop() for _ in range(maker.n_outs)][::-1]
+    made_scratch = [scratch.pop() for _ in range(maker.n_scratch)][::-1]
+    left = maker(ins, made_outs, made_scratch, chunk)
+    w_in = ins.pop(0)
     resid_in = ins.pop(0)
     gain_in = ins.pop(0) if (back or gather == "norm") else None
     x_in = ins.pop(0) if back else None
@@ -499,19 +682,22 @@
     dgain_ref = scratch.pop(0) if back else None
     ids = group_ids()
     me, core, across, far = ids
+    slots = [0, 1, 2, 3]
 
     def partial(owner, store):
-        r0 = pl.multiple_of(owner * chunk, chunk)
-        r1 = pl.multiple_of((TP + owner) * chunk, chunk)
+        slot = slots.pop(0)
+        for rows in left.by_rows:
+            rows.wait(owner, slot)
+        pair = [
+            pl.ds(pl.multiple_of((TP * j + owner) * chunk, chunk), chunk) for j in range(2)
+        ]
+        left.make(pair, slot)
+        a = left.pick(left.ref, pair)
 
         @pl.loop(0, D // 256)
         def _(n):
             cols = pl.ds(pl.multiple_of(n * 256, 256), 256)
-            total = None
-            for a_ref, w_ref, flip in pairs:
-                a = jnp.concatenate([a_ref[pl.ds(r0, chunk)], a_ref[pl.ds(r1, chunk)]], axis=0)
-                term = mm_nt(a, w_ref[cols, :]) if flip else mm(a, w_ref[:, cols])
-                total = term if total is None else total + term
+            total = mm_nt(a, w_ref[cols, :]) if flip else mm(a, w_ref[:, cols])
             for j in range(2):
                 store(j, cols, total[j * chunk : (j + 1) * chunk])
 
@@ -521,18 +707,24 @@
 
         return store
 
-    shipper.greet()
+    order = (far, across, core, me)
+    for rows in left.by_rows:
+        rows.start(order)
+    shipper.signal()
+    left.prepare()
+    w_ref = w_in.get()
+    partial(far, into(s_far))
+    shipper.met()
+    c_far = send(s_far, r_far, sems.at[0], sems.at[1], core)
+    c_far.start()
     shipper.start()
     g = Gatherer(gath_ref, g_stage, g_sems, chunk, ids) if gather else None
     if gather == "given":
         given_ref = given_in.get()
         for j in range(2):
             g.put(j, given_ref[j])
-    pairs = [(a.get(), w.get(), flip) for a, w, flip in pairs]
-    partial(far, into(s_far))
-    c_far = send(s_far, r_far, sems.at[0], sems.at[1], core)
-    c_far.start()
     partial(across, into(keep))
+    filler.prefetch()
     c_far.wait_recv()
     c_x = []
     for j in range(2):
@@ -590,9 +782,9 @@
         for j in range(2):
             g.forward(j)
     filler.advance(1.0)
+    filler.end()
     if gather:
         g.finish()
-    filler.end()
     c_far.wait_send()
     c_core.wait_send()
     for j in range(2):
@@ -600,17 +792,30 @@
     shipper.finish()
     for copy in stores:
         copy.wait()
+    left.finish()
 
 
 def stage(
-    number, planes, pairs, resid, *, back=None, gather=None, gain=None, given=None, dtype=F32, jobs=(), filler=None
+    number,
+    planes,
+    left,
+    weight,
+    resid,
+    *,
+    flip=False,
+    maker=Rows,
+    back=None,
+    gather=None,
+    gain=None,
+    given=None,
+    dtype=F32,
+    jobs=(),
+    filler=None,
 ):
     chunk = resid.shape[1]
-    operands, flips, cost = [], [], 0
-    for a, w, flip in pairs:
-        operands += [a, w]
-        flips.append(flip)
-        cost += 2 * a.shape[0] * a.shape[1] * D
+    operands = list(left) + [weight]
+    cost = 4 * left[0].shape[0] * D * D
+    by_rows = {Rows: (0,), FeedForward: (0,), FeedForwardBack: (0, 1)}[maker]
     operands.append(resid)
     if back:
         operands += [back[1], back[0]]
@@ -633,9 +838,24 @@
         scratch += [half, pltpu.SemaphoreType.DMA((7, 2))]
     if back:
         scratch.append(pltpu.VMEM((1, D), F32))
-    kernel = functools.partial(stage_kernel, (chunk, tuple(flips), bool(back), gather))
+    if maker is not Rows:
+        width = weight.shape[1] if flip else weight.shape[0]
+        more, more_scratch = maker.extras(2 * TP * chunk, width)
+        outs += more
+        scratch += more_scratch
+    kernel = functools.partial(stage_kernel, (chunk, maker, flip, bool(back), gather))
     got, moved, made = call_with_jobs(
-        kernel, number, planes, list(jobs), operands, outs, scratch, "stage", cost, filler
+        kernel,
+        number,
+        planes,
+        list(jobs),
+        operands,
+        outs,
+        scratch,
+        "stage",
+        cost,
+        filler,
+        by_rows,
     )
     return (got, moved, made) if filler else (got, moved)
 
@@ -643,6 +863,7 @@
 class Attention:
     def __init__(self, parts, q, kv, bias, mkv, causal):
         self.parts, self.causal = parts, causal
+        self.q_shape, self.kv_shape = q.shape, kv.shape
         self.rows, self.keys = q.shape[0], kv.shape[0]
         self.chunk = self.rows // (2 * TP)
         self.joint = q is kv
@@ -651,15 +872,14 @@
         self.bias = bias
         self.blocks = self.rows // (2 * self.chunk)
         self.n_steps = HQ * self.blocks
-        self.loads = [q] + ([] if self.joint else [kv]) + ([mkv] if self.extra else [])
+        self.loads = [q] + ([] if self.joint else [kv])
+        self.mem = [mkv] if self.extra else []
         self.raws = []
 
     def heads(self, *widths_dtypes):
         return [pltpu.VMEM((HQ, n, DH), dtype) for n, dtype in widths_dtypes]
 
-    def split_qkv(self, loads, qs, ks, vs):
-        q_ref = loads.pop(0).get()
-        kv_ref = q_ref if self.joint else loads.pop(0).get()
+    def split_qkv(self, q_ref, kv_ref, loads, qs, ks, vs):
         at = QC if self.joint else 0
         keys = self.keys
         for i in range(HQ):
@@ -687,9 +907,12 @@
 
 
 class AttentionForward(Attention):
-    def __init__(self, parts, q, kv, segq, segk, bvec, mkv, causal):
+    def __init__(self, parts, q, kv, segq, segk, bvec, mkv, causal, products=None):
         super().__init__(parts, q, kv, bvec is not None, mkv, causal)
-        self.loads += [segq, segk] + ([bvec] if self.bias else [])
+        self.products = products
+        if products:
+            self.loads = [v for pair in products for v in pair]
+        self.loads += self.mem + [segq, segk] + ([bvec] if self.bias else [])
         self.outs = [
             jax.ShapeDtypeStruct((self.rows, QC), BF),
             jax.ShapeDtypeStruct((HQ, self.rows, self.total), BF),
@@ -698,17 +921,38 @@
         self.scratch += [
             pltpu.VMEM((2, 2 * self.chunk, self.total), BF),
             pltpu.VMEM((self.rows, QC), BF),
-            pltpu.SemaphoreType.DMA((3,)),
+            pltpu.SemaphoreType.DMA((5,)),
         ]
         if self.bias:
             self.scratch.append(pltpu.VMEM((self.chunk, 2 * self.keys), F32))
+        if products:
+            for x, w in products:
+                self.outs.append(jax.ShapeDtypeStruct((x.shape[0], w.shape[1]), BF))
+                self.scratch.append(pltpu.VMEM((x.shape[0], w.shape[1]), BF))
 
     def begin(self, loads, raws, outs, scratch):
-        self.att_out, self.p_out = outs
+        self.att_out, self.p_out = outs[:2]
         self.qs, self.ks, self.vs, self.os, self.p_buf, self.att, self.sems = scratch[:7]
         self.toep = scratch[7] if self.bias else None
         loads = list(loads)
-        self.split_qkv(loads, self.qs, self.ks, self.vs)
+        self.copies = []
+        if self.products:
+            made = scratch[-len(self.products) :]
+            for n, (out, to) in enumerate(zip(made, outs[2:])):
+                x, w = loads.pop(0).get(), loads.pop(0).get()
+
+                @pl.loop(0, x.shape[0] // 256)
+                def _(r):
+                    rows = pl.ds(pl.multiple_of(r * 256, 256), 256)
+                    out[rows] = mm(x[rows], w[...]).astype(BF)
+
+                self.copies.append(pltpu.make_async_copy(out, to, self.sems.at[3 + n]))
+                self.copies[-1].start()
+            q_ref, kv_ref = made[0], made[-1]
+        else:
+            q_ref = loads.pop(0).get()
+            kv_ref = q_ref if self.joint else loads.pop(0).get()
+        self.split_qkv(q_ref, kv_ref, loads, self.qs, self.ks, self.vs)
         self.segq, self.segk = loads.pop(0).get(), loads.pop(0).get()
         self.bvec = loads.pop(0).get() if self.bias else None
 
@@ -762,12 +1006,15 @@
         self.keep(self.n_steps - 2).wait()
         self.keep(self.n_steps - 1).wait()
         out.wait()
+        for copy in self.copies:
+            copy.wait()
 
 
 class AttentionBackward(Attention):
-    def __init__(self, parts, p, q, kv, grad, att, bias, mkv):
+    def __init__(self, parts, p, q, kv, up, w_proj, att, bias, mkv, xs, proj=True):
         super().__init__(parts, q, kv, bias, mkv, False)
-        self.loads += [grad, att]
+        self.xs, self.proj = xs if parts == 1 else [], proj
+        self.loads += self.mem + [up, w_proj, att] + self.xs
         self.raws = [p]
         rows, total, keys = self.rows, self.total, self.keys
         if self.joint:
@@ -782,6 +1029,10 @@
             self.outs.append(jax.ShapeDtypeStruct((HQ, 1, 2 * keys), F32))
         if self.extra:
             self.outs.append(jax.ShapeDtypeStruct((self.extra, 2 * QC), BF))
+        if proj:
+            self.outs.append(jax.ShapeDtypeStruct((QC, D), BF))
+        for n in range(len(self.xs)):
+            self.outs.append(jax.ShapeDtypeStruct((D, self.outs[n].shape[1]), BF))
         self.scratch = self.heads(
             (rows, BF), (total, BF), (total, BF), (rows, BF), (rows, BF), (total, F32), (total, F32)
         )
@@ -807,18 +1058,35 @@
         self.made = scratch[10 : 10 + len(outs)]
         self.diag = scratch[-1] if self.bias else None
         self.fetch(0).start()
-        self.split_qkv(loads, self.qs, self.ks, self.vs)
-        do_ref, att_ref = loads.pop(0).get(), loads.pop(0).get()
-        for i in range(HQ):
-            grad = do_ref[:, DH * i : DH * (i + 1)]
-            self.dos[i] = grad
-            out = att_ref[:, DH * i : DH * (i + 1)]
-            self.rds[i] = jnp.sum(grad.astype(F32) * out.astype(F32), axis=-1, keepdims=True)
+        q_ref = loads.pop(0).get()
+        kv_ref = q_ref if self.joint else loads.pop(0).get()
+        self.split_qkv(q_ref, kv_ref, loads, self.qs, self.ks, self.vs)
+        up_ref, w_ref, att_ref = (loads.pop(0).get() for _ in range(3))
+
+        @pl.loop(0, self.rows // 256)
+        def _(r):
+            rows = pl.ds(pl.multiple_of(r * 256, 256), 256)
+            grads = mm_nt(up_ref[rows], w_ref[...]).astype(BF)
+            att = att_ref[rows]
+            for i in range(HQ):
+                span = slice(DH * i, DH * (i + 1))
+                self.dos[i, rows] = grads[:, span]
+                dots = grads[:, span].astype(F32) * att[:, span].astype(F32)
+                self.rds[i, rows] = jnp.sum(dots, axis=-1, keepdims=True)
+
         made = list(self.made)
         self.dq = made.pop(0)
         self.dkv = self.dq if self.joint else made.pop(0)
         self.dbvec = made.pop(0) if self.bias else None
         self.dmkv = made.pop(0) if self.extra else None
+        g_proj = made.pop(0) if self.proj else None
+        self.g_rows, self.x_loads = made, loads
+        if self.proj:
+
+            @pl.loop(0, D // 256)
+            def _(n):
+                cols = pl.ds(pl.multiple_of(n * 256, 256), 256)
+                g_proj[:, cols] = mm_tn(att_ref[...], up_ref[:, cols]).astype(BF)
 
     def run(self, low, high):
         keys, chunk = self.keys, self.chunk
@@ -870,6 +1138,14 @@
             if self.extra:
                 self.dmkv[:, DH * i : DH * (i + 1)] = self.dks[i, keys:].astype(BF)
                 self.dmkv[:, QC + DH * i : QC + DH * (i + 1)] = self.dvs[i, keys:].astype(BF)
+        for load, out, grad in zip(self.x_loads, self.g_rows, (self.dq, self.dkv)):
+            x_ref = load.get()
+
+            @pl.loop(0, D // 256)
+            def _(n):
+                cols = pl.ds(pl.multiple_of(n * 256, 256), 256)
+                out[cols] = mm_tn(x_ref[:, cols], grad[...]).astype(BF)
+
         copies = [
             pltpu.make_async_copy(src, dst, self.sems.at[2 + n])
             for n, (src, dst) in enumerate(zip(self.made, self.results))
@@ -895,6 +1171,7 @@
 
 def attend(number, planes, filler, jobs):
     def kernel(shipper, ins, outs, scratch, filler):
+        filler.prefetch()
         shipper.greet(())
         shipper.start()
         filler.begin()
@@ -906,6 +1183,11 @@
         kernel, number, planes, jobs, [], [], [], "attend", 4 * 10**9, filler
     )
     return made, moved
+
+
+class Chain:
+    def __init__(self, value, steps):
+        self.value, self.steps = value, steps
 
 
 ALL = ("seq", "part", "tp", "fsdp")
@@ -1075,11 +1357,20 @@
             return got.pop(0)
         return jnp.concatenate([got.pop(0), collect(got.pop(0))], axis=1)
 
-    e_qkv = self_kv(mm(en, w_eqkv).astype(BF))
-    e_fill = AttentionForward(
-        parts, *e_qkv, segq, segk_mem, bias_vector(rels[0]), mkv, False
-    )
-    dn, (w_dqkv, w_effin, w_effout, *got), (e_att, e_p) = gather_norm(
+    def self_fill(x, w, segk_now, bvec, mem, causal):
+        if parts == 1:
+            rows = jax.ShapeDtypeStruct((x.shape[0], w.shape[1]), BF)
+            return AttentionForward(
+                parts, rows, rows, segq, segk_now, bvec, mem, causal, [(x, w)]
+            ), None
+        rows = self_kv(mm(x, w).astype(BF))
+        return AttentionForward(parts, *rows, segq, segk_now, bvec, mem, causal), rows
+
+    def self_made(got, rows):
+        return got[0], got[1], rows or (got[2], got[2])
+
+    e_fill, e_qkv = self_fill(en, w_eqkv, segk_mem, bias_vector(rels[0]), mkv, False)
+    dn, (w_dqkv, w_effin, *got), made = gather_norm(
         2,
         planes,
         xd,
@@ -1087,74 +1378,97 @@
         [
             over_seq(w_dqkv),
             over_planes(ffin_part(enc_ffin)),
-            over_planes(ffout_part(enc_ffout)),
         ]
         + proj_jobs(dec_proj),
         e_fill,
     )
+    e_att, e_p, e_qkv = self_made(made, e_qkv)
     w_dproj = proj_of(got, dec_proj)
     w_dqkv = matrix(w_dqkv)
-    d_qkv = self_kv(mm(dn, w_dqkv).astype(BF))
-    d_fill = AttentionForward(parts, *d_qkv, segq, segk, bias_vector(rels[1]), None, True)
-    (e_mid, e_fn), (w_effin, w_effout, w_cq, w_ckv, w_dffin), (d_att, d_p) = stage(
+    d_fill, d_qkv = self_fill(dn, w_dqkv, segk, bias_vector(rels[1]), None, True)
+    (e_mid, e_fn), (w_effin, w_effout, w_cq, w_ckv), made = stage(
         3,
         planes,
-        [(e_att, w_eproj, False)],
+        [e_att],
+        w_eproj,
         xe,
         gather="norm",
         gain=g_effn,
         jobs=[
             over_seq(w_effin),
-            over_seq(w_effout),
+            over_planes(ffout_part(enc_ffout)),
             over_planes(qkv_part(cross_query)),
             over_planes(qkv_part(cross_kv)),
-            over_planes(ffin_part(dec_ffin)),
         ],
         filler=d_fill,
     )
-    w_effin, w_effout = matrix(w_effin), matrix(w_effout)
-    e_pre = mm(e_fn, w_effin)
-    e_act = gelu(e_pre).astype(BF)
-    (d_mid, c_n), (w_cq, w_ckv, w_dffin, w_dffout, *got) = stage(
+    d_att, d_p, d_qkv = self_made(made, d_qkv)
+    w_effin = matrix(w_effin)
+    (d_mid, c_n), (w_effout, w_cq, w_ckv, w_dffin, *got) = stage(
         4,
         planes,
-        [(d_att, w_dproj, False)],
+        [d_att],
+        w_dproj,
         xd,
         gather="norm",
         gain=g_cross,
         jobs=[
+            over_seq(w_effout),
             over_seq(w_cq),
             over_seq(w_ckv),
-            over_seq(w_dffin),
-            over_planes(ffout_part(dec_ffout)),
+            over_planes(ffin_part(dec_ffin)),
         ]
         + proj_jobs(cross_proj),
     )
     w_cproj = proj_of(got, cross_proj)
-    w_cq, w_ckv, w_dffin = matrix(w_cq), matrix(w_ckv), matrix(w_dffin)
-    (e_low, e_gath), (w_dffout, xdc, xec) = stage(
+    w_effout, w_cq, w_ckv = matrix(w_effout), matrix(w_cq), matrix(w_ckv)
+    (e_low, e_gath, e_pre, e_act), (w_dffin, w_dffout, xdc) = stage(
         5,
         planes,
-        [(e_act, w_effout, False)],
+        [e_fn, w_effin],
+        w_effout,
         e_mid,
+        maker=FeedForward,
         gather="low",
         dtype=BF,
-        jobs=[over_seq(w_dffout), swap_job(dec_cotan), swap_job(enc_cotan)],
-    )
-    xdc, xec = joined(dec_cotan, xdc), joined(enc_cotan, xec)
+        jobs=[over_seq(w_dffin), over_planes(ffout_part(dec_ffout)), swap_job(dec_cotan)],
+    )
+    xdc = joined(dec_cotan, xdc)
+    w_dffin = matrix(w_dffin)
+    products = None
+    if parts == 1:
+        c_q = jax.ShapeDtypeStruct((c_n.shape[0], QC), BF)
+        c_kv = jax.ShapeDtypeStruct((e_gath.shape[0], 2 * QC), BF)
+        products = [(c_n, w_cq), (e_gath, w_ckv)]
+    else:
+        c_q = mm(c_n, w_cq).astype(BF)
+        c_kv = spread(mm(e_gath, w_ckv).astype(BF))
+    c_fill = AttentionForward(parts, c_q, c_kv, segq, segk, None, None, False, products)
+    (c_att, c_p, *made), (w_dffout,) = attend(19, planes, c_fill, [over_seq(w_dffout)])
+    if parts == 1:
+        c_q, c_kv = made
     w_dffout = matrix(w_dffout)
-    c_q = mm(c_n, w_cq).astype(BF)
-    c_kv = spread(mm(e_gath, w_ckv).astype(BF))
-    c_fill = AttentionForward(parts, c_q, c_kv, segq, segk, None, None, False)
-    (c_att, c_p), (came,) = attend(19, planes, c_fill, [swap_job(e_low)])
-    enc_output = joined(e_low, came)
-    (d_cross, d_fn), _ = stage(
-        6, planes, [(c_att, w_cproj, False)], d_mid, gather="norm", gain=g_dffn
-    )
-    d_pre = mm(d_fn, w_dffin)
-    d_act = gelu(d_pre).astype(BF)
-    (d_low, up_g), _ = stage(
-        7, planes, [(d_act, w_dffout, False)], d_cross, gather="given", given=xdc, dtype=BF
+    (d_cross, d_fn), (came, xec) = stage(
+        6,
+        planes,
+        [c_att],
+        w_cproj,
+        d_mid,
+        gather="norm",
+        gain=g_dffn,
+        jobs=[swap_job(e_low), swap_job(enc_cotan)],
+    )
+    enc_output, xec = joined(e_low, came), joined(enc_cotan, xec)
+    (d_low, up_g, d_pre, d_act), _ = stage(
+        7,
+        planes,
+        [d_fn, w_dffin],
+        w_dffout,
+        d_cross,
+        maker=FeedForward,
+        gather="given",
+        given=xdc,
+        dtype=BF,
     )
 
     def pieces(g):
@@ -1162,138 +1476,145 @@
             g = lax.psum(g, "part")
         return g.reshape(planes, 2, g.shape[0] // split, g.shape[1])
 
-    def proj_pieces(g):
-        return pieces(g.reshape(2 * QC, D // 2))
-
-    def step1(gs):
-        return [swap_job(g, 1, True) for g in gs]
-
-    def step2(gs):
-        return [deal_job("fsdp", g) for g in gs]
-
-    def step3(gs):
-        return [gather_job("across", g) for g in gs]
-
-    def step4(gs):
-        return [gather_job("seq", g) for g in gs]
-
-    def step5(gs, widths):
-        return [last_job(g, width) for g, width in zip(gs, widths)]
-
-    ff_widths, qkv_widths, proj_widths = [hidden, 0], [QC, QC], [0]
-
-    def take(got, n):
-        out = got[:n]
-        del got[:n]
-        return out
-
-    def ff_grads(up_rows, fn, act, pre, w_out):
-        d_out = mm_tn(act, up_rows).astype(BF)
-        pre_grad = gelu_back(pre, mm_nt(up_rows, w_out)).astype(BF)
-        d_in = mm_tn(fn, pre_grad).astype(BF)
-        return pre_grad, [pieces(d_in), pieces(d_out)]
-
-    pre_grad, g_dff = ff_grads(up_g, d_fn, d_act, d_pre, w_dffout)
-    (up, up_g, dg_dffn), got = stage(
+    def to_ctx(width):
+        return [
+            lambda g: gather_job("across", g),
+            lambda g: gather_job("seq", g),
+            lambda g: last_job(g, width),
+        ]
+
+    def chain(g, width):
+        steps = [lambda g: swap_job(g, 1, True), lambda g: deal_job("fsdp", g)]
+        return Chain(pieces(g), steps + to_ctx(width))
+
+    def proj_chain(g):
+        if not turned:
+            return Chain(g, [])
+        steps = [lambda g: swap_job(g, "cols", True), lambda g: deal_job("fsdp", g), turn_job]
+        return Chain(g.reshape(planes, -1, D), steps + to_ctx(-1))
+
+    def steps_of(chains):
+        return [c.steps[0](c.value) for c in chains if c.steps]
+
+    def settle(chains, got):
+        got = list(got)
+        for c in chains:
+            if c.steps:
+                c.value = got.pop(0)
+                c.steps.pop(0)
+        return got
+
+    k_dffout = chain(mm_tn(d_act, up_g).astype(BF), 0)
+    moving = [k_dffout]
+    (up, up_rows, dg_dffn, pre_grad), got = stage(
         8,
         planes,
-        [(pre_grad, w_dffin, True)],
+        [up_g, d_pre, w_dffout],
+        w_dffin,
         xdc,
+        flip=True,
+        maker=FeedForwardBack,
         back=(d_cross, g_dffn),
         gather="low",
-        jobs=step1(g_dff) + [swap_job(d_low)],
-    )
-    dec_output = joined(d_low, got.pop())
+        jobs=steps_of(moving) + [swap_job(d_low)],
+    )
+    (came,) = settle(moving, got)
+    dec_output = joined(d_low, came)
+    k_dffin = chain(mm_tn(d_fn, pre_grad).astype(BF), hidden)
     c_fill = AttentionBackward(
-        parts, c_p, c_q, c_kv, mm_nt(up_g, w_cproj).astype(BF), c_att, False, None
-    )
-    (c_dq, c_dkv), g_dff = attend(20, planes, c_fill, step2(got))
+        parts, c_p, c_q, c_kv, up_rows, w_cproj, c_att, False, None, [c_n, e_gath]
+    )
+    moving = [k_dffin, k_dffout]
+    (c_dq, c_dkv, g_cproj, *made), got = attend(20, planes, c_fill, steps_of(moving))
+    settle(moving, got)
     c_dkv = collect(c_dkv)
-    g_cproj = mm_tn(c_att, up_g).astype(BF)
-    g_c = [pieces(mm_tn(c_n, c_dq).astype(BF)), pieces(mm_tn(e_gath, c_dkv).astype(BF))]
-    if turned:
-        g_c.append(proj_pieces(g_cproj))
-    (up, up_g, dg_cross), got = stage(
+    if parts > 1:
+        made = [mm_tn(c_n, c_dq).astype(BF), mm_tn(e_gath, c_dkv).astype(BF)]
+    k_cproj, k_cq, k_ckv = proj_chain(g_cproj), chain(made[0], QC), chain(made[1], QC)
+    moving = [k_dffin, k_dffout, k_cq, k_ckv, k_cproj]
+    (up, up_rows, dg_cross), got = stage(
         9,
         planes,
-        [(c_dq, w_cq, True)],
+        [c_dq],
+        w_cq,
         up,
+        flip=True,
         back=(d_mid, g_cross),
         gather="low",
-        jobs=step3(g_dff) + step1(g_c),
-    )
-    g_dff, g_c = take(got, 2), got
+        jobs=steps_of(moving),
+    )
+    settle(moving, got)
+
+    def self_grads(made, x):
+        grad = joint_grad(made)
+        g_rows = made.pop() if parts == 1 else mm_tn(x, grad).astype(BF)
+        return grad, chain(g_rows, QC), made
+
     d_fill = AttentionBackward(
-        parts, d_p, *d_qkv, mm_nt(up_g, w_dproj).astype(BF), d_att, True, None
-    )
-    g_dproj = mm_tn(d_att, up_g).astype(BF)
-    (e_up, e_up_g), got, made = stage(
+        parts, d_p, *d_qkv, up_rows, w_dproj, d_att, True, None, [dn]
+    )
+    (e_up, e_up_rows), got, made = stage(
         10,
         planes,
-        [(c_dkv, w_ckv, True)],
+        [c_dkv],
+        w_ckv,
         xec,
+        flip=True,
         gather="low",
-        jobs=step4(g_dff) + step2(g_c),
+        jobs=steps_of(moving),
         filler=d_fill,
     )
-    g_dff, g_c = take(got, 2), got
-    d_rows_grad = joint_grad(made)
-    (d_dbv,) = made
-    g_d = [pieces(mm_tn(dn, d_rows_grad).astype(BF))]
-    turn = []
-    if turned:
-        g_d.append(proj_pieces(g_dproj))
-        turn = [turn_job(g_c.pop())]
-    pre_grad, g_eff = ff_grads(e_up_g, e_fn, e_act, e_pre, w_effout)
-    (e_up, e_up_g, dg_effn), got = stage(
+    settle(moving, got)
+    d_rows_grad, k_dqkv, (d_dbv, g_dproj) = self_grads(made, dn)
+    k_dproj = proj_chain(g_dproj)
+    k_effout = chain(mm_tn(e_act, e_up_rows).astype(BF), 0)
+    moving = [k_dffout, k_cq, k_ckv, k_cproj, k_dqkv, k_dproj, k_effout]
+    (e_up, e_up_rows, dg_effn, pre_grad), got = stage(
         12,
         planes,
-        [(pre_grad, w_effin, True)],
+        [e_up_rows, e_pre, w_effout],
+        w_effin,
         e_up,
+        flip=True,
+        maker=FeedForwardBack,
         back=(e_mid, g_effn),
         gather="low",
-        jobs=step5(g_dff, ff_widths) + step1(g_d) + step3(g_c) + turn,
-    )
-    o_dff, g_d, g_c, g_cp = take(got, 2), take(got, len(g_d)), take(got, 2), got
+        jobs=steps_of(moving),
+    )
+    settle(moving, got)
+    k_effin = chain(mm_tn(e_fn, pre_grad).astype(BF), hidden)
     e_fill = AttentionBackward(
-        parts, e_p, *e_qkv, mm_nt(e_up_g, w_eproj).astype(BF), e_att, True, mkv
-    )
-    g_eproj = mm_tn(e_att, e_up_g).astype(BF)
-    g_ep = [proj_pieces(g_eproj)] if turned else []
+        parts, e_p, *e_qkv, e_up_rows, w_eproj, e_att, True, mkv, [en], False
+    )
+    k_eproj = proj_chain(mm_tn(e_att, e_up_rows).astype(BF))
+    moving = [k_dffin, k_cq, k_ckv, k_cproj, k_dqkv, k_dproj, k_effout, k_effin, k_eproj]
     (d_in, dg_dec), got, made = stage(
         11,
         planes,
-        [(d_rows_grad, w_dqkv, True)],
+        [d_rows_grad],
+        w_dqkv,
         up,
+        flip=True,
         back=(xd, g_dec),
-        jobs=step1(g_eff) + step1(g_ep) + step2(g_d) + step4(g_c) + step3(g_cp),
+        jobs=steps_of(moving),
         filler=e_fill,
     )
-    g_eff, g_ep = take(got, 2), take(got, len(g_ep))
-    g_d, g_c, g_cp = take(got, len(g_d)), take(got, 2), got
-    d_in_low = d_in.astype(BF)
-    e_rows_grad = joint_grad(made)
-    e_dbv, d_mkv = made
-    turn = [turn_job(g_d.pop())] if turned else []
+    settle(moving, got)
+    e_rows_grad, k_eqkv, (e_dbv, d_mkv) = self_grads(made, en)
+    k_table = chain(mm_tn(pick, d_mkv).astype(BF), QC)
+    moving += [k_eqkv, k_table]
     (e_in, dg_enc), got = stage(
         13,
         planes,
-        [(e_rows_grad, w_eqkv, True)],
+        [e_rows_grad],
+        w_eqkv,
         e_up,
+        flip=True,
         back=(xe, g_enc),
-        jobs=step2(g_eff)
-        + step2(g_ep)
-        + step3(g_d)
-        + turn
-        + step5(g_c, qkv_widths)
-        + step4(g_cp)
-        + [swap_job(d_in_low)],
-    )
-    dec_ingrad = joined(d_in, got.pop())
-    g_eff, g_ep = take(got, 2), take(got, len(g_ep))
-    g_d, g_dp, o_c, g_cp = take(got, 1), take(got, len(turn)), take(got, 2), got
-    g_eqkv = mm_tn(en, e_rows_grad).astype(BF)
-    g_e = [pieces(g_eqkv), pieces(mm_tn(pick, d_mkv).astype(BF))]
+        jobs=steps_of(moving) + [swap_job(d_in.astype(BF))],
+    )
+    (came,) = settle(moving, got)
+    dec_ingrad = joined(d_in, came)
     def rel_grad(dbv):
         own = lax.dot_general(
             onehot.astype(F32),
@@ -1311,64 +1632,31 @@
     tiny = tiny.reshape(-1, 128)
     if parts > 1:
         tiny = lax.psum(tiny, "part")
-    got = ship(
-        14,
-        planes,
-        step1(g_e)
-        + step3(g_eff)
-        + [turn_job(g) for g in g_ep]
-        + step4(g_d)
-        + step3(g_dp)
-        + step5(g_cp, proj_widths)
-        + [total_job("fsdp", tiny, planes), swap_job(e_in.astype(BF))],
-    )
-    enc_ingrad = joined(e_in, got.pop())
-    tiny = got.pop()
-    g_e, g_eff, g_ep = take(got, 2), take(got, 2), take(got, len(g_ep))
-    g_d, g_dp, o_cp = take(got, 1), take(got, len(g_dp)), got
-    got = ship(
-        15,
-        planes,
-        step2(g_e)
-        + step4(g_eff)
-        + step3(g_ep)
-        + step5(g_d, qkv_widths)
-        + step4(g_dp)
-        + [total_job("seq", tiny)],
-    )
-    tiny = got.pop()
-    g_e, g_eff, g_ep = take(got, 2), take(got, 2), take(got, len(g_ep))
-    o_d, g_dp = take(got, 1), got
-    got = ship(
-        16,
-        planes,
-        step3(g_e)
-        + step5(g_eff, ff_widths)
-        + step4(g_ep)
-        + step5(g_dp, proj_widths)
-        + [total_job("across", tiny)],
-    )
-    tiny = got.pop()
-    g_e, o_eff, g_ep, o_dp = take(got, 2), take(got, 2), take(got, len(g_ep)), got
-    got = ship(17, planes, step4(g_e) + step5(g_ep, proj_widths) + [total_job("core", tiny)])
-    tiny = got.pop()
-    g_e, o_ep = take(got, 2), got
-    o_e = ship(18, planes, step5(g_e, qkv_widths))
-
-    def proj_rows(got, g):
+    swapped = [swap_job(e_in.astype(BF))]
+    for number, axis in enumerate(("fsdp", "seq", "across", "core", None)):
+        if axis is None and not steps_of(moving):
+            break
+        total = [total_job(axis, tiny, planes if axis == "fsdp" else 2)] if axis else []
+        got = ship(14 + number, planes, total + swapped + steps_of(moving))
+        if axis:
+            tiny, *got = got
+        if swapped:
+            enc_ingrad = joined(e_in, got.pop(0))
+            swapped = []
+        settle(moving, got)
+
+    def proj_rows(k):
         if turned:
-            return got[0].reshape(-1, D)
-        full = lax.dynamic_update_slice_in_dim(jnp.zeros((D, D), BF), g, QC * tp, 0)
+            return k.value
+        full = lax.dynamic_update_slice_in_dim(jnp.zeros((D, D), BF), k.value, QC * tp, 0)
         full = lax.psum_scatter(full, "fsdp", scatter_dimension=0, tiled=True)
         return lax.psum(full.astype(F32), CTX)
 
-    o_eproj = proj_rows(o_ep, g_eproj)
-    o_dproj = proj_rows(o_dp, g_dproj)
-    o_cproj = proj_rows(o_cp, g_cproj)
-    o_dffin, o_dffout = o_dff
-    o_effin, o_effout = o_eff
-    o_cq, o_ckv = o_c
-    (o_dqkv,), (o_eqkv, o_table) = o_d, o_e
+    o_eproj, o_dproj, o_cproj = (proj_rows(k) for k in (k_eproj, k_dproj, k_cproj))
+    o_dffin, o_dffout, o_effin, o_effout, o_cq, o_ckv, o_dqkv, o_eqkv, o_table = (
+        k.value
+        for k in (k_dffin, k_dffout, k_effin, k_effout, k_cq, k_ckv, k_dqkv, k_eqkv, k_table)
+    )
     tiny = lax.dynamic_index_in_dim(tiny.reshape(planes, -1), plane, 0, keepdims=False)
     o_gains = [tiny[per * i : per * (i + 1)] for i in range(5)]
     o_rels = [

time: 684 us -> 585 us (0.86)
  matrix products: 70.4 us -> 22.9 us
  Pallas kernels: 535 us -> 492 us
  local copies, waits for them, and re-layouts: 50 us -> 41.5 us
    pallas_call x21 -> x20, Pallas kernels: 535 us -> 492 us  [call_with_jobs(): pl.pallas_call(body, out_shape=tuple(outs) + tuple((jax.ShapeDtypeStruct(...]
    dot_general x7 -> x1, matrix products: 23.2 us -> 1.88 us  [mm(): return jnp.dot(a, b, preferred_element_type=F32)]
    dot_general x5 -> x0, matrix products: 15 us -> none  [mm_nt(): lax.dot_general(a, b, (((1,), (1,)), ((), ())), preferred_element_type=F32)]
    dot_general x12 -> x6, matrix products: 29.1 us -> 17.9 us  [mm_tn(): lax.dot_general(a, b, (((0,), (0,)), ((), ())), preferred_element_type=F32)]
    unnamed x143 -> x94, local copies, waits for them, and re-layouts: 16.1 us -> 19.9 us
where the time goes in v4:
time: 585 us; the launch traced here: 580 us
  Pallas kernels  492 us (84%)
  local copies, waits for them, and re-layouts  41.5 us (7%)
  matrix products  22.9 us (4%)
  other arithmetic  22.4 us (4%)
    pallas_call x20, Pallas kernels, call_with_jobs(): pl.pallas_call(body, out_shape=tuple(outs) + tuple((jax.ShapeDtypeStruct(...  492 us
    unnamed x94, local copies, waits for them, and re-layouts  19.9 us
    dot_general x6, matrix products, mm_tn(): lax.dot_general(a, b, (((0,), (0,)), ((), ())), preferred_element_type=F32)  17.9 us

profile of v4, /device:TPU:0, one launch (start us, length us, event | category | flops | bytes accessed | tf_op | source)
XLA Modules:
  0.0 580.1 jit_solution(1588437432006393620)
XLA Ops:
  4.7 1.3 maximum_convert_fusion.refs_2_
  6.0 1.3 fusion.37
  8.0 0.9 fusion.40
  9.6 22.2 %ship.5 = (bf16[128,768]{1,0:T(8,128)(2,1)}, f32[4,5,192]{2,1,0:T(8,128)}, f32[4,2,8,12]{3,2,1,0:T(8,128)}, bf16[4,96,576]{2,1,0:T(8,128)(2,1)}, bf16[4,32,384]{...) custom-call(bf16[2,128,768]{2,1,0:T(8,128)(2,1)} %refs_0_.1, f32[5,192]{1,0:T(8,128)} %convert_element_type.49.refs_1_, ...), custom_call_target="tpu_custom_call" | custom-call | bytes 8388608 | tf_op jit(solution)/shard_map/ship/pallas_call | solution.py:473
  31.8 1.0 fusion.25
  32.8 0.8 pad_maximum_fusion.2.refs_0_.refs_2_.refs_4_
  34.4 0.8 pad_maximum_fusion.3.refs_0_.refs_2_.refs_4_
  36.5 18.6 %gather_norm.2 = (bf16[1024,768]{1,0:T(8,128)(2,1)}, bf16[4,2,96,576]{3,2,1,0:T(8,128)(2,1)}, bf16[4,2,32,384]{3,2,1,0:T(8,128)(2,1)}, bf16[4,96,576]{2,1,0:T(8,128)(2,1)}, bf16[192,768]{1,0:T(8,128)(2,1)}) custom-call(bf16[2,128,768]{2,1,0:T(8,128)(2,1)} %pad_maximum_fusion.3.refs_0_.refs_2_.refs_4_, f32[1,768]{1,0:T(1,128)} %reshape_squeeze.22.refs_1_.refs_3_, ...), custom_call_target="tpu_custom_call" | custom-call | flops 1000000 | bytes 8388608 | tf_op jit(solution)/shard_map/gather_norm/pallas_call | solution.py:473
  55.2 1.5 fusion.35
  57.5 1.9 convolution_convert_fusion.6.refs_7_.refs_15_
  59.4 1.0 copy.52.refs_8_.refs_10_.refs_5_
  62.2 32.7 %gather_norm.3 = (bf16[1024,768]{1,0:T(8,128)(2,1)}, bf16[4,2,96,576]{3,2,1,0:T(8,128)(2,1)}, bf16[4,96,768]{2,1,0:T(8,128)(2,1)}, bf16[192,768]{1,0:T(8,128)(2,...) custom-call(bf16[2,128,768]{2,1,0:T(8,128)(2,1)} %pad_maximum_fusion.2.refs_0_.refs_2_.refs, ...), custom_call_target="tpu_custom_call" | custom-call | flops 1000000 | bytes 8388608 | tf_op jit(solution)/shard_map/gather_norm/pallas_call | solution.py:473
  95.6 1.7 constant_dynamic-slice_fusion.1
  97.3 1.6 dynamic_slice.129.refs_6_
  98.9 1.0 fusion.39
  101.9 32.9 %stage.11 = (f32[2,128,768]{2,1,0:T(8,128)}, bf16[1024,768]{1,0:T(8,128)(2,1)}, bf16[4,2,96,768]{3,2,1,0:T(8,128)(2,1)}, bf16[4,96,768]{2,1,0:T(8,128)(2,1)}, bf...) custom-call(bf16[1024,192]{1,0:T(8,128)(2,1)} %get-tuple-element.189, ...), custom_call_target="tpu_custom_call" | custom-call | flops 2415919104 | bytes 8388608 | tf_op jit(solution)/shard_map/stage/pallas_call | solution.py:473
  136.2 27.3 %stage.12 = (f32[2,128,768]{2,1,0:T(8,128)}, bf16[1024,768]{1,0:T(8,128)(2,1)}, bf16[4,2,96,768]{3,2,1,0:T(8,128)(2,1)}, bf16[4,2,96,192]{3,2,1,0:T(8,128)(2,1)}...) custom-call(bf16[1024,192]{1,0:T(8,128)(2,1)} %get-tuple-element.196.refs_0_.refs_11_, ...), custom_call_target="tpu_custom_call" | custom-call | flops 2415919104 | bytes 8388608 | tf_op jit(solution)/shard_map/stage/pallas_call | solution.py:473
  163.6 30.6 %stage.13 = (bf16[2,128,768]{2,1,0:T(8,128)(2,1)}, bf16[1024,768]{1,0:T(8,128)(2,1)}, f32[1024,768]{1,0:T(8,128)}, bf16[1024,768]{1,0:T(8,128)(2,1)}, bf16[4,2,9...) custom-call(bf16[1024,768]{1,0:T(8,128)(2,1)} %get-tuple-element.194.refs_0_, ...), custom_call_target="tpu_custom_call" | custom-call | flops 2415919104 | bytes 8388608 | tf_op jit(solution)/shard_map/stage/pallas_call | solution.py:473
  194.2 17.6 %attend.2 = (bf16[4,2,96,768]{3,2,1,0:T(8,128)(2,1)}, bf16[1024,192]{1,0:T(8,128)(2,1)}, bf16[3,1024,1024]{2,1,0:T(8,128)(2,1)}, bf16[1024,192]{1,0:T(8,128)(2,1)}, bf16[1024,384]{1,0:T(8,128)(2,1)}) custom-call(bf16[4,96,768]{2,1,0:T(8,128)(2,1)} %get-tuple-element.205.refs_0_, bf16[1024,768]{1,0:T(8,128)(2,1)} %get-tuple-element.206.refs_1_.refs_7_, ...), custom_call_target="tpu_custom_call" | custom-call | flops 4000000000 | bytes 8388608 | tf_op jit(solution)/shard_map/attend/pallas_call | solution.py:473
  212.5 23.4 %stage.14 = (f32[2,128,768]{2,1,0:T(8,128)}, bf16[1024,768]{1,0:T(8,128)(2,1)}, bf16[128,768]{1,0:T(8,128)(2,1)}, bf16[128,768]{1,0:T(8,128)(2,1)}) custom-call(bf16[1024,192]{1,0:T(8,128)(2,1)} %get-tuple-element.210.refs_0_.refs_6_, bf16[192,768]{1,0:T(8,128)(2,1)} %get-tuple-element.211.refs_1_.refs_5_, ...), custom_call_target="tpu_custom_call" | custom-call | flops 2415919104 | bytes 8388608 | tf_op jit(solution)/shard_map/stage/pallas_call | solution.py:473
  236.0 1.0 fusion.21
  237.8 0.8 pad_maximum_fusion.5.refs_4_
  238.6 24.6 %stage.15 = (bf16[2,128,768]{2,1,0:T(8,128)(2,1)}, bf16[1024,768]{1,0:T(8,128)(2,1)}, f32[1024,768]{1,0:T(8,128)}, bf16[1024,768]{1,0:T(8,128)(2,1)}) custom-call(bf16[1024,768]{1,0:T(8,128)(2,1)} %get-tuple-element.214.refs_0_, bf16[768,768]{1,0:T(8,128)(2,1)} %bitcast.139, bf16[768,768]{1,0:T(8,128)(2,1)} %bitcast.141, ...), custom_call_target="tpu_custom_call" | custom-call | flops 2415919104 | bytes 8388608 | tf_op jit(solution)/shard_map/stage/pallas_call | solution.py:473
  263.2 4.3 convolution_convert_fusion.3
  267.6 27.5 %stage.16 = (f32[2,128,768]{2,1,0:T(8,128)}, bf16[1024,768]{1,0:T(8,128)(2,1)}, f32[1,768]{1,0:T(1,128)}, bf16[1024,768]{1,0:T(8,128)(2,1)}, bf16[4,96,768]{2,1,0:T(8,128)(2,1)}, /*index=5*/bf16[128,768]{1,0:T(8,128)(2,1)}) custom-call(bf16[1024,768]{1,0:T(8,128)(2,1)} %get-tuple-element.220.refs_0_, f32[1024,768]{1,0:T(8,128)} %get-tuple-element.221.refs_1_, ...), custom_call_target="tpu_custom_call" | custom-call | flops 2415919104 | bytes 8388608 | tf_op jit(solution)/shard_map/stage/pallas_call | solution.py:473
  295.1 1.1 fusion.17
  297.0 2.5 convolution_convert_fusion.2
  299.4 25.6 %attend.3 = (bf16[4,96,768]{2,1,0:T(8,128)(2,1)}, bf16[96,768]{1,0:T(8,128)(2,1)}, bf16[1024,192]{1,0:T(8,128)(2,1)}, bf16[1024,384]{1,0:T(8,128)(2,1)}, bf16[19...) custom-call(bf16[4,2,96,768]{3,2,1,0:T(8,128)(2,1)} %bitcast.134, ...), custom_call_target="tpu_custom_call" | custom-call | flops 4000000000 | bytes 8388608 | tf_op jit(solution)/shard_map/attend/pallas_call | solution.py:473
  325.1 0.8 pad_maximum_fusion.7.refs_2_
  325.9 28.2 %stage.17 = (f32[2,128,768]{2,1,0:T(8,128)}, bf16[1024,768]{1,0:T(8,128)(2,1)}, f32[1,768]{1,0:T(1,128)}, bf16[96,768]{1,0:T(8,128)(2,1)}, bf16[2,96,768]{2,1,0:...) custom-call(bf16[1024,192]{1,0:T(8,128)(2,1)} %get-tuple-element.232.refs_0_, ...), custom_call_target="tpu_custom_call" | custom-call | flops 2415919104 | bytes 8388608 | tf_op jit(solution)/shard_map/stage/pallas_call | solution.py:473
  354.1 33.8 %stage.18 = (f32[2,128,768]{2,1,0:T(8,128)}, bf16[1024,768]{1,0:T(8,128)(2,1)}, bf16[2,96,768]{2,1,0:T(8,128)(2,1)}, bf16[2,2,96,768]{3,2,1,0:T(8,128)(2,1)}, bf...) custom-call(bf16[1024,384]{1,0:T(8,128)(2,1)} %get-tuple-element.230, ...), custom_call_target="tpu_custom_call" | custom-call | flops 2415919104 | bytes 8388608 | tf_op jit(solution)/shard_map/stage/pallas_call | solution.py:473
  387.9 3.9 convolution_convert_fusion.1
  391.7 35.0 %stage.19 = (f32[2,128,768]{2,1,0:T(8,128)}, bf16[1024,768]{1,0:T(8,128)(2,1)}, f32[1,768]{1,0:T(1,128)}, bf16[1024,768]{1,0:T(8,128)(2,1)}, f32[768,768]{1,0:T(...) custom-call(bf16[1024,768]{1,0:T(8,128)(2,1)} %get-tuple-element.250, ...), custom_call_target="tpu_custom_call" | custom-call | flops 2415919104 | bytes 8388608 | tf_op jit(solution)/shard_map/stage/pallas_call | solution.py:473
  426.8 4.0 convolution_convert_fusion
  430.8 1.2 convolution_convert_fusion.4
  432.0 33.5 %stage.20 = (f32[2,128,768]{2,1,0:T(8,128)}, f32[1,768]{1,0:T(1,128)}, bf16[2,2,96,768]{3,2,1,0:T(8,128)(2,1)}, bf16[2,2,96,192]{3,2,1,0:T(8,128)(2,1)}, bf16[2,...) custom-call(bf16[1024,576]{1,0:T(8,128)(2,1)} %get-tuple-element.247, ...), custom_call_target="tpu_custom_call" | custom-call | flops 2415919104 | bytes 8388608 | tf_op jit(solution)/shard_map/stage/pallas_call | solution.py:473
  465.6 2.0 convolution_convert_fusion.5
  467.5 1.9 convert_element_type.60.refs_16_
  469.5 25.6 %stage.21 = (f32[2,128,768]{2,1,0:T(8,128)}, f32[1,768]{1,0:T(1,128)}, f32[192,3072]{1,0:T(8,128)}, f32[192,768]{1,0:T(8,128)}, f32[192,1536]{1,0:T(8,128)}, /*i...) custom-call(bf16[1024,576]{1,0:T(8,128)(2,1)} %get-tuple-element.270, ...), custom_call_target="tpu_custom_call" | custom-call | flops 2415919104 | bytes 8388608 | tf_op jit(solution)/shard_map/stage/pallas_call | solution.py:473
  496.3 1.0 fusion.5
  497.6 1.0 fusion.3
  499.7 1.9 convert_element_type.61.refs_1_
  501.6 21.3 %ship.6 = (f32[36,128]{1,0:T(8,128)}, bf16[128,768]{1,0:T(8,128)(2,1)}, f32[192,768]{1,0:T(8,128)}, bf16[2,2,96,576]{3,2,1,0:T(8,128)(2,1)}, bf16[2,48,384]{2,1,...) custom-call(f32[36,128]{1,0:T(8,128)} %reshape.212.refs_0_, ...), custom_call_target="tpu_custom_call" | custom-call | bytes 8388608 | tf_op jit(solution)/shard_map/ship/pallas_call | solution.py:473
  522.9 1.1 fusion.11
  524.0 0.9 pad_maximum_fusion
  525.0 0.9 pad_maximum_fusion.1
  525.9 14.9 %ship.7 = (f32[36,128]{1,0:T(8,128)}, f32[192,2304]{1,0:T(8,128)}, bf16[2,2,48,384]{3,2,1,0:T(8,128)(2,1)}, f32[768,768]{1,0:T(8,128)}, bf16[2,2,96,768]{3,2,1,0...) custom-call(f32[36,128]{1,0:T(8,128)} %get-tuple-element.302.refs_0_, ...), custom_call_target="tpu_custom_call" | custom-call | bytes 8388608 | tf_op jit(solution)/shard_map/ship/pallas_call | solution.py:473
  540.8 12.1 %ship.8 = (f32[36,128]{1,0:T(8,128)}, f32[192,768]{1,0:T(8,128)}, f32[192,3072]{1,0:T(8,128)}, bf16[2,2,48,384]{3,2,1,0:T(8,128)(2,1)}, bf16[2,2,96,576]{3,2,1,0...) custom-call(f32[36,128]{1,0:T(8,128)} %get-tuple-element.310.refs_0_, bf16[2,2,48,384]{3,2,1,0:T(8,128)(2,1)} %get-tuple-element.311.refs_1_, ...), custom_call_target="tpu_custom_call" | custom-call | bytes 8388608 | tf_op jit(solution)/shard_map/ship/pallas_call | solution.py:473
  552.9 4.5 ship.9
  560.2 1.8 copy.83
  562.0 2.9 copy.84
  564.9 0.8 copy.85
  565.7 1.4 copy.86
  567.1 1.1 copy-done.4
  568.2 1.4 copy.87
  569.6 0.9 copy-done.6
  570.6 1.2 copy.88
  572.0 0.8 copy.89
  572.8 0.8 copy.90
  573.7 1.0 copy.91
  574.7 0.8 copy.92
  576.0 1.4 copy.93
  577.4 1.1 copy-done.2
  578.5 1.4 copy.94
  (136 shorter events, 22.7 us)
Async XLA Ops:
  0.7 56.8 %copy-start = (s32[2,8,20]{2,1,0:T(8,128)S(1)}, s32[2,8,20]{2,1,0:T(8,128)}, u32[]{:S(2)}) copy-start(s32[2,8,20]{2,1,0:T(8,128)} %param.30) | copy-start | bytes 3844
  0.7 31.1 %copy-start.12 = (bf16[2,128,768]{2,1,0:T(8,128)(2,1)S(1)}, bf16[2,128,768]{2,1,0:T(8,128)(2,1)}, u32[]{:S(2)}) copy-start(bf16[2,128,768]{2,1,0:T(8,128)(2,1)} %refs_5_.3) | copy-start | bytes 1179652
  7.3 27.1 %copy-start.13 = (bf16[2,128,768]{2,1,0:T(8,128)(2,1)S(1)}, bf16[2,128,768]{2,1,0:T(8,128)(2,1)}, u32[]{:S(2)}) copy-start(bf16[2,128,768]{2,1,0:T(8,128)(2,1)} %refs_0_.1) | copy-start | bytes 1179652
  31.8 1.8 copy-start.27
  31.8 2.6 copy-start.21
  35.8 23.6 %copy-start.26 = (s32[8,1,128]{2,1,0:T(1,128)S(1)}, s32[8,1,128]{2,1,0:T(1,128)}, u32[]{:S(2)}) copy-start(s32[8,1,128]{2,1,0:T(1,128)} %get-tuple-element.187) | copy-start | bytes 12292
  36.5 23.9 %copy-start.33 = (s32[1,256]{1,0:T(1,128)S(1)}, s32[1,256]{1,0:T(1,128)}, u32[]{:S(2)}) copy-start(s32[1,256]{1,0:T(1,128)} %constant.288) | copy-start | bytes 3076
  36.5 24.5 %copy-start.28 = (f32[4,2,8,12]{3,2,1,0:T(8,128)S(1)}, f32[4,2,8,12]{3,2,1,0:T(8,128)}, u32[]{:S(2)}) copy-start(f32[4,2,8,12]{3,2,1,0:T(8,128)} %get-tuple-element.188) | copy-start | bytes 9220
  36.5 24.5 %copy-start.37 = (s32[2048]{0:T(1024)S(1)}, s32[2048]{0:T(1024)}, u32[]{:S(2)}) copy-start(s32[2048]{0:T(1024)} %param.31) | copy-start | bytes 24580
  212.5 23.5 %copy-start.25 = (bf16[2,128,768]{2,1,0:T(8,128)(2,1)S(1)}, bf16[2,128,768]{2,1,0:T(8,128)(2,1)}, u32[]{:S(2)}) copy-start(bf16[2,128,768]{2,1,0:T(8,128)(2,1)} %get-tuple-element.204.refs_4_) | copy-start | bytes 1179652
  235.9 1.8 copy-start.22
  235.9 1.8 copy-start.23
  267.5 27.5 %copy-start.11 = (bf16[2,128,768]{2,1,0:T(8,128)(2,1)S(1)}, bf16[2,128,768]{2,1,0:T(8,128)(2,1)}, u32[]{:S(2)}) copy-start(bf16[2,128,768]{2,1,0:T(8,128)(2,1)} %get-tuple-element.219.refs_8_) | copy-start | bytes 1179652
  267.6 29.4 %copy-start.40 = (bf16[1024,768]{1,0:T(8,128)(2,1)S(1)}, bf16[1024,768]{1,0:T(8,128)(2,1)}, u32[]{:S(2)}) copy-start(bf16[1024,768]{1,0:T(8,128)(2,1)} %get-tuple-element.214.refs_0_) | copy-start | bytes 4718596
  295.1 1.9 copy-start.34
  299.4 25.6 %copy-start.20 = (bf16[128,768]{1,0:T(8,128)(2,1)S(1)}, bf16[128,768]{1,0:T(8,128)(2,1)}, u32[]{:S(2)}) copy-start(bf16[128,768]{1,0:T(8,128)(2,1)} %get-tuple-element.231) | copy-start | bytes 589828
  299.4 25.6 %copy-start.24 = (bf16[2,128,768]{2,1,0:T(8,128)(2,1)S(1)}, bf16[2,128,768]{2,1,0:T(8,128)(2,1)}, u32[]{:S(2)}) copy-start(bf16[2,128,768]{2,1,0:T(8,128)(2,1)} %refs_5_.5) | copy-start | bytes 1179652
  354.1 33.8 %copy-start.39 = (bf16[1024,768]{1,0:T(8,128)(2,1)S(1)}, bf16[1024,768]{1,0:T(8,128)(2,1)}, u32[]{:S(2)}) copy-start(bf16[1024,768]{1,0:T(8,128)(2,1)} %get-tuple-element.259) | copy-start | bytes 4718596
  391.7 35.0 %copy-start.38 = (bf16[1024,768]{1,0:T(8,128)(2,1)S(1)}, bf16[1024,768]{1,0:T(8,128)(2,1)}, u32[]{:S(2)}) copy-start(bf16[1024,768]{1,0:T(8,128)(2,1)} %get-tuple-element.194.refs_0_) | copy-start | bytes 4718596
  426.8 4.0 copy-start.9
  426.8 4.0 copy-start.18
  469.5 26.5 %copy-start.31 = (f32[1,768]{1,0:T(1,128)S(1)}, f32[1,768]{1,0:T(1,128)}, u32[]{:S(2)}) copy-start(f32[1,768]{1,0:T(1,128)} %get-tuple-element.286) | copy-start | bytes 9220
  469.5 26.6 %copy-start.32 = (f32[1,768]{1,0:T(1,128)S(1)}, f32[1,768]{1,0:T(1,128)}, u32[]{:S(2)}) copy-start(f32[1,768]{1,0:T(1,128)} %get-tuple-element.287) | copy-start | bytes 9220
  469.5 26.6 %copy-start.30 = (f32[1,768]{1,0:T(1,128)S(1)}, f32[1,768]{1,0:T(1,128)}, u32[]{:S(2)}) copy-start(f32[1,768]{1,0:T(1,128)} %get-tuple-element.288) | copy-start | bytes 9220
  469.5 26.7 %copy-start.29 = (f32[1,768]{1,0:T(1,128)S(1)}, f32[1,768]{1,0:T(1,128)}, u32[]{:S(2)}) copy-start(f32[1,768]{1,0:T(1,128)} %get-tuple-element.289) | copy-start | bytes 9220
  469.5 26.8 %copy-start.36 = (f32[3,1,2048]{2,1,0:T(1,128)S(1)}, f32[3,1,2048]{2,1,0:T(1,128)}, u32[]{:S(2)}) copy-start(f32[3,1,2048]{2,1,0:T(1,128)} %get-tuple-element.290) | copy-start | bytes 73732
  469.5 28.2 %copy-start.35 = (f32[3,1,2048]{2,1,0:T(1,128)S(1)}, f32[3,1,2048]{2,1,0:T(1,128)}, u32[]{:S(2)}) copy-start(f32[3,1,2048]{2,1,0:T(1,128)} %get-tuple-element.291) | copy-start | bytes 73732
  499.1 23.8 %copy-start.8 = (f32[2,128,768]{2,1,0:T(8,128)S(1)}, f32[2,128,768]{2,1,0:T(8,128)}, u32[]{:S(2)}) copy-start(f32[2,128,768]{2,1,0:T(8,128)} %get-tuple-element.284) | copy-start | bytes 2359300
  522.9 2.0 copy-start.7
  522.9 2.0 copy-start.19
  562.0 3.0 copy-start.17
  562.0 3.8 copy-start.5
  565.7 2.5 copy-start.4
  568.2 2.3 copy-start.6
  570.6 1.4 copy-start.16
  570.6 2.3 copy-start.14
  572.0 1.6 copy-start.10
  572.8 1.8 copy-start.15
  573.7 2.3 copy-start.3
  576.0 2.5 copy-start.2
  576.0 3.9 copy-start.1

commit v5 on v4

--- a/solution.py
+++ b/solution.py
@@ -144,21 +144,13 @@
     return Job("ctx", 0, 0, True, src, (2 * TP,) + src.shape[1:], None)
 
 
-def last_job(src, width):
-    return gather_job("core", src, 2, 2)._replace(finish=("layout", width))
+def spread_job(src, add=False):
+    return Job("all", None, None, True, src, (2, 2, 2) + src.shape, "sum3" if add else None)
 
 
 def result_of(job):
-    if job.finish == "sum":
-        return job.shape[1:], job.src.dtype
-    if isinstance(job.finish, tuple):
-        seqs, halves, cores, rows, cols = job.shape
-        if job.finish[1] < 0:
-            return (halves * cores * rows, seqs * cols), F32
-        if job.finish[1]:
-            return (seqs * rows, halves * cores * cols), F32
-        return (seqs * halves * cores * rows, cols), F32
-    return job.shape, job.src.dtype
+    skip = {"sum": 1, "sum3": 3}.get(job.finish, 0)
+    return job.shape[skip:], job.src.dtype
 
 
 def entry(ref, axis, index):
@@ -194,6 +186,8 @@
                     shapes.append(pltpu.VMEM(job.shape, dtype))
                 else:
                     shapes.append(pltpu.VMEM(*result_of(job)))
+            elif job.axis == "all":
+                shapes.append(pltpu.VMEM(job.src.shape, dtype))
             elif job.local:
                 drop = job.dst_axis
                 own = job.shape if drop is None else job.shape[:drop] + job.shape[drop + 1 :]
@@ -206,7 +200,7 @@
 
     @staticmethod
     def n_peers(job, planes):
-        return {"fsdp": planes - 1, "ctx": 2 * TP - 1}.get(job.axis, 1)
+        return {"fsdp": planes - 1, "ctx": 2 * TP - 1, "all": 2 * TP - 1}.get(job.axis, 1)
 
     def coord(self, axis):
         half = self.tp // 2
@@ -242,7 +236,10 @@
             yield other, {"tp": to}, other
 
     def signal(self, always=("core", "across")):
-        axes = list(always) + sorted({job.axis for job in self.jobs} - set(always))
+        wanted = {job.axis for job in self.jobs}
+        if "all" in wanted:
+            wanted = (wanted - {"all"}) | {"seq", "across", "core"}
+        axes = list(always) + sorted(wanted - set(always))
         barrier = pltpu.get_barrier_semaphore()
         self.expected, self.turns = 0, "turn" in axes
         for axis in axes:
@@ -281,6 +278,9 @@
     def each(self, act_remote, act_local):
         base = 0
         for n, (job, src, dst) in enumerate(zip(self.jobs, self.srcs, self.dsts)):
+            if job.axis == "all":
+                base += 2 * self.n_peers(job, self.planes) + 2
+                continue
             mine = self.coord(job.axis)
             peers = list(self.peers(job.axis))
             for i, (to, device, source) in enumerate(peers):
@@ -323,7 +323,69 @@
             base += 2 * len(peers) + 2
         return base
 
+    def spreads(self):
+        s, x, c = self.coord("seq"), self.coord("across"), self.coord("core")
+        seq, across, core = (next(self.peers(axis))[1] for axis in ("seq", "across", "core"))
+        moves = [
+            ((s, x, c), across, (s, 1 - x, c)),
+            ((s, x, c), seq, (1 - s, x, c)),
+            ((s, x, c), core, (s, x, 1 - c)),
+            ((s, 1 - x, c), seq, (1 - s, 1 - x, c)),
+            ((s, 1 - x, c), core, (s, 1 - x, 1 - c)),
+            ((1 - s, x, c), core, (1 - s, x, 1 - c)),
+            ((1 - s, 1 - x, c), core, (1 - s, 1 - x, 1 - c)),
+        ]
+        base = 0
+        for job, src, dst, bounce in zip(self.jobs, self.srcs, self.dsts, self.bounce):
+            if job.axis == "all":
+
+                def copy(k, arrives=False, src=src, dst=dst, base=base):
+                    what, device, other = moves[k]
+                    return pltpu.make_async_remote_copy(
+                        src_ref=src if k < 3 else dst.at[what],
+                        dst_ref=dst.at[other if arrives else what],
+                        send_sem=self.sems.at[base + 2 * k],
+                        recv_sem=self.sems.at[base + 2 * k + 1],
+                        device_id=device,
+                        device_id_type=MESH_ID,
+                    )
+
+                own = dst.at[s, x, c]
+                legs = [(src, own)] if bounce is None else [(src, bounce), (bounce, own)]
+                legs = [
+                    pltpu.make_async_copy(*leg, self.sems.at[base + 14 + n])
+                    for n, leg in enumerate(legs)
+                ]
+                yield copy, legs
+            base += 2 * self.n_peers(job, self.planes) + 2
+
+    def start_spreads(self):
+        for copy, legs in self.spreads():
+            for k in range(3):
+                copy(k).start()
+            legs[0].start()
+
+    def finish_spreads(self):
+        jobs = list(self.spreads())
+        for copy, legs in jobs:
+            if len(legs) > 1:
+                legs[0].wait()
+                legs[1].start()
+        for first, then in ((0, (3, 4)), (1, (5,)), (3, (6,))):
+            for copy, legs in jobs:
+                copy(first, True).wait_recv()
+                for k in then:
+                    copy(k).start()
+        for copy, legs in jobs:
+            for k in (2, 4, 5, 6):
+                copy(k, True).wait_recv()
+            for k in range(7):
+                copy(k).wait_send()
+            legs[-1].wait()
+
     def start(self):
+        if any(job.axis == "all" for job in self.jobs):
+            self.start_spreads()
         self.each(
             lambda copy_into, mine, source: copy_into(mine).start(),
             lambda legs, sem: pltpu.make_async_copy(*legs[0], sem).start(),
@@ -339,6 +401,8 @@
             copy_into(source).wait_recv()
             copy_into(mine).wait_send()
 
+        if any(job.axis == "all" for job in self.jobs):
+            self.finish_spreads()
         self.each(lambda *_: None, turn_round)
         self.each(remote, lambda legs, sem: pltpu.make_async_copy(*legs[-1], sem).wait())
         stores, base = [], 0
@@ -355,42 +419,81 @@
                 def _(i):
                     bounce[i] = (bounce[i].astype(F32) + dst[i].astype(F32)).astype(bounce.dtype)
 
-            elif job.finish == "sum":
-                total = dst[0].astype(F32)
-                for i in range(1, dst.shape[0]):
-                    total = total + dst[i].astype(F32)
+            else:
+                pieces = [dst.at[i] for i in range(dst.shape[0])]
+                if job.finish == "sum3":
+                    pieces = [dst.at[i, j, k] for i in range(2) for j in range(2) for k in range(2)]
+                total = pieces[0][...].astype(F32)
+                for piece in pieces[1:]:
+                    total = total + piece[...].astype(F32)
                 made[...] = total.astype(made.dtype)
-            else:
-                self.lay_out(dst, made, job.finish[1])
             store = pltpu.make_async_copy(made, out, self.sems.at[base - 1])
             store.start()
             stores.append(store)
         for store in stores:
             store.wait()
 
-    @staticmethod
-    def lay_out(src, dst, width):
-        seqs, halves, cores, rows, cols = src.shape
+
+def lay_out(src, dst, width):
+    seqs, halves, cores, rows, cols = src.shape
+    if width < 0:
+        for i in range(seqs):
+            for q in range(TP):
+                block = slice(i * cols, (i + 1) * cols)
+                dst[q * rows : (q + 1) * rows, block] = src[i, q // 2, q % 2].astype(F32)
+        return
+
+    @pl.loop(0, seqs)
+    def _(i):
+        if not width:
+            for q in range(TP):
+                at = pl.multiple_of((q * seqs + i) * rows, rows)
+                dst[pl.ds(at, rows)] = src[i, q // 2, q % 2].astype(F32)
+        else:
+            at = pl.multiple_of(i * rows, rows)
+            for n in range(cols // width):
+                span = slice(n * width, (n + 1) * width)
+                parts = [src[i, q // 2, q % 2, :, span].astype(F32) for q in range(TP)]
+                block = slice(n * width * TP, (n + 1) * width * TP)
+                dst[pl.ds(at, rows), block] = jnp.concatenate(parts, axis=1)
+
+
+def laid_out(pieces, widths):
+    shapes = []
+    for p, width in zip(pieces, widths):
+        seqs, halves, cores, rows, cols = p.shape
         if width < 0:
-            for i in range(seqs):
-                for q in range(TP):
-                    block = slice(i * cols, (i + 1) * cols)
-                    dst[q * rows : (q + 1) * rows, block] = src[i, q // 2, q % 2].astype(F32)
-            return
-
-        @pl.loop(0, seqs)
-        def _(i):
-            if not width:
-                for q in range(TP):
-                    at = pl.multiple_of((q * seqs + i) * rows, rows)
-                    dst[pl.ds(at, rows)] = src[i, q // 2, q % 2].astype(F32)
-            else:
-                at = pl.multiple_of(i * rows, rows)
-                for n in range(cols // width):
-                    span = slice(n * width, (n + 1) * width)
-                    parts = [src[i, q // 2, q % 2, :, span].astype(F32) for q in range(TP)]
-                    block = slice(n * width * TP, (n + 1) * width * TP)
-                    dst[pl.ds(at, rows), block] = jnp.concatenate(parts, axis=1)
+            shapes.append((halves * cores * rows, seqs * cols))
+        elif width:
+            shapes.append((seqs * rows, halves * cores * cols))
+        else:
+            shapes.append((seqs * halves * cores * rows, cols))
+    n = len(pieces)
+
+    def body(*refs):
+        srcs, outs, got, made, sems = refs[:n], refs[n : 2 * n], refs[2 * n : 3 * n], refs[3 * n : 4 * n], refs[4 * n]
+        loads = [pltpu.make_async_copy(srcs[i], got[i], sems.at[0, i]) for i in range(n)]
+        stores = [pltpu.make_async_copy(made[i], outs[i], sems.at[1, i]) for i in range(n)]
+        for load in loads:
+            load.start()
+        for i in range(n):
+            loads[i].wait()
+            lay_out(got[i], made[i], widths[i])
+            stores[i].start()
+        for store in stores:
+            store.wait()
+
+    return pl.pallas_call(
+        body,
+        out_shape=tuple(jax.ShapeDtypeStruct(shape, F32) for shape in shapes),
+        in_specs=[HBM_SPEC] * n,
+        out_specs=(HBM_SPEC,) * n,
+        scratch_shapes=[pltpu.VMEM(p.shape, p.dtype) for p in pieces]
+        + [pltpu.VMEM(shape, F32) for shape in shapes]
+        + [pltpu.SemaphoreType.DMA((2, n))],
+        compiler_params=pltpu.CompilerParams(vmem_limit_bytes=VMEM_LIMIT),
+        name="lay_out",
+    )(*pieces)
 
 
 HBM_SPEC = pl.BlockSpec(memory_space=pltpu.HBM)
@@ -520,33 +623,37 @@
     return call_with_jobs(kernel, number, planes, jobs, [], [], [], "ship", 0)[1]
 
 
-def gather_norm(number, planes, x, gain, jobs, filler=None):
-    chunk = x.shape[1]
-
-    def kernel(shipper, ins, outs, scratch, filler):
-        shipper.signal()
-        x_ref, gain_ref = (v.get() for v in ins)
-        shipper.met()
-        shipper.start()
-        g = Gatherer(outs[0], scratch[0], scratch[1], chunk, group_ids())
+class GatherNormed:
+    by_rows = ()
+
+    def __init__(self, x, gain):
+        self.chunk = x.shape[1]
+        self.operands, self.cost = [x, gain], 10**6
+        self.outs = [jax.ShapeDtypeStruct((2 * TP * self.chunk, D), BF)]
+        self.scratch = [pltpu.VMEM((2, self.chunk, D), BF), pltpu.SemaphoreType.DMA((7, 2))]
+
+    def bind(self, ins, outs, scratch):
+        self.x, self.gain = ins
+        self.g = Gatherer(outs[0], scratch[0], scratch[1], self.chunk, group_ids())
+
+    def load(self):
+        pass
+
+    def first(self, met):
+        x_ref, gain_ref = self.x.get(), self.gain.get()
+        met()
         for j in range(2):
-            g.put(j, normed(x_ref[j].astype(F32), gain_ref[...]).astype(BF))
-        filler.prefetch()
-        filler.begin()
-        filler.advance(0.4)
+            self.g.put(j, normed(x_ref[j].astype(F32), gain_ref[...]).astype(BF))
+
+    def second(self, between):
+        between()
+
+    def third(self):
         for j in range(2):
-            g.forward(j)
-        filler.advance(1.0)
-        filler.end()
-        g.finish()
-        shipper.finish()
-
-    outs = [jax.ShapeDtypeStruct((2 * TP * chunk, D), BF)]
-    scratch = [pltpu.VMEM((2, chunk, D), BF), pltpu.SemaphoreType.DMA((7, 2))]
-    got, moved, made = call_with_jobs(
-        kernel, number, planes, jobs, [x, gain], outs, scratch, "gather_norm", 10**6, filler
-    )
-    return got[0], moved, made
+            self.g.forward(j)
+
+    def last(self):
+        self.g.finish()
 
 
 GELU_C = float(np.sqrt(2.0 / np.pi))
@@ -663,29 +770,86 @@
         self.write(0, self.ref, self.out, slot, pair)
 
 
-def stage_kernel(conf, shipper, ins, outs, scratch, filler):
-    chunk, maker, flip, back, gather = conf
-    made_outs = [outs.pop() for _ in range(maker.n_outs)][::-1]
-    made_scratch = [scratch.pop() for _ in range(maker.n_scratch)][::-1]
-    left = maker(ins, made_outs, made_scratch, chunk)
-    w_in = ins.pop(0)
-    resid_in = ins.pop(0)
-    gain_in = ins.pop(0) if (back or gather == "norm") else None
-    x_in = ins.pop(0) if back else None
-    given_in = ins.pop(0) if gather == "given" else None
-    y_out = outs.pop(0)
-    gath_ref = outs.pop(0) if gather else None
-    dgain_out = outs.pop(0) if back else None
-    s_far, r_far, s_x, r_x, s_core, r_core, keep, own, y_ref, sems = scratch[:10]
-    scratch = scratch[10:]
-    g_stage, g_sems = (scratch.pop(0), scratch.pop(0)) if gather else (None, None)
-    dgain_ref = scratch.pop(0) if back else None
-    ids = group_ids()
-    me, core, across, far = ids
-    slots = [0, 1, 2, 3]
-
-    def partial(owner, store):
-        slot = slots.pop(0)
+class Stage:
+    def __init__(
+        self,
+        left,
+        weight,
+        resid,
+        *,
+        flip=False,
+        maker=Rows,
+        back=None,
+        gather=None,
+        gain=None,
+        given=None,
+        dtype=F32,
+        low=False,
+    ):
+        self.maker, self.flip, self.back, self.gather, self.low = maker, flip, bool(back), gather, low
+        self.chunk = chunk = resid.shape[1]
+        self.operands = list(left) + [weight, resid]
+        self.cost = 4 * left[0].shape[0] * D * D
+        self.by_rows = {Rows: (0,), FeedForward: (0,), FeedForwardBack: (0, 1)}[maker]
+        if back:
+            self.operands += [back[1], back[0]]
+        elif gather == "norm":
+            self.operands.append(gain)
+        if gather == "given":
+            self.operands.append(given)
+        self.outs = [jax.ShapeDtypeStruct((2, chunk, D), dtype)]
+        if gather:
+            self.outs.append(jax.ShapeDtypeStruct((2 * TP * chunk, D), BF))
+        if back:
+            self.outs.append(jax.ShapeDtypeStruct((1, D), F32))
+        half = pltpu.VMEM((2, chunk, D), BF)
+        full = pltpu.VMEM((2, chunk, D), F32)
+        self.scratch = [half] * 6 + [full] * 2
+        self.scratch += [pltpu.VMEM((2, chunk, D), dtype), pltpu.SemaphoreType.DMA((13,))]
+        if gather:
+            self.scratch += [half, pltpu.SemaphoreType.DMA((7, 2))]
+        if back:
+            self.scratch.append(pltpu.VMEM((1, D), F32))
+        if low:
+            self.outs.append(jax.ShapeDtypeStruct((2, chunk, D), BF))
+            self.scratch.append(half)
+        if maker is not Rows:
+            width = weight.shape[1] if flip else weight.shape[0]
+            more, more_scratch = maker.extras(2 * TP * chunk, width)
+            self.outs += more
+            self.scratch += more_scratch
+
+    def bind(self, ins, outs, scratch):
+        maker = self.maker
+        made_outs = [outs.pop() for _ in range(maker.n_outs)][::-1]
+        made_scratch = [scratch.pop() for _ in range(maker.n_scratch)][::-1]
+        self.left = maker(ins, made_outs, made_scratch, self.chunk)
+        self.w_in, self.resid_in = ins.pop(0), ins.pop(0)
+        self.gain_in = ins.pop(0) if (self.back or self.gather == "norm") else None
+        self.x_in = ins.pop(0) if self.back else None
+        self.given_in = ins.pop(0) if self.gather == "given" else None
+        self.y_out = outs.pop(0)
+        gath_ref = outs.pop(0) if self.gather else None
+        self.dgain_out = outs.pop(0) if self.back else None
+        self.low_out = outs.pop(0) if self.low else None
+        self.s_far, self.r_far, self.s_x, self.r_x, self.s_core, self.r_core = scratch[:6]
+        self.keep, self.own, self.y_ref, self.sems = scratch[6:10]
+        scratch = scratch[10:]
+        self.ids = group_ids()
+        self.g = None
+        if self.gather:
+            self.g = Gatherer(gath_ref, scratch.pop(0), scratch.pop(0), self.chunk, self.ids)
+        self.dgain_ref = scratch.pop(0) if self.back else None
+        self.low_ref = scratch.pop(0) if self.low else None
+        self.slots, self.stores = [0, 1, 2, 3], []
+
+    def load(self):
+        me, core, across, far = self.ids
+        for rows in self.left.by_rows:
+            rows.start((far, across, core, me))
+
+    def partial(self, owner, ref):
+        slot, chunk, left = self.slots.pop(0), self.chunk, self.left
         for rows in left.by_rows:
             rows.wait(owner, slot)
         pair = [
@@ -697,167 +861,143 @@
         @pl.loop(0, D // 256)
         def _(n):
             cols = pl.ds(pl.multiple_of(n * 256, 256), 256)
-            total = mm_nt(a, w_ref[cols, :]) if flip else mm(a, w_ref[:, cols])
+            total = mm_nt(a, self.w_ref[cols, :]) if self.flip else mm(a, self.w_ref[:, cols])
             for j in range(2):
-                store(j, cols, total[j * chunk : (j + 1) * chunk])
-
-    def into(ref):
-        def store(j, cols, value):
-            ref[j, :, cols] = value.astype(ref.dtype)
-
-        return store
-
-    order = (far, across, core, me)
-    for rows in left.by_rows:
-        rows.start(order)
-    shipper.signal()
-    left.prepare()
-    w_ref = w_in.get()
-    partial(far, into(s_far))
-    shipper.met()
-    c_far = send(s_far, r_far, sems.at[0], sems.at[1], core)
-    c_far.start()
-    shipper.start()
-    g = Gatherer(gath_ref, g_stage, g_sems, chunk, ids) if gather else None
-    if gather == "given":
-        given_ref = given_in.get()
+                ref[j, :, cols] = total[j * chunk : (j + 1) * chunk].astype(ref.dtype)
+
+    def first(self, met):
+        me, core, across, far = self.ids
+        sems = self.sems
+        self.left.prepare()
+        self.w_ref = self.w_in.get()
+        self.partial(far, self.s_far)
+        met()
+        self.c_far = send(self.s_far, self.r_far, sems.at[0], sems.at[1], core)
+        self.c_far.start()
+        if self.gather == "given":
+            given_ref = self.given_in.get()
+            for j in range(2):
+                self.g.put(j, given_ref[j])
+        self.partial(across, self.keep)
+        self.c_far.wait_recv()
+        self.c_x = []
         for j in range(2):
-            g.put(j, given_ref[j])
-    partial(across, into(keep))
-    filler.prefetch()
-    c_far.wait_recv()
-    c_x = []
-    for j in range(2):
-        s_x[j] = (keep[j] + r_far[j].astype(F32)).astype(BF)
-        c_x.append(send(s_x.at[j], r_x.at[j], sems.at[2 + j], sems.at[4 + j], across))
-        c_x[j].start()
-    partial(core, into(s_core))
-    c_core = send(s_core, r_core, sems.at[6], sems.at[7], core)
-    c_core.start()
-    partial(me, into(own))
-    c_core.wait_recv()
-    filler.begin()
-    filler.advance(SHARE[0])
-    resid_ref = resid_in.get()
-    x_ref = x_in.get() if back else None
-    gains = gain_in.get()[...] if gain_in else None
-    if gather == "given":
+            self.s_x[j] = (self.keep[j] + self.r_far[j].astype(F32)).astype(BF)
+            copy = send(self.s_x.at[j], self.r_x.at[j], sems.at[2 + j], sems.at[4 + j], across)
+            copy.start()
+            self.c_x.append(copy)
+        self.partial(core, self.s_core)
+        self.c_core = send(self.s_core, self.r_core, sems.at[6], sems.at[7], core)
+        self.c_core.start()
+        self.partial(me, self.own)
+
+    def keep_out(self, src, dst, sem):
+        copy = pltpu.make_async_copy(src, dst, self.sems.at[sem])
+        copy.start()
+        self.stores.append(copy)
+
+    def second(self, between):
+        self.c_core.wait_recv()
+        resid_ref = self.resid_in.get()
+        x_ref = self.x_in.get() if self.back else None
+        gains = self.gain_in.get()[...] if self.gain_in else None
+        if self.gather == "given":
+            for j in range(2):
+                self.g.forward(j)
         for j in range(2):
-            g.forward(j)
-    stores = []
-
-    def keep_out(src, dst, sem):
-        copy = pltpu.make_async_copy(src, dst, sems.at[sem])
-        copy.start()
-        stores.append(copy)
-
-    for j in range(2):
-        c_x[j].wait_recv()
-        if j == 1:
-            filler.advance(SHARE[1])
-        total = own[j] + r_core[j].astype(F32) + r_x[j].astype(F32)
-        if back:
-            x = x_ref[j].astype(F32)
-            r = lax.rsqrt(jnp.mean(x * x, axis=-1, keepdims=True) + EPS)
-            scaled = total * gains
-            inner = jnp.mean(scaled * x, axis=-1, keepdims=True)
-            y = resid_ref[j].astype(F32) + r * scaled - x * (r * r * r * inner)
-            dgain = jnp.sum(total * x * r, axis=0, keepdims=True)
-            if j == 0:
-                dgain_ref[...] = dgain
+            self.c_x[j].wait_recv()
+            if j == 1:
+                between()
+            total = self.own[j] + self.r_core[j].astype(F32) + self.r_x[j].astype(F32)
+            if self.back:
+                x = x_ref[j].astype(F32)
+                r = lax.rsqrt(jnp.mean(x * x, axis=-1, keepdims=True) + EPS)
+                scaled = total * gains
+                inner = jnp.mean(scaled * x, axis=-1, keepdims=True)
+                y = resid_ref[j].astype(F32) + r * scaled - x * (r * r * r * inner)
+                dgain = jnp.sum(total * x * r, axis=0, keepdims=True)
+                if j == 0:
+                    self.dgain_ref[...] = dgain
+                else:
+                    self.dgain_ref[...] += dgain
             else:
-                dgain_ref[...] += dgain
-        else:
-            y = resid_ref[j].astype(F32) + total
-        y_ref[j] = y.astype(y_ref.dtype)
-        if gather == "norm":
-            g.put(j, normed(y, gains).astype(BF))
-        elif gather == "low":
-            g.put(j, y.astype(BF))
-        keep_out(y_ref.at[j], y_out.at[j], 8 + j)
-    if back:
-        keep_out(dgain_ref, dgain_out, 10)
-    if gather in ("norm", "low"):
+                y = resid_ref[j].astype(F32) + total
+            if self.gather == "norm":
+                self.g.put(j, normed(y, gains).astype(BF))
+            elif self.gather == "low":
+                self.g.put(j, y.astype(BF))
+            self.y_ref[j] = y.astype(self.y_ref.dtype)
+            self.keep_out(self.y_ref.at[j], self.y_out.at[j], 8 + j)
+            if self.low:
+                self.low_ref[j] = y.astype(BF)
+                self.keep_out(self.low_ref.at[j], self.low_out.at[j], 11 + j)
+        if self.back:
+            self.keep_out(self.dgain_ref, self.dgain_out, 10)
+
+    def third(self):
+        if self.gather in ("norm", "low"):
+            for j in range(2):
+                self.g.forward(j)
+
+    def last(self):
+        if self.gather:
+            self.g.finish()
+        for copy in [self.c_far, self.c_core] + self.c_x:
+            copy.wait_send()
+        for copy in self.stores:
+            copy.wait()
+        self.left.finish()
+
+
+def stage(number, planes, stages, jobs=(), filler=None):
+    operands = [v for st in stages for v in st.operands]
+    outs = [v for st in stages for v in st.outs]
+    scratch = [v for st in stages for v in st.scratch]
+    by_rows, base = [], 0
+    for st in stages:
+        by_rows += [base + i for i in st.by_rows]
+        base += len(st.operands)
+
+    def kernel(shipper, ins, results, refs, filler):
+        for st in stages:
+            parts = []
+            for have, n in ((ins, st.operands), (results, st.outs), (refs, st.scratch)):
+                parts.append(have[: len(n)])
+                del have[: len(n)]
+            st.bind(*parts)
+            st.load()
+        shipper.signal()
+
+        def met():
+            shipper.met()
+            shipper.start()
+
+        for n, st in enumerate(stages):
+            st.first(met if n == 0 else (lambda: None))
+        filler.prefetch()
+        filler.begin()
+        filler.advance(SHARE[0])
+        for n, st in enumerate(stages):
+            st.second(lambda: filler.advance(SHARE[1]) if n == 0 else None)
         filler.advance(SHARE[2])
-        for j in range(2):
-            g.forward(j)
-    filler.advance(1.0)
-    filler.end()
-    if gather:
-        g.finish()
-    c_far.wait_send()
-    c_core.wait_send()
-    for j in range(2):
-        c_x[j].wait_send()
-    shipper.finish()
-    for copy in stores:
-        copy.wait()
-    left.finish()
-
-
-def stage(
-    number,
-    planes,
-    left,
-    weight,
-    resid,
-    *,
-    flip=False,
-    maker=Rows,
-    back=None,
-    gather=None,
-    gain=None,
-    given=None,
-    dtype=F32,
-    jobs=(),
-    filler=None,
-):
-    chunk = resid.shape[1]
-    operands = list(left) + [weight]
-    cost = 4 * left[0].shape[0] * D * D
-    by_rows = {Rows: (0,), FeedForward: (0,), FeedForwardBack: (0, 1)}[maker]
-    operands.append(resid)
-    if back:
-        operands += [back[1], back[0]]
-    elif gather == "norm":
-        operands.append(gain)
-    if gather == "given":
-        operands.append(given)
-    outs = [jax.ShapeDtypeStruct((2, chunk, D), dtype)]
-    if gather:
-        outs.append(jax.ShapeDtypeStruct((2 * TP * chunk, D), BF))
-    if back:
-        outs.append(jax.ShapeDtypeStruct((1, D), F32))
-    half = pltpu.VMEM((2, chunk, D), BF)
-    full = pltpu.VMEM((2, chunk, D), F32)
-    scratch = [half] * 6 + [full] * 2 + [
-        pltpu.VMEM((2, chunk, D), dtype),
-        pltpu.SemaphoreType.DMA((11,)),
-    ]
-    if gather:
-        scratch += [half, pltpu.SemaphoreType.DMA((7, 2))]
-    if back:
-        scratch.append(pltpu.VMEM((1, D), F32))
-    if maker is not Rows:
-        width = weight.shape[1] if flip else weight.shape[0]
-        more, more_scratch = maker.extras(2 * TP * chunk, width)
-        outs += more
-        scratch += more_scratch
-    kernel = functools.partial(stage_kernel, (chunk, maker, flip, bool(back), gather))
+        for st in stages:
+            st.third()
+        filler.advance(1.0)
+        filler.end()
+        for st in stages:
+            st.last()
+        shipper.finish()
+
+    cost = sum(st.cost for st in stages)
     got, moved, made = call_with_jobs(
-        kernel,
-        number,
-        planes,
-        list(jobs),
-        operands,
-        outs,
-        scratch,
-        "stage",
-        cost,
-        filler,
-        by_rows,
-    )
-    return (got, moved, made) if filler else (got, moved)
+        kernel, number, planes, jobs, operands, outs, scratch, "stage", cost, filler, tuple(by_rows)
+    )
+    got = list(got)
+    each = []
+    for st in stages:
+        each.append(got[: len(st.outs)])
+        del got[: len(st.outs)]
+    return each, moved, made
 
 
 class Attention:
@@ -870,8 +1010,9 @@
         self.extra = 0 if mkv is None else mkv.shape[0]
         self.total = self.keys + self.extra
         self.bias = bias
-        self.blocks = self.rows // (2 * self.chunk)
-        self.n_steps = HQ * self.blocks
+        self.size = 2 * self.chunk
+        self.blocks = self.rows // self.size
+        self.n_steps = 2 * HQ
         self.loads = [q] + ([] if self.joint else [kv])
         self.mem = [mkv] if self.extra else []
         self.raws = []
@@ -897,13 +1038,26 @@
         part = lax.axis_index("part") if self.parts > 1 else 0
         return (upper * (TP * self.parts) + TP * part + (row_chunk - TP * upper)) * self.chunk
 
-    def step_rows(self, i):
-        h = i // self.blocks
-        b = i - h * self.blocks
-        return h, b, pl.ds(pl.multiple_of(b * (2 * self.chunk), 2 * self.chunk), 2 * self.chunk)
+    def halves(self, low, high):
+        for half in range(2):
+            first = max(low - HQ * half, 0)
+            last = min(high - HQ * half, HQ)
+            if first < last:
+                n = self.blocks // 2
+                yield half, range(half * n, (half + 1) * n), first, last
+
+    def width(self, b):
+        if self.causal and self.parts == 1:
+            return (b + 1) * self.size
+        return self.total
+
+    def block(self, b):
+        return pl.ds(b * self.size, self.size)
 
     def diagonal(self, b, u):
-        return pl.ds(pl.multiple_of(self.keys - self.place(2 * b + u), 128), self.keys)
+        keys = min(self.width(b), self.keys)
+        start = self.keys - self.place(2 * b + u)
+        return pl.ds(start if isinstance(start, int) else pl.multiple_of(start, 128), keys)
 
 
 class AttentionForward(Attention):
@@ -919,9 +1073,9 @@
         ]
         self.scratch = self.heads((self.rows, BF), (self.total, BF), (self.total, BF), (self.rows, BF))
         self.scratch += [
-            pltpu.VMEM((2, 2 * self.chunk, self.total), BF),
+            pltpu.VMEM((self.blocks, self.size, self.total), BF),
             pltpu.VMEM((self.rows, QC), BF),
-            pltpu.SemaphoreType.DMA((5,)),
+            pltpu.SemaphoreType.DMA((3 + self.blocks,)),
         ]
         if self.bias:
             self.scratch.append(pltpu.VMEM((self.chunk, 2 * self.keys), F32))
@@ -946,7 +1100,7 @@
                     rows = pl.ds(pl.multiple_of(r * 256, 256), 256)
                     out[rows] = mm(x[rows], w[...]).astype(BF)
 
-                self.copies.append(pltpu.make_async_copy(out, to, self.sems.at[3 + n]))
+                self.copies.append(pltpu.make_async_copy(out, to, self.sems.at[1 + n]))
                 self.copies[-1].start()
             q_ref, kv_ref = made[0], made[-1]
         else:
@@ -956,63 +1110,69 @@
         self.segq, self.segk = loads.pop(0).get(), loads.pop(0).get()
         self.bvec = loads.pop(0).get() if self.bias else None
 
-    def keep(self, i):
-        h, b, rows = self.step_rows(i)
-        slot = lax.rem(i, 2)
-        return pltpu.make_async_copy(self.p_buf.at[slot], self.p_out.at[h, rows], self.sems.at[slot])
+    def keep(self, h, b):
+        wide = pl.ds(0, self.width(b))
+        return pltpu.make_async_copy(
+            self.p_buf.at[b, :, wide], self.p_out.at[h, self.block(b), wide], self.sems.at[3 + b]
+        )
+
+    def one_block(self, h, b):
+        wide, chunk, rows = self.width(b), self.chunk, self.block(b)
+        keys = min(wide, self.keys)
+        s = mm_nt(self.qs[h, rows], self.ks[h, :wide])
+        if self.bias:
+            parts = [self.toep[:, self.diagonal(b, u)] for u in range(2)]
+            biased = s[:, :keys] + jnp.concatenate(parts, axis=0)
+            s = jnp.concatenate([biased, s[:, keys:]], axis=1) if self.extra else biased
+        allowed = self.segq[rows] == self.segk[:, :wide]
+        s = jnp.where(allowed, s, MASKED)
+        if self.causal:
+            row = lax.broadcasted_iota(jnp.int32, (chunk, 1), 0)
+            places = jnp.concatenate([row + self.place(2 * b + u) for u in range(2)], axis=0)
+            seen = wide - self.size if self.parts == 1 else 0
+            later = lax.broadcasted_iota(jnp.int32, (1, wide - seen), 1) + seen
+            last = jnp.where(later <= places, s[:, seen:], MASKED)
+            s = jnp.concatenate([s[:, :seen], last], axis=1) if seen else last
+        top = jnp.max(s, axis=-1, keepdims=True)
+        e = jnp.exp(s - top)
+        p = (e * (1.0 / jnp.sum(e, axis=-1, keepdims=True))).astype(BF)
+        self.p_buf[b, :, :wide] = p
+        self.os[h, rows] = mm(p, self.vs[h, :wide]).astype(BF)
 
     def run(self, low, high):
-        keys, chunk = self.keys, self.chunk
-
-        @pl.loop(low, high)
-        def _(i):
-            h, b, rows = self.step_rows(i)
-            slot = lax.rem(i, 2)
-            if self.bias:
-
-                @pl.when(b == 0)
+        for half, blocks, first, last in self.halves(low, high):
+
+            @pl.loop(first, last)
+            def _(h):
+                if self.bias:
+                    row = jnp.broadcast_to(self.bvec[h], (self.chunk, 2 * self.keys))
+                    self.toep[...] = pltpu.roll(row, 0, 1, stride=1, stride_axis=0)
+
+                @pl.when(h > 0)
                 def _():
-                    row = jnp.broadcast_to(self.bvec[h], (chunk, 2 * keys))
-                    self.toep[...] = pltpu.roll(row, 0, 1, stride=1, stride_axis=0)
-
-            s = mm_nt(self.qs[h, rows], self.ks[h])
-            allowed = self.segq[rows] == self.segk[...]
-            if self.bias:
-                parts = [self.toep[:, self.diagonal(b, u)] for u in range(2)]
-                biased = s[:, :keys] + jnp.concatenate(parts, axis=0)
-                s = jnp.concatenate([biased, s[:, keys:]], axis=1) if self.extra else biased
-            if self.causal:
-                row = lax.broadcasted_iota(jnp.int32, (chunk, 1), 0)
-                places = jnp.concatenate([row + self.place(2 * b + u) for u in range(2)], axis=0)
-                allowed = allowed & (lax.broadcasted_iota(jnp.int32, (1, keys), 1) <= places)
-            s = jnp.where(allowed, s, MASKED)
-            top = jnp.max(s, axis=-1, keepdims=True)
-            e = jnp.exp(s - top)
-            p = (e * (1.0 / jnp.sum(e, axis=-1, keepdims=True))).astype(BF)
-
-            @pl.when(i >= 2)
-            def _():
-                self.keep(i - 2).wait()
-
-            self.p_buf[slot] = p
-            self.keep(i).start()
-            self.os[h, rows] = mm(p, self.vs[h]).astype(BF)
+                    for b in blocks:
+                        self.keep(h - 1, b).wait()
+
+                for b in blocks:
+                    self.one_block(h, b)
+                for b in blocks:
+                    self.keep(h, b).start()
 
     def end(self):
         for i in range(HQ):
             self.att[:, DH * i : DH * (i + 1)] = self.os[i]
-        out = pltpu.make_async_copy(self.att, self.att_out, self.sems.at[2])
+        out = pltpu.make_async_copy(self.att, self.att_out, self.sems.at[0])
         out.start()
-        self.keep(self.n_steps - 2).wait()
-        self.keep(self.n_steps - 1).wait()
+        for b in range(self.blocks):
+            self.keep(HQ - 1, b).wait()
         out.wait()
         for copy in self.copies:
             copy.wait()
 
 
 class AttentionBackward(Attention):
-    def __init__(self, parts, p, q, kv, up, w_proj, att, bias, mkv, xs, proj=True):
-        super().__init__(parts, q, kv, bias, mkv, False)
+    def __init__(self, parts, p, q, kv, up, w_proj, att, bias, mkv, xs, proj=True, causal=False):
+        super().__init__(parts, q, kv, bias, mkv, causal)
         self.xs, self.proj = xs if parts == 1 else [], proj
         self.loads += self.mem + [up, w_proj, att] + self.xs
         self.raws = [p]
@@ -1038,17 +1198,20 @@
         )
         self.scratch += [
             pltpu.VMEM((HQ, rows, 1), F32),
-            pltpu.VMEM((2, 2 * self.chunk, total), BF),
-            pltpu.SemaphoreType.DMA((2 + len(self.outs),)),
+            pltpu.VMEM((self.blocks, self.size, total), BF),
+            pltpu.SemaphoreType.DMA((self.blocks + len(self.outs),)),
         ]
         self.scratch += [pltpu.VMEM(o.shape, o.dtype) for o in self.outs]
         if bias:
-            self.scratch.append(pltpu.VMEM((self.chunk, 2 * keys), F32))
-
-    def fetch(self, i):
-        h, b, rows = self.step_rows(i)
-        slot = lax.rem(i, 2)
-        return pltpu.make_async_copy(self.p_in.at[h, rows], self.p_buf.at[slot], self.sems.at[slot])
+            self.scratch.append(pltpu.VMEM((HQ, self.chunk, 2 * keys), F32))
+
+    def fetch(self, h, b):
+        n = self.blocks // 2
+        slot = n * lax.rem(h + (b // n) * HQ, 2) + b % n
+        wide = pl.ds(0, self.width(b))
+        return pltpu.make_async_copy(
+            self.p_in.at[h, self.block(b), wide], self.p_buf.at[slot, :, wide], self.sems.at[slot]
+        )
 
     def begin(self, loads, raws, outs, scratch):
         self.results, (self.p_in,) = outs, raws
@@ -1057,7 +1220,8 @@
         self.rds, self.p_buf, self.sems = scratch[7:10]
         self.made = scratch[10 : 10 + len(outs)]
         self.diag = scratch[-1] if self.bias else None
-        self.fetch(0).start()
+        for b in range(self.blocks // 2):
+            self.fetch(0, b).start()
         q_ref = loads.pop(0).get()
         kv_ref = q_ref if self.joint else loads.pop(0).get()
         self.split_qkv(q_ref, kv_ref, loads, self.qs, self.ks, self.vs)
@@ -1089,38 +1253,45 @@
                 g_proj[:, cols] = mm_tn(att_ref[...], up_ref[:, cols]).astype(BF)
 
     def run(self, low, high):
-        keys, chunk = self.keys, self.chunk
-
-        @pl.loop(low, high)
-        def _(i):
-            h, b, rows = self.step_rows(i)
-            self.fetch(i).wait()
-
-            @pl.when(i + 1 < self.n_steps)
-            def _():
-                self.fetch(i + 1).start()
-
-            @pl.when(b == 0)
-            def _():
-                self.dks[h] = jnp.zeros(self.dks.shape[1:], F32)
-                self.dvs[h] = jnp.zeros(self.dvs.shape[1:], F32)
-                if self.bias:
-                    self.diag[...] = jnp.zeros_like(self.diag)
-
-            q, grad, p = self.qs[h, rows], self.dos[h, rows], self.p_buf[lax.rem(i, 2)]
-            dp = mm_nt(grad, self.vs[h])
-            ds = (p.astype(F32) * (dp - self.rds[h, rows])).astype(BF)
-            self.dqs[h, rows] = mm(ds, self.ks[h]).astype(BF)
-            self.dks[h] += mm_tn(ds, q)
-            self.dvs[h] += mm_tn(p, grad)
-            if self.bias:
-                for u in range(2):
-                    part = ds[u * chunk : (u + 1) * chunk, :keys]
-                    self.diag[:, self.diagonal(b, u)] += part.astype(F32)
-
-                @pl.when(b == self.blocks - 1)
+        keys, chunk, n = self.keys, self.chunk, self.blocks // 2
+        for half, blocks, first, last in self.halves(low, high):
+
+            @pl.loop(first, last)
+            def _(h):
+                for b in blocks:
+                    self.fetch(h, b).wait()
+
+                @pl.when(h + 1 < HQ)
                 def _():
-                    x = self.diag[...]
+                    for b in blocks:
+                        self.fetch(h + 1, b).start()
+
+                if half == 0:
+
+                    @pl.when(h + 1 == HQ)
+                    def _():
+                        for b in range(n, 2 * n):
+                            self.fetch(0, b).start()
+
+                    self.dks[h] = jnp.zeros(self.dks.shape[1:], F32)
+                    self.dvs[h] = jnp.zeros(self.dvs.shape[1:], F32)
+                    if self.bias:
+                        self.diag[h] = jnp.zeros(self.diag.shape[1:], F32)
+                for b in blocks:
+                    wide, rows = self.width(b), self.block(b)
+                    slot = n * lax.rem(h + half * HQ, 2) + b % n
+                    q, grad, p = self.qs[h, rows], self.dos[h, rows], self.p_buf[slot, :, :wide]
+                    dp = mm_nt(grad, self.vs[h, :wide])
+                    ds = (p.astype(F32) * (dp - self.rds[h, rows])).astype(BF)
+                    self.dqs[h, rows] = mm(ds, self.ks[h, :wide]).astype(BF)
+                    self.dks[h, :wide] += mm_tn(ds, q)
+                    self.dvs[h, :wide] += mm_tn(p, grad)
+                    if self.bias:
+                        for u in range(2):
+                            part = ds[u * chunk : (u + 1) * chunk, : min(wide, keys)]
+                            self.diag[h, :, self.diagonal(b, u)] += part.astype(F32)
+                if self.bias and half == 1:
+                    x = self.diag[h]
                     size = chunk
                     while size > 1:
                         size //= 2
@@ -1147,7 +1318,7 @@
                 out[cols] = mm_tn(x_ref[:, cols], grad[...]).astype(BF)
 
         copies = [
-            pltpu.make_async_copy(src, dst, self.sems.at[2 + n])
+            pltpu.make_async_copy(src, dst, self.sems.at[self.blocks + n])
             for n, (src, dst) in enumerate(zip(self.made, self.results))
         ]
         for copy in copies:
@@ -1186,8 +1357,8 @@
 
 
 class Chain:
-    def __init__(self, value, steps):
-        self.value, self.steps = value, steps
+    def __init__(self, value, steps, width):
+        self.value, self.steps, self.width = value, steps, width
 
 
 ALL = ("seq", "part", "tp", "fsdp")
@@ -1270,8 +1441,10 @@
         return w.reshape(-1, w.shape[-1])
 
     gains = (enc_gain, enc_ffnorm, dec_gain, cross_gain, dec_ffnorm)
-    gain_stack = jnp.stack(gains).astype(F32)
-    rel_stack = jnp.stack([enc_rel, dec_rel]).astype(F32)
+    which = jnp.arange(len(gains), dtype=jnp.int32)[:, None]
+    gain_stack = sum(jnp.where(which == i, v.astype(F32)[None], 0.0) for i, v in enumerate(gains))
+    which = jnp.arange(2, dtype=jnp.int32)[:, None, None]
+    rel_stack = jnp.where(which == 0, enc_rel.astype(F32)[None], dec_rel.astype(F32)[None])
     segments = segments.reshape(2, 1, chunk)
     first_jobs = [
         swap_job(enc_input),
@@ -1314,14 +1487,17 @@
         full = lax.all_gather(w, "fsdp", axis=0, tiled=True)
         return lax.dynamic_slice_in_dim(full, QC * tp, QC, 0)
 
-    en, (w_eqkv, table, w_dqkv, *got), _ = gather_norm(
+    ((en,), (dn,)), (w_eqkv, table, w_dqkv, w_effin), _ = stage(
         1,
         planes,
-        xe,
-        g_enc,
-        [over_seq(w_eqkv), over_seq(table), over_planes(qkv_part(dec_qkv))] + proj_jobs(enc_proj),
-    )
-    w_eproj = proj_of(got, enc_proj)
+        [GatherNormed(xe, g_enc), GatherNormed(xd, g_dec)],
+        jobs=[
+            over_seq(w_eqkv),
+            over_seq(table),
+            over_planes(qkv_part(dec_qkv)),
+            over_planes(ffin_part(enc_ffin)),
+        ],
+    )
     w_eqkv, table = matrix(w_eqkv), matrix(table)
 
     segq = lax.dynamic_index_in_dim(seg.reshape(2, parts, TP * chunk), part, 1, keepdims=False)
@@ -1370,71 +1546,54 @@
         return got[0], got[1], rows or (got[2], got[2])
 
     e_fill, e_qkv = self_fill(en, w_eqkv, segk_mem, bias_vector(rels[0]), mkv, False)
-    dn, (w_dqkv, w_effin, *got), made = gather_norm(
+    made, (w_dqkv, w_effin, w_effout, *got) = attend(
         2,
         planes,
-        xd,
-        g_dec,
+        e_fill,
+        [over_seq(w_dqkv), over_seq(w_effin), over_planes(ffout_part(enc_ffout))]
+        + proj_jobs(enc_proj),
+    )
+    e_att, e_p, e_qkv = self_made(made, e_qkv)
+    w_eproj = proj_of(got, enc_proj)
+    w_dqkv, w_effin = matrix(w_dqkv), matrix(w_effin)
+    d_fill, d_qkv = self_fill(dn, w_dqkv, segk, bias_vector(rels[1]), None, True)
+    ((e_mid, e_fn),), (w_effout, w_cq, w_ckv, *got), made = stage(
+        3,
+        planes,
+        [Stage([e_att], w_eproj, xe, gather="norm", gain=g_effn)],
         [
-            over_seq(w_dqkv),
-            over_planes(ffin_part(enc_ffin)),
+            over_seq(w_effout),
+            over_planes(qkv_part(cross_query)),
+            over_planes(qkv_part(cross_kv)),
         ]
         + proj_jobs(dec_proj),
-        e_fill,
-    )
-    e_att, e_p, e_qkv = self_made(made, e_qkv)
+        d_fill,
+    )
+    d_att, d_p, d_qkv = self_made(made, d_qkv)
     w_dproj = proj_of(got, dec_proj)
-    w_dqkv = matrix(w_dqkv)
-    d_fill, d_qkv = self_fill(dn, w_dqkv, segk, bias_vector(rels[1]), None, True)
-    (e_mid, e_fn), (w_effin, w_effout, w_cq, w_ckv), made = stage(
-        3,
-        planes,
-        [e_att],
-        w_eproj,
-        xe,
-        gather="norm",
-        gain=g_effn,
-        jobs=[
-            over_seq(w_effin),
-            over_planes(ffout_part(enc_ffout)),
-            over_planes(qkv_part(cross_query)),
-            over_planes(qkv_part(cross_kv)),
-        ],
-        filler=d_fill,
-    )
-    d_att, d_p, d_qkv = self_made(made, d_qkv)
-    w_effin = matrix(w_effin)
-    (d_mid, c_n), (w_effout, w_cq, w_ckv, w_dffin, *got) = stage(
+    w_effout = matrix(w_effout)
+    ((d_mid, c_n), (e_low, e_gath, e_pre, e_act)), moved, _ = stage(
         4,
         planes,
-        [d_att],
-        w_dproj,
-        xd,
-        gather="norm",
-        gain=g_cross,
-        jobs=[
-            over_seq(w_effout),
+        [
+            Stage([d_att], w_dproj, xd, gather="norm", gain=g_cross),
+            Stage(
+                [e_fn, w_effin], w_effout, e_mid, maker=FeedForward, gather="low", dtype=BF
+            ),
+        ],
+        [
             over_seq(w_cq),
             over_seq(w_ckv),
             over_planes(ffin_part(dec_ffin)),
+            over_planes(ffout_part(dec_ffout)),
+            swap_job(dec_cotan),
         ]
         + proj_jobs(cross_proj),
     )
+    w_cq, w_ckv, w_dffin, w_dffout, xdc, *got = moved
     w_cproj = proj_of(got, cross_proj)
-    w_effout, w_cq, w_ckv = matrix(w_effout), matrix(w_cq), matrix(w_ckv)
-    (e_low, e_gath, e_pre, e_act), (w_dffin, w_dffout, xdc) = stage(
-        5,
-        planes,
-        [e_fn, w_effin],
-        w_effout,
-        e_mid,
-        maker=FeedForward,
-        gather="low",
-        dtype=BF,
-        jobs=[over_seq(w_dffin), over_planes(ffout_part(dec_ffout)), swap_job(dec_cotan)],
-    )
+    w_cq, w_ckv = matrix(w_cq), matrix(w_ckv)
     xdc = joined(dec_cotan, xdc)
-    w_dffin = matrix(w_dffin)
     products = None
     if parts == 1:
         c_q = jax.ShapeDtypeStruct((c_n.shape[0], QC), BF)
@@ -1444,31 +1603,31 @@
         c_q = mm(c_n, w_cq).astype(BF)
         c_kv = spread(mm(e_gath, w_ckv).astype(BF))
     c_fill = AttentionForward(parts, c_q, c_kv, segq, segk, None, None, False, products)
-    (c_att, c_p, *made), (w_dffout,) = attend(19, planes, c_fill, [over_seq(w_dffout)])
+    (c_att, c_p, *made), (w_dffin,) = attend(5, planes, c_fill, [over_seq(w_dffin)])
     if parts == 1:
         c_q, c_kv = made
-    w_dffout = matrix(w_dffout)
-    (d_cross, d_fn), (came, xec) = stage(
+    ((d_cross, d_fn),), (w_dffout, came, xec), _ = stage(
         6,
         planes,
-        [c_att],
-        w_cproj,
-        d_mid,
-        gather="norm",
-        gain=g_dffn,
-        jobs=[swap_job(e_low), swap_job(enc_cotan)],
+        [Stage([c_att], w_cproj, d_mid, gather="norm", gain=g_dffn)],
+        [over_seq(w_dffout), swap_job(e_low), swap_job(enc_cotan)],
     )
     enc_output, xec = joined(e_low, came), joined(enc_cotan, xec)
-    (d_low, up_g, d_pre, d_act), _ = stage(
+    w_dffin, w_dffout = matrix(w_dffin), matrix(w_dffout)
+    ((d_low, up_g, d_pre, d_act),), _, _ = stage(
         7,
         planes,
-        [d_fn, w_dffin],
-        w_dffout,
-        d_cross,
-        maker=FeedForward,
-        gather="given",
-        given=xdc,
-        dtype=BF,
+        [
+            Stage(
+                [d_fn, w_dffin],
+                w_dffout,
+                d_cross,
+                maker=FeedForward,
+                gather="given",
+                given=xdc,
+                dtype=BF,
+            )
+        ],
     )
 
     def pieces(g):
@@ -1476,25 +1635,34 @@
             g = lax.psum(g, "part")
         return g.reshape(planes, 2, g.shape[0] // split, g.shape[1])
 
-    def to_ctx(width):
-        return [
-            lambda g: gather_job("across", g),
-            lambda g: gather_job("seq", g),
-            lambda g: last_job(g, width),
-        ]
-
-    def chain(g, width):
+    to_ctx = [
+        lambda g: gather_job("across", g),
+        lambda g: gather_job("seq", g),
+        lambda g: gather_job("core", g, 2, 2),
+    ]
+    to_ctx_seq = [
+        lambda g: gather_job("seq", g),
+        lambda g: gather_job("across", g, 2, 1),
+        lambda g: gather_job("core", g, 2, 2),
+    ]
+
+    def chain(g, width, seq_first=False):
         steps = [lambda g: swap_job(g, 1, True), lambda g: deal_job("fsdp", g)]
-        return Chain(pieces(g), steps + to_ctx(width))
+        return Chain(pieces(g), steps + (to_ctx_seq if seq_first else to_ctx), width)
 
     def proj_chain(g):
         if not turned:
-            return Chain(g, [])
+            return Chain(g, [], -1)
         steps = [lambda g: swap_job(g, "cols", True), lambda g: deal_job("fsdp", g), turn_job]
-        return Chain(g.reshape(planes, -1, D), steps + to_ctx(-1))
+        return Chain(g.reshape(planes, -1, D), steps + to_ctx, -1)
 
     def steps_of(chains):
         return [c.steps[0](c.value) for c in chains if c.steps]
+
+    def hurry(chains):
+        for c in chains:
+            if len(c.steps) == 3:
+                c.steps = [spread_job]
 
     def settle(chains, got):
         got = list(got)
@@ -1504,44 +1672,46 @@
                 c.steps.pop(0)
         return got
 
-    k_dffout = chain(mm_tn(d_act, up_g).astype(BF), 0)
+    k_dffout = chain(mm_tn(d_act, up_g).astype(BF), 0, True)
     moving = [k_dffout]
-    (up, up_rows, dg_dffn, pre_grad), got = stage(
+    ((up, up_rows, dg_dffn, pre_grad),), got, _ = stage(
         8,
         planes,
-        [up_g, d_pre, w_dffout],
-        w_dffin,
-        xdc,
-        flip=True,
-        maker=FeedForwardBack,
-        back=(d_cross, g_dffn),
-        gather="low",
-        jobs=steps_of(moving) + [swap_job(d_low)],
+        [
+            Stage(
+                [up_g, d_pre, w_dffout],
+                w_dffin,
+                xdc,
+                flip=True,
+                maker=FeedForwardBack,
+                back=(d_cross, g_dffn),
+                gather="low",
+            )
+        ],
+        steps_of(moving) + [swap_job(d_low)],
     )
     (came,) = settle(moving, got)
     dec_output = joined(d_low, came)
-    k_dffin = chain(mm_tn(d_fn, pre_grad).astype(BF), hidden)
+    k_dffin = chain(mm_tn(d_fn, pre_grad).astype(BF), hidden, True)
     c_fill = AttentionBackward(
         parts, c_p, c_q, c_kv, up_rows, w_cproj, c_att, False, None, [c_n, e_gath]
     )
     moving = [k_dffin, k_dffout]
-    (c_dq, c_dkv, g_cproj, *made), got = attend(20, planes, c_fill, steps_of(moving))
+    (c_dq, c_dkv, g_cproj, *made), got = attend(9, planes, c_fill, steps_of(moving))
     settle(moving, got)
     c_dkv = collect(c_dkv)
     if parts > 1:
         made = [mm_tn(c_n, c_dq).astype(BF), mm_tn(e_gath, c_dkv).astype(BF)]
     k_cproj, k_cq, k_ckv = proj_chain(g_cproj), chain(made[0], QC), chain(made[1], QC)
     moving = [k_dffin, k_dffout, k_cq, k_ckv, k_cproj]
-    (up, up_rows, dg_cross), got = stage(
-        9,
+    ((e_up, e_up_rows), (up, up_rows, dg_cross)), got, _ = stage(
+        10,
         planes,
-        [c_dq],
-        w_cq,
-        up,
-        flip=True,
-        back=(d_mid, g_cross),
-        gather="low",
-        jobs=steps_of(moving),
+        [
+            Stage([c_dkv], w_ckv, xec, flip=True, gather="low"),
+            Stage([c_dq], w_cq, up, flip=True, back=(d_mid, g_cross), gather="low"),
+        ],
+        steps_of(moving),
     )
     settle(moving, got)
 
@@ -1551,112 +1721,99 @@
         return grad, chain(g_rows, QC), made
 
     d_fill = AttentionBackward(
-        parts, d_p, *d_qkv, up_rows, w_dproj, d_att, True, None, [dn]
-    )
-    (e_up, e_up_rows), got, made = stage(
-        10,
+        parts, d_p, *d_qkv, up_rows, w_dproj, d_att, True, None, [dn], causal=True
+    )
+    k_effout = chain(mm_tn(e_act, e_up_rows).astype(BF), 0, True)
+    moving = [k_dffin, k_dffout, k_cq, k_ckv, k_cproj, k_effout]
+    ((e_up, e_up_rows, dg_effn, pre_grad),), got, made = stage(
+        12,
         planes,
-        [c_dkv],
-        w_ckv,
-        xec,
-        flip=True,
-        gather="low",
-        jobs=steps_of(moving),
-        filler=d_fill,
+        [
+            Stage(
+                [e_up_rows, e_pre, w_effout],
+                w_effin,
+                e_up,
+                flip=True,
+                maker=FeedForwardBack,
+                back=(e_mid, g_effn),
+                gather="low",
+            )
+        ],
+        steps_of(moving),
+        d_fill,
     )
     settle(moving, got)
     d_rows_grad, k_dqkv, (d_dbv, g_dproj) = self_grads(made, dn)
     k_dproj = proj_chain(g_dproj)
-    k_effout = chain(mm_tn(e_act, e_up_rows).astype(BF), 0)
-    moving = [k_dffout, k_cq, k_ckv, k_cproj, k_dqkv, k_dproj, k_effout]
-    (e_up, e_up_rows, dg_effn, pre_grad), got = stage(
-        12,
-        planes,
-        [e_up_rows, e_pre, w_effout],
-        w_effin,
-        e_up,
-        flip=True,
-        maker=FeedForwardBack,
-        back=(e_mid, g_effn),
-        gather="low",
-        jobs=steps_of(moving),
-    )
-    settle(moving, got)
     k_effin = chain(mm_tn(e_fn, pre_grad).astype(BF), hidden)
+    k_eproj = proj_chain(mm_tn(e_att, e_up_rows).astype(BF))
     e_fill = AttentionBackward(
         parts, e_p, *e_qkv, e_up_rows, w_eproj, e_att, True, mkv, [en], False
     )
-    k_eproj = proj_chain(mm_tn(e_att, e_up_rows).astype(BF))
-    moving = [k_dffin, k_cq, k_ckv, k_cproj, k_dqkv, k_dproj, k_effout, k_effin, k_eproj]
-    (d_in, dg_dec), got, made = stage(
+    moving += [k_dqkv, k_dproj, k_effin, k_eproj]
+    ((d_in, dg_dec, d_in_low),), got, made = stage(
         11,
         planes,
-        [d_rows_grad],
-        w_dqkv,
-        up,
-        flip=True,
-        back=(xd, g_dec),
-        jobs=steps_of(moving),
-        filler=e_fill,
+        [Stage([d_rows_grad], w_dqkv, up, flip=True, back=(xd, g_dec), low=True)],
+        steps_of(moving),
+        e_fill,
     )
     settle(moving, got)
     e_rows_grad, k_eqkv, (e_dbv, d_mkv) = self_grads(made, en)
     k_table = chain(mm_tn(pick, d_mkv).astype(BF), QC)
     moving += [k_eqkv, k_table]
-    (e_in, dg_enc), got = stage(
+    ((e_in, dg_enc, e_in_low),), got, _ = stage(
         13,
         planes,
-        [e_rows_grad],
-        w_eqkv,
-        e_up,
-        flip=True,
-        back=(xe, g_enc),
-        jobs=steps_of(moving) + [swap_job(d_in.astype(BF))],
+        [Stage([e_rows_grad], w_eqkv, e_up, flip=True, back=(xe, g_enc), low=True)],
+        steps_of(moving) + [swap_job(d_in_low)],
     )
     (came,) = settle(moving, got)
     dec_ingrad = joined(d_in, came)
-    def rel_grad(dbv):
+
+    def rel_grads(*dbvs):
         own = lax.dot_general(
             onehot.astype(F32),
-            dbv.reshape(HQ, -1),
+            jnp.concatenate(dbvs, axis=0).reshape(len(dbvs) * HQ, -1),
             (((0,), (1,)), ((), ())),
             precision=lax.Precision.HIGHEST,
             preferred_element_type=F32,
         )
-        return lax.dynamic_update_slice_in_dim(jnp.zeros((BUCKETS, HEADS), F32), own, HQ * tp, 1)
-
-    tiny = [dg_enc, dg_effn, dg_dec, dg_cross, dg_dffn]
-    tiny = jnp.concatenate([v.reshape(planes, -1) for v in tiny] + [
-        rel_grad(v).reshape(planes, -1) for v in (e_dbv, d_dbv)
-    ], axis=1)
-    tiny = tiny.reshape(-1, 128)
+        heads = jnp.arange(HEADS, dtype=jnp.int32)[None, :] // HQ == tp
+        return [
+            jnp.where(heads, jnp.tile(own[:, HQ * i : HQ * (i + 1)], (1, TP)), 0.0)
+            for i in range(len(dbvs))
+        ]
+
+    tiny = [v.reshape(planes, -1) for v in (dg_enc, dg_effn, dg_dec, dg_cross, dg_dffn)]
+    tiny += [v.reshape(planes, -1) for v in rel_grads(e_dbv, d_dbv)]
+    tiny = jnp.concatenate(tiny, axis=1).reshape(-1, 128)
     if parts > 1:
         tiny = lax.psum(tiny, "part")
-    swapped = [swap_job(e_in.astype(BF))]
-    for number, axis in enumerate(("fsdp", "seq", "across", "core", None)):
-        if axis is None and not steps_of(moving):
-            break
-        total = [total_job(axis, tiny, planes if axis == "fsdp" else 2)] if axis else []
-        got = ship(14 + number, planes, total + swapped + steps_of(moving))
-        if axis:
-            tiny, *got = got
-        if swapped:
-            enc_ingrad = joined(e_in, got.pop(0))
-            swapped = []
-        settle(moving, got)
+    hurry(moving)
+    tiny, came, *got = ship(
+        14,
+        planes,
+        [total_job("fsdp", tiny, planes), swap_job(e_in_low)] + steps_of(moving),
+    )
+    enc_ingrad = joined(e_in, came)
+    settle(moving, got)
+    hurry(moving)
+    tiny, *got = ship(15, planes, [spread_job(tiny, True)] + steps_of(moving))
+    settle(moving, got)
 
     def proj_rows(k):
-        if turned:
-            return k.value
         full = lax.dynamic_update_slice_in_dim(jnp.zeros((D, D), BF), k.value, QC * tp, 0)
         full = lax.psum_scatter(full, "fsdp", scatter_dimension=0, tiled=True)
         return lax.psum(full.astype(F32), CTX)
 
-    o_eproj, o_dproj, o_cproj = (proj_rows(k) for k in (k_eproj, k_dproj, k_cproj))
-    o_dffin, o_dffout, o_effin, o_effout, o_cq, o_ckv, o_dqkv, o_eqkv, o_table = (
-        k.value
-        for k in (k_dffin, k_dffout, k_effin, k_effout, k_cq, k_ckv, k_dqkv, k_eqkv, k_table)
-    )
+    ready = [k_dffin, k_dffout, k_effin, k_effout, k_cq, k_ckv, k_dqkv, k_eqkv, k_table]
+    k_projs = [k_eproj, k_dproj, k_cproj]
+    if turned:
+        ready += k_projs
+    results = laid_out([k.value for k in ready], [k.width for k in ready])
+    o_eproj, o_dproj, o_cproj = results[9:] if turned else [proj_rows(k) for k in k_projs]
+    o_dffin, o_dffout, o_effin, o_effout, o_cq, o_ckv, o_dqkv, o_eqkv, o_table = results[:9]
     tiny = lax.dynamic_index_in_dim(tiny.reshape(planes, -1), plane, 0, keepdims=False)
     o_gains = [tiny[per * i : per * (i + 1)] for i in range(5)]
     o_rels = [

time: 585 us -> 558 us (0.954)
  local copies, waits for them, and re-layouts: 41.5 us -> 17.6 us
    unnamed x94 -> x64, local copies, waits for them, and re-layouts: 19.9 us -> 0.14 us
    pallas_call x20 -> x16, Pallas kernels: 492 us -> 479 us  [call_with_jobs(): pl.pallas_call(body, out_shape=tuple(outs) + tuple((jax.ShapeDtypeStruct(...]
    pallas_call x0 -> x1, Pallas kernels: none -> 8.23 us  [laid_out(): pl.pallas_call(body, out_shape=tuple((jax.ShapeDtypeStruct(shape, F32) fo...]
where the time goes in v5:
time: 558 us; the launch traced here: 550 us
  Pallas kernels  487 us (87%)
  other arithmetic  22.8 us (4%)
  matrix products  21.4 us (4%)
  local copies, waits for them, and re-layouts  17.6 us (3%)
    pallas_call x16, Pallas kernels, call_with_jobs(): pl.pallas_call(body, out_shape=tuple(outs) + tuple((jax.ShapeDtypeStruct(...  479 us
    dot_general x6, matrix products, mm_tn(): lax.dot_general(a, b, (((0,), (0,)), ((), ())), preferred_element_type=F32)  17.9 us

profile of v5, /device:TPU:0, one launch (start us, length us, event | category | flops | bytes accessed | tf_op | source)
XLA Modules:
  0.0 550.3 jit_solution(11397011665297313437)
XLA Ops:
  0.7 0.7 convert_element_type.61
  1.4 0.7 convert_element_type.60
  4.0 0.7 select_add_fusion.refs_1_
  4.7 0.7 convert_element_type.63
  5.4 0.7 convert_element_type.62
  6.1 0.7 broadcast_select_fusion.refs_2_
  6.8 1.3 fusion.31
  8.1 0.7 pad_maximum_fusion.10.refs_3_
  8.8 0.9 fusion.34
  9.7 0.7 pad_maximum_fusion.14.refs_4_
  10.4 22.2 %ship.3 = (bf16[128,768]{1,0:T(8,128)(2,1)}, f32[4,5,192]{2,1,0:T(8,128)}, f32[4,2,8,12]{3,2,1,0:T(8,128)}, bf16[4,96,576]{2,1,0:T(8,128)(2,1)}, bf16[4,32,384]{...) custom-call(bf16[2,128,768]{2,1,0:T(8,128)(2,1)} %refs_0_.1, f32[5,192]{1,0:T(8,128)} %select_add_fusion.refs_1_, ...), custom_call_target="tpu_custom_call" | custom-call | bytes 8388608 | tf_op jit(solution)/shard_map/ship/pallas_call | solution.py:576
  32.6 1.0 fusion.20
  33.6 0.8 pad_maximum_fusion.2.refs_0_.refs_2_.refs_4_
  34.5 0.7 reshape_squeeze.21.refs_1_.refs_3_
  35.2 0.8 pad_maximum_fusion.3.refs_2_.refs_4_
  36.0 0.7 reshape_squeeze.22.refs_3_
  36.6 0.7 pad_maximum_fusion.11.refs_6_
  37.4 1.4 fusion.29
  38.8 0.8 pad_maximum_fusion.8.refs_7_
  39.6 24.7 %stage.10 = (bf16[1024,768]{1,0:T(8,128)(2,1)}, bf16[1024,768]{1,0:T(8,128)(2,1)}, bf16[4,2,96,576]{3,2,1,0:T(8,128)(2,1)}, bf16[4,2,32,384]{3,2,1,0:T(8,128)(2,...) custom-call(bf16[2,128,768]{2,1,0:T(8,128)(2,1)} %pad_maximum_fusion.2.refs_0_.refs_2_.refs_4_, ...), custom_call_target="tpu_custom_call" | custom-call | flops 2000000 | bytes 8388608 | tf_op jit(solution)/shard_map/stage/pallas_call | solution.py:576
  64.3 1.7 constant_dynamic-slice_fusion.1
  66.1 1.9 convolution_convert_fusion.6.refs_6_.refs_16_
  68.0 1.0 copy.52.refs_7_.refs_10_.refs_5_
  70.8 28.0 %attend.3 = (bf16[4,2,96,576]{3,2,1,0:T(8,128)(2,1)}, bf16[4,2,96,768]{3,2,1,0:T(8,128)(2,1)}, bf16[4,96,768]{2,1,0:T(8,128)(2,1)}, bf16[192,768]{1,0:T(8,128)(2...) custom-call(bf16[4,96,576]{2,1,0:T(8,128)(2,1)} %get-tuple-element.183.refs_0_, ...), custom_call_target="tpu_custom_call" | custom-call | flops 4000000000 | bytes 8388608 | tf_op jit(solution)/shard_map/attend/pallas_call | solution.py:576
  98.8 0.7 reshape_squeeze.24.refs_3_.refs_5_
  99.5 1.6 dynamic_slice.129.refs_5_
  101.1 1.0 fusion.33
  102.1 0.7 pad_maximum_fusion.12.refs_6_
  104.0 31.8 %stage.11 = (f32[2,128,768]{2,1,0:T(8,128)}, bf16[1024,768]{1,0:T(8,128)(2,1)}, bf16[4,2,96,768]{3,2,1,0:T(8,128)(2,1)}, bf16[4,96,192]{2,1,0:T(8,128)(2,1)}, bf...) custom-call(bf16[1024,192]{1,0:T(8,128)(2,1)} %get-tuple-element.190, ...), custom_call_target="tpu_custom_call" | custom-call | flops 2415919104 | bytes 8388608 | tf_op jit(solution)/shard_map/stage/pallas_call | solution.py:576
  135.8 0.7 reshape_squeeze.26.refs_3_.refs_6_
  136.5 0.8 pad_maximum_fusion.9.refs_10_
  137.2 53.1 %stage.12 = (f32[2,128,768]{2,1,0:T(8,128)}, bf16[1024,768]{1,0:T(8,128)(2,1)}, bf16[2,128,768]{2,1,0:T(8,128)(2,1)}, bf16[1024,768]{1,0:T(8,128)(2,1)}, f32[102...) custom-call(bf16[1024,192]{1,0:T(8,128)(2,1)} %get-tuple-element.195, ...), custom_call_target="tpu_custom_call" | custom-call | flops 4831838208 | bytes 8388608 | tf_op jit(solution)/shard_map/stage/pallas_call | solution.py:576
  190.3 19.3 %attend.4 = (bf16[4,2,96,768]{3,2,1,0:T(8,128)(2,1)}, bf16[1024,192]{1,0:T(8,128)(2,1)}, bf16[3,1024,1024]{2,1,0:T(8,128)(2,1)}, bf16[1024,192]{1,0:T(8,128)(2,1)}, bf16[1024,384]{1,0:T(8,128)(2,1)}) custom-call(bf16[4,96,768]{2,1,0:T(8,128)(2,1)} %get-tuple-element.204.refs_0_, bf16[1024,768]{1,0:T(8,128)(2,1)} %get-tuple-element.205.refs_1_.refs_7_, ...), custom_call_target="tpu_custom_call" | custom-call | flops 4000000000 | bytes 8388608 | tf_op jit(solution)/shard_map/attend/pallas_call | solution.py:576
  209.6 0.7 reshape_squeeze.27.refs_3_.refs_5_
  210.3 28.0 %stage.13 = (f32[2,128,768]{2,1,0:T(8,128)}, bf16[1024,768]{1,0:T(8,128)(2,1)}, bf16[4,2,96,768]{3,2,1,0:T(8,128)(2,1)}, bf16[128,768]{1,0:T(8,128)(2,1)}, bf16[128,768]{1,0:T(8,128)(2,1)}) custom-call(bf16[1024,192]{1,0:T(8,128)(2,1)} %get-tuple-element.209.refs_0_.refs_6_, bf16[192,768]{1,0:T(8,128)(2,1)} %get-tuple-element.210.refs_1_.refs_5_, ...), custom_call_target="tpu_custom_call" | custom-call | flops 2415919104 | bytes 8388608 | tf_op jit(solution)/shard_map/stage/pallas_call | solution.py:576
  238.3 1.0 fusion.16
  239.4 0.8 pad_maximum_fusion.4
  240.2 0.8 pad_maximum_fusion.5.refs_4_
  241.0 23.9 %stage.14 = (bf16[2,128,768]{2,1,0:T(8,128)(2,1)}, bf16[1024,768]{1,0:T(8,128)(2,1)}, f32[1024,768]{1,0:T(8,128)}, bf16[1024,768]{1,0:T(8,128)(2,1)}) custom-call(bf16[1024,768]{1,0:T(8,128)(2,1)} %get-tuple-element.214.refs_0_, bf16[768,768]{1,0:T(8,128)(2,1)} %bitcast.135, bf16[768,768]{1,0:T(8,128)(2,1)} %bitcast.137, ...), custom_call_target="tpu_custom_call" | custom-call | flops 2415919104 | bytes 8388608 | tf_op jit(solution)/shard_map/stage/pallas_call | solution.py:576
  264.9 4.3 convolution_convert_fusion.3
  269.3 28.2 %stage.15 = (f32[2,128,768]{2,1,0:T(8,128)}, bf16[1024,768]{1,0:T(8,128)(2,1)}, f32[1,768]{1,0:T(1,128)}, bf16[1024,768]{1,0:T(8,128)(2,1)}, bf16[4,96,768]{2,1,0:T(8,128)(2,1)}, /*index=5*/bf16[128,768]{1,0:T(8,128)(2,1)}) custom-call(bf16[1024,768]{1,0:T(8,128)(2,1)} %get-tuple-element.220.refs_0_, f32[1024,768]{1,0:T(8,128)} %get-tuple-element.221.refs_1_, ...), custom_call_target="tpu_custom_call" | custom-call | flops 2415919104 | bytes 8388608 | tf_op jit(solution)/shard_map/stage/pallas_call | solution.py:576
  297.5 1.1 fusion.12
  298.6 0.8 pad_maximum_fusion.6
  299.4 2.5 convolution_convert_fusion.2
  301.9 20.3 %attend.5 = (bf16[4,96,768]{2,1,0:T(8,128)(2,1)}, bf16[96,768]{1,0:T(8,128)(2,1)}, bf16[1024,192]{1,0:T(8,128)(2,1)}, bf16[1024,384]{1,0:T(8,128)(2,1)}, bf16[19...) custom-call(bf16[4,2,96,768]{3,2,1,0:T(8,128)(2,1)} %bitcast.134, ...), custom_call_target="tpu_custom_call" | custom-call | flops 4000000000 | bytes 8388608 | tf_op jit(solution)/shard_map/attend/pallas_call | solution.py:576
  322.3 0.8 pad_maximum_fusion.7.refs_2_
  323.0 43.9 %stage.16 = (f32[2,128,768]{2,1,0:T(8,128)}, bf16[1024,768]{1,0:T(8,128)(2,1)}, f32[2,128,768]{2,1,0:T(8,128)}, bf16[1024,768]{1,0:T(8,128)(2,1)}, f32[1,768]{1,...) custom-call(bf16[1024,384]{1,0:T(8,128)(2,1)} %get-tuple-element.230, ...), custom_call_target="tpu_custom_call" | custom-call | flops 4831838208 | bytes 8388608 | tf_op jit(solution)/shard_map/stage/pallas_call | solution.py:576
  367.0 3.9 convolution_convert_fusion.1
  370.9 40.0 %stage.17 = (f32[2,128,768]{2,1,0:T(8,128)}, bf16[1024,768]{1,0:T(8,128)(2,1)}, f32[1,768]{1,0:T(1,128)}, bf16[1024,768]{1,0:T(8,128)(2,1)}, bf16[2,96,768]{2,1,...) custom-call(bf16[1024,768]{1,0:T(8,128)(2,1)} %get-tuple-element.239, ...), custom_call_target="tpu_custom_call" | custom-call | flops 2415919104 | bytes 8388608 | tf_op jit(solution)/shard_map/stage/pallas_call | solution.py:576
  410.9 4.0 convolution_convert_fusion
  414.9 1.2 convolution_convert_fusion.4
  416.2 37.0 %stage.18 = (f32[2,128,768]{2,1,0:T(8,128)}, f32[1,768]{1,0:T(1,128)}, bf16[2,128,768]{2,1,0:T(8,128)(2,1)}, bf16[2,2,96,768]{3,2,1,0:T(8,128)(2,1)}, bf16[2,2,2...) custom-call(bf16[1024,576]{1,0:T(8,128)(2,1)} %get-tuple-element.251, ...), custom_call_target="tpu_custom_call" | custom-call | flops 2415919104 | bytes 8388608 | tf_op jit(solution)/shard_map/stage/pallas_call | solution.py:576
  453.1 2.0 convolution_convert_fusion.5
  455.1 35.3 %stage.19 = (f32[2,128,768]{2,1,0:T(8,128)}, f32[1,768]{1,0:T(1,128)}, bf16[2,128,768]{2,1,0:T(8,128)(2,1)}, bf16[2,2,2,96,768]{4,3,2,1,0:T(8,128)(2,1)}, bf16[2...) custom-call(bf16[1024,576]{1,0:T(8,128)(2,1)} %get-tuple-element.265, ...), custom_call_target="tpu_custom_call" | custom-call | flops 2415919104 | bytes 8388608 | tf_op jit(solution)/shard_map/stage/pallas_call | solution.py:576
  490.4 0.7 reduce.5
  493.6 24.7 %ship.4 = (f32[36,128]{1,0:T(8,128)}, bf16[128,768]{1,0:T(8,128)(2,1)}, bf16[2,2,2,96,192]{4,3,2,1,0:T(8,128)(2,1)}, bf16[2,2,2,96,384]{4,3,2,1,0:T(8,128)(2,1)}...) custom-call(f32[36,128]{1,0:T(8,128)} %reshape.276.refs_0_, ...), custom_call_target="tpu_custom_call" | custom-call | bytes 8388608 | tf_op jit(solution)/shard_map/ship/pallas_call | solution.py:576
  518.3 1.1 fusion.6
  519.4 0.9 pad_maximum_fusion
  520.4 0.9 pad_maximum_fusion.1
  521.4 18.3 %ship.5 = (f32[36,128]{1,0:T(8,128)}, bf16[2,2,2,48,384]{4,3,2,1,0:T(8,128)(2,1)}, bf16[2,2,2,96,768]{4,3,2,1,0:T(8,128)(2,1)}, bf16[2,2,2,48,384]{4,3,2,1,0:T(8...) custom-call(f32[36,128]{1,0:T(8,128)} %get-tuple-element.304.refs_0_, ...), custom_call_target="tpu_custom_call" | custom-call | bytes 8388608 | tf_op jit(solution)/shard_map/ship/pallas_call | solution.py:576
  539.7 8.2 %lay_out.1 = (f32[192,3072]{1,0:T(8,128)}, f32[768,768]{1,0:T(8,128)}, f32[192,3072]{1,0:T(8,128)}, f32[768,768]{1,0:T(8,128)}, f32[192,768]{1,0:T(8,128)}, /*in...) custom-call(bf16[2,2,2,96,768]{4,3,2,1,0:T(8,128)(2,1)} %get-tuple-e, ...), custom_call_target="tpu_custom_call" | custom-call | tf_op jit(solution)/shard_map/lay_out/pallas_call | solution.py:486
  548.0 0.7 fusion.35
  548.8 0.7 reshape.278
  549.4 0.7 reshape.279
  (111 shorter events, 7.8 us)
Async XLA Ops:
  0.7 65.3 %copy-start = (s32[2,8,20]{2,1,0:T(8,128)S(1)}, s32[2,8,20]{2,1,0:T(8,128)}, u32[]{:S(2)}) copy-start(s32[2,8,20]{2,1,0:T(8,128)} %param.30) | copy-start | bytes 3844
  0.7 31.9 %copy-start.4 = (bf16[2,128,768]{2,1,0:T(8,128)(2,1)S(1)}, bf16[2,128,768]{2,1,0:T(8,128)(2,1)}, u32[]{:S(2)}) copy-start(bf16[2,128,768]{2,1,0:T(8,128)(2,1)} %refs_0_.1) | copy-start | bytes 1179652
  8.1 27.1 %copy-start.5 = (bf16[2,128,768]{2,1,0:T(8,128)(2,1)S(1)}, bf16[2,128,768]{2,1,0:T(8,128)(2,1)}, u32[]{:S(2)}) copy-start(bf16[2,128,768]{2,1,0:T(8,128)(2,1)} %refs_5_.1) | copy-start | bytes 1179652
  32.6 1.8 copy-start.20
  32.6 2.6 copy-start.12
  38.8 29.2 %copy-start.19 = (s32[8,1,128]{2,1,0:T(1,128)S(1)}, s32[8,1,128]{2,1,0:T(1,128)}, u32[]{:S(2)}) copy-start(s32[8,1,128]{2,1,0:T(1,128)} %get-tuple-element.188) | copy-start | bytes 12292
  39.6 29.4 %copy-start.26 = (s32[1,256]{1,0:T(1,128)S(1)}, s32[1,256]{1,0:T(1,128)}, u32[]{:S(2)}) copy-start(s32[1,256]{1,0:T(1,128)} %constant.301) | copy-start | bytes 3076
  39.6 30.0 %copy-start.21 = (f32[4,2,8,12]{3,2,1,0:T(8,128)S(1)}, f32[4,2,8,12]{3,2,1,0:T(8,128)}, u32[]{:S(2)}) copy-start(f32[4,2,8,12]{3,2,1,0:T(8,128)} %get-tuple-element.189) | copy-start | bytes 9220
  39.6 30.0 %copy-start.28 = (s32[2048]{0:T(1024)S(1)}, s32[2048]{0:T(1024)}, u32[]{:S(2)}) copy-start(s32[2048]{0:T(1024)} %param.31) | copy-start | bytes 24580
  210.3 28.0 %copy-start.15 = (bf16[2,128,768]{2,1,0:T(8,128)(2,1)S(1)}, bf16[2,128,768]{2,1,0:T(8,128)(2,1)}, u32[]{:S(2)}) copy-start(bf16[2,128,768]{2,1,0:T(8,128)(2,1)} %get-tuple-element.203.refs_5_) | copy-start | bytes 1179652
  238.3 1.8 copy-start.11
  238.3 1.8 copy-start.13
  269.2 28.3 %copy-start.3 = (bf16[2,128,768]{2,1,0:T(8,128)(2,1)S(1)}, bf16[2,128,768]{2,1,0:T(8,128)(2,1)}, u32[]{:S(2)}) copy-start(bf16[2,128,768]{2,1,0:T(8,128)(2,1)} %get-tuple-element.219.refs_8_) | copy-start | bytes 1179652
  269.3 30.1 %copy-start.31 = (bf16[1024,768]{1,0:T(8,128)(2,1)S(1)}, bf16[1024,768]{1,0:T(8,128)(2,1)}, u32[]{:S(2)}) copy-start(bf16[1024,768]{1,0:T(8,128)(2,1)} %get-tuple-element.214.refs_0_) | copy-start | bytes 4718596
  297.5 1.9 copy-start.27
  301.8 20.4 %copy-start.10 = (bf16[128,768]{1,0:T(8,128)(2,1)S(1)}, bf16[128,768]{1,0:T(8,128)(2,1)}, u32[]{:S(2)}) copy-start(bf16[128,768]{1,0:T(8,128)(2,1)} %get-tuple-element.231) | copy-start | bytes 589828
  301.9 20.4 %copy-start.14 = (bf16[2,128,768]{2,1,0:T(8,128)(2,1)S(1)}, bf16[2,128,768]{2,1,0:T(8,128)(2,1)}, u32[]{:S(2)}) copy-start(bf16[2,128,768]{2,1,0:T(8,128)(2,1)} %refs_6_.1) | copy-start | bytes 1179652
  323.0 44.0 %copy-start.30 = (bf16[1024,768]{1,0:T(8,128)(2,1)S(1)}, bf16[1024,768]{1,0:T(8,128)(2,1)}, u32[]{:S(2)}) copy-start(bf16[1024,768]{1,0:T(8,128)(2,1)} %get-tuple-element.247) | copy-start | bytes 4718596
  370.9 40.0 %copy-start.29 = (bf16[1024,768]{1,0:T(8,128)(2,1)S(1)}, bf16[1024,768]{1,0:T(8,128)(2,1)}, u32[]{:S(2)}) copy-start(bf16[1024,768]{1,0:T(8,128)(2,1)} %get-tuple-element.197.refs_4_) | copy-start | bytes 4718596
  410.9 4.0 copy-start.2
  410.9 4.0 copy-start.6
  455.1 36.1 %copy-start.24 = (f32[1,768]{1,0:T(1,128)S(1)}, f32[1,768]{1,0:T(1,128)}, u32[]{:S(2)}) copy-start(f32[1,768]{1,0:T(1,128)} %get-tuple-element.281) | copy-start | bytes 9220
  455.1 36.2 %copy-start.25 = (f32[1,768]{1,0:T(1,128)S(1)}, f32[1,768]{1,0:T(1,128)}, u32[]{:S(2)}) copy-start(f32[1,768]{1,0:T(1,128)} %get-tuple-element.282) | copy-start | bytes 9220
  455.1 36.3 %copy-start.23 = (f32[1,768]{1,0:T(1,128)S(1)}, f32[1,768]{1,0:T(1,128)}, u32[]{:S(2)}) copy-start(f32[1,768]{1,0:T(1,128)} %get-tuple-element.283) | copy-start | bytes 9220
  455.1 36.4 %copy-start.22 = (f32[1,768]{1,0:T(1,128)S(1)}, f32[1,768]{1,0:T(1,128)}, u32[]{:S(2)}) copy-start(f32[1,768]{1,0:T(1,128)} %get-tuple-element.284) | copy-start | bytes 9220
  455.1 36.5 %copy-start.16 = (f32[3,1,2048]{2,1,0:T(1,128)S(1)}, f32[3,1,2048]{2,1,0:T(1,128)}, u32[]{:S(2)}) copy-start(f32[3,1,2048]{2,1,0:T(1,128)} %get-tuple-element.286) | copy-start | bytes 73732
  455.1 36.5 %copy-start.17 = (f32[3,1,2048]{2,1,0:T(1,128)S(1)}, f32[3,1,2048]{2,1,0:T(1,128)}, u32[]{:S(2)}) copy-start(f32[3,1,2048]{2,1,0:T(1,128)} %get-tuple-element.285) | copy-start | bytes 73732
  491.3 27.0 %copy-start.9 = (f32[2,128,768]{2,1,0:T(8,128)S(1)}, f32[2,128,768]{2,1,0:T(8,128)}, u32[]{:S(2)}) copy-start(f32[2,128,768]{2,1,0:T(8,128)} %get-tuple-element.279) | copy-start | bytes 2359300
  518.3 2.0 copy-start.7
  518.3 2.0 copy-start.8
  539.7 8.3 %copy-start.18 = (f32[36,128]{1,0:T(8,128)S(1)}, f32[36,128]{1,0:T(8,128)}, u32[]{:S(2)}) copy-start(f32[36,128]{1,0:T(8,128)} %get-tuple-element.321) | copy-start | bytes 55300
  539.7 10.4 %copy-start.1 = (s32[2,8,20]{2,1,0:T(8,128)S(1)}, s32[2,8,20]{2,1,0:T(8,128)}, u32[]{:S(2)}) copy-start(s32[2,8,20]{2,1,0:T(8,128)} %param.30) | copy-start | bytes 3844

commit v6 on v5

--- a/solution.py
+++ b/solution.py
@@ -949,7 +949,7 @@
         self.left.finish()
 
 
-def stage(number, planes, stages, jobs=(), filler=None):
+def stage(number, planes, stages, jobs=(), filler=None, share=SHARE):
     operands = [v for st in stages for v in st.operands]
     outs = [v for st in stages for v in st.outs]
     scratch = [v for st in stages for v in st.scratch]
@@ -976,10 +976,10 @@
             st.first(met if n == 0 else (lambda: None))
         filler.prefetch()
         filler.begin()
-        filler.advance(SHARE[0])
+        filler.advance(share[0])
         for n, st in enumerate(stages):
-            st.second(lambda: filler.advance(SHARE[1]) if n == 0 else None)
-        filler.advance(SHARE[2])
+            st.second(lambda: filler.advance(share[1]) if n == 0 else None)
+        filler.advance(share[2])
         for st in stages:
             st.third()
         filler.advance(1.0)
@@ -1110,10 +1110,14 @@
         self.segq, self.segk = loads.pop(0).get(), loads.pop(0).get()
         self.bvec = loads.pop(0).get() if self.bias else None
 
+    def slot(self, h, b):
+        n = self.blocks // 2
+        return n * lax.rem(h + (b // n) * HQ, 2) + b % n
+
     def keep(self, h, b):
-        wide = pl.ds(0, self.width(b))
+        wide, slot = pl.ds(0, self.width(b)), self.slot(h, b)
         return pltpu.make_async_copy(
-            self.p_buf.at[b, :, wide], self.p_out.at[h, self.block(b), wide], self.sems.at[3 + b]
+            self.p_buf.at[slot, :, wide], self.p_out.at[h, self.block(b), wide], self.sems.at[3 + slot]
         )
 
     def one_block(self, h, b):
@@ -1136,7 +1140,8 @@
         top = jnp.max(s, axis=-1, keepdims=True)
         e = jnp.exp(s - top)
         p = (e * (1.0 / jnp.sum(e, axis=-1, keepdims=True))).astype(BF)
-        self.p_buf[b, :, :wide] = p
+        self.p_buf[self.slot(h, b), :, :wide] = p
+        self.keep(h, b).start()
         self.os[h, rows] = mm(p, self.vs[h, :wide]).astype(BF)
 
     def run(self, low, high):
@@ -1148,23 +1153,29 @@
                     row = jnp.broadcast_to(self.bvec[h], (self.chunk, 2 * self.keys))
                     self.toep[...] = pltpu.roll(row, 0, 1, stride=1, stride_axis=0)
 
-                @pl.when(h > 0)
+                @pl.when(h >= 2)
                 def _():
                     for b in blocks:
-                        self.keep(h - 1, b).wait()
+                        self.keep(h - 2, b).wait()
+
+                if half == 1:
+
+                    @pl.when(h < 2)
+                    def _():
+                        for b in range(self.blocks // 2):
+                            self.keep(h + 1, b).wait()
 
                 for b in blocks:
                     self.one_block(h, b)
-                for b in blocks:
-                    self.keep(h, b).start()
 
     def end(self):
         for i in range(HQ):
             self.att[:, DH * i : DH * (i + 1)] = self.os[i]
         out = pltpu.make_async_copy(self.att, self.att_out, self.sems.at[0])
         out.start()
-        for b in range(self.blocks):
-            self.keep(HQ - 1, b).wait()
+        for h in (HQ - 2, HQ - 1):
+            for b in range(self.blocks // 2, self.blocks):
+                self.keep(h, b).wait()
         out.wait()
         for copy in self.copies:
             copy.wait()
@@ -1327,6 +1338,40 @@
             copy.wait()
 
 
+class FeedForwardGrads:
+    n_steps = 6
+
+    def __init__(self, at_stage, act, x):
+        self.at_stage, self.loads, self.raws = at_stage, [act, x], []
+        self.outs = [jax.ShapeDtypeStruct((v.shape[1], D), BF) for v in (act, x)]
+        self.outs[1] = jax.ShapeDtypeStruct((x.shape[1], act.shape[1]), BF)
+        self.scratch = [pltpu.VMEM(o.shape, BF) for o in self.outs] + [pltpu.SemaphoreType.DMA((2,))]
+
+    def begin(self, loads, raws, outs, scratch):
+        self.left = [load.get() for load in loads]
+        self.right = [self.at_stage.left.rows.ref, self.at_stage.left.ref]
+        self.made, self.results, self.sems = scratch[:2], outs, scratch[2]
+
+    def run(self, low, high):
+        for n in range(2):
+            first, last = max(low - 3 * n, 0), min(high - 3 * n, 3)
+            if first < last:
+
+                @pl.loop(first, last)
+                def _(i):
+                    cols = pl.ds(pl.multiple_of(i * 256, 256), 256)
+                    self.made[n][cols] = mm_tn(self.left[n][:, cols], self.right[n][...]).astype(BF)
+
+    def end(self):
+        copies = [
+            pltpu.make_async_copy(self.made[n], self.results[n], self.sems.at[n]) for n in range(2)
+        ]
+        for copy in copies:
+            copy.start()
+        for copy in copies:
+            copy.wait()
+
+
 class Idle:
     n_steps, loads, raws, outs, scratch = 0, [], [], [], []
 
@@ -1587,11 +1632,9 @@
             over_planes(ffin_part(dec_ffin)),
             over_planes(ffout_part(dec_ffout)),
             swap_job(dec_cotan),
-        ]
-        + proj_jobs(cross_proj),
-    )
-    w_cq, w_ckv, w_dffin, w_dffout, xdc, *got = moved
-    w_cproj = proj_of(got, cross_proj)
+        ],
+    )
+    w_cq, w_ckv, w_dffin, w_dffout, xdc = moved
     w_cq, w_ckv = matrix(w_cq), matrix(w_ckv)
     xdc = joined(dec_cotan, xdc)
     products = None
@@ -1603,7 +1646,10 @@
         c_q = mm(c_n, w_cq).astype(BF)
         c_kv = spread(mm(e_gath, w_ckv).astype(BF))
     c_fill = AttentionForward(parts, c_q, c_kv, segq, segk, None, None, False, products)
-    (c_att, c_p, *made), (w_dffin,) = attend(5, planes, c_fill, [over_seq(w_dffin)])
+    (c_att, c_p, *made), (w_dffin, *got) = attend(
+        5, planes, c_fill, [over_seq(w_dffin)] + proj_jobs(cross_proj)
+    )
+    w_cproj = proj_of(got, cross_proj)
     if parts == 1:
         c_q, c_kv = made
     ((d_cross, d_fn),), (w_dffout, came, xec), _ = stage(
@@ -1672,45 +1718,35 @@
                 c.steps.pop(0)
         return got
 
-    k_dffout = chain(mm_tn(d_act, up_g).astype(BF), 0, True)
-    moving = [k_dffout]
-    ((up, up_rows, dg_dffn, pre_grad),), got, _ = stage(
-        8,
-        planes,
-        [
-            Stage(
-                [up_g, d_pre, w_dffout],
-                w_dffin,
-                xdc,
-                flip=True,
-                maker=FeedForwardBack,
-                back=(d_cross, g_dffn),
-                gather="low",
-            )
-        ],
-        steps_of(moving) + [swap_job(d_low)],
-    )
-    (came,) = settle(moving, got)
+    at = Stage(
+        [up_g, d_pre, w_dffout],
+        w_dffin,
+        xdc,
+        flip=True,
+        maker=FeedForwardBack,
+        back=(d_cross, g_dffn),
+        gather="low",
+    )
+    ((up, up_rows, dg_dffn, _),), (came,), made = stage(
+        8, planes, [at], [swap_job(d_low)], FeedForwardGrads(at, d_act, d_fn)
+    )
     dec_output = joined(d_low, came)
-    k_dffin = chain(mm_tn(d_fn, pre_grad).astype(BF), hidden, True)
+    k_dffout, k_dffin = chain(made[0], 0, True), chain(made[1], hidden, True)
     c_fill = AttentionBackward(
         parts, c_p, c_q, c_kv, up_rows, w_cproj, c_att, False, None, [c_n, e_gath]
     )
-    moving = [k_dffin, k_dffout]
+    moving = [k_dffout]
     (c_dq, c_dkv, g_cproj, *made), got = attend(9, planes, c_fill, steps_of(moving))
     settle(moving, got)
     c_dkv = collect(c_dkv)
     if parts > 1:
         made = [mm_tn(c_n, c_dq).astype(BF), mm_tn(e_gath, c_dkv).astype(BF)]
-    k_cproj, k_cq, k_ckv = proj_chain(g_cproj), chain(made[0], QC), chain(made[1], QC)
-    moving = [k_dffin, k_dffout, k_cq, k_ckv, k_cproj]
-    ((e_up, e_up_rows), (up, up_rows, dg_cross)), got, _ = stage(
+    k_cproj, k_cq, k_ckv = proj_chain(g_cproj), chain(made[0], QC, True), chain(made[1], QC, True)
+    moving = [k_dffout, k_cq, k_ckv, k_cproj]
+    ((up, up_rows, dg_cross),), got, _ = stage(
         10,
         planes,
-        [
-            Stage([c_dkv], w_ckv, xec, flip=True, gather="low"),
-            Stage([c_dq], w_cq, up, flip=True, back=(d_mid, g_cross), gather="low"),
-        ],
+        [Stage([c_dq], w_cq, up, flip=True, back=(d_mid, g_cross), gather="low")],
         steps_of(moving),
     )
     settle(moving, got)
@@ -1718,14 +1754,25 @@
     def self_grads(made, x):
         grad = joint_grad(made)
         g_rows = made.pop() if parts == 1 else mm_tn(x, grad).astype(BF)
-        return grad, chain(g_rows, QC), made
+        return grad, chain(g_rows, QC, True), made
 
     d_fill = AttentionBackward(
         parts, d_p, *d_qkv, up_rows, w_dproj, d_att, True, None, [dn], causal=True
     )
+    moving = [k_dffin, k_cq, k_ckv, k_cproj]
+    ((e_up, e_up_rows),), got, made = stage(
+        16,
+        planes,
+        [Stage([c_dkv], w_ckv, xec, flip=True, gather="low")],
+        steps_of(moving),
+        d_fill,
+    )
+    settle(moving, got)
+    d_rows_grad, k_dqkv, (d_dbv, g_dproj) = self_grads(made, dn)
+    k_dproj = proj_chain(g_dproj)
     k_effout = chain(mm_tn(e_act, e_up_rows).astype(BF), 0, True)
-    moving = [k_dffin, k_dffout, k_cq, k_ckv, k_cproj, k_effout]
-    ((e_up, e_up_rows, dg_effn, pre_grad),), got, made = stage(
+    moving = [k_dffin, k_dffout, k_cproj, k_dqkv, k_dproj, k_effout]
+    ((e_up, e_up_rows, dg_effn, pre_grad),), got, _ = stage(
         12,
         planes,
         [
@@ -1740,17 +1787,14 @@
             )
         ],
         steps_of(moving),
-        d_fill,
     )
     settle(moving, got)
-    d_rows_grad, k_dqkv, (d_dbv, g_dproj) = self_grads(made, dn)
-    k_dproj = proj_chain(g_dproj)
     k_effin = chain(mm_tn(e_fn, pre_grad).astype(BF), hidden)
     k_eproj = proj_chain(mm_tn(e_att, e_up_rows).astype(BF))
     e_fill = AttentionBackward(
         parts, e_p, *e_qkv, e_up_rows, w_eproj, e_att, True, mkv, [en], False
     )
-    moving += [k_dqkv, k_dproj, k_effin, k_eproj]
+    moving += [k_cq, k_ckv, k_effin, k_eproj]
     ((d_in, dg_dec, d_in_low),), got, made = stage(
         11,
         planes,

time: 558 us -> 538 us (0.964)
  Pallas kernels: 487 us -> 474 us
  matrix products: 21.4 us -> 14.6 us
    pallas_call x16 -> x17, Pallas kernels: 479 us -> 466 us  [call_with_jobs(): pl.pallas_call(body, out_shape=tuple(outs) + tuple((jax.ShapeDtypeStruct(...]
    dot_general x6 -> x4, matrix products: 17.9 us -> 11.1 us  [mm_tn(): lax.dot_general(a, b, (((0,), (0,)), ((), ())), preferred_element_type=F32)]
where the time goes in v6:
time: 538 us; the launch traced here: 530 us
  Pallas kernels  474 us (88%)
  other arithmetic  22.7 us (4%)
  local copies, waits for them, and re-layouts  17.6 us (3%)
  matrix products  14.6 us (3%)
    pallas_call x17, Pallas kernels, call_with_jobs(): pl.pallas_call(body, out_shape=tuple(outs) + tuple((jax.ShapeDtypeStruct(...  466 us
    dot_general x4, matrix products, mm_tn(): lax.dot_general(a, b, (((0,), (0,)), ((), ())), preferred_element_type=F32)  11.1 us
    another operation x16, other arithmetic, joined(): jnp.stack([jnp.where(first, mine, came), jnp.where(first, came, mine)])  10.8 us

profile of v6, /device:TPU:0, one launch (start us, length us, event | category | flops | bytes accessed | tf_op | source)
XLA Modules:
  0.0 530.3 jit_solution(9439718982553395392)
XLA Ops:
  0.7 0.7 convert_element_type.55
  1.4 0.7 convert_element_type.54
  2.1 0.7 convert_element_type.53
  4.0 0.7 select_add_fusion.refs_1_
  4.7 0.7 convert_element_type.57
  5.4 0.7 convert_element_type.56
  6.1 0.7 broadcast_select_fusion.refs_2_
  6.8 1.3 fusion.31
  8.1 0.7 pad_maximum_fusion.10.refs_3_
  8.8 0.9 fusion.34
  9.7 0.7 pad_maximum_fusion.14.refs_4_
  10.4 22.2 %ship.3 = (bf16[128,768]{1,0:T(8,128)(2,1)}, f32[4,5,192]{2,1,0:T(8,128)}, f32[4,2,8,12]{3,2,1,0:T(8,128)}, bf16[4,96,576]{2,1,0:T(8,128)(2,1)}, bf16[4,32,384]{...) custom-call(bf16[2,128,768]{2,1,0:T(8,128)(2,1)} %refs_0_.1, f32[5,192]{1,0:T(8,128)} %select_add_fusion.refs_1_, ...), custom_call_target="tpu_custom_call" | custom-call | bytes 8388608 | tf_op jit(solution)/shard_map/ship/pallas_call | solution.py:576
  32.6 1.0 fusion.20
  33.6 0.8 pad_maximum_fusion.2.refs_0_.refs_2_.refs_4_
  34.5 0.7 reshape_squeeze.21.refs_1_.refs_3_
  35.2 0.8 pad_maximum_fusion.3.refs_2_.refs_4_
  36.0 0.7 reshape_squeeze.22.refs_3_
  36.6 0.7 pad_maximum_fusion.11.refs_6_
  37.4 1.4 fusion.29
  38.8 0.8 pad_maximum_fusion.8.refs_7_
  39.6 24.7 %stage.11 = (bf16[1024,768]{1,0:T(8,128)(2,1)}, bf16[1024,768]{1,0:T(8,128)(2,1)}, bf16[4,2,96,576]{3,2,1,0:T(8,128)(2,1)}, bf16[4,2,32,384]{3,2,1,0:T(8,128)(2,...) custom-call(bf16[2,128,768]{2,1,0:T(8,128)(2,1)} %pad_maximum_fusion.2.refs_0_.refs_2_.refs_4_, ...), custom_call_target="tpu_custom_call" | custom-call | flops 2000000 | bytes 8388608 | tf_op jit(solution)/shard_map/stage/pallas_call | solution.py:576
  64.3 1.7 constant_dynamic-slice_fusion.1
  66.1 1.9 convolution_convert_fusion.4.refs_6_.refs_16_
  68.0 1.0 copy.52.refs_7_.refs_10_.refs_6_
  70.8 28.0 %attend.3 = (bf16[4,2,96,576]{3,2,1,0:T(8,128)(2,1)}, bf16[4,2,96,768]{3,2,1,0:T(8,128)(2,1)}, bf16[4,96,768]{2,1,0:T(8,128)(2,1)}, bf16[192,768]{1,0:T(8,128)(2...) custom-call(bf16[4,96,576]{2,1,0:T(8,128)(2,1)} %get-tuple-element.186.refs_0_, ...), custom_call_target="tpu_custom_call" | custom-call | flops 4000000000 | bytes 8388608 | tf_op jit(solution)/shard_map/attend/pallas_call | solution.py:576
  98.8 0.7 reshape_squeeze.24.refs_3_.refs_5_
  99.5 1.6 dynamic_slice.129.refs_5_
  101.1 1.0 fusion.33
  102.1 0.7 pad_maximum_fusion.12.refs_6_
  104.0 31.2 %stage.12 = (f32[2,128,768]{2,1,0:T(8,128)}, bf16[1024,768]{1,0:T(8,128)(2,1)}, bf16[4,2,96,768]{3,2,1,0:T(8,128)(2,1)}, bf16[4,96,192]{2,1,0:T(8,128)(2,1)}, bf...) custom-call(bf16[1024,192]{1,0:T(8,128)(2,1)} %get-tuple-element.193, ...), custom_call_target="tpu_custom_call" | custom-call | flops 2415919104 | bytes 8388608 | tf_op jit(solution)/shard_map/stage/pallas_call | solution.py:576
  135.2 0.7 reshape_squeeze.26.refs_3_
  135.9 0.8 pad_maximum_fusion.9.refs_10_
  136.6 48.5 %stage.13 = (f32[2,128,768]{2,1,0:T(8,128)}, bf16[1024,768]{1,0:T(8,128)(2,1)}, bf16[2,128,768]{2,1,0:T(8,128)(2,1)}, bf16[1024,768]{1,0:T(8,128)(2,1)}, f32[102...) custom-call(bf16[1024,192]{1,0:T(8,128)(2,1)} %get-tuple-element.198, ...), custom_call_target="tpu_custom_call" | custom-call | flops 4831838208 | bytes 8388608 | tf_op jit(solution)/shard_map/stage/pallas_call | solution.py:576
  185.2 16.4 %attend.4 = (bf16[4,2,96,768]{3,2,1,0:T(8,128)(2,1)}, bf16[192,768]{1,0:T(8,128)(2,1)}, bf16[1024,192]{1,0:T(8,128)(2,1)}, bf16[3,1024,1024]{2,1,0:T(8,128)(2,1)...) custom-call(bf16[4,96,768]{2,1,0:T(8,128)(2,1)} %get-tuple-element.207.refs_0_, bf16[192,768]{1,0:T(8,128)(2,1)} %refs_1_.1, ...), custom_call_target="tpu_custom_call" | custom-call | flops 4000000000 | bytes 8388608 | tf_op jit(solution)/shard_map/attend/pallas_call | solution.py:576
  201.6 0.7 reshape_squeeze.27.refs_3_.refs_5_
  202.3 26.6 %stage.14 = (f32[2,128,768]{2,1,0:T(8,128)}, bf16[1024,768]{1,0:T(8,128)(2,1)}, bf16[4,2,96,768]{3,2,1,0:T(8,128)(2,1)}, bf16[128,768]{1,0:T(8,128)(2,1)}, bf16[128,768]{1,0:T(8,128)(2,1)}) custom-call(bf16[1024,192]{1,0:T(8,128)(2,1)} %get-tuple-element.212.refs_0_.refs_5_, bf16[192,768]{1,0:T(8,128)(2,1)} %get-tuple-element.213.refs_1_.refs_4_, ...), custom_call_target="tpu_custom_call" | custom-call | flops 2415919104 | bytes 8388608 | tf_op jit(solution)/shard_map/stage/pallas_call | solution.py:576
  229.0 1.0 fusion.16
  230.0 0.8 pad_maximum_fusion.4
  230.8 0.8 pad_maximum_fusion.5.refs_4_
  231.6 23.1 %stage.15 = (bf16[2,128,768]{2,1,0:T(8,128)(2,1)}, bf16[1024,768]{1,0:T(8,128)(2,1)}, f32[1024,768]{1,0:T(8,128)}, bf16[1024,768]{1,0:T(8,128)(2,1)}) custom-call(bf16[1024,768]{1,0:T(8,128)(2,1)} %get-tuple-element.217.refs_0_.refs_9_, bf16[768,768]{1,0:T(8,128)(2,1)} %bitcast.129, bf16[768,768]{1,0:T(8,128)(2,1)} %bitcast.132, ...), custom_call_target="tpu_custom_call" | custom-call | flops 2415919104 | bytes 8388608 | tf_op jit(solution)/shard_map/stage/pallas_call | solution.py:576
  254.7 29.1 %stage.16 = (f32[2,128,768]{2,1,0:T(8,128)}, bf16[1024,768]{1,0:T(8,128)(2,1)}, f32[1,768]{1,0:T(1,128)}, bf16[1024,768]{1,0:T(8,128)(2,1)}, bf16[128,768]{1,0:T...) custom-call(bf16[1024,768]{1,0:T(8,128)(2,1)} %get-tuple-element.223.refs_0_, ...), custom_call_target="tpu_custom_call" | custom-call | flops 2415919104 | bytes 8388608 | tf_op jit(solution)/shard_map/stage/pallas_call | solution.py:576
  283.8 1.0 fusion.12
  284.8 0.8 pad_maximum_fusion.6
  285.6 19.8 %attend.5 = (bf16[4,96,768]{2,1,0:T(8,128)(2,1)}, bf16[1024,192]{1,0:T(8,128)(2,1)}, bf16[1024,384]{1,0:T(8,128)(2,1)}, bf16[192,768]{1,0:T(8,128)(2,1)}, bf16[7...) custom-call(bf16[4,2,96,768]{3,2,1,0:T(8,128)(2,1)} %bitcast.154, bf16[1024,192]{1,0:T(8,128)(2,1)} %get-tuple-element.228.refs_1_, ...), custom_call_target="tpu_custom_call" | custom-call | flops 4000000000 | bytes 8388608 | tf_op jit(solution)/shard_map/attend/pallas_call | solution.py:576
  305.5 0.8 pad_maximum_fusion.7.refs_2_
  306.3 25.2 %stage.17 = (f32[2,128,768]{2,1,0:T(8,128)}, bf16[1024,768]{1,0:T(8,128)(2,1)}, f32[1,768]{1,0:T(1,128)}, bf16[96,768]{1,0:T(8,128)(2,1)}, bf16[4,96,192]{2,1,0:...) custom-call(bf16[1024,192]{1,0:T(8,128)(2,1)} %get-tuple-element.235.refs_0_, ...), custom_call_target="tpu_custom_call" | custom-call | flops 2415919104 | bytes 8388608 | tf_op jit(solution)/shard_map/stage/pallas_call | solution.py:576
  331.5 33.0 %stage.18 = (f32[2,128,768]{2,1,0:T(8,128)}, bf16[1024,768]{1,0:T(8,128)(2,1)}, bf16[4,96,768]{2,1,0:T(8,128)(2,1)}, bf16[96,192]{1,0:T(8,128)(2,1)}, bf16[96,38...) custom-call(bf16[1024,384]{1,0:T(8,128)(2,1)} %get-tuple-element.232, ...), custom_call_target="tpu_custom_call" | custom-call | flops 2415919104 | bytes 8388608 | tf_op jit(solution)/shard_map/stage/pallas_call | solution.py:576
  364.4 3.9 convolution_convert_fusion.1
  368.3 37.9 %stage.19 = (f32[2,128,768]{2,1,0:T(8,128)}, bf16[1024,768]{1,0:T(8,128)(2,1)}, f32[1,768]{1,0:T(1,128)}, bf16[1024,768]{1,0:T(8,128)(2,1)}, bf16[96,768]{1,0:T(...) custom-call(bf16[1024,768]{1,0:T(8,128)(2,1)} %get-tuple-element.249, ...), custom_call_target="tpu_custom_call" | custom-call | flops 2415919104 | bytes 8388608 | tf_op jit(solution)/shard_map/stage/pallas_call | solution.py:576
  406.2 4.0 convolution_convert_fusion
  410.2 1.2 convolution_convert_fusion.2
  411.5 33.5 %stage.20 = (f32[2,128,768]{2,1,0:T(8,128)}, f32[1,768]{1,0:T(1,128)}, bf16[2,128,768]{2,1,0:T(8,128)(2,1)}, bf16[2,96,768]{2,1,0:T(8,128)(2,1)}, bf16[2,2,96,76...) custom-call(bf16[1024,576]{1,0:T(8,128)(2,1)} %get-tuple-element.247, ...), custom_call_target="tpu_custom_call" | custom-call | flops 2415919104 | bytes 8388608 | tf_op jit(solution)/shard_map/stage/pallas_call | solution.py:576
  444.9 2.0 convolution_convert_fusion.3
  446.9 29.4 %stage.21 = (f32[2,128,768]{2,1,0:T(8,128)}, f32[1,768]{1,0:T(1,128)}, bf16[2,128,768]{2,1,0:T(8,128)(2,1)}, bf16[2,2,96,768]{3,2,1,0:T(8,128)(2,1)}, bf16[2,2,2...) custom-call(bf16[1024,576]{1,0:T(8,128)(2,1)} %get-tuple-element.270, ...), custom_call_target="tpu_custom_call" | custom-call | flops 2415919104 | bytes 8388608 | tf_op jit(solution)/shard_map/stage/pallas_call | solution.py:576
  476.4 0.7 reduce.5
  479.5 22.1 %ship.4 = (f32[36,128]{1,0:T(8,128)}, bf16[128,768]{1,0:T(8,128)(2,1)}, bf16[2,2,2,96,768]{4,3,2,1,0:T(8,128)(2,1)}, bf16[2,2,2,48,384]{4,3,2,1,0:T(8,128)(2,1)}...) custom-call(f32[36,128]{1,0:T(8,128)} %reshape.276.refs_0_, ...), custom_call_target="tpu_custom_call" | custom-call | bytes 8388608 | tf_op jit(solution)/shard_map/ship/pallas_call | solution.py:576
  501.6 1.1 fusion.6
  502.7 0.9 pad_maximum_fusion
  503.7 0.9 pad_maximum_fusion.1
  504.6 14.8 %ship.5 = (f32[36,128]{1,0:T(8,128)}, bf16[2,2,2,96,576]{4,3,2,1,0:T(8,128)(2,1)}, bf16[2,2,2,96,768]{4,3,2,1,0:T(8,128)(2,1)}, bf16[2,2,2,48,384]{4,3,2,1,0:T(8...) custom-call(f32[36,128]{1,0:T(8,128)} %get-tuple-element.311.refs_0_, ...), custom_call_target="tpu_custom_call" | custom-call | bytes 8388608 | tf_op jit(solution)/shard_map/ship/pallas_call | solution.py:576
  519.5 8.2 %lay_out.1 = (f32[192,3072]{1,0:T(8,128)}, f32[768,768]{1,0:T(8,128)}, f32[192,3072]{1,0:T(8,128)}, f32[768,768]{1,0:T(8,128)}, f32[192,768]{1,0:T(8,128)}, /*in...) custom-call(bf16[2,2,2,96,768]{4,3,2,1,0:T(8,128)(2,1)} %get-tuple-e, ...), custom_call_target="tpu_custom_call" | custom-call | tf_op jit(solution)/shard_map/lay_out/pallas_call | solution.py:486
  527.7 0.7 fusion.35
  528.5 0.7 reshape.278
  529.2 0.7 reshape.279
  (106 shorter events, 7.2 us)
Async XLA Ops:
  0.7 65.3 %copy-start = (s32[2,8,20]{2,1,0:T(8,128)S(1)}, s32[2,8,20]{2,1,0:T(8,128)}, u32[]{:S(2)}) copy-start(s32[2,8,20]{2,1,0:T(8,128)} %param.30) | copy-start | bytes 3844
  0.7 31.9 %copy-start.4 = (bf16[2,128,768]{2,1,0:T(8,128)(2,1)S(1)}, bf16[2,128,768]{2,1,0:T(8,128)(2,1)}, u32[]{:S(2)}) copy-start(bf16[2,128,768]{2,1,0:T(8,128)(2,1)} %refs_0_.1) | copy-start | bytes 1179652
  8.1 27.1 %copy-start.5 = (bf16[2,128,768]{2,1,0:T(8,128)(2,1)S(1)}, bf16[2,128,768]{2,1,0:T(8,128)(2,1)}, u32[]{:S(2)}) copy-start(bf16[2,128,768]{2,1,0:T(8,128)(2,1)} %refs_5_.1) | copy-start | bytes 1179652
  32.6 1.8 copy-start.20
  32.6 2.6 copy-start.12
  38.8 29.2 %copy-start.19 = (s32[8,1,128]{2,1,0:T(1,128)S(1)}, s32[8,1,128]{2,1,0:T(1,128)}, u32[]{:S(2)}) copy-start(s32[8,1,128]{2,1,0:T(1,128)} %get-tuple-element.191) | copy-start | bytes 12292
  39.6 29.4 %copy-start.26 = (s32[1,256]{1,0:T(1,128)S(1)}, s32[1,256]{1,0:T(1,128)}, u32[]{:S(2)}) copy-start(s32[1,256]{1,0:T(1,128)} %constant.301) | copy-start | bytes 3076
  39.6 30.0 %copy-start.21 = (f32[4,2,8,12]{3,2,1,0:T(8,128)S(1)}, f32[4,2,8,12]{3,2,1,0:T(8,128)}, u32[]{:S(2)}) copy-start(f32[4,2,8,12]{3,2,1,0:T(8,128)} %get-tuple-element.192) | copy-start | bytes 9220
  39.6 30.0 %copy-start.27 = (s32[2048]{0:T(1024)S(1)}, s32[2048]{0:T(1024)}, u32[]{:S(2)}) copy-start(s32[2048]{0:T(1024)} %param.31) | copy-start | bytes 24580
  202.3 26.7 %copy-start.15 = (bf16[2,128,768]{2,1,0:T(8,128)(2,1)S(1)}, bf16[2,128,768]{2,1,0:T(8,128)(2,1)}, u32[]{:S(2)}) copy-start(bf16[2,128,768]{2,1,0:T(8,128)(2,1)} %get-tuple-element.206.refs_5_) | copy-start | bytes 1179652
  228.9 1.8 copy-start.11
  228.9 1.8 copy-start.13
  254.7 29.1 %copy-start.3 = (bf16[2,128,768]{2,1,0:T(8,128)(2,1)S(1)}, bf16[2,128,768]{2,1,0:T(8,128)(2,1)}, u32[]{:S(2)}) copy-start(bf16[2,128,768]{2,1,0:T(8,128)(2,1)} %get-tuple-element.222.refs_7_) | copy-start | bytes 1179652
  285.6 19.8 %copy-start.10 = (bf16[128,768]{1,0:T(8,128)(2,1)S(1)}, bf16[128,768]{1,0:T(8,128)(2,1)}, u32[]{:S(2)}) copy-start(bf16[128,768]{1,0:T(8,128)(2,1)} %get-tuple-element.233) | copy-start | bytes 589828
  285.6 19.8 %copy-start.14 = (bf16[2,128,768]{2,1,0:T(8,128)(2,1)S(1)}, bf16[2,128,768]{2,1,0:T(8,128)(2,1)}, u32[]{:S(2)}) copy-start(bf16[2,128,768]{2,1,0:T(8,128)(2,1)} %refs_6_.1) | copy-start | bytes 1179652
  331.5 33.0 %copy-start.29 = (bf16[1024,768]{1,0:T(8,128)(2,1)S(1)}, bf16[1024,768]{1,0:T(8,128)(2,1)}, u32[]{:S(2)}) copy-start(bf16[1024,768]{1,0:T(8,128)(2,1)} %get-tuple-element.257) | copy-start | bytes 4718596
  368.3 37.9 %copy-start.28 = (bf16[1024,768]{1,0:T(8,128)(2,1)S(1)}, bf16[1024,768]{1,0:T(8,128)(2,1)}, u32[]{:S(2)}) copy-start(bf16[1024,768]{1,0:T(8,128)(2,1)} %get-tuple-element.200.refs_4_) | copy-start | bytes 4718596
  406.2 4.0 copy-start.2
  406.2 4.0 copy-start.6
  446.9 30.2 %copy-start.24 = (f32[1,768]{1,0:T(1,128)S(1)}, f32[1,768]{1,0:T(1,128)}, u32[]{:S(2)}) copy-start(f32[1,768]{1,0:T(1,128)} %get-tuple-element.287) | copy-start | bytes 9220
  446.9 30.3 %copy-start.25 = (f32[1,768]{1,0:T(1,128)S(1)}, f32[1,768]{1,0:T(1,128)}, u32[]{:S(2)}) copy-start(f32[1,768]{1,0:T(1,128)} %get-tuple-element.288) | copy-start | bytes 9220
  446.9 30.4 %copy-start.23 = (f32[1,768]{1,0:T(1,128)S(1)}, f32[1,768]{1,0:T(1,128)}, u32[]{:S(2)}) copy-start(f32[1,768]{1,0:T(1,128)} %get-tuple-element.289) | copy-start | bytes 9220
  446.9 30.5 %copy-start.22 = (f32[1,768]{1,0:T(1,128)S(1)}, f32[1,768]{1,0:T(1,128)}, u32[]{:S(2)}) copy-start(f32[1,768]{1,0:T(1,128)} %get-tuple-element.290) | copy-start | bytes 9220
  446.9 30.6 %copy-start.16 = (f32[3,1,2048]{2,1,0:T(1,128)S(1)}, f32[3,1,2048]{2,1,0:T(1,128)}, u32[]{:S(2)}) copy-start(f32[3,1,2048]{2,1,0:T(1,128)} %get-tuple-element.292) | copy-start | bytes 73732
  446.9 30.6 %copy-start.17 = (f32[3,1,2048]{2,1,0:T(1,128)S(1)}, f32[3,1,2048]{2,1,0:T(1,128)}, u32[]{:S(2)}) copy-start(f32[3,1,2048]{2,1,0:T(1,128)} %get-tuple-element.291) | copy-start | bytes 73732
  478.7 22.8 %copy-start.9 = (f32[2,128,768]{2,1,0:T(8,128)S(1)}, f32[2,128,768]{2,1,0:T(8,128)}, u32[]{:S(2)}) copy-start(f32[2,128,768]{2,1,0:T(8,128)} %get-tuple-element.285) | copy-start | bytes 2359300
  501.6 2.0 copy-start.7
  501.6 2.0 copy-start.8
  519.4 8.3 %copy-start.18 = (f32[36,128]{1,0:T(8,128)S(1)}, f32[36,128]{1,0:T(8,128)}, u32[]{:S(2)}) copy-start(f32[36,128]{1,0:T(8,128)} %get-tuple-element.327) | copy-start | bytes 55300
  519.4 10.4 %copy-start.1 = (s32[2,8,20]{2,1,0:T(8,128)S(1)}, s32[2,8,20]{2,1,0:T(8,128)}, u32[]{:S(2)}) copy-start(s32[2,8,20]{2,1,0:T(8,128)} %param.30) | copy-start | bytes 3844

commit v7 on v6

--- a/solution.py
+++ b/solution.py
@@ -1401,6 +1401,26 @@
     return made, moved
 
 
+def stacked(gains, rels):
+    n = len(gains)
+
+    def body(*refs):
+        rows, table = refs[-2:]
+        for i in range(n):
+            rows[i : i + 1] = refs[i][...].astype(F32).reshape(1, -1)
+        for i in range(len(rels)):
+            table[i] = refs[n + i][...].astype(F32)
+
+    return pl.pallas_call(
+        body,
+        out_shape=(
+            jax.ShapeDtypeStruct((n, gains[0].shape[0]), F32),
+            jax.ShapeDtypeStruct((len(rels),) + rels[0].shape, F32),
+        ),
+        name="stacked",
+    )(*gains, *rels)
+
+
 class Chain:
     def __init__(self, value, steps, width):
         self.value, self.steps, self.width = value, steps, width
@@ -1486,10 +1506,7 @@
         return w.reshape(-1, w.shape[-1])
 
     gains = (enc_gain, enc_ffnorm, dec_gain, cross_gain, dec_ffnorm)
-    which = jnp.arange(len(gains), dtype=jnp.int32)[:, None]
-    gain_stack = sum(jnp.where(which == i, v.astype(F32)[None], 0.0) for i, v in enumerate(gains))
-    which = jnp.arange(2, dtype=jnp.int32)[:, None, None]
-    rel_stack = jnp.where(which == 0, enc_rel.astype(F32)[None], dec_rel.astype(F32)[None])
+    gain_stack, rel_stack = stacked(gains, (enc_rel, dec_rel))
     segments = segments.reshape(2, 1, chunk)
     first_jobs = [
         swap_job(enc_input),
@@ -1591,22 +1608,23 @@
         return got[0], got[1], rows or (got[2], got[2])
 
     e_fill, e_qkv = self_fill(en, w_eqkv, segk_mem, bias_vector(rels[0]), mkv, False)
-    made, (w_dqkv, w_effin, w_effout, *got) = attend(
+    made, (w_dqkv, w_effout, *got) = attend(
         2,
         planes,
         e_fill,
-        [over_seq(w_dqkv), over_seq(w_effin), over_planes(ffout_part(enc_ffout))]
+        [over_seq(w_dqkv), over_planes(ffout_part(enc_ffout))]
         + proj_jobs(enc_proj),
     )
     e_att, e_p, e_qkv = self_made(made, e_qkv)
     w_eproj = proj_of(got, enc_proj)
-    w_dqkv, w_effin = matrix(w_dqkv), matrix(w_effin)
+    w_dqkv = matrix(w_dqkv)
     d_fill, d_qkv = self_fill(dn, w_dqkv, segk, bias_vector(rels[1]), None, True)
-    ((e_mid, e_fn),), (w_effout, w_cq, w_ckv, *got), made = stage(
+    ((e_mid, e_fn),), (w_effin, w_effout, w_cq, w_ckv, *got), made = stage(
         3,
         planes,
         [Stage([e_att], w_eproj, xe, gather="norm", gain=g_effn)],
         [
+            over_seq(w_effin),
             over_seq(w_effout),
             over_planes(qkv_part(cross_query)),
             over_planes(qkv_part(cross_kv)),
@@ -1616,7 +1634,7 @@
     )
     d_att, d_p, d_qkv = self_made(made, d_qkv)
     w_dproj = proj_of(got, dec_proj)
-    w_effout = matrix(w_effout)
+    w_effin, w_effout = matrix(w_effin), matrix(w_effout)
     ((d_mid, c_n), (e_low, e_gath, e_pre, e_act)), moved, _ = stage(
         4,
         planes,
@@ -1771,7 +1789,7 @@
     d_rows_grad, k_dqkv, (d_dbv, g_dproj) = self_grads(made, dn)
     k_dproj = proj_chain(g_dproj)
     k_effout = chain(mm_tn(e_act, e_up_rows).astype(BF), 0, True)
-    moving = [k_dffin, k_dffout, k_cproj, k_dqkv, k_dproj, k_effout]
+    moving = [k_dffin, k_dffout, k_cproj, k_dqkv, k_effout]
     ((e_up, e_up_rows, dg_effn, pre_grad),), got, _ = stage(
         12,
         planes,
@@ -1794,7 +1812,7 @@
     e_fill = AttentionBackward(
         parts, e_p, *e_qkv, e_up_rows, w_eproj, e_att, True, mkv, [en], False
     )
-    moving += [k_cq, k_ckv, k_effin, k_eproj]
+    moving += [k_cq, k_ckv, k_dproj, k_effin, k_eproj]
     ((d_in, dg_dec, d_in_low),), got, made = stage(
         11,
         planes,
@@ -1810,10 +1828,9 @@
         13,
         planes,
         [Stage([e_rows_grad], w_eqkv, e_up, flip=True, back=(xe, g_enc), low=True)],
-        steps_of(moving) + [swap_job(d_in_low)],
-    )
-    (came,) = settle(moving, got)
-    dec_ingrad = joined(d_in, came)
+        steps_of(moving),
+    )
+    settle(moving, got)
 
     def rel_grads(*dbvs):
         own = lax.dot_general(
@@ -1835,12 +1852,13 @@
     if parts > 1:
         tiny = lax.psum(tiny, "part")
     hurry(moving)
-    tiny, came, *got = ship(
+    tiny, came, d_came, *got = ship(
         14,
         planes,
-        [total_job("fsdp", tiny, planes), swap_job(e_in_low)] + steps_of(moving),
-    )
-    enc_ingrad = joined(e_in, came)
+        [total_job("fsdp", tiny, planes), swap_job(e_in_low), swap_job(d_in_low)]
+        + steps_of(moving),
+    )
+    enc_ingrad, dec_ingrad = joined(e_in, came), joined(d_in, d_came)
     settle(moving, got)
     hurry(moving)
     tiny, *got = ship(15, planes, [spread_job(tiny, True)] + steps_of(moving))

time: 538 us -> 532 us (0.989)
  other arithmetic: 22.7 us -> 16.6 us
where the time goes in v7:
time: 532 us; the launch traced here: 525 us
  Pallas kernels  474 us (89%)
  local copies, waits for them, and re-layouts  17.6 us (3%)
  other arithmetic  16.6 us (3%)
  matrix products  14.6 us (3%)
    pallas_call x17, Pallas kernels, call_with_jobs(): pl.pallas_call(body, out_shape=tuple(outs) + tuple((jax.ShapeDtypeStruct(...  464 us
    dot_general x4, matrix products, mm_tn(): lax.dot_general(a, b, (((0,), (0,)), ((), ())), preferred_element_type=F32)  11.1 us
    another operation x16, other arithmetic, joined(): jnp.stack([jnp.where(first, mine, came), jnp.where(first, came, mine)])  10.8 us

profile of v7, /device:TPU:0, one launch (start us, length us, event | category | flops | bytes accessed | tf_op | source)
XLA Modules:
  0.0 524.6 jit_solution(161680741291493695)
XLA Ops:
  0.7 1.4 stacked.1
  2.1 1.3 fusion.31
  3.4 0.7 pad_maximum_fusion.10.refs_3_
  4.2 0.9 fusion.34
  5.0 0.7 pad_maximum_fusion.14.refs_4_
  5.7 22.2 %ship.3 = (bf16[128,768]{1,0:T(8,128)(2,1)}, f32[4,5,192]{2,1,0:T(8,128)}, f32[4,2,8,12]{3,2,1,0:T(8,128)}, bf16[4,96,576]{2,1,0:T(8,128)(2,1)}, bf16[4,32,384]{...) custom-call(bf16[2,128,768]{2,1,0:T(8,128)(2,1)} %refs_0_.3, f32[5,192]{1,0:T(8,128)} %get-tuple-element.183.refs_1_, ...), custom_call_target="tpu_custom_call" | custom-call | bytes 8388608 | tf_op jit(solution)/shard_map/ship/pallas_call | solution.py:576
  28.0 1.0 fusion.20
  29.0 0.8 pad_maximum_fusion.2.refs_0_.refs_2_.refs_4_
  29.8 0.7 reshape_squeeze.21.refs_1_.refs_3_
  30.5 0.8 pad_maximum_fusion.3.refs_2_.refs_4_
  31.3 0.7 reshape_squeeze.22.refs_3_
  32.0 0.7 pad_maximum_fusion.11.refs_6_
  32.7 1.4 fusion.29
  34.2 0.8 pad_maximum_fusion.8.refs_7_
  34.9 24.7 %stage.11 = (bf16[1024,768]{1,0:T(8,128)(2,1)}, bf16[1024,768]{1,0:T(8,128)(2,1)}, bf16[4,2,96,576]{3,2,1,0:T(8,128)(2,1)}, bf16[4,2,32,384]{3,2,1,0:T(8,128)(2,...) custom-call(bf16[2,128,768]{2,1,0:T(8,128)(2,1)} %pad_maximum_fusion.2.refs_0_.refs_2_.refs_4_, ...), custom_call_target="tpu_custom_call" | custom-call | flops 2000000 | bytes 8388608 | tf_op jit(solution)/shard_map/stage/pallas_call | solution.py:576
  59.6 1.7 constant_dynamic-slice_fusion.1
  61.5 1.9 convolution_convert_fusion.4.refs_5_.refs_16_
  63.3 1.0 copy.52.refs_6_.refs_11_
  64.4 0.6 pad_add_fusion.refs_7_
  65.0 0.5 fusion.2
  65.5 0.6 reshape.212.refs_8_
  66.2 22.6 %attend.3 = (bf16[4,2,96,576]{3,2,1,0:T(8,128)(2,1)}, bf16[4,96,768]{2,1,0:T(8,128)(2,1)}, bf16[192,768]{1,0:T(8,128)(2,1)}, bf16[1024,192]{1,0:T(8,128)(2,1)}, ...) custom-call(bf16[4,96,576]{2,1,0:T(8,128)(2,1)} %get-tuple-element.190.refs_0_, ...), custom_call_target="tpu_custom_call" | custom-call | flops 4000000000 | bytes 8388608 | tf_op jit(solution)/shard_map/attend/pallas_call | solution.py:576
  88.8 0.7 reshape_squeeze.24.refs_3_.refs_5_
  89.4 1.6 dynamic_slice.129.refs_6_
  91.0 1.0 fusion.33
  92.1 0.7 pad_maximum_fusion.12.refs_7_
  93.3 0.6 reshape.214.refs_13_
  93.9 36.7 %stage.12 = (f32[2,128,768]{2,1,0:T(8,128)}, bf16[1024,768]{1,0:T(8,128)(2,1)}, bf16[4,2,96,768]{3,2,1,0:T(8,128)(2,1)}, bf16[4,2,96,768]{3,2,1,0:T(8,128)(2,1)}...) custom-call(bf16[1024,192]{1,0:T(8,128)(2,1)} %get-tuple-element.196, ...), custom_call_target="tpu_custom_call" | custom-call | flops 2415919104 | bytes 8388608 | tf_op jit(solution)/shard_map/stage/pallas_call | solution.py:576
  130.6 0.7 reshape_squeeze.26.refs_3_
  131.3 0.8 pad_maximum_fusion.9.refs_10_
  132.1 48.5 %stage.13 = (f32[2,128,768]{2,1,0:T(8,128)}, bf16[1024,768]{1,0:T(8,128)(2,1)}, bf16[2,128,768]{2,1,0:T(8,128)(2,1)}, bf16[1024,768]{1,0:T(8,128)(2,1)}, f32[102...) custom-call(bf16[1024,192]{1,0:T(8,128)(2,1)} %get-tuple-element.202, ...), custom_call_target="tpu_custom_call" | custom-call | flops 4831838208 | bytes 8388608 | tf_op jit(solution)/shard_map/stage/pallas_call | solution.py:576
  180.6 16.4 %attend.4 = (bf16[4,2,96,768]{3,2,1,0:T(8,128)(2,1)}, bf16[192,768]{1,0:T(8,128)(2,1)}, bf16[1024,192]{1,0:T(8,128)(2,1)}, bf16[3,1024,1024]{2,1,0:T(8,128)(2,1)...) custom-call(bf16[4,96,768]{2,1,0:T(8,128)(2,1)} %get-tuple-element.211.refs_0_, bf16[192,768]{1,0:T(8,128)(2,1)} %refs_1_.3, ...), custom_call_target="tpu_custom_call" | custom-call | flops 4000000000 | bytes 8388608 | tf_op jit(solution)/shard_map/attend/pallas_call | solution.py:576
  197.0 0.7 reshape_squeeze.27.refs_3_.refs_5_
  197.7 26.6 %stage.14 = (f32[2,128,768]{2,1,0:T(8,128)}, bf16[1024,768]{1,0:T(8,128)(2,1)}, bf16[4,2,96,768]{3,2,1,0:T(8,128)(2,1)}, bf16[128,768]{1,0:T(8,128)(2,1)}, bf16[128,768]{1,0:T(8,128)(2,1)}) custom-call(bf16[1024,192]{1,0:T(8,128)(2,1)} %get-tuple-element.216.refs_0_.refs_5_, bf16[192,768]{1,0:T(8,128)(2,1)} %get-tuple-element.217.refs_1_.refs_4_, ...), custom_call_target="tpu_custom_call" | custom-call | flops 2415919104 | bytes 8388608 | tf_op jit(solution)/shard_map/stage/pallas_call | solution.py:576
  224.3 1.0 fusion.16
  225.4 0.8 pad_maximum_fusion.4
  226.2 0.8 pad_maximum_fusion.5.refs_4_
  227.0 23.1 %stage.15 = (bf16[2,128,768]{2,1,0:T(8,128)(2,1)}, bf16[1024,768]{1,0:T(8,128)(2,1)}, f32[1024,768]{1,0:T(8,128)}, bf16[1024,768]{1,0:T(8,128)(2,1)}) custom-call(bf16[1024,768]{1,0:T(8,128)(2,1)} %get-tuple-element.221.refs_0_.refs_9_, bf16[768,768]{1,0:T(8,128)(2,1)} %bitcast.129, bf16[768,768]{1,0:T(8,128)(2,1)} %bitcast.132, ...), custom_call_target="tpu_custom_call" | custom-call | flops 2415919104 | bytes 8388608 | tf_op jit(solution)/shard_map/stage/pallas_call | solution.py:576
  250.1 28.9 %stage.16 = (f32[2,128,768]{2,1,0:T(8,128)}, bf16[1024,768]{1,0:T(8,128)(2,1)}, f32[1,768]{1,0:T(1,128)}, bf16[1024,768]{1,0:T(8,128)(2,1)}, bf16[128,768]{1,0:T...) custom-call(bf16[1024,768]{1,0:T(8,128)(2,1)} %get-tuple-element.227.refs_0_, ...), custom_call_target="tpu_custom_call" | custom-call | flops 2415919104 | bytes 8388608 | tf_op jit(solution)/shard_map/stage/pallas_call | solution.py:576
  279.0 1.0 fusion.12
  280.0 0.8 pad_maximum_fusion.6
  280.8 20.0 %attend.5 = (bf16[4,96,768]{2,1,0:T(8,128)(2,1)}, bf16[1024,192]{1,0:T(8,128)(2,1)}, bf16[1024,384]{1,0:T(8,128)(2,1)}, bf16[192,768]{1,0:T(8,128)(2,1)}, bf16[7...) custom-call(bf16[4,2,96,768]{3,2,1,0:T(8,128)(2,1)} %bitcast.154, bf16[1024,192]{1,0:T(8,128)(2,1)} %get-tuple-element.232.refs_1_, ...), custom_call_target="tpu_custom_call" | custom-call | flops 4000000000 | bytes 8388608 | tf_op jit(solution)/shard_map/attend/pallas_call | solution.py:576
  300.9 0.8 pad_maximum_fusion.7.refs_2_
  301.7 25.3 %stage.17 = (f32[2,128,768]{2,1,0:T(8,128)}, bf16[1024,768]{1,0:T(8,128)(2,1)}, f32[1,768]{1,0:T(1,128)}, bf16[96,768]{1,0:T(8,128)(2,1)}, bf16[4,96,192]{2,1,0:...) custom-call(bf16[1024,192]{1,0:T(8,128)(2,1)} %get-tuple-element.239.refs_0_, ...), custom_call_target="tpu_custom_call" | custom-call | flops 2415919104 | bytes 8388608 | tf_op jit(solution)/shard_map/stage/pallas_call | solution.py:576
  327.0 32.8 %stage.18 = (f32[2,128,768]{2,1,0:T(8,128)}, bf16[1024,768]{1,0:T(8,128)(2,1)}, bf16[4,96,768]{2,1,0:T(8,128)(2,1)}, bf16[96,192]{1,0:T(8,128)(2,1)}, bf16[96,38...) custom-call(bf16[1024,384]{1,0:T(8,128)(2,1)} %get-tuple-element.236, ...), custom_call_target="tpu_custom_call" | custom-call | flops 2415919104 | bytes 8388608 | tf_op jit(solution)/shard_map/stage/pallas_call | solution.py:576
  359.9 3.9 convolution_convert_fusion.1
  363.7 34.8 %stage.19 = (f32[2,128,768]{2,1,0:T(8,128)}, bf16[1024,768]{1,0:T(8,128)(2,1)}, f32[1,768]{1,0:T(1,128)}, bf16[1024,768]{1,0:T(8,128)(2,1)}, bf16[96,768]{1,0:T(...) custom-call(bf16[1024,768]{1,0:T(8,128)(2,1)} %get-tuple-element.253, ...), custom_call_target="tpu_custom_call" | custom-call | flops 2415919104 | bytes 8388608 | tf_op jit(solution)/shard_map/stage/pallas_call | solution.py:576
  398.5 4.0 convolution_convert_fusion
  402.6 1.2 convolution_convert_fusion.2
  403.8 33.5 %stage.20 = (f32[2,128,768]{2,1,0:T(8,128)}, f32[1,768]{1,0:T(1,128)}, bf16[2,128,768]{2,1,0:T(8,128)(2,1)}, bf16[2,96,768]{2,1,0:T(8,128)(2,1)}, bf16[2,2,96,76...) custom-call(bf16[1024,576]{1,0:T(8,128)(2,1)} %get-tuple-element.251, ...), custom_call_target="tpu_custom_call" | custom-call | flops 2415919104 | bytes 8388608 | tf_op jit(solution)/shard_map/stage/pallas_call | solution.py:576
  437.3 2.0 convolution_convert_fusion.3
  439.2 27.3 %stage.21 = (f32[2,128,768]{2,1,0:T(8,128)}, f32[1,768]{1,0:T(1,128)}, bf16[2,128,768]{2,1,0:T(8,128)(2,1)}, bf16[2,2,96,768]{3,2,1,0:T(8,128)(2,1)}, bf16[2,2,2...) custom-call(bf16[1024,576]{1,0:T(8,128)(2,1)} %get-tuple-element.273, ...), custom_call_target="tpu_custom_call" | custom-call | flops 2415919104 | bytes 8388608 | tf_op jit(solution)/shard_map/stage/pallas_call | solution.py:576
  466.5 0.7 reduce.5
  467.7 0.6 fusion
  469.0 0.6 reshape.239.refs_0_
  469.6 22.3 %ship.4 = (f32[36,128]{1,0:T(8,128)}, bf16[128,768]{1,0:T(8,128)(2,1)}, bf16[128,768]{1,0:T(8,128)(2,1)}, bf16[2,2,2,96,768]{4,3,2,1,0:T(8,128)(2,1)}, bf16[2,2,...) custom-call(f32[36,128]{1,0:T(8,128)} %reshape.239.refs_0_, ...), custom_call_target="tpu_custom_call" | custom-call | bytes 8388608 | tf_op jit(solution)/shard_map/ship/pallas_call | solution.py:576
  492.0 1.1 fusion.6
  493.1 0.9 pad_maximum_fusion
  494.1 0.9 pad_maximum_fusion.1
  495.0 18.7 %ship.5 = (f32[36,128]{1,0:T(8,128)}, bf16[2,2,2,96,576]{4,3,2,1,0:T(8,128)(2,1)}, bf16[2,2,2,96,768]{4,3,2,1,0:T(8,128)(2,1)}, bf16[2,2,2,48,384]{4,3,2,1,0:T(8...) custom-call(f32[36,128]{1,0:T(8,128)} %get-tuple-element.314.refs_0_, ...), custom_call_target="tpu_custom_call" | custom-call | bytes 8388608 | tf_op jit(solution)/shard_map/ship/pallas_call | solution.py:576
  513.7 8.2 %lay_out.1 = (f32[192,3072]{1,0:T(8,128)}, f32[768,768]{1,0:T(8,128)}, f32[192,3072]{1,0:T(8,128)}, f32[768,768]{1,0:T(8,128)}, f32[192,768]{1,0:T(8,128)}, /*in...) custom-call(bf16[2,2,2,96,768]{4,3,2,1,0:T(8,128)(2,1)} %get-tuple-e, ...), custom_call_target="tpu_custom_call" | custom-call | tf_op jit(solution)/shard_map/lay_out/pallas_call | solution.py:486
  522.0 0.7 fusion.35
  522.8 0.7 reshape.241
  523.4 0.7 reshape.242
  (94 shorter events, 2.3 us)
Async XLA Ops:
  0.7 60.7 %copy-start = (s32[2,8,20]{2,1,0:T(8,128)S(1)}, s32[2,8,20]{2,1,0:T(8,128)}, u32[]{:S(2)}) copy-start(s32[2,8,20]{2,1,0:T(8,128)} %param.30) | copy-start | bytes 3844
  0.7 27.3 %copy-start.4 = (bf16[2,128,768]{2,1,0:T(8,128)(2,1)S(1)}, bf16[2,128,768]{2,1,0:T(8,128)(2,1)}, u32[]{:S(2)}) copy-start(bf16[2,128,768]{2,1,0:T(8,128)(2,1)} %refs_0_.3) | copy-start | bytes 1179652
  3.4 27.1 %copy-start.5 = (bf16[2,128,768]{2,1,0:T(8,128)(2,1)S(1)}, bf16[2,128,768]{2,1,0:T(8,128)(2,1)}, u32[]{:S(2)}) copy-start(bf16[2,128,768]{2,1,0:T(8,128)(2,1)} %refs_5_.3) | copy-start | bytes 1179652
  27.9 1.8 copy-start.20
  27.9 2.6 copy-start.12
  34.2 29.2 %copy-start.19 = (s32[8,1,128]{2,1,0:T(1,128)S(1)}, s32[8,1,128]{2,1,0:T(1,128)}, u32[]{:S(2)}) copy-start(s32[8,1,128]{2,1,0:T(1,128)} %get-tuple-element.194) | copy-start | bytes 12292
  34.9 29.4 %copy-start.26 = (s32[1,256]{1,0:T(1,128)S(1)}, s32[1,256]{1,0:T(1,128)}, u32[]{:S(2)}) copy-start(s32[1,256]{1,0:T(1,128)} %constant.295) | copy-start | bytes 3076
  34.9 30.0 %copy-start.21 = (f32[4,2,8,12]{3,2,1,0:T(8,128)S(1)}, f32[4,2,8,12]{3,2,1,0:T(8,128)}, u32[]{:S(2)}) copy-start(f32[4,2,8,12]{3,2,1,0:T(8,128)} %get-tuple-element.195) | copy-start | bytes 9220
  34.9 30.0 %copy-start.27 = (s32[2048]{0:T(1024)S(1)}, s32[2048]{0:T(1024)}, u32[]{:S(2)}) copy-start(s32[2048]{0:T(1024)} %param.31) | copy-start | bytes 24580
  197.7 26.6 %copy-start.15 = (bf16[2,128,768]{2,1,0:T(8,128)(2,1)S(1)}, bf16[2,128,768]{2,1,0:T(8,128)(2,1)}, u32[]{:S(2)}) copy-start(bf16[2,128,768]{2,1,0:T(8,128)(2,1)} %get-tuple-element.210.refs_5_) | copy-start | bytes 1179652
  224.3 1.8 copy-start.11
  224.3 1.8 copy-start.13
  250.1 28.9 %copy-start.3 = (bf16[2,128,768]{2,1,0:T(8,128)(2,1)S(1)}, bf16[2,128,768]{2,1,0:T(8,128)(2,1)}, u32[]{:S(2)}) copy-start(bf16[2,128,768]{2,1,0:T(8,128)(2,1)} %get-tuple-element.226.refs_7_) | copy-start | bytes 1179652
  280.8 20.1 %copy-start.10 = (bf16[128,768]{1,0:T(8,128)(2,1)S(1)}, bf16[128,768]{1,0:T(8,128)(2,1)}, u32[]{:S(2)}) copy-start(bf16[128,768]{1,0:T(8,128)(2,1)} %get-tuple-element.237) | copy-start | bytes 589828
  280.8 20.1 %copy-start.14 = (bf16[2,128,768]{2,1,0:T(8,128)(2,1)S(1)}, bf16[2,128,768]{2,1,0:T(8,128)(2,1)}, u32[]{:S(2)}) copy-start(bf16[2,128,768]{2,1,0:T(8,128)(2,1)} %refs_6_.3) | copy-start | bytes 1179652
  327.0 32.9 %copy-start.29 = (bf16[1024,768]{1,0:T(8,128)(2,1)S(1)}, bf16[1024,768]{1,0:T(8,128)(2,1)}, u32[]{:S(2)}) copy-start(bf16[1024,768]{1,0:T(8,128)(2,1)} %get-tuple-element.260) | copy-start | bytes 4718596
  363.7 34.8 %copy-start.28 = (bf16[1024,768]{1,0:T(8,128)(2,1)S(1)}, bf16[1024,768]{1,0:T(8,128)(2,1)}, u32[]{:S(2)}) copy-start(bf16[1024,768]{1,0:T(8,128)(2,1)} %get-tuple-element.204.refs_4_) | copy-start | bytes 4718596
  398.5 4.0 copy-start.2
  398.5 4.0 copy-start.6
  439.2 28.1 %copy-start.24 = (f32[1,768]{1,0:T(1,128)S(1)}, f32[1,768]{1,0:T(1,128)}, u32[]{:S(2)}) copy-start(f32[1,768]{1,0:T(1,128)} %get-tuple-element.289) | copy-start | bytes 9220
  439.2 28.2 %copy-start.25 = (f32[1,768]{1,0:T(1,128)S(1)}, f32[1,768]{1,0:T(1,128)}, u32[]{:S(2)}) copy-start(f32[1,768]{1,0:T(1,128)} %get-tuple-element.290) | copy-start | bytes 9220
  439.2 28.3 %copy-start.23 = (f32[1,768]{1,0:T(1,128)S(1)}, f32[1,768]{1,0:T(1,128)}, u32[]{:S(2)}) copy-start(f32[1,768]{1,0:T(1,128)} %get-tuple-element.291) | copy-start | bytes 9220
  439.2 28.4 %copy-start.22 = (f32[1,768]{1,0:T(1,128)S(1)}, f32[1,768]{1,0:T(1,128)}, u32[]{:S(2)}) copy-start(f32[1,768]{1,0:T(1,128)} %get-tuple-element.292) | copy-start | bytes 9220
  439.2 28.5 %copy-start.16 = (f32[3,1,2048]{2,1,0:T(1,128)S(1)}, f32[3,1,2048]{2,1,0:T(1,128)}, u32[]{:S(2)}) copy-start(f32[3,1,2048]{2,1,0:T(1,128)} %get-tuple-element.294) | copy-start | bytes 73732
  439.2 28.5 %copy-start.17 = (f32[3,1,2048]{2,1,0:T(1,128)S(1)}, f32[3,1,2048]{2,1,0:T(1,128)}, u32[]{:S(2)}) copy-start(f32[3,1,2048]{2,1,0:T(1,128)} %get-tuple-element.293) | copy-start | bytes 73732
  469.6 22.3 %copy-start.9 = (f32[2,128,768]{2,1,0:T(8,128)S(1)}, f32[2,128,768]{2,1,0:T(8,128)}, u32[]{:S(2)}) copy-start(f32[2,128,768]{2,1,0:T(8,128)} %get-tuple-element.287) | copy-start | bytes 2359300
  492.0 2.0 copy-start.7
  492.0 2.0 copy-start.8
  513.7 8.3 %copy-start.18 = (f32[36,128]{1,0:T(8,128)S(1)}, f32[36,128]{1,0:T(8,128)}, u32[]{:S(2)}) copy-start(f32[36,128]{1,0:T(8,128)} %get-tuple-element.331) | copy-start | bytes 55300
  513.7 10.4 %copy-start.1 = (s32[2,8,20]{2,1,0:T(8,128)S(1)}, s32[2,8,20]{2,1,0:T(8,128)}, u32[]{:S(2)}) copy-start(s32[2,8,20]{2,1,0:T(8,128)} %param.30) | copy-start | bytes 3844

commit v8 on v7

--- a/solution.py
+++ b/solution.py
@@ -1339,21 +1339,21 @@
 
 
 class FeedForwardGrads:
-    n_steps = 6
-
     def __init__(self, at_stage, act, x):
-        self.at_stage, self.loads, self.raws = at_stage, [act, x], []
-        self.outs = [jax.ShapeDtypeStruct((v.shape[1], D), BF) for v in (act, x)]
-        self.outs[1] = jax.ShapeDtypeStruct((x.shape[1], act.shape[1]), BF)
+        self.at_stage, self.raws, self.both = at_stage, [], act is not None
+        self.loads = ([act] if self.both else []) + [x]
+        self.n_steps = 3 * len(self.loads)
+        self.outs = [jax.ShapeDtypeStruct((v.shape[1], D), BF) for v in self.loads]
         self.scratch = [pltpu.VMEM(o.shape, BF) for o in self.outs] + [pltpu.SemaphoreType.DMA((2,))]
 
     def begin(self, loads, raws, outs, scratch):
         self.left = [load.get() for load in loads]
-        self.right = [self.at_stage.left.rows.ref, self.at_stage.left.ref]
-        self.made, self.results, self.sems = scratch[:2], outs, scratch[2]
+        self.right = [self.at_stage.left.rows.ref] if self.both else []
+        self.right.append(self.at_stage.left.ref)
+        self.made, self.results, self.sems = scratch[:-1], outs, scratch[-1]
 
     def run(self, low, high):
-        for n in range(2):
+        for n in range(len(self.left)):
             first, last = max(low - 3 * n, 0), min(high - 3 * n, 3)
             if first < last:
 
@@ -1364,7 +1364,8 @@
 
     def end(self):
         copies = [
-            pltpu.make_async_copy(self.made[n], self.results[n], self.sems.at[n]) for n in range(2)
+            pltpu.make_async_copy(self.made[n], self.results[n], self.sems.at[n])
+            for n in range(len(self.left))
         ]
         for copy in copies:
             copy.start()
@@ -1790,24 +1791,20 @@
     k_dproj = proj_chain(g_dproj)
     k_effout = chain(mm_tn(e_act, e_up_rows).astype(BF), 0, True)
     moving = [k_dffin, k_dffout, k_cproj, k_dqkv, k_effout]
-    ((e_up, e_up_rows, dg_effn, pre_grad),), got, _ = stage(
-        12,
-        planes,
-        [
-            Stage(
-                [e_up_rows, e_pre, w_effout],
-                w_effin,
-                e_up,
-                flip=True,
-                maker=FeedForwardBack,
-                back=(e_mid, g_effn),
-                gather="low",
-            )
-        ],
-        steps_of(moving),
+    at = Stage(
+        [e_up_rows, e_pre, w_effout],
+        w_effin,
+        e_up,
+        flip=True,
+        maker=FeedForwardBack,
+        back=(e_mid, g_effn),
+        gather="low",
+    )
+    ((e_up, e_up_rows, dg_effn, _),), got, made = stage(
+        12, planes, [at], steps_of(moving), FeedForwardGrads(at, None, e_fn)
     )
     settle(moving, got)
-    k_effin = chain(mm_tn(e_fn, pre_grad).astype(BF), hidden)
+    k_effin = chain(made[0], hidden)
     k_eproj = proj_chain(mm_tn(e_att, e_up_rows).astype(BF))
     e_fill = AttentionBackward(
         parts, e_p, *e_qkv, e_up_rows, w_eproj, e_att, True, mkv, [en], False

time: 532 us -> 530 us (level)
    dot_general x4 -> x3, matrix products: 11.1 us -> 8.45 us  [mm_tn(): lax.dot_general(a, b, (((0,), (0,)), ((), ())), preferred_element_type=F32)]
where the time goes in v8:
time: 530 us; the launch traced here: 522 us
  Pallas kernels  474 us (89%)
  local copies, waits for them, and re-layouts  17.6 us (3%)
  other arithmetic  16.6 us (3%)
  matrix products  12 us (2%)
    pallas_call x17, Pallas kernels, call_with_jobs(): pl.pallas_call(body, out_shape=tuple(outs) + tuple((jax.ShapeDtypeStruct(...  464 us
    another operation x16, other arithmetic, joined(): jnp.stack([jnp.where(first, mine, came), jnp.where(first, came, mine)])  10.8 us

profile of v8, /device:TPU:0, one launch (start us, length us, event | category | flops | bytes accessed | tf_op | source)
XLA Modules:
  0.0 521.9 jit_solution(10727342013876430039)
XLA Ops:
  0.7 1.4 stacked.1
  2.1 1.3 fusion.31
  3.4 0.7 pad_maximum_fusion.10.refs_3_
  4.2 0.9 fusion.34
  5.0 0.7 pad_maximum_fusion.14.refs_4_
  5.7 22.2 %ship.3 = (bf16[128,768]{1,0:T(8,128)(2,1)}, f32[4,5,192]{2,1,0:T(8,128)}, f32[4,2,8,12]{3,2,1,0:T(8,128)}, bf16[4,96,576]{2,1,0:T(8,128)(2,1)}, bf16[4,32,384]{...) custom-call(bf16[2,128,768]{2,1,0:T(8,128)(2,1)} %refs_0_.3, f32[5,192]{1,0:T(8,128)} %get-tuple-element.183.refs_1_, ...), custom_call_target="tpu_custom_call" | custom-call | bytes 8388608 | tf_op jit(solution)/shard_map/ship/pallas_call | solution.py:576
  28.0 1.0 fusion.20
  29.0 0.8 pad_maximum_fusion.2.refs_0_.refs_2_.refs_4_
  29.8 0.7 reshape_squeeze.21.refs_1_.refs_3_
  30.5 0.8 pad_maximum_fusion.3.refs_2_.refs_4_
  31.3 0.7 reshape_squeeze.22.refs_3_
  32.0 0.7 pad_maximum_fusion.11.refs_6_
  32.7 1.4 fusion.29
  34.2 0.8 pad_maximum_fusion.8.refs_7_
  34.9 24.7 %stage.11 = (bf16[1024,768]{1,0:T(8,128)(2,1)}, bf16[1024,768]{1,0:T(8,128)(2,1)}, bf16[4,2,96,576]{3,2,1,0:T(8,128)(2,1)}, bf16[4,2,32,384]{3,2,1,0:T(8,128)(2,...) custom-call(bf16[2,128,768]{2,1,0:T(8,128)(2,1)} %pad_maximum_fusion.2.refs_0_.refs_2_.refs_4_, ...), custom_call_target="tpu_custom_call" | custom-call | flops 2000000 | bytes 8388608 | tf_op jit(solution)/shard_map/stage/pallas_call | solution.py:576
  59.6 1.7 constant_dynamic-slice_fusion.1
  61.5 1.9 convolution_convert_fusion.3.refs_5_.refs_16_
  63.3 1.0 copy.52.refs_6_.refs_11_
  64.4 0.6 pad_add_fusion.refs_7_
  65.0 0.5 fusion.2
  65.5 0.6 reshape.212.refs_8_
  66.2 22.6 %attend.3 = (bf16[4,2,96,576]{3,2,1,0:T(8,128)(2,1)}, bf16[4,96,768]{2,1,0:T(8,128)(2,1)}, bf16[192,768]{1,0:T(8,128)(2,1)}, bf16[1024,192]{1,0:T(8,128)(2,1)}, ...) custom-call(bf16[4,96,576]{2,1,0:T(8,128)(2,1)} %get-tuple-element.190.refs_0_, ...), custom_call_target="tpu_custom_call" | custom-call | flops 4000000000 | bytes 8388608 | tf_op jit(solution)/shard_map/attend/pallas_call | solution.py:576
  88.8 0.7 reshape_squeeze.24.refs_3_.refs_5_
  89.4 1.6 dynamic_slice.129.refs_6_
  91.0 1.0 fusion.33
  92.1 0.7 pad_maximum_fusion.12.refs_7_
  92.8 0.5 fusion.1
  93.3 0.6 reshape.214.refs_13_
  93.9 36.7 %stage.12 = (f32[2,128,768]{2,1,0:T(8,128)}, bf16[1024,768]{1,0:T(8,128)(2,1)}, bf16[4,2,96,768]{3,2,1,0:T(8,128)(2,1)}, bf16[4,2,96,768]{3,2,1,0:T(8,128)(2,1)}...) custom-call(bf16[1024,192]{1,0:T(8,128)(2,1)} %get-tuple-element.196, ...), custom_call_target="tpu_custom_call" | custom-call | flops 2415919104 | bytes 8388608 | tf_op jit(solution)/shard_map/stage/pallas_call | solution.py:576
  130.7 0.7 reshape_squeeze.26.refs_3_
  131.3 0.8 pad_maximum_fusion.9.refs_10_
  132.1 48.5 %stage.13 = (f32[2,128,768]{2,1,0:T(8,128)}, bf16[1024,768]{1,0:T(8,128)(2,1)}, bf16[2,128,768]{2,1,0:T(8,128)(2,1)}, bf16[1024,768]{1,0:T(8,128)(2,1)}, f32[102...) custom-call(bf16[1024,192]{1,0:T(8,128)(2,1)} %get-tuple-element.202, ...), custom_call_target="tpu_custom_call" | custom-call | flops 4831838208 | bytes 8388608 | tf_op jit(solution)/shard_map/stage/pallas_call | solution.py:576
  180.6 16.4 %attend.4 = (bf16[4,2,96,768]{3,2,1,0:T(8,128)(2,1)}, bf16[192,768]{1,0:T(8,128)(2,1)}, bf16[1024,192]{1,0:T(8,128)(2,1)}, bf16[3,1024,1024]{2,1,0:T(8,128)(2,1)...) custom-call(bf16[4,96,768]{2,1,0:T(8,128)(2,1)} %get-tuple-element.211.refs_0_, bf16[192,768]{1,0:T(8,128)(2,1)} %refs_1_.3, ...), custom_call_target="tpu_custom_call" | custom-call | flops 4000000000 | bytes 8388608 | tf_op jit(solution)/shard_map/attend/pallas_call | solution.py:576
  197.0 0.7 reshape_squeeze.27.refs_3_.refs_5_
  197.7 26.6 %stage.14 = (f32[2,128,768]{2,1,0:T(8,128)}, bf16[1024,768]{1,0:T(8,128)(2,1)}, bf16[4,2,96,768]{3,2,1,0:T(8,128)(2,1)}, bf16[128,768]{1,0:T(8,128)(2,1)}, bf16[128,768]{1,0:T(8,128)(2,1)}) custom-call(bf16[1024,192]{1,0:T(8,128)(2,1)} %get-tuple-element.216.refs_0_.refs_5_, bf16[192,768]{1,0:T(8,128)(2,1)} %get-tuple-element.217.refs_1_.refs_4_, ...), custom_call_target="tpu_custom_call" | custom-call | flops 2415919104 | bytes 8388608 | tf_op jit(solution)/shard_map/stage/pallas_call | solution.py:576
  224.3 1.0 fusion.16
  225.3 0.8 pad_maximum_fusion.4
  226.2 0.8 pad_maximum_fusion.5.refs_4_
  226.9 23.1 %stage.15 = (bf16[2,128,768]{2,1,0:T(8,128)(2,1)}, bf16[1024,768]{1,0:T(8,128)(2,1)}, f32[1024,768]{1,0:T(8,128)}, bf16[1024,768]{1,0:T(8,128)(2,1)}) custom-call(bf16[1024,768]{1,0:T(8,128)(2,1)} %get-tuple-element.221.refs_0_.refs_9_, bf16[768,768]{1,0:T(8,128)(2,1)} %bitcast.124, bf16[768,768]{1,0:T(8,128)(2,1)} %bitcast.126, ...), custom_call_target="tpu_custom_call" | custom-call | flops 2415919104 | bytes 8388608 | tf_op jit(solution)/shard_map/stage/pallas_call | solution.py:576
  250.1 28.9 %stage.16 = (f32[2,128,768]{2,1,0:T(8,128)}, bf16[1024,768]{1,0:T(8,128)(2,1)}, f32[1,768]{1,0:T(1,128)}, bf16[1024,768]{1,0:T(8,128)(2,1)}, bf16[128,768]{1,0:T...) custom-call(bf16[1024,768]{1,0:T(8,128)(2,1)} %get-tuple-element.227.refs_0_, ...), custom_call_target="tpu_custom_call" | custom-call | flops 2415919104 | bytes 8388608 | tf_op jit(solution)/shard_map/stage/pallas_call | solution.py:576
  279.0 1.0 fusion.12
  279.9 0.8 pad_maximum_fusion.6
  280.7 20.1 %attend.5 = (bf16[4,96,768]{2,1,0:T(8,128)(2,1)}, bf16[1024,192]{1,0:T(8,128)(2,1)}, bf16[1024,384]{1,0:T(8,128)(2,1)}, bf16[192,768]{1,0:T(8,128)(2,1)}, bf16[7...) custom-call(bf16[4,2,96,768]{3,2,1,0:T(8,128)(2,1)} %bitcast.152, bf16[1024,192]{1,0:T(8,128)(2,1)} %get-tuple-element.232.refs_1_, ...), custom_call_target="tpu_custom_call" | custom-call | flops 4000000000 | bytes 8388608 | tf_op jit(solution)/shard_map/attend/pallas_call | solution.py:576
  300.8 0.8 pad_maximum_fusion.7.refs_2_
  301.6 25.4 %stage.17 = (f32[2,128,768]{2,1,0:T(8,128)}, bf16[1024,768]{1,0:T(8,128)(2,1)}, f32[1,768]{1,0:T(1,128)}, bf16[96,768]{1,0:T(8,128)(2,1)}, bf16[4,96,192]{2,1,0:...) custom-call(bf16[1024,192]{1,0:T(8,128)(2,1)} %get-tuple-element.239.refs_0_, ...), custom_call_target="tpu_custom_call" | custom-call | flops 2415919104 | bytes 8388608 | tf_op jit(solution)/shard_map/stage/pallas_call | solution.py:576
  327.0 32.8 %stage.18 = (f32[2,128,768]{2,1,0:T(8,128)}, bf16[1024,768]{1,0:T(8,128)(2,1)}, bf16[4,96,768]{2,1,0:T(8,128)(2,1)}, bf16[96,192]{1,0:T(8,128)(2,1)}, bf16[96,38...) custom-call(bf16[1024,384]{1,0:T(8,128)(2,1)} %get-tuple-element.236, ...), custom_call_target="tpu_custom_call" | custom-call | flops 2415919104 | bytes 8388608 | tf_op jit(solution)/shard_map/stage/pallas_call | solution.py:576
  359.8 3.9 convolution_convert_fusion
  363.7 34.7 %stage.19 = (f32[2,128,768]{2,1,0:T(8,128)}, bf16[1024,768]{1,0:T(8,128)(2,1)}, f32[1,768]{1,0:T(1,128)}, bf16[1024,768]{1,0:T(8,128)(2,1)}, bf16[96,768]{1,0:T(...) custom-call(bf16[1024,768]{1,0:T(8,128)(2,1)} %get-tuple-element.253, ...), custom_call_target="tpu_custom_call" | custom-call | flops 2415919104 | bytes 8388608 | tf_op jit(solution)/shard_map/stage/pallas_call | solution.py:576
  398.4 2.6 convolution_convert_fusion.1
  401.0 33.5 %stage.20 = (f32[2,128,768]{2,1,0:T(8,128)}, f32[1,768]{1,0:T(1,128)}, bf16[2,128,768]{2,1,0:T(8,128)(2,1)}, bf16[2,96,768]{2,1,0:T(8,128)(2,1)}, bf16[2,2,96,76...) custom-call(bf16[1024,576]{1,0:T(8,128)(2,1)} %get-tuple-element.251, ...), custom_call_target="tpu_custom_call" | custom-call | flops 2415919104 | bytes 8388608 | tf_op jit(solution)/shard_map/stage/pallas_call | solution.py:576
  434.6 2.0 convolution_convert_fusion.2
  436.6 27.0 %stage.21 = (f32[2,128,768]{2,1,0:T(8,128)}, f32[1,768]{1,0:T(1,128)}, bf16[2,128,768]{2,1,0:T(8,128)(2,1)}, bf16[2,2,96,768]{3,2,1,0:T(8,128)(2,1)}, bf16[2,2,2...) custom-call(bf16[1024,576]{1,0:T(8,128)(2,1)} %get-tuple-element.273, ...), custom_call_target="tpu_custom_call" | custom-call | flops 2415919104 | bytes 8388608 | tf_op jit(solution)/shard_map/stage/pallas_call | solution.py:576
  463.6 0.7 reduce.5
  464.8 0.6 fusion
  466.1 0.6 reshape.239.refs_0_
  466.7 22.5 %ship.4 = (f32[36,128]{1,0:T(8,128)}, bf16[128,768]{1,0:T(8,128)(2,1)}, bf16[128,768]{1,0:T(8,128)(2,1)}, bf16[2,2,2,96,768]{4,3,2,1,0:T(8,128)(2,1)}, bf16[2,2,...) custom-call(f32[36,128]{1,0:T(8,128)} %reshape.239.refs_0_, ...), custom_call_target="tpu_custom_call" | custom-call | bytes 8388608 | tf_op jit(solution)/shard_map/ship/pallas_call | solution.py:576
  489.2 1.1 fusion.6
  490.3 0.9 pad_maximum_fusion
  491.3 0.9 pad_maximum_fusion.1
  492.3 18.7 %ship.5 = (f32[36,128]{1,0:T(8,128)}, bf16[2,2,2,96,576]{4,3,2,1,0:T(8,128)(2,1)}, bf16[2,2,2,96,768]{4,3,2,1,0:T(8,128)(2,1)}, bf16[2,2,2,48,384]{4,3,2,1,0:T(8...) custom-call(f32[36,128]{1,0:T(8,128)} %get-tuple-element.314.refs_0_, ...), custom_call_target="tpu_custom_call" | custom-call | bytes 8388608 | tf_op jit(solution)/shard_map/ship/pallas_call | solution.py:576
  511.0 8.2 %lay_out.1 = (f32[192,3072]{1,0:T(8,128)}, f32[768,768]{1,0:T(8,128)}, f32[192,3072]{1,0:T(8,128)}, f32[768,768]{1,0:T(8,128)}, f32[192,768]{1,0:T(8,128)}, /*in...) custom-call(bf16[2,2,2,96,768]{4,3,2,1,0:T(8,128)(2,1)} %get-tuple-e, ...), custom_call_target="tpu_custom_call" | custom-call | tf_op jit(solution)/shard_map/lay_out/pallas_call | solution.py:486
  519.3 0.7 fusion.35
  520.0 0.7 reshape.241
  520.7 0.7 reshape.242
  (89 shorter events, 1.7 us)
Async XLA Ops:
  0.7 60.7 %copy-start = (s32[2,8,20]{2,1,0:T(8,128)S(1)}, s32[2,8,20]{2,1,0:T(8,128)}, u32[]{:S(2)}) copy-start(s32[2,8,20]{2,1,0:T(8,128)} %param.30) | copy-start | bytes 3844
  0.7 27.3 %copy-start.3 = (bf16[2,128,768]{2,1,0:T(8,128)(2,1)S(1)}, bf16[2,128,768]{2,1,0:T(8,128)(2,1)}, u32[]{:S(2)}) copy-start(bf16[2,128,768]{2,1,0:T(8,128)(2,1)} %refs_0_.3) | copy-start | bytes 1179652
  3.4 27.1 %copy-start.4 = (bf16[2,128,768]{2,1,0:T(8,128)(2,1)S(1)}, bf16[2,128,768]{2,1,0:T(8,128)(2,1)}, u32[]{:S(2)}) copy-start(bf16[2,128,768]{2,1,0:T(8,128)(2,1)} %refs_5_.3) | copy-start | bytes 1179652
  27.9 1.8 copy-start.19
  27.9 2.6 copy-start.11
  34.2 29.2 %copy-start.18 = (s32[8,1,128]{2,1,0:T(1,128)S(1)}, s32[8,1,128]{2,1,0:T(1,128)}, u32[]{:S(2)}) copy-start(s32[8,1,128]{2,1,0:T(1,128)} %get-tuple-element.194) | copy-start | bytes 12292
  34.9 29.4 %copy-start.25 = (s32[1,256]{1,0:T(1,128)S(1)}, s32[1,256]{1,0:T(1,128)}, u32[]{:S(2)}) copy-start(s32[1,256]{1,0:T(1,128)} %constant.295) | copy-start | bytes 3076
  34.9 30.0 %copy-start.20 = (f32[4,2,8,12]{3,2,1,0:T(8,128)S(1)}, f32[4,2,8,12]{3,2,1,0:T(8,128)}, u32[]{:S(2)}) copy-start(f32[4,2,8,12]{3,2,1,0:T(8,128)} %get-tuple-element.195) | copy-start | bytes 9220
  34.9 30.0 %copy-start.26 = (s32[2048]{0:T(1024)S(1)}, s32[2048]{0:T(1024)}, u32[]{:S(2)}) copy-start(s32[2048]{0:T(1024)} %param.31) | copy-start | bytes 24580
  197.7 26.6 %copy-start.14 = (bf16[2,128,768]{2,1,0:T(8,128)(2,1)S(1)}, bf16[2,128,768]{2,1,0:T(8,128)(2,1)}, u32[]{:S(2)}) copy-start(bf16[2,128,768]{2,1,0:T(8,128)(2,1)} %get-tuple-element.210.refs_5_) | copy-start | bytes 1179652
  224.3 1.8 copy-start.10
  224.3 1.8 copy-start.12
  250.1 28.9 %copy-start.2 = (bf16[2,128,768]{2,1,0:T(8,128)(2,1)S(1)}, bf16[2,128,768]{2,1,0:T(8,128)(2,1)}, u32[]{:S(2)}) copy-start(bf16[2,128,768]{2,1,0:T(8,128)(2,1)} %get-tuple-element.226.refs_7_) | copy-start | bytes 1179652
  280.7 20.1 %copy-start.9 = (bf16[128,768]{1,0:T(8,128)(2,1)S(1)}, bf16[128,768]{1,0:T(8,128)(2,1)}, u32[]{:S(2)}) copy-start(bf16[128,768]{1,0:T(8,128)(2,1)} %get-tuple-element.237) | copy-start | bytes 589828
  280.7 20.1 %copy-start.13 = (bf16[2,128,768]{2,1,0:T(8,128)(2,1)S(1)}, bf16[2,128,768]{2,1,0:T(8,128)(2,1)}, u32[]{:S(2)}) copy-start(bf16[2,128,768]{2,1,0:T(8,128)(2,1)} %refs_6_.3) | copy-start | bytes 1179652
  327.0 32.8 %copy-start.27 = (bf16[1024,768]{1,0:T(8,128)(2,1)S(1)}, bf16[1024,768]{1,0:T(8,128)(2,1)}, u32[]{:S(2)}) copy-start(bf16[1024,768]{1,0:T(8,128)(2,1)} %get-tuple-element.260) | copy-start | bytes 4718596
  363.7 34.7 %copy-start.5 = (bf16[1024,192]{1,0:T(8,128)(2,1)S(1)}, bf16[1024,192]{1,0:T(8,128)(2,1)}, u32[]{:S(2)}) copy-start(bf16[1024,192]{1,0:T(8,128)(2,1)} %get-tuple-element.196.refs_0_.refs_19_) | copy-start | bytes 1179652
  436.5 27.8 %copy-start.23 = (f32[1,768]{1,0:T(1,128)S(1)}, f32[1,768]{1,0:T(1,128)}, u32[]{:S(2)}) copy-start(f32[1,768]{1,0:T(1,128)} %get-tuple-element.289) | copy-start | bytes 9220
  436.5 27.9 %copy-start.24 = (f32[1,768]{1,0:T(1,128)S(1)}, f32[1,768]{1,0:T(1,128)}, u32[]{:S(2)}) copy-start(f32[1,768]{1,0:T(1,128)} %get-tuple-element.290) | copy-start | bytes 9220
  436.5 28.0 %copy-start.22 = (f32[1,768]{1,0:T(1,128)S(1)}, f32[1,768]{1,0:T(1,128)}, u32[]{:S(2)}) copy-start(f32[1,768]{1,0:T(1,128)} %get-tuple-element.291) | copy-start | bytes 9220
  436.5 28.1 %copy-start.21 = (f32[1,768]{1,0:T(1,128)S(1)}, f32[1,768]{1,0:T(1,128)}, u32[]{:S(2)}) copy-start(f32[1,768]{1,0:T(1,128)} %get-tuple-element.292) | copy-start | bytes 9220
  436.5 28.2 %copy-start.15 = (f32[3,1,2048]{2,1,0:T(1,128)S(1)}, f32[3,1,2048]{2,1,0:T(1,128)}, u32[]{:S(2)}) copy-start(f32[3,1,2048]{2,1,0:T(1,128)} %get-tuple-element.294) | copy-start | bytes 73732
  436.5 28.2 %copy-start.16 = (f32[3,1,2048]{2,1,0:T(1,128)S(1)}, f32[3,1,2048]{2,1,0:T(1,128)}, u32[]{:S(2)}) copy-start(f32[3,1,2048]{2,1,0:T(1,128)} %get-tuple-element.293) | copy-start | bytes 73732
  466.7 22.5 %copy-start.8 = (f32[2,128,768]{2,1,0:T(8,128)S(1)}, f32[2,128,768]{2,1,0:T(8,128)}, u32[]{:S(2)}) copy-start(f32[2,128,768]{2,1,0:T(8,128)} %get-tuple-element.287) | copy-start | bytes 2359300
  489.2 2.0 copy-start.6
  489.2 2.0 copy-start.7
  511.0 8.3 %copy-start.17 = (f32[36,128]{1,0:T(8,128)S(1)}, f32[36,128]{1,0:T(8,128)}, u32[]{:S(2)}) copy-start(f32[36,128]{1,0:T(8,128)} %get-tuple-element.331) | copy-start | bytes 55300
  511.0 10.4 %copy-start.1 = (s32[2,8,20]{2,1,0:T(8,128)S(1)}, s32[2,8,20]{2,1,0:T(8,128)}, u32[]{:S(2)}) copy-start(s32[2,8,20]{2,1,0:T(8,128)} %param.30) | copy-start | bytes 3844
